TPU v7x, 512 devices: a whole 4x8x8 slice. The times are simulated.
512 devices in a mesh: outer: 16 (over x_lo, z), inner: 32 (over x_hi, y, core).
Axes of the slice: x: 4 (x_hi: 2, x_lo: 2; x = x_hi * 2 + x_lo), y: 8, z: 8, core: 2. Of those that a mesh axis runs over, the one named last changes fastest.
Arguments:
- video: bfloat16 [1536, 32, 256], P(('outer', 'inner')), as said below
- gloss: bfloat16 [1536, 16, 256], P(('outer', 'inner'))
- frame_count: int32 [1536], P(('outer', 'inner')), may hold values from 1 to 32
- gloss_count: int32 [1536], P(('outer', 'inner')), may hold values from 1 to 16
Outputs:
- loss_mean: float32 [], replicated
- grad_video: float32 [1536, 32, 256], P(('outer', 'inner'))
- grad_gloss: float32 [1536, 16, 256], P(('outer', 'inner'))
Inputs may be any that keep to these rules, and one draw needn't show every extreme that they name: `video`: embeddings of a clip's frames and of its text share a per-clip component; clips differ in it.
All inputs are finite; a program needn't handle non-finite values.
Results may differ from a plain program's by a relative error of at most 0.0045.
Values may be sent and summed in bfloat16 or wider, within the bound.
No kernel may reach another device: no remote copies, remote signals or barrier semaphores. Data moves between devices by JAX's collectives and lax.ppermute only.
A program may use at most 64 MiB of HBM per device.

v0:
```python
import math

import jax
import jax.numpy as jnp
from jax import lax
from jax.sharding import PartitionSpec as P

SOFTMAX_TEMPER = 0.1
LOGIT_SCALE = 10.0
EPSILON = 1e-06


def unit_tokens(raw):
    values = raw.astype(jnp.float32)
    mean_sq = jnp.mean(values * values, axis=-1, keepdims=True) + EPSILON
    factor = lax.rsqrt(mean_sq) / math.sqrt(values.shape[-1])
    return ((values * factor).astype(jnp.bfloat16), values, factor)


def unit_grad(grad_unit, values, factor):
    features = values.shape[-1]
    mean_sq = jnp.mean(values * values, axis=-1, keepdims=True) + EPSILON
    inner_sum = jnp.sum(grad_unit * values, axis=-1, keepdims=True)
    return factor * grad_unit - factor * values * inner_sum / (features * mean_sq)


def block_size(count, limit):
    best = 1
    for candidate in range(1, count + 1):
        if count % candidate == 0 and candidate <= limit:
            best = candidate
    return best


def block_parts(clip_units, video_clip_counts, text_units, gloss_text_counts):
    video_clip_total, frame_tokens, features = clip_units.shape
    gloss_text_total, gloss_tokens, _ = text_units.shape
    similarity_scores = lax.dot_general(
        clip_units.reshape(video_clip_total * frame_tokens, features),
        text_units.reshape(gloss_text_total * gloss_tokens, features),
        (((1,), (1,)), ((), ())),
        preferred_element_type=jnp.float32,
    )
    softmax_weights = jnp.exp(
        similarity_scores.reshape(video_clip_total, frame_tokens, gloss_text_total, gloss_tokens)
        / SOFTMAX_TEMPER
    )
    video_frame_mask = (
        jnp.arange(frame_tokens, dtype=jnp.float32)[None, :] < video_clip_counts[:, None]
    ).astype(jnp.float32)
    gloss_token_mask = (
        jnp.arange(gloss_tokens, dtype=jnp.float32)[None, :] < gloss_text_counts[:, None]
    ).astype(jnp.float32)
    row_totals = jnp.sum(softmax_weights * gloss_token_mask[None, None], axis=3)
    column_totals = jnp.sum(softmax_weights * video_frame_mask[:, :, None, None], axis=1)
    video_direction = (
        jnp.sum(
            video_frame_mask[:, :, None]
            * SOFTMAX_TEMPER
            * jnp.log(row_totals / gloss_text_counts[None, None, :]),
            axis=1,
        )
        / video_clip_counts[:, None]
    )
    text_direction = (
        jnp.sum(
            gloss_token_mask[None]
            * SOFTMAX_TEMPER
            * jnp.log(column_totals / video_clip_counts[:, None, None]),
            axis=2,
        )
        / gloss_text_counts[None, :]
    )
    logits = LOGIT_SCALE * 0.5 * (video_direction + text_direction)
    return (logits, softmax_weights, row_totals, column_totals, video_frame_mask, gloss_token_mask)


def block_grads(clip_units, video_clip_counts, text_units, gloss_text_counts, pair_grad):
    video_clip_total, frame_tokens, features = clip_units.shape
    gloss_text_total, gloss_tokens, _ = text_units.shape
    logits, softmax_weights, row_totals, column_totals, video_frame_mask, gloss_token_mask = (
        block_parts(clip_units, video_clip_counts, text_units, gloss_text_counts)
    )
    valid = video_frame_mask[:, :, None, None] * gloss_token_mask[None, None]
    row_part = (
        valid * softmax_weights / row_totals[..., None] / video_clip_counts[:, None, None, None]
    )
    col_part = (
        valid * softmax_weights / column_totals[:, None] / gloss_text_counts[None, None, :, None]
    )
    score_grad = (0.5 * LOGIT_SCALE * pair_grad[:, None, :, None] * (row_part + col_part)).astype(
        jnp.bfloat16
    )
    score_grad = score_grad.reshape(
        video_clip_total * frame_tokens, gloss_text_total * gloss_tokens
    )
    clip_grad = jnp.dot(
        score_grad,
        text_units.reshape(gloss_text_total * gloss_tokens, features),
        preferred_element_type=jnp.float32,
    )
    text_grad = lax.dot_general(
        score_grad,
        clip_units.reshape(video_clip_total * frame_tokens, features),
        (((0,), (0,)), ((), ())),
        preferred_element_type=jnp.float32,
    )
    return (clip_grad, text_grad)


def on_device(video, gloss, frame_count, gloss_count):
    clips_dev, frame_tokens, features = video.shape
    gloss_tokens = gloss.shape[1]
    n_outer = lax.axis_size("outer")
    n_inner = lax.axis_size("inner")
    outer_at = lax.axis_index("outer")
    inner_at = lax.axis_index("inner")
    clips_all = clips_dev * n_outer * n_inner
    unit_v, video_f, video_fac = unit_tokens(video)
    unit_g, gloss_f, gloss_fac = unit_tokens(gloss)
    frame_half = frame_count.astype(jnp.bfloat16)
    gloss_half = gloss_count.astype(jnp.bfloat16)
    group_ids = outer_at * (n_inner * clips_dev) + jnp.arange(n_inner * clips_dev, dtype=jnp.int32)
    strided_ids = (
        (jnp.arange(n_outer, dtype=jnp.int32)[:, None] * n_inner + inner_at) * clips_dev
        + jnp.arange(clips_dev, dtype=jnp.int32)[None, :]
    ).reshape(-1)
    clip_units, clip_half = (
        lax.all_gather(unit_v, "inner", axis=0, tiled=True),
        lax.all_gather(frame_half, "inner", axis=0, tiled=True),
    )
    text_units, text_half = (
        lax.all_gather(unit_g, "outer", axis=0, tiled=True),
        lax.all_gather(gloss_half, "outer", axis=0, tiled=True),
    )
    video_clip_counts = clip_half.astype(jnp.float32)
    gloss_text_counts = text_half.astype(jnp.float32)
    video_clip_total = clip_units.shape[0]
    gloss_text_total = text_units.shape[0]
    block = block_size(video_clip_total, max(1, 512 // frame_tokens))
    blocks = video_clip_total // block
    clip_blocks = clip_units.reshape(blocks, block, frame_tokens, features)
    count_blocks = video_clip_counts.reshape(blocks, block)
    logits = lax.map(
        lambda pieces: block_parts(pieces[0], pieces[1], text_units, gloss_text_counts)[0],
        (clip_blocks, count_blocks),
    ).reshape(video_clip_total, gloss_text_total)
    exp_logits = jnp.exp(logits)
    matched = (group_ids[:, None] == strided_ids[None, :]).astype(jnp.float32)
    empty = jnp.zeros((clips_all,), jnp.float32)
    row_part = empty.at[group_ids].add(jnp.sum(exp_logits, axis=1))
    col_part = empty.at[strided_ids].add(jnp.sum(exp_logits, axis=0))
    row_all, col_all = lax.psum((row_part, col_part), ("outer", "inner"))
    local_term = 0.5 * jnp.sum(
        matched
        * (
            jnp.log(row_all[group_ids])[:, None]
            + jnp.log(col_all[strided_ids])[None, :]
            - 2.0 * logits
        )
    )
    loss_mean = lax.psum(local_term, ("outer", "inner")) / clips_all
    pair_grad = (
        0.5
        * (exp_logits / row_all[group_ids][:, None] + exp_logits / col_all[strided_ids][None, :])
        - matched
    )

    def backward_step(text_acc, pieces):
        clip_grad, text_grad = block_grads(
            pieces[0], pieces[1], text_units, gloss_text_counts, pieces[2]
        )
        return (text_acc + text_grad, clip_grad)

    text_sum, clip_grads = lax.scan(
        backward_step,
        jnp.zeros((gloss_text_total * gloss_tokens, features), jnp.float32),
        (clip_blocks, count_blocks, pair_grad.reshape(blocks, block, gloss_text_total)),
    )
    clip_grads = clip_grads.reshape(video_clip_total, frame_tokens, features)
    text_sum = text_sum.reshape(gloss_text_total, gloss_tokens, features)
    own_video = lax.psum_scatter(clip_grads, "inner", scatter_dimension=0, tiled=True)
    own_gloss = lax.psum_scatter(text_sum, "outer", scatter_dimension=0, tiled=True)
    grad_video = unit_grad(own_video, video_f, video_fac)
    grad_gloss = unit_grad(own_gloss, gloss_f, gloss_fac)
    return (loss_mean, grad_video, grad_gloss)


def solution(mesh):
    in_specs = (
        P(("outer", "inner"), None, None),
        P(("outer", "inner"), None, None),
        P(("outer", "inner")),
        P(("outer", "inner")),
    )
    out_specs = (P(), P(("outer", "inner"), None, None), P(("outer", "inner"), None, None))
    return jax.shard_map(
        on_device, mesh=mesh, in_specs=in_specs, out_specs=out_specs, check_vma=False
    )
```

profile of v0, /device:TPU:16, one launch (start us, length us, event | category | flops | bytes accessed | tf_op | source)
XLA Modules:
  0.0 609.3 jit_solution(9710953599931029710)
XLA Ops:
  12.8 59.6 %all-reduce = bf16[96]{0:T(256)(128)(2,1)S(1)} all-reduce(bf16[96]{0:T(256)(128)(2,1)S(1)} %dynamic-update-slice), channel_id=1, replica_groups=mesh['outer'=16,'inner'=32] {'inner'}, use_global_device_ids=true, to_apply=%add | all-reduce | flops 96 | bytes 384
  75.3 39.7 %all-reduce.1 = bf16[48]{0:T(256)(128)(2,1)S(1)} all-reduce(bf16[48]{0:T(256)(128)(2,1)S(1)} %dynamic-update-slice.1), channel_id=1, replica_groups=mesh['outer'=16,'inner'=32] {'outer'}, use_global_device_ids=true, to_apply=%add.1 | all-reduce | flops 48 | bytes 192
  116.7 31.6 %all_gather.14 = bf16[48,16,256]{2,1,0:T(8,128)(2,1)S(1)} all-gather(bf16[3,16,256]{2,1,0:T(8,128)(2,1)S(1)} %fusion.39), channel_id=1, replica_groups=mesh['outer'=16,'inner'=32] {'outer'}, dimensions={0}, use_global_device_ids=true | all-gather | bytes 417792 | tf_op jit(solution)/shard_map/all_gather | solution.py:133
  148.5 19.5 %while.25 = (s32[]{:T(128)}, f32[6,16,48]{2,1,0:T(8,128)S(1)}, f32[6,16]{1,0:T(8,128)S(1)}, bf16[6,16,32,256]{3,2,1,0:T(8,128)(2,1)}, bf16[48,16,256]{2,0,1:T(8,128)(2,1)S(1)}, /*index=5*/f32[48]{0:T(128)S(1)}) while((s32[]{:T(128)}, f32[6,16,48]{2,1,0:T(8,128)S(1)}, f32[6,16]{1,0:T(8,128)S(1)}, ...), condition=%wide.region_7.8_spmd.clone, body=%wide.region_2.7_spmd.sunk.clone | while | flops 203373056 | bytes 1003981 | solution.py:144
  148.6 2.7 multiply_reduce_fusion.14
  151.9 2.7 multiply_reduce_fusion.14
  155.1 2.7 multiply_reduce_fusion.14
  158.4 2.7 multiply_reduce_fusion.14
  161.6 2.7 multiply_reduce_fusion.14
  164.9 2.7 multiply_reduce_fusion.14
  170.3 103.3 %all-reduce.2 = (f32[1536]{0:T(1024)S(1)}, f32[1536]{0:T(1024)S(1)}) all-reduce(f32[1536]{0:T(1024)S(1)} %scatter_custom_fusion.1, f32[1536]{0:T(1024)S(1)} %scatter_custom_fusion), channel_id=1, replica_groups=mesh['outer'=16,'inner'=32] {'outer','inner'}, use_global_device_ids=true, to_apply=%region_13.14 | all-reduce | flops 3072 | bytes 24576 | tf_op jit(solution)/shard_map/psum | solution.py:153
  276.3 122.3 %while.26 = (s32[]{:T(128)}, f32[768,256]{1,0:T(8,128)}, f32[6,512,256]{2,1,0:T(8,128)}, f32[6,16,48]{2,1,0:T(8,128)S(1)}, f32[6,16]{1,0:T(8,128)S(1)}, /*index=...) while((s32[]{:T(128)}, f32[768,256]{1,0:T(8,128)}, ...), condition=%wide.region_19.20_spmd.clone.clone, body=%wide.region_16.19_spmd.clone.sunk.clone | while | flops 610262272 | bytes 15949091 | solution.py:175
  278.8 3.0 multiply_convert_fusion.3
  281.9 6.0 copy.33
  287.9 3.8 reshape.478
  299.0 3.0 multiply_convert_fusion.3
  302.0 6.0 copy.33
  308.0 3.8 reshape.478
  319.4 3.0 multiply_convert_fusion.3
  322.5 6.0 copy.33
  328.4 3.8 reshape.478
  339.8 3.0 multiply_convert_fusion.3
  342.9 6.0 copy.33
  348.9 3.8 reshape.478
  360.2 3.0 multiply_convert_fusion.3
  363.3 6.0 copy.33
  369.3 3.8 reshape.478
  380.7 3.0 multiply_convert_fusion.3
  383.7 6.0 copy.33
  389.7 3.8 reshape.478
  400.0 95.1 %psum.23 = f32[]{:T(128)} all-reduce(f32[]{:T(128)S(6)} %mul.233), channel_id=1, replica_groups=mesh['outer'=16,'inner'=32] {'outer','inner'}, use_global_device_ids=true, to_apply=%region_15.16 | all-reduce | flops 1 | bytes 8 | tf_op jit(solution)/shard_map/psum | solution.py:162
  497.5 102.3 %reduce-scatter.3.cloned.1.call-done = f32[3,32,256]{2,1,0:T(8,128)} async-done(((f32[96,32,256]{2,1,0:T(8,128)}), f32[3,32,256]{2,1,0:T(8,128)}) %reduce-scatter.3.cloned.1.call-update) | async-done | bytes 98320 | tf_op jit(solution)/shard_map/reduce_scatter | solution.py:182
  (173 shorter events, 66.7 us)
Async XLA Ops:
  7.2 141.3 %all-gather.2.cloned.1.call-start = ((), (), s32[]{:S(2)}) async-start(), calls=%async_computation.2 | async-start | bytes 1622016 | tf_op jit(solution)/shard_map/all_gather | solution.py:129
  9.6 486.1 %reduce-scatter.5.cloned.1.call-start = ((), (), s32[]{:S(2)}) async-start(), calls=%async_computation.4 | async-start | bytes 835584 | tf_op jit(solution)/shard_map/reduce_scatter | solution.py:183
  276.3 219.5 %copy-start.3 = (bf16[3,16,256]{2,1,0:T(8,128)(2,1)S(1)}, bf16[3,16,256]{2,1,0:T(8,128)(2,1)}, u32[]{:S(2)}) copy-start(bf16[3,16,256]{2,1,0:T(8,128)(2,1)} %param.9) | copy-start | bytes 73732
  276.3 2.5 copy-start
  291.6 4.9 copy-start.1
  296.5 2.5 copy-start
  311.8 5.1 copy-start.1
  316.9 2.5 copy-start
  332.2 5.1 copy-start.1
  337.4 2.5 copy-start
  352.6 5.1 copy-start.1
  357.8 2.5 copy-start
  373.0 5.1 copy-start.1
  378.2 2.5 copy-start
  393.5 5.1 copy-start.1
  398.6 201.2 %copy-start.2 = (bf16[3,32,256]{2,1,0:T(8,128)(2,1)S(1)}, bf16[3,32,256]{2,1,0:T(8,128)(2,1)}, u32[]{:S(2)}) copy-start(bf16[3,32,256]{2,1,0:T(8,128)(2,1)} %param.8) | copy-start | bytes 147460
  398.6 201.1 %reduce-scatter.3.cloned.1.call-start = ((), (), s32[]{:S(2)}) async-start(), calls=%async_computation.3 | async-start | bytes 3244032 | tf_op jit(solution)/shard_map/reduce_scatter | solution.py:182
Sparse Core Ops, SparseCore 0:
  11.9 87.7 all-gather.1
  398.7 68.5 reduce-scatter.4
  472.8 126.9 reduce-scatter.2
where the time goes:
time: 611 us; the launch traced here: 609 us
  blocking collectives  329 us (54%)
  waiting for transfers between devices  103 us (17%)
  local copies, waits for them, and re-layouts  70.7 us (12%)
  matrix products  54.2 us (9%)
  other arithmetic  33.8 us (6%)
  between operations  17.7 us (3%)
    psum x1, blocking collectives, on_device(): row_all, col_all = lax.psum((row_part, col_part), ('outer', 'inner'))  103 us
    reduce_scatter x1, waiting for transfers between devices, on_device(): lax.psum_scatter(clip_grads, 'inner', scatter_dimension=0, tiled=True)  102 us
    unnamed x2, blocking collectives  99.3 us
    psum x1, blocking collectives, on_device(): loss_mean = lax.psum(local_term, ('outer', 'inner')) / clips_all  95.1 us
    convert_element_type x6, local copies, waits for them, and re-layouts, block_grads(): (0.5 * LOGIT_SCALE * pair_grad[:, None, :, None] * (row_part + col_part))...  35.8 us
    all_gather x1, blocking collectives, on_device(): lax.all_gather(unit_g, 'outer', axis=0, tiled=True)  31.6 us
    dot_general x12, matrix products, block_parts(): lax.dot_general(clip_units.reshape(video_clip_total * frame_tokens, featu...  23.6 us
    reshape x6, local copies, waits for them, and re-layouts, block_grads(): score_grad.reshape(video_clip_total * frame_tokens, gloss_text_total * gl...  22.6 us
  transfers between devices with their start and end apart: 3, of which 1 were waited for; matrix products, arithmetic and copies ran while one was open for 1% of the time, Pallas kernels for 0%

commit v1 on v0

v1 whole, which is shorter than its diff:
```python
import functools
import math

import jax
import jax.numpy as jnp
from jax import lax
from jax.experimental import pallas as pl
from jax.experimental.pallas import tpu as pltpu
from jax.sharding import PartitionSpec as P

F32 = jnp.float32
BF16 = jnp.bfloat16
EPSILON = 1e-06
EXP_SCALE = 10.0 * math.log2(math.e)
MARK = 2.0
MARK_LIMIT = 1.5
FAR = -1e30

NZ, NY, NX, NCORE = 8, 8, 4, 2
OWN = 3
FRAMES, GLOSSES, WIDTH = 32, 16, 256
CLIPS_DEV = NZ * NCORE * OWN
TEXTS_DEV = NY * NX * OWN
LANES = 128
VROWS = FRAMES * CLIPS_DEV
GROWS = GLOSSES * LANES
VOWN = FRAMES * OWN
GOWN = GLOSSES * OWN
EXTRA = 16
PAIRS = GLOSSES // 2

Z_GROUPS = [[h * NZ + i for i in range(NZ)] for h in range(2)]
Y_GROUPS = [[h * 16 + 2 * i + c for i in range(NY)] for h in range(2) for c in range(NCORE)]


def params(limit_mb=40):
    return pltpu.CompilerParams(vmem_limit_bytes=limit_mb * 1024 * 1024)


def cost(flops, nbytes, trans=0):
    return pl.CostEstimate(flops=int(flops), bytes_accessed=int(nbytes), transcendentals=int(trans))


def iota(shape, dim):
    return lax.broadcasted_iota(jnp.int32, shape, dim)


def nt(a, b, **kw):
    return lax.dot_general(a, b, (((1,), (1,)), ((), ())), preferred_element_type=F32, **kw)


def nn(a, b, **kw):
    return lax.dot_general(a, b, (((1,), (0,)), ((), ())), preferred_element_type=F32, **kw)


def tn(a, b, **kw):
    return lax.dot_general(a, b, (((0,), (0,)), ((), ())), preferred_element_type=F32, **kw)


def column_of(row, n):
    eye = iota((n, LANES), 0) == iota((n, LANES), 1)
    return jnp.sum(jnp.where(eye, jnp.broadcast_to(row[0:1], (n, LANES)), 0.0), axis=1, keepdims=True)


def pieces(value):
    lane = iota((EXTRA, WIDTH), 1)
    full = jnp.broadcast_to(value, (EXTRA, WIDTH))
    hi = full.astype(BF16).astype(F32)
    mid = (full - hi).astype(BF16).astype(F32)
    low = full - hi - mid
    return jnp.where(lane == 0, hi, jnp.where(lane == 1, mid, jnp.where(lane == 2, low, 0.0)))


def unpiece(block):
    mine = (iota((EXTRA, WIDTH), 0) == 0) & (iota((EXTRA, WIDTH), 1) < 3)
    return jnp.sum(jnp.where(mine, block, 0.0), keepdims=True).reshape(1, 1)


def put(ref, at, value):
    ref[0, at, :] = value[:, :LANES]
    ref[1, at, :] = value[:, LANES:]


def get(ref, at):
    return jnp.concatenate([ref[0, at, :], ref[1, at, :]], axis=1)


def two_halves(rows):
    return pltpu.VMEM((2, rows, LANES), F32)


def units_kernel(fc, gc, video, gloss, v_out, g_out, v_scr, g_scr):
    for count, raw, scr, tokens in ((fc, video, v_scr, FRAMES), (gc, gloss, g_scr, GLOSSES)):
        row, lane = iota((tokens, WIDTH), 0), iota((tokens, WIDTH), 1)
        for c in range(OWN):
            x = raw[c].astype(F32)
            mean_sq = jnp.mean(x * x, axis=-1, keepdims=True) + EPSILON
            unit = x * (lax.rsqrt(mean_sq) / math.sqrt(WIDTH))
            mark = jnp.where(lane == 0, MARK, 0.0)
            put(scr, pl.ds(c, tokens, stride=OWN), jnp.where(row < count[c], unit, mark))
    v = get(v_scr, pl.ds(0, VOWN)).astype(BF16)
    g = get(g_scr, pl.ds(0, GOWN)).astype(BF16)
    for i in range(NZ):
        v_out[i] = v
    for i in range(NY):
        g_out[i] = g


def diagonal_kernel(fc, gc, v_ref, g_ref, dv, dg, logit_sum):
    def pick(count, which):
        return jnp.where(which == 0, count[0], jnp.where(which == 1, count[1], count[2]))

    v, g = v_ref[0], g_ref[0]
    shape = (VOWN, GOWN)
    r, q = iota(shape, 0), iota(shape, 1)
    rc, qc = lax.rem(r, OWN), lax.rem(q, OWN)
    valid = (rc == qc) & (lax.div(r, OWN) < pick(fc, rc)) & (lax.div(q, OWN) < pick(gc, qc))
    e = jnp.where(valid, jnp.exp2(nt(v, g) * EXP_SCALE), 0.0)
    r1, q1 = iota((VOWN, 1), 0), iota((1, GOWN), 1)
    rc1, qc1 = lax.rem(r1, OWN), lax.rem(q1, OWN)
    frames_r, glosses_r = pick(fc, rc1), pick(gc, rc1)
    frames_q, glosses_q = pick(fc, qc1), pick(gc, qc1)
    row_ok = lax.div(r1, OWN) < frames_r
    col_ok = lax.div(q1, OWN) < glosses_q
    frames_r, glosses_r = frames_r.astype(F32), glosses_r.astype(F32)
    frames_q, glosses_q = frames_q.astype(F32), glosses_q.astype(F32)
    rows = jnp.where(row_ok, jnp.sum(e, axis=1, keepdims=True), 1.0)
    cols = jnp.where(col_ok, jnp.sum(e, axis=0, keepdims=True), 1.0)
    by_row = jnp.where(row_ok, jnp.log(rows / glosses_r) / frames_r, 0.0)
    by_col = jnp.where(col_ok, jnp.log(cols / frames_q) / glosses_q, 0.0)
    total = jnp.sum(by_row, axis=0, keepdims=True) + jnp.sum(by_col, axis=1, keepdims=True)
    logit_sum[...] = jnp.broadcast_to(0.5 * total, (8, LANES))
    weight = -5.0 * e * (1.0 / (rows * frames_r) + 1.0 / (cols * glosses_q))
    dv[...] = nn(weight, g.astype(F32), precision=lax.Precision.HIGHEST)
    dg[...] = tn(weight, v.astype(F32), precision=lax.Precision.HIGHEST)


def exp_scores(v, g):
    return jnp.exp2(nt(v, g) * EXP_SCALE)


def forward_kernel(
    v_mine, v_twin, g0, g1, g2, g3, diag,
    v_out, g_out, row_out, col_out, e_out, r_mine, r_twin, c_out,
    v_scr, g_scr, frame_mask, gloss_mask, rows, cols,
):
    for t, ref in enumerate((v_mine, v_twin)):
        put(v_scr.at[t], pl.ds(0, NZ * VOWN), ref[...].reshape(NZ * VOWN, WIDTH).astype(F32))
    for f in range(FRAMES):
        parts = [get(v_scr.at[t], pl.ds(f * OWN + c, NZ, stride=VOWN)) for t in range(NCORE) for c in range(OWN)]
        v_out[pl.ds(f * CLIPS_DEV, CLIPS_DEV), :] = jnp.concatenate(parts, axis=0).astype(BF16)
    for s, ref in enumerate((g0, g1, g2, g3)):
        put(g_scr.at[s], pl.ds(0, NY * GOWN), ref[...].reshape(NY * GOWN, WIDTH).astype(F32))
    pad = jnp.where(iota((LANES - TEXTS_DEV, WIDTH), 1) == 0, MARK, 0.0)
    for g in range(GLOSSES):
        parts = [get(g_scr.at[s], pl.ds(g * OWN + c, NY, stride=GOWN)) for s in range(NX) for c in range(OWN)]
        g_out[pl.ds(g * LANES, LANES), :] = jnp.concatenate(parts + [pad], axis=0).astype(BF16)

    first = jnp.where(iota((WIDTH, LANES), 0) == 0, 1.0, 0.0).astype(BF16)
    frame_mask[...] = jnp.where(nn(v_out[...], first) < MARK_LIMIT, 1.0, 0.0)
    first_row = jnp.where(iota((16, WIDTH), 1) == 0, 1.0, 0.0).astype(BF16)
    for g in range(GLOSSES):
        gloss_mask[g] = jnp.where(nt(first_row, g_out[pl.ds(g * LANES, LANES), :])[0:8] < MARK_LIMIT, 1.0, 0.0)
    frames = jnp.zeros((CLIPS_DEV, LANES), F32)
    for f in range(FRAMES):
        frames = frames + frame_mask[pl.ds(f * CLIPS_DEV, CLIPS_DEV), :]
    glosses = gloss_mask[0]
    for g in range(1, GLOSSES):
        glosses = glosses + gloss_mask[g]
    glosses = jnp.maximum(glosses, 1.0)[0:1]

    rows[...] = jnp.zeros_like(rows)

    def two_glosses(p, _):
        e = exp_scores(v_out[...], g_out[pl.ds(pl.multiple_of(p * WIDTH, WIDTH), WIDTH), :])
        m0, m1 = gloss_mask[2 * p][0:1], gloss_mask[2 * p + 1][0:1]
        col0 = jnp.zeros((CLIPS_DEV, LANES), F32)
        col1 = jnp.zeros((CLIPS_DEV, LANES), F32)
        for f in range(FRAMES):
            at = pl.ds(f * CLIPS_DEV, CLIPS_DEV)
            block = e[f * CLIPS_DEV : (f + 1) * CLIPS_DEV]
            e0, e1 = block[:, :LANES], block[:, LANES:]
            mask = frame_mask[at, :]
            rows[at, :] = rows[at, :] + (e0 * m0 + e1 * m1)
            col0 = col0 + e0 * mask
            col1 = col1 + e1 * mask
        cols[2 * p] = col0
        cols[2 * p + 1] = col1
        return 0

    lax.fori_loop(0, PAIRS, two_glosses, 0)

    lane = iota((CLIPS_DEV, LANES), 1)
    real = lane < TEXTS_DEV
    video_part = jnp.zeros((CLIPS_DEV, LANES), F32)
    for f in range(FRAMES):
        at = pl.ds(f * CLIPS_DEV, CLIPS_DEV)
        mask = frame_mask[at, :]
        total = jnp.where(real, rows[at, :], 1.0)
        video_part = video_part + mask * jnp.log(total / glosses)
        row_out[at, :] = jnp.where(mask > 0.0, 1.0 / (total * frames), FAR)
    gloss_part = jnp.zeros((CLIPS_DEV, LANES), F32)
    for g in range(GLOSSES):
        mask = gloss_mask[g][0:1]
        total = cols[g]
        gloss_part = gloss_part + mask * jnp.log(total / frames)
        col_out[g] = jnp.where(mask > 0.0, 1.0 / (total * glosses), FAR)
    logits = 0.5 * (video_part / frames + gloss_part / glosses)
    e_pair = jnp.where(real, jnp.exp(logits), 0.0)
    e_out[...] = e_pair

    sums = jnp.sum(e_pair, axis=1, keepdims=True)
    clip = iota((CLIPS_DEV, LANES), 0)
    half = CLIPS_DEV // 2
    swapped = jnp.where(clip < half, clip + half, clip - half)
    spread = jnp.broadcast_to(sums, (CLIPS_DEV, LANES))
    row_mine = jnp.sum(jnp.where(lane == clip, spread, 0.0), axis=0, keepdims=True)
    row_twin = jnp.sum(jnp.where(lane == swapped, spread, 0.0), axis=0, keepdims=True)
    at_diag = iota((8, LANES), 1) == CLIPS_DEV
    r_mine[...] = jnp.where(at_diag, diag[...], jnp.broadcast_to(row_mine, (8, LANES)))
    r_twin[...] = jnp.where(at_diag, diag[...], jnp.broadcast_to(row_twin, (8, LANES)))
    c_row = jnp.broadcast_to(jnp.sum(e_pair, axis=0, keepdims=True), (8, LANES))
    for i in range(NY):
        c_out[i] = c_row


def weights_kernel(v_ref, g_ref, row_ref, col_ref, e_ref, p_out, av_out, ag_out):
    p = pl.program_id(0)
    e = exp_scores(v_ref[...], g_ref[...])
    scale = 2.5 * e_ref[...]
    col0, col1 = col_ref[0], col_ref[1]
    for f in range(FRAMES):
        at = pl.ds(f * CLIPS_DEV, CLIPS_DEV)
        block = e[f * CLIPS_DEV : (f + 1) * CLIPS_DEV]
        row = row_ref[at, :]
        w0 = scale * block[:, :LANES] * jnp.maximum(row + col0, 0.0)
        w1 = scale * block[:, LANES:] * jnp.maximum(row + col1, 0.0)
        p_out[0, at, :] = jnp.concatenate([w0, w1], axis=1).astype(BF16)
    weights = p_out[0]
    part = nn(weights, g_ref[...])

    @pl.when(p == 0)
    def _():
        av_out[...] = part

    @pl.when(p > 0)
    def _():
        av_out[...] = av_out[...] + part

    ag_out[...] = tn(weights, v_ref[...])


def text_sums(q0, q1, q2, q3):
    lane = iota((8, LANES), 1)
    slot = OWN * NY
    total = q0[...]
    for s, q in enumerate((q1, q2, q3), start=1):
        part = q[...]
        ahead = pltpu.roll(part, slot * s, 1)
        behind = pltpu.roll(part, (slot * s - TEXTS_DEV) % LANES, 1)
        total = total + jnp.where(lane < slot * s, behind, ahead)
    return jnp.where(lane < TEXTS_DEV, total, 0.0)


def by_text_kernel(q0, q1, q2, q3, p_ref, g_ref, out):
    step = pl.program_id(0)
    c_row = text_sums(q0, q1, q2, q3)
    inverse = jnp.where(c_row > 0.0, 1.0 / c_row, 0.0)
    col = jnp.broadcast_to(column_of(inverse, LANES), (LANES, WIDTH))
    scaled = g_ref[...].astype(F32) * jnp.concatenate([col, col], axis=0)
    hi = scaled.astype(BF16)
    low = (scaled - hi.astype(F32)).astype(BF16)
    part = nn(p_ref[0], hi) + nn(p_ref[0], low)

    @pl.when(step == 0)
    def _():
        out[...] = part

    @pl.when(step > 0)
    def _():
        out[...] = out[...] + part


def clip_sums(z_ref):
    total = z_ref[0]
    for i in range(1, NZ):
        total = total + z_ref[i]
    return total


def video_partial_kernel(z_ref, q0, q1, q2, q3, av_ref, bv_ref, mine, twin):
    r_row = clip_sums(z_ref)
    inverse = jnp.broadcast_to(1.0 / column_of(r_row, CLIPS_DEV), (CLIPS_DEV, WIDTH))
    half = CLIPS_DEV // 2
    for pair in range(FRAMES // 2):
        blocks = []
        for f in (2 * pair, 2 * pair + 1):
            at = pl.ds(f * CLIPS_DEV, CLIPS_DEV)
            block = av_ref[at, :] * inverse + bv_ref[at, :]
            mine[pl.ds(f * half, half), :] = block[:half]
            blocks.append(block[half:])
        twin[pl.ds(pair * CLIPS_DEV, CLIPS_DEV), :] = jnp.concatenate(blocks, axis=0).astype(BF16)
    c_row = text_sums(q0, q1, q2, q3)[0:1]
    logs = jnp.where(iota((1, LANES), 1) < TEXTS_DEV, jnp.log(jnp.where(c_row > 0.0, c_row, 1.0)), 0.0)
    total = pieces(jnp.sum(logs, axis=1, keepdims=True))
    mine[pl.ds(FRAMES * half, EXTRA), :] = total
    twin[pl.ds(FRAMES * half, EXTRA), :] = total.astype(BF16)


def gloss_partial_kernel(z_ref, q0, q1, q2, q3, p_ref, v_ref, ag_ref, s0, s1, s2, s3, v_hi, v_low):
    step = pl.program_id(0)
    r_row = clip_sums(z_ref)
    slot = OWN * NY

    @pl.when(step == 0)
    def _():
        inverse = jnp.broadcast_to(1.0 / column_of(r_row, CLIPS_DEV), (CLIPS_DEV, WIDTH))
        for f in range(FRAMES):
            at = pl.ds(f * CLIPS_DEV, CLIPS_DEV)
            scaled = v_ref[at, :].astype(F32) * inverse
            hi = scaled.astype(BF16)
            v_hi[at, :] = hi
            v_low[at, :] = (scaled - hi.astype(F32)).astype(BF16)
        lane = iota((1, LANES), 1)
        r_real = jnp.where(lane < CLIPS_DEV, r_row[0:1], 1.0)
        logs = jnp.where(lane < CLIPS_DEV, jnp.log(r_real), 0.0)
        logs = logs - jnp.where(lane == CLIPS_DEV, 2.0 * r_row[0:1], 0.0)
        total = pieces(jnp.sum(logs, axis=1, keepdims=True))
        at = pl.ds(GLOSSES * slot, EXTRA)
        s0[at, :] = total
        for out in (s1, s2, s3):
            out[at, :] = total.astype(BF16)

    c_row = text_sums(q0, q1, q2, q3)
    inverse = jnp.where(c_row > 0.0, 1.0 / c_row, 0.0)
    col = jnp.broadcast_to(column_of(inverse, LANES), (LANES, WIDTH))
    part = tn(p_ref[0], v_hi[...]) + tn(p_ref[0], v_low[...])
    part = part + ag_ref[...] * jnp.concatenate([col, col], axis=0)
    at = pl.ds(pl.multiple_of(step * 2 * slot, 2 * slot), 2 * slot)
    for s, out in enumerate((s0, s1, s2, s3)):
        both = [part[g * LANES + s * slot : g * LANES + (s + 1) * slot] for g in range(2)]
        out[at, :] = jnp.concatenate(both, axis=0).astype(out.dtype)


def spread_kernel(rows, peers, *refs):
    mine, others, out, scr = refs[0], refs[1:-2], refs[-2], refs[-1]
    height = rows + EXTRA

    def block(at, n):
        total = mine[pl.ds(at, n), :]
        for other in others:
            total = total + other[pl.ds(at, n), :].astype(F32)
        return total

    step = 2 * peers
    for i in range(rows // 2):
        two = block(i * step, step)
        for k in range(2):
            put(scr, pl.ds(2 * i + k, peers, stride=height), two[k * peers : (k + 1) * peers])
    tail = mine[pl.ds(rows * peers, EXTRA), :]
    value = unpiece(tail)
    for other in others:
        value = value + unpiece(other[pl.ds(rows * peers, EXTRA), :].astype(F32))
    extra = pieces(value)
    for i in range(peers):
        put(scr, pl.ds(i * height + rows, EXTRA), extra)
    out[...] = get(scr, pl.ds(0, peers * height)).astype(BF16).reshape(peers, height, WIDTH)


def token_grads(total, scr, raw, out, tokens):
    put(scr, pl.ds(0, OWN * tokens), total)
    for c in range(OWN):
        x = raw[c].astype(F32)
        d = get(scr, pl.ds(c, tokens, stride=OWN))
        mean_sq = jnp.mean(x * x, axis=-1, keepdims=True) + EPSILON
        factor = lax.rsqrt(mean_sq) / math.sqrt(WIDTH)
        inner = jnp.sum(d * x, axis=-1, keepdims=True)
        out[c] = factor * d - factor * x * (inner / (WIDTH * mean_sq))


def summed(ref, rows):
    total = ref[0].astype(F32)
    for i in range(1, ref.shape[0]):
        total = total + ref[i].astype(F32)
    return total[:rows], unpiece(total[rows:])


def video_grad_kernel(got, diag, video, out, logs, scr):
    total, value = summed(got, VOWN)
    token_grads(total + diag[...], scr, video, out, FRAMES)
    logs[...] = jnp.broadcast_to(value, (8, LANES))


def gloss_grad_kernel(clips, got, diag, gloss, logs, out, loss, scr):
    total, value = summed(got, GOWN)
    token_grads(total + diag[...], scr, gloss, out, GLOSSES)
    loss[...] = (value + logs[0:1, 0:1]) * (0.5 / clips)


def shape(*dims, dtype=F32):
    return jax.ShapeDtypeStruct(dims, dtype)


def on_device(clips, video, gloss, frame_count, gloss_count):
    vmem, smem = pl.BlockSpec(memory_space=pltpu.VMEM), pl.BlockSpec(memory_space=pltpu.SMEM)
    core_pairs = [(i, i ^ 1) for i in range(NX // 2 * NY * NCORE)]

    def x_shift(s):
        pairs = []
        for x in range(NX):
            for z in range(NZ):
                for rest in range(NY * NCORE):
                    flat = [((a % 2) * NZ + z) * 32 + (a // 2) * 16 + rest for a in (x, (x + s) % NX)]
                    pairs.append((flat[0], flat[1]))
        return sorted(pairs)

    def to_core(a):
        return lax.ppermute(a, "inner", core_pairs)

    def to_x(a, s):
        return lax.ppermute(a, ("outer", "inner"), x_shift(s % NX))

    def over_y(a):
        return lax.all_to_all(a, "inner", 0, 0, axis_index_groups=Y_GROUPS, tiled=True)

    def over_z(a):
        return lax.all_to_all(a, "outer", 0, 0, axis_index_groups=Z_GROUPS, tiled=True)

    with jax.named_scope("unit_tokens"):
        v_own, g_own = pl.pallas_call(
            units_kernel,
            in_specs=[smem, smem, vmem, vmem],
            out_shape=(shape(NZ, VOWN, WIDTH, dtype=BF16), shape(NY, GOWN, WIDTH, dtype=BF16)),
            scratch_shapes=[two_halves(VOWN), two_halves(GOWN)],
            compiler_params=params(),
            cost_estimate=cost(2e5, 7e5),
        )(frame_count, gloss_count, video, gloss)

    with jax.named_scope("gather"):
        g_mine = over_y(g_own)
        g_parts = [g_mine] + [to_x(g_mine, s) for s in range(1, NX)]
        v_mine = over_z(v_own)
        v_twin = to_core(v_mine)

    def first(rows):
        return pl.BlockSpec((1, rows, WIDTH), lambda i: (0, 0, 0))

    def whole(*dims):
        return pl.BlockSpec(dims, lambda i: (0,) * len(dims))

    with jax.named_scope("diagonal"):
        dv_diag, dg_diag, logit_sum = pl.pallas_call(
            diagonal_kernel,
            grid=(1,),
            in_specs=[smem, smem, first(VOWN), first(GOWN)],
            out_specs=(whole(VOWN, WIDTH), whole(GOWN, WIDTH), whole(8, LANES)),
            out_shape=(shape(VOWN, WIDTH), shape(GOWN, WIDTH), shape(8, LANES)),
            compiler_params=params(),
            cost_estimate=cost(2e7, 3e5),
        )(frame_count, gloss_count, v_own, g_own)

    with jax.named_scope("forward"):
        v_all, g_all, row_inv, col_inv, e_pair, r_mine, r_twin, c_part = pl.pallas_call(
            forward_kernel,
            in_specs=[vmem] * 7,
            out_shape=(
                shape(VROWS, WIDTH, dtype=BF16),
                shape(GROWS, WIDTH, dtype=BF16),
                shape(VROWS, LANES),
                shape(GLOSSES, CLIPS_DEV, LANES),
                shape(CLIPS_DEV, LANES),
                shape(8, LANES),
                shape(8, LANES),
                shape(NY, 8, LANES),
            ),
            scratch_shapes=[
                pltpu.VMEM((NCORE, 2, NZ * VOWN, LANES), F32),
                pltpu.VMEM((NX, 2, NY * GOWN, LANES), F32),
                pltpu.VMEM((VROWS, LANES), F32),
                pltpu.VMEM((GLOSSES, 8, LANES), F32),
                pltpu.VMEM((VROWS, LANES), F32),
                pltpu.VMEM((GLOSSES, CLIPS_DEV, LANES), F32),
            ],
            compiler_params=params(),
            cost_estimate=cost(2 * VROWS * GROWS * WIDTH, 8e6, VROWS * GROWS),
        )(v_mine, v_twin, *g_parts, logit_sum)

    with jax.named_scope("batch_sums"):
        c_mine = jnp.sum(over_y(c_part), axis=0)
        c_parts = [c_mine] + [to_x(c_mine, s) for s in range(1, NX)]
        r_pair = r_mine + to_core(r_twin)
        r_got = over_z(jnp.broadcast_to(r_pair[None], (NZ, 8, LANES)))

    def halves(rows):
        return pl.BlockSpec((rows, WIDTH), lambda i: (i, 0))

    p_spec = pl.BlockSpec((1, VROWS, WIDTH), lambda i: (i, 0, 0))
    with jax.named_scope("weights"):
        weights, av, ag = pl.pallas_call(
            weights_kernel,
            grid=(PAIRS,),
            in_specs=[
                whole(VROWS, WIDTH),
                halves(2 * LANES),
                whole(VROWS, LANES),
                pl.BlockSpec((2, CLIPS_DEV, LANES), lambda i: (i, 0, 0)),
                whole(CLIPS_DEV, LANES),
            ],
            out_specs=(p_spec, whole(VROWS, WIDTH), halves(2 * LANES)),
            out_shape=(shape(PAIRS, VROWS, WIDTH, dtype=BF16), shape(VROWS, WIDTH), shape(GROWS, WIDTH)),
            compiler_params=params(),
            cost_estimate=cost(6 * VROWS * GROWS * WIDTH, 16e6, VROWS * GROWS),
        )(v_all, g_all, row_inv, col_inv, e_pair)

    part_spec = whole(8, LANES)
    with jax.named_scope("by_text"):
        bv = pl.pallas_call(
            by_text_kernel,
            grid=(PAIRS,),
            in_specs=[part_spec] * 4 + [p_spec, halves(2 * LANES)],
            out_specs=whole(VROWS, WIDTH),
            out_shape=shape(VROWS, WIDTH),
            compiler_params=params(),
            cost_estimate=cost(4 * VROWS * GROWS * WIDTH, 9e6),
        )(*c_parts, weights, g_all)

    with jax.named_scope("video_partial"):
        v_rows = FRAMES * CLIPS_DEV // 2 + EXTRA
        dv_mine, dv_twin = pl.pallas_call(
            video_partial_kernel,
            in_specs=[vmem] * 7,
            out_shape=(shape(v_rows, WIDTH), shape(v_rows, WIDTH, dtype=BF16)),
            compiler_params=params(),
            cost_estimate=cost(2e6, 5e6),
        )(r_got, *c_parts, av, bv)
    with jax.named_scope("video_to_owner"):
        dv_got = to_core(dv_twin)
        dv_send = pl.pallas_call(
            functools.partial(spread_kernel, VOWN, NZ),
            in_specs=[vmem] * 2,
            out_shape=shape(NZ, VOWN + EXTRA, WIDTH, dtype=BF16),
            scratch_shapes=[two_halves(NZ * (VOWN + EXTRA))],
            compiler_params=params(),
            cost_estimate=cost(1e6, 2e6),
        )(dv_mine, dv_got)
        dv_parts = over_z(dv_send)

    with jax.named_scope("gloss_partial"):
        g_rows = GLOSSES * OWN * NY + EXTRA
        dg_slots = pl.pallas_call(
            gloss_partial_kernel,
            grid=(PAIRS,),
            in_specs=[whole(NZ, 8, LANES)] + [part_spec] * 4 + [p_spec, whole(VROWS, WIDTH), halves(2 * LANES)],
            out_specs=(whole(g_rows, WIDTH),) * NX,
            out_shape=(shape(g_rows, WIDTH),) + (shape(g_rows, WIDTH, dtype=BF16),) * (NX - 1),
            scratch_shapes=[pltpu.VMEM((VROWS, WIDTH), BF16), pltpu.VMEM((VROWS, WIDTH), BF16)],
            compiler_params=params(),
            cost_estimate=cost(4 * VROWS * GROWS * WIDTH, 9e6),
        )(r_got, *c_parts, weights, v_all, ag)
    with jax.named_scope("gloss_to_owner"):
        dg_got = [to_x(dg_slots[s], -s) for s in range(1, NX)]
        dg_send = pl.pallas_call(
            functools.partial(spread_kernel, GOWN, NY),
            in_specs=[vmem] * NX,
            out_shape=shape(NY, GOWN + EXTRA, WIDTH, dtype=BF16),
            scratch_shapes=[two_halves(NY * (GOWN + EXTRA))],
            compiler_params=params(),
            cost_estimate=cost(1e6, 2e6),
        )(dg_slots[0], *dg_got)
        dg_parts = over_y(dg_send)

    with jax.named_scope("video_grad"):
        grad_video, logs = pl.pallas_call(
            video_grad_kernel,
            in_specs=[vmem] * 3,
            out_shape=(shape(OWN, FRAMES, WIDTH), shape(8, LANES)),
            scratch_shapes=[two_halves(VOWN)],
            compiler_params=params(),
            cost_estimate=cost(1e6, 1e6),
        )(dv_parts, dv_diag, video)
    with jax.named_scope("gloss_grad"):
        grad_gloss, loss = pl.pallas_call(
            functools.partial(gloss_grad_kernel, clips),
            in_specs=[vmem] * 4,
            out_shape=(shape(OWN, GLOSSES, WIDTH), shape(1, 1)),
            scratch_shapes=[two_halves(GOWN)],
            compiler_params=params(),
            cost_estimate=cost(1e6, 1e6),
        )(dg_parts, dg_diag, gloss, logs)
    return loss.reshape(()), grad_video, grad_gloss


def solution(mesh):
    clips = OWN * mesh.shape["outer"] * mesh.shape["inner"]
    over_all = ("outer", "inner")
    tokens, counts = P(over_all, None, None), P(over_all)
    return jax.shard_map(
        functools.partial(on_device, clips),
        mesh=mesh,
        in_specs=(tokens, tokens, counts, counts),
        out_specs=(P(), tokens, tokens),
        check_vma=False,
    )
```

time: 611 us -> 183 us (0.30)
  the two profiles are of different devices: /device:TPU:16 before, /device:TPU:64 now
where the time goes in v1:
time: 183 us; the launch traced here: 182 us
  starting transfers between devices  60.8 us (33%)
  Pallas kernels  38.1 us (21%)
  waiting for transfers between devices  37.3 us (20%)
  blocking collectives  23 us (13%)
  local copies, waits for them, and re-layouts  21.3 us (12%)
    ppermute x9, starting transfers between devices, to_x(): return lax.ppermute(a, ('outer', 'inner'), x_shift(s % NX))  29.2 us
    all_to_all x3, waiting for transfers between devices, over_y(): lax.all_to_all(a, 'inner', 0, 0, axis_index_groups=Y_GROUPS, tiled=True)  24.5 us
    all_to_all x1, blocking collectives, over_z(): lax.all_to_all(a, 'outer', 0, 0, axis_index_groups=Z_GROUPS, tiled=True)  23 us
    unnamed x40, local copies, waits for them, and re-layouts  20.7 us
    all_to_all x3, starting transfers between devices, over_y(): lax.all_to_all(a, 'inner', 0, 0, axis_index_groups=Y_GROUPS, tiled=True)  13.9 us
    pallas_call x1, Pallas kernels, on_device(): pl.pallas_call(weights_kernel, grid=(PAIRS,), in_specs=[whole(VROWS, WIDT...  12.1 us
    all_to_all x2, starting transfers between devices, over_z(): lax.all_to_all(a, 'outer', 0, 0, axis_index_groups=Z_GROUPS, tiled=True)  11.9 us
    ppermute x9, waiting for transfers between devices, to_x(): return lax.ppermute(a, ('outer', 'inner'), x_shift(s % NX))  11.1 us
  transfers between devices with their start and end apart: 17, of which 9 were waited for; matrix products, arithmetic and copies ran while one was open for 0% of the time, Pallas kernels for 15%

profile of v1, /device:TPU:64, one launch (start us, length us, event | category | flops | bytes accessed | tf_op | source)
XLA Modules:
  0.0 181.5 jit_solution(13493405406335894706)
XLA Ops:
  4.8 23.0 %all_to_all.30.v_mine = bf16[8,96,256]{2,1,0:T(8,128)(2,1)S(1)} all-to-all(bf16[8,96,256]{2,1,0:T(8,128)(2,1)S(1)} %get-tuple-element.29.v_ref), channel_id=1, replica_groups={{0,32,64,96,128,160,192,224},{256,288,320,352,384,416,448,480},{1,33,65..., dimensions={0} | all-to-all | bytes 786432 | tf_op jit(solution)/shard_map/gather/all_to_all | solution.py:427
  27.8 7.1 %all-to-all-start.1 = ((bf16[8,48,256]{2,1,0:T(8,128)(2,1)}), bf16[8,48,256]{2,1,0:T(8,128)(2,1)S(1)}, u32[]{:S(2)}, u32[]{:S(2)}) async-start(bf16[8,48,256]{2,1,0:T(8,128)(2,1)} %get-tuple-element.30.g_ref), calls=%async_computation.1 | async-start | bytes 393216 | tf_op jit(solution)/shard_map/gather/all_to_all | solution.py:424
  34.9 1.9 %collective-permute-start = (bf16[8,96,256]{2,1,0:T(8,128)(2,1)S(1)}, bf16[8,96,256]{2,1,0:T(8,128)(2,1)S(1)}, u32[]{:S(2)}, u32[]{:S(2)}) collective-permute-start(bf16[8,96,256]{2,1,0:T(8,128)(2,1)S(1)} %all_to_all.30.v_mine), channel_id=1, source_target_pairs={{0,1},{1,0},{2,3},{3,2},{4,5},{5,4},{6,7},{7,6},{8,9},{9,8},{10,11... | collective-permute-start | bytes 1179656 | tf_op jit(solution)/shard_map/gather/ppermute | solution.py:418
  36.8 7.9 %all-to-all-done.1.g0 = bf16[8,48,256]{2,1,0:T(8,128)(2,1)S(1)} async-done(((bf16[8,48,256]{2,1,0:T(8,128)(2,1)}), bf16[8,48,256]{2,1,0:T(8,128)(2,1)S(1)}, u32[]{:S(2)}, u32[]{:S(2)}) %all-to-all-start.1) | async-done | bytes 196640 | tf_op jit(solution)/shard_map/gather/all_to_all | solution.py:424
  44.7 4.7 %collective-permute-start.3 = (bf16[8,48,256]{2,1,0:T(8,128)(2,1)S(1)}, bf16[8,48,256]{2,1,0:T(8,128)(2,1)S(1)}, u32[]{:S(2)}, u32[]{:S(2)}) collective-permute-start(bf16[8,48,256]{2,1,0:T(8,128)(2,1)S(1)} %all-to-all-done.1.g0), channel_id=1, source_target_pairs={{0,272},{1,273},{2,274},{3,275},{4,276},{5,277},{6,278},{7,279},{8... | collective-permute-start | bytes 589832 | tf_op jit(solution)/shard_map/gather/ppermute | solution.py:421
  49.3 2.7 %collective-permute-start.2 = (bf16[8,48,256]{2,1,0:T(8,128)(2,1)S(1)}, bf16[8,48,256]{2,1,0:T(8,128)(2,1)S(1)}, u32[]{:S(2)}, u32[]{:S(2)}) collective-permute-start(bf16[8,48,256]{2,1,0:T(8,128)(2,1)S(1)} %all-to-all-done.1.g0), channel_id=1, source_target_pairs={{0,16},{1,17},{2,18},{3,19},{4,20},{5,21},{6,22},{7,23},{8,24},{9,... | collective-permute-start | bytes 589832 | tf_op jit(solution)/shard_map/gather/ppermute | solution.py:421
  52.1 2.8 %collective-permute-start.1 = (bf16[8,48,256]{2,1,0:T(8,128)(2,1)S(1)}, bf16[8,48,256]{2,1,0:T(8,128)(2,1)S(1)}, u32[]{:S(2)}, u32[]{:S(2)}) collective-permute-start(bf16[8,48,256]{2,1,0:T(8,128)(2,1)S(1)} %all-to-all-done.1.g0), channel_id=1, source_target_pairs={{0,256},{1,257},{2,258},{3,259},{4,260},{5,261},{6,262},{7,263},{8... | collective-permute-start | bytes 589832 | tf_op jit(solution)/shard_map/gather/ppermute | solution.py:421
  58.4 2.4 %collective-permute-done.1.g1 = bf16[8,48,256]{2,1,0:T(8,128)(2,1)S(1)} collective-permute-done((bf16[8,48,256]{2,1,0:T(8,128)(2,1)S(1)}, bf16[8,48,256]{2,1,0:T(8,128)(2,1)S(1)}, u32[]{:S(2)}, u32[]{:S(2)}) %collective-permute-start.1) | collective-permute-done | bytes 196640 | tf_op jit(solution)/shard_map/gather/ppermute | solution.py:421
  60.8 7.0 %forward.1 = (bf16[1536,256]{1,0:T(8,128)(2,1)S(1)}, bf16[2048,256]{1,0:T(8,128)(2,1)S(1)}, f32[1536,128]{1,0:T(8,128)S(1)}, f32[16,48,128]{2,1,0:T(8,128)S(1)},...) custom-call(bf16[8,96,256]{2,1,0:T(8,128)(2,1)S(1)} %all_to_all.30.v_mine, ...), custom_call_target="tpu_custom_call" | custom-call | flops 1610612736 | bytes 8000000 | tf_op jit(solution)/shard_map/forward/pallas_call | solution.py:463
  69.6 3.3 %all-to-all-start.3 = ((f32[8,8,128]{2,1,0:T(8,128)}), f32[8,8,128]{2,1,0:T(8,128)S(1)}, u32[]{:S(2)}, u32[]{:S(2)}) async-start(f32[8,8,128]{2,1,0:T(8,128)} %get-tuple-element.34), calls=%async_computation.3 | async-start | bytes 65536 | tf_op jit(solution)/shard_map/batch_sums/all_to_all | solution.py:424
  73.0 1.9 %collective-permute-start.4 = (f32[8,128]{1,0:T(8,128)S(1)}, f32[8,128]{1,0:T(8,128)S(1)}, u32[]{:S(2)}, u32[]{:S(2)}) collective-permute-start(f32[8,128]{1,0:T(8,128)S(1)} %get-tuple-element.33), channel_id=1, source_target_pairs={{0,1},{1,0},{2,3},{3,2},{4,5},{5,4},{6,7},{7,6},{8,9},{9,8},{10,11... | collective-permute-start | bytes 12296 | tf_op jit(solution)/shard_map/batch_sums/ppermute | solution.py:418
  74.9 6.0 %all-to-all-done.3 = f32[8,8,128]{2,1,0:T(8,128)S(1)} async-done(((f32[8,8,128]{2,1,0:T(8,128)}), f32[8,8,128]{2,1,0:T(8,128)S(1)}, u32[]{:S(2)}, u32[]{:S(2)}) %all-to-all-start.3) | async-done | bytes 32800 | tf_op jit(solution)/shard_map/batch_sums/all_to_all | solution.py:424
  80.9 2.2 %collective-permute-start.7 = (f32[8,128]{1,0:T(8,128)S(1)}, f32[8,128]{1,0:T(8,128)S(1)}, u32[]{:S(2)}, u32[]{:S(2)}) collective-permute-start(f32[8,128]{1,0:T(8,128)S(1)} %reduce_sum.9.q0), channel_id=1, source_target_pairs={{0,272},{1,273},{2,274},{3,275},{4,276},{5,277},{6,278},{7,279},{8... | collective-permute-start | bytes 12296 | tf_op jit(solution)/shard_map/batch_sums/ppermute | solution.py:421
  83.1 3.4 %collective-permute-start.6 = (f32[8,128]{1,0:T(8,128)S(1)}, f32[8,128]{1,0:T(8,128)S(1)}, u32[]{:S(2)}, u32[]{:S(2)}) collective-permute-start(f32[8,128]{1,0:T(8,128)S(1)} %reduce_sum.9.q0), channel_id=1, source_target_pairs={{0,16},{1,17},{2,18},{3,19},{4,20},{5,21},{6,22},{7,23},{8,24},{9,... | collective-permute-start | bytes 12296 | tf_op jit(solution)/shard_map/batch_sums/ppermute | solution.py:421
  86.5 3.1 %collective-permute-start.5 = (f32[8,128]{1,0:T(8,128)S(1)}, f32[8,128]{1,0:T(8,128)S(1)}, u32[]{:S(2)}, u32[]{:S(2)}) collective-permute-start(f32[8,128]{1,0:T(8,128)S(1)} %reduce_sum.9.q0), channel_id=1, source_target_pairs={{0,256},{1,257},{2,258},{3,259},{4,260},{5,261},{6,262},{7,263},{8... | collective-permute-start | bytes 12296 | tf_op jit(solution)/shard_map/batch_sums/ppermute | solution.py:421
  91.9 12.1 %weights.1 = (bf16[8,1536,256]{2,1,0:T(8,128)(2,1)S(1)}, f32[1536,256]{1,0:T(8,128)S(1)}, f32[2048,256]{1,0:T(8,128)S(1)}) custom-call(bf16[1536,256]{1,0:T(8,128)(2,1)S(1)} %copy-done.16, bf16[2048,256]{1,0:T(8,128)(2,1)S(1)} %get-tuple-element.36.g_ref, f32[1536,128]{1,0:T(8,128)S(1)} %copy-done.19, f32[16,48,128]{2,1,0:T(8,128)S(1)} %get-tuple-element.38.col_ref, ...), custom_call_target="tpu_custom_call" | custom-call | flops 4831838208 | bytes 16000000 | tf_op jit(solution)/shard_map/weights/pallas_call | solution.py:499
  104.0 2.7 %copy-done.8 = bf16[8,1536,256]{2,1,0:T(8,128)(2,1)} copy-done((bf16[8,1536,256]{2,1,0:T(8,128)(2,1)}, bf16[8,1536,256]{2,1,0:T(8,128)(2,1)S(1)}, u32[]{:S(2)}) %copy-start.8) | copy-done | bytes 6291480
  108.7 4.7 %all-to-all-start.2 = ((f32[8,8,128]{2,1,0:T(8,128)}), f32[8,8,128]{2,1,0:T(8,128)S(1)}, u32[]{:S(2)}, u32[]{:S(2)}) async-start(f32[8,8,128]{2,1,0:T(8,128)} %broadcast_in_dim.2), calls=%async_computation.2 | async-start | bytes 65536 | tf_op jit(solution)/shard_map/batch_sums/all_to_all | solution.py:427
  113.4 2.8 %copy-done.9 = bf16[8,1536,256]{2,1,0:T(8,128)(2,1)S(1)} copy-done((bf16[8,1536,256]{2,1,0:T(8,128)(2,1)S(1)}, bf16[8,1536,256]{2,1,0:T(8,128)(2,1)}, u32[]{:S(2)}) %copy-start.9) | copy-done | bytes 6291480
  117.4 7.1 %by_text.1.bv_ref = f32[1536,256]{1,0:T(8,128)S(1)} custom-call(f32[8,128]{1,0:T(8,128)S(1)} %reduce_sum.9.q0, f32[8,128]{1,0:T(8,128)S(1)} %collective-permute-done.5.q1, f32[8,128]{1,0:T(8,128)S(1)} %collective-permute-done.6.q2, f32[8,128]{1,0:T(8,128)S(1)} %collective-permute-done.7.q3, bf16[8,1536,256]{2,1,0:T(8,128)(2,1)S(1)} %copy-done.9, ...), custom_call_target="tpu_custom_call" | custom-call | flops 3221225472 | bytes 9000000 | tf_op jit(solution)/shard_map/by_text/pallas_call | solution.py:517
  124.8 2.1 %collective-permute-start.11 = (bf16[784,256]{1,0:T(8,128)(2,1)S(1)}, bf16[784,256]{1,0:T(8,128)(2,1)S(1)}, u32[]{:S(2)}, u32[]{:S(2)}) collective-permute-start(bf16[784,256]{1,0:T(8,128)(2,1)S(1)} %get-tuple-element.49), channel_id=1, source_target_pairs={{0,1},{1,0},{2,3},{3,2},{4,5},{5,4},{6,7},{7,6},{8,9},{9,8},{10,11... | collective-permute-start | bytes 1204232 | tf_op jit(solution)/shard_map/video_to_owner/ppermute | solution.py:418
  129.7 7.2 %all-to-all-start.5 = ((bf16[8,112,256]{2,1,0:T(8,128)(2,1)}), bf16[8,112,256]{2,1,0:T(8,128)(2,1)S(1)}, u32[]{:S(2)}, u32[]{:S(2)}) async-start(bf16[8,112,256]{2,1,0:T(8,128)(2,1)} %video_to_owner.1), calls=%async_computation.5 | async-start | bytes 917504 | tf_op jit(solution)/shard_map/video_to_owner/all_to_all | solution.py:427
  137.0 2.8 %copy-done.10 = bf16[8,1536,256]{2,1,0:T(8,128)(2,1)S(1)} copy-done((bf16[8,1536,256]{2,1,0:T(8,128)(2,1)S(1)}, bf16[8,1536,256]{2,1,0:T(8,128)(2,1)}, u32[]{:S(2)}) %copy-start.10) | copy-done | bytes 6291480
  141.4 5.3 %gloss_partial.1 = (f32[400,256]{1,0:T(8,128)S(1)}, bf16[400,256]{1,0:T(8,128)(2,1)S(1)}, bf16[400,256]{1,0:T(8,128)(2,1)S(1)}, bf16[400,256]{1,0:T(8,128)(2,1)S(1)}) custom-call(f32[8,8,128]{2,1,0:T(8,128)S(1)} %all-to-all-done.2.z_ref, f32[8,128]{1,0:T(8,128)S(1)} %reduce_sum.9.q0, f32[8,128]{1,0:T(8,128)S(1)} %collective-permute-done.5.q1, ...), custom_call_target="tpu_custom_call" | custom-call | flops 3221225472 | bytes 9000000 | tf_op jit(solution)/shard_map/gloss_partial/pallas_call | solution.py:550
  146.7 3.9 %collective-permute-start.8 = (bf16[400,256]{1,0:T(8,128)(2,1)S(1)}, bf16[400,256]{1,0:T(8,128)(2,1)S(1)}, u32[]{:S(2)}, u32[]{:S(2)}) collective-permute-start(bf16[400,256]{1,0:T(8,128)(2,1)S(1)} %get-tuple-element.43), channel_id=1, source_target_pairs={{0,272},{1,273},{2,274},{3,275},{4,276},{5,277},{6,278},{7,279},{8... | collective-permute-start | bytes 614408 | tf_op jit(solution)/shard_map/gloss_to_owner/ppermute | solution.py:421
  150.6 3.1 %collective-permute-start.9 = (bf16[400,256]{1,0:T(8,128)(2,1)S(1)}, bf16[400,256]{1,0:T(8,128)(2,1)S(1)}, u32[]{:S(2)}, u32[]{:S(2)}) collective-permute-start(bf16[400,256]{1,0:T(8,128)(2,1)S(1)} %get-tuple-element.44), channel_id=1, source_target_pairs={{0,16},{1,17},{2,18},{3,19},{4,20},{5,21},{6,22},{7,23},{8,24},{9,... | collective-permute-start | bytes 614408 | tf_op jit(solution)/shard_map/gloss_to_owner/ppermute | solution.py:421
  153.7 3.3 %collective-permute-start.10 = (bf16[400,256]{1,0:T(8,128)(2,1)S(1)}, bf16[400,256]{1,0:T(8,128)(2,1)S(1)}, u32[]{:S(2)}, u32[]{:S(2)}) collective-permute-start(bf16[400,256]{1,0:T(8,128)(2,1)S(1)} %get-tuple-element.45), channel_id=1, source_target_pairs={{0,256},{1,257},{2,258},{3,259},{4,260},{5,261},{6,262},{7,263},{8... | collective-permute-start | bytes 614408 | tf_op jit(solution)/shard_map/gloss_to_owner/ppermute | solution.py:421
  157.0 2.0 %collective-permute-done.8.refs_1_ = bf16[400,256]{1,0:T(8,128)(2,1)S(1)} collective-permute-done((bf16[400,256]{1,0:T(8,128)(2,1)S(1)}, bf16[400,256]{1,0:T(8,128)(2,1)S(1)}, u32[]{:S(2)}, u32[]{:S(2)}) %collective-permute-start.8) | collective-permute-done | bytes 204832 | tf_op jit(solution)/shard_map/gloss_to_owner/ppermute | solution.py:421
  159.1 2.9 %collective-permute-done.9.refs_2_ = bf16[400,256]{1,0:T(8,128)(2,1)S(1)} collective-permute-done((bf16[400,256]{1,0:T(8,128)(2,1)S(1)}, bf16[400,256]{1,0:T(8,128)(2,1)S(1)}, u32[]{:S(2)}, u32[]{:S(2)}) %collective-permute-start.9) | collective-permute-done | bytes 204832 | tf_op jit(solution)/shard_map/gloss_to_owner/ppermute | solution.py:421
  162.0 2.7 %collective-permute-done.10.refs_3_ = bf16[400,256]{1,0:T(8,128)(2,1)S(1)} collective-permute-done((bf16[400,256]{1,0:T(8,128)(2,1)S(1)}, bf16[400,256]{1,0:T(8,128)(2,1)S(1)}, u32[]{:S(2)}, u32[]{:S(2)}) %collective-permute-start.10) | collective-permute-done | bytes 204832 | tf_op jit(solution)/shard_map/gloss_to_owner/ppermute | solution.py:421
  165.9 3.4 %all-to-all-start.4 = ((bf16[8,64,256]{2,1,0:T(8,128)(2,1)}), bf16[8,64,256]{2,1,0:T(8,128)(2,1)S(1)}, u32[]{:S(2)}, u32[]{:S(2)}) async-start(bf16[8,64,256]{2,1,0:T(8,128)(2,1)} %gloss_to_owner.1), calls=%async_computation.4 | async-start | bytes 524288 | tf_op jit(solution)/shard_map/gloss_to_owner/all_to_all | solution.py:424
  170.1 10.6 %all-to-all-done.4.got = bf16[8,64,256]{2,1,0:T(8,128)(2,1)S(1)} async-done(((bf16[8,64,256]{2,1,0:T(8,128)(2,1)}), bf16[8,64,256]{2,1,0:T(8,128)(2,1)S(1)}, u32[]{:S(2)}, u32[]{:S(2)}) %all-to-all-start.4) | async-done | bytes 262176 | tf_op jit(solution)/shard_map/gloss_to_owner/all_to_all | solution.py:424
  (57 shorter events, 22.5 us)
Async XLA Ops:
  0.6 0.8 copy-start
  27.8 16.9 %all-to-all-start.1 = ((bf16[8,48,256]{2,1,0:T(8,128)(2,1)}), bf16[8,48,256]{2,1,0:T(8,128)(2,1)S(1)}, u32[]{:S(2)}, u32[]{:S(2)}) async-start(bf16[8,48,256]{2,1,0:T(8,128)(2,1)} %get-tuple-element.30.g_ref), calls=%async_computation.1 | async-start | bytes 393216 | tf_op jit(solution)/shard_map/gather/all_to_all | solution.py:424
  34.9 25.9 %collective-permute-start = (bf16[8,96,256]{2,1,0:T(8,128)(2,1)S(1)}, bf16[8,96,256]{2,1,0:T(8,128)(2,1)S(1)}, u32[]{:S(2)}, u32[]{:S(2)}) collective-permute-start(bf16[8,96,256]{2,1,0:T(8,128)(2,1)S(1)} %all_to_all.30.v_mine), channel_id=1, source_target_pairs={{0,1},{1,0},{2,3},{3,2},{4,5},{5,4},{6,7},{7,6},{8,9},{9,8},{10,11... | collective-permute-start | bytes 1179656 | tf_op jit(solution)/shard_map/gather/ppermute | solution.py:418
  44.7 12.7 %collective-permute-start.3 = (bf16[8,48,256]{2,1,0:T(8,128)(2,1)S(1)}, bf16[8,48,256]{2,1,0:T(8,128)(2,1)S(1)}, u32[]{:S(2)}, u32[]{:S(2)}) collective-permute-start(bf16[8,48,256]{2,1,0:T(8,128)(2,1)S(1)} %all-to-all-done.1.g0), channel_id=1, source_target_pairs={{0,272},{1,273},{2,274},{3,275},{4,276},{5,277},{6,278},{7,279},{8... | collective-permute-start | bytes 589832 | tf_op jit(solution)/shard_map/gather/ppermute | solution.py:421
  49.3 9.1 %collective-permute-start.2 = (bf16[8,48,256]{2,1,0:T(8,128)(2,1)S(1)}, bf16[8,48,256]{2,1,0:T(8,128)(2,1)S(1)}, u32[]{:S(2)}, u32[]{:S(2)}) collective-permute-start(bf16[8,48,256]{2,1,0:T(8,128)(2,1)S(1)} %all-to-all-done.1.g0), channel_id=1, source_target_pairs={{0,16},{1,17},{2,18},{3,19},{4,20},{5,21},{6,22},{7,23},{8,24},{9,... | collective-permute-start | bytes 589832 | tf_op jit(solution)/shard_map/gather/ppermute | solution.py:421
  52.1 8.8 %collective-permute-start.1 = (bf16[8,48,256]{2,1,0:T(8,128)(2,1)S(1)}, bf16[8,48,256]{2,1,0:T(8,128)(2,1)S(1)}, u32[]{:S(2)}, u32[]{:S(2)}) collective-permute-start(bf16[8,48,256]{2,1,0:T(8,128)(2,1)S(1)} %all-to-all-done.1.g0), channel_id=1, source_target_pairs={{0,256},{1,257},{2,258},{3,259},{4,260},{5,261},{6,262},{7,263},{8... | collective-permute-start | bytes 589832 | tf_op jit(solution)/shard_map/gather/ppermute | solution.py:421
  67.8 0.9 copy-start.15
  68.7 0.9 copy-start.18
  69.6 34.3 %copy-start.13 = (bf16[2048,256]{1,0:T(8,128)(2,1)}, bf16[2048,256]{1,0:T(8,128)(2,1)S(1)}, u32[]{:S(2)}) copy-start(bf16[2048,256]{1,0:T(8,128)(2,1)S(1)} %get-tuple-element.36.g_ref) | copy-start | bytes 3145732
  69.6 11.3 %all-to-all-start.3 = ((f32[8,8,128]{2,1,0:T(8,128)}), f32[8,8,128]{2,1,0:T(8,128)S(1)}, u32[]{:S(2)}, u32[]{:S(2)}) async-start(f32[8,8,128]{2,1,0:T(8,128)} %get-tuple-element.34), calls=%async_computation.3 | async-start | bytes 65536 | tf_op jit(solution)/shard_map/batch_sums/all_to_all | solution.py:424
  73.0 35.1 %collective-permute-start.4 = (f32[8,128]{1,0:T(8,128)S(1)}, f32[8,128]{1,0:T(8,128)S(1)}, u32[]{:S(2)}, u32[]{:S(2)}) collective-permute-start(f32[8,128]{1,0:T(8,128)S(1)} %get-tuple-element.33), channel_id=1, source_target_pairs={{0,1},{1,0},{2,3},{3,2},{4,5},{5,4},{6,7},{7,6},{8,9},{9,8},{10,11... | collective-permute-start | bytes 12296 | tf_op jit(solution)/shard_map/batch_sums/ppermute | solution.py:418
  80.9 32.5 %collective-permute-start.7 = (f32[8,128]{1,0:T(8,128)S(1)}, f32[8,128]{1,0:T(8,128)S(1)}, u32[]{:S(2)}, u32[]{:S(2)}) collective-permute-start(f32[8,128]{1,0:T(8,128)S(1)} %reduce_sum.9.q0), channel_id=1, source_target_pairs={{0,272},{1,273},{2,274},{3,275},{4,276},{5,277},{6,278},{7,279},{8... | collective-permute-start | bytes 12296 | tf_op jit(solution)/shard_map/batch_sums/ppermute | solution.py:421
  83.1 30.3 %collective-permute-start.6 = (f32[8,128]{1,0:T(8,128)S(1)}, f32[8,128]{1,0:T(8,128)S(1)}, u32[]{:S(2)}, u32[]{:S(2)}) collective-permute-start(f32[8,128]{1,0:T(8,128)S(1)} %reduce_sum.9.q0), channel_id=1, source_target_pairs={{0,16},{1,17},{2,18},{3,19},{4,20},{5,21},{6,22},{7,23},{8,24},{9,... | collective-permute-start | bytes 12296 | tf_op jit(solution)/shard_map/batch_sums/ppermute | solution.py:421
  86.5 26.9 %collective-permute-start.5 = (f32[8,128]{1,0:T(8,128)S(1)}, f32[8,128]{1,0:T(8,128)S(1)}, u32[]{:S(2)}, u32[]{:S(2)}) collective-permute-start(f32[8,128]{1,0:T(8,128)S(1)} %reduce_sum.9.q0), channel_id=1, source_target_pairs={{0,256},{1,257},{2,258},{3,259},{4,260},{5,261},{6,262},{7,263},{8... | collective-permute-start | bytes 12296 | tf_op jit(solution)/shard_map/batch_sums/ppermute | solution.py:421
  89.6 1.1 copy-start.16
  90.8 1.1 copy-start.19
  104.0 2.7 %copy-start.8 = (bf16[8,1536,256]{2,1,0:T(8,128)(2,1)}, bf16[8,1536,256]{2,1,0:T(8,128)(2,1)S(1)}, u32[]{:S(2)}) copy-start(bf16[8,1536,256]{2,1,0:T(8,128)(2,1)S(1)} %get-tuple-element.40.p_ref) | copy-start | bytes 18874372
  106.7 1.4 copy-start.11
  108.7 15.9 %all-to-all-start.2 = ((f32[8,8,128]{2,1,0:T(8,128)}), f32[8,8,128]{2,1,0:T(8,128)S(1)}, u32[]{:S(2)}, u32[]{:S(2)}) async-start(f32[8,8,128]{2,1,0:T(8,128)} %broadcast_in_dim.2), calls=%async_computation.2 | async-start | bytes 65536 | tf_op jit(solution)/shard_map/batch_sums/all_to_all | solution.py:427
  113.4 2.8 %copy-start.9 = (bf16[8,1536,256]{2,1,0:T(8,128)(2,1)S(1)}, bf16[8,1536,256]{2,1,0:T(8,128)(2,1)}, u32[]{:S(2)}) copy-start(bf16[8,1536,256]{2,1,0:T(8,128)(2,1)} %copy-done.8) | copy-start | bytes 18874372
  116.2 1.2 copy-start.14
  124.8 12.1 %copy-start.17 = (bf16[1536,256]{1,0:T(8,128)(2,1)S(1)}, bf16[1536,256]{1,0:T(8,128)(2,1)}, u32[]{:S(2)}) copy-start(bf16[1536,256]{1,0:T(8,128)(2,1)} %copy-done.15) | copy-start | bytes 2359300
  124.8 3.8 %collective-permute-start.11 = (bf16[784,256]{1,0:T(8,128)(2,1)S(1)}, bf16[784,256]{1,0:T(8,128)(2,1)S(1)}, u32[]{:S(2)}, u32[]{:S(2)}) collective-permute-start(bf16[784,256]{1,0:T(8,128)(2,1)S(1)} %get-tuple-element.49), channel_id=1, source_target_pairs={{0,1},{1,0},{2,3},{3,2},{4,5},{5,4},{6,7},{7,6},{8,9},{9,8},{10,11... | collective-permute-start | bytes 1204232 | tf_op jit(solution)/shard_map/video_to_owner/ppermute | solution.py:418
  129.7 36.1 %all-to-all-start.5 = ((bf16[8,112,256]{2,1,0:T(8,128)(2,1)}), bf16[8,112,256]{2,1,0:T(8,128)(2,1)S(1)}, u32[]{:S(2)}, u32[]{:S(2)}) async-start(bf16[8,112,256]{2,1,0:T(8,128)(2,1)} %video_to_owner.1), calls=%async_computation.5 | async-start | bytes 917504 | tf_op jit(solution)/shard_map/video_to_owner/all_to_all | solution.py:427
  137.0 2.8 %copy-start.10 = (bf16[8,1536,256]{2,1,0:T(8,128)(2,1)S(1)}, bf16[8,1536,256]{2,1,0:T(8,128)(2,1)}, u32[]{:S(2)}) copy-start(bf16[8,1536,256]{2,1,0:T(8,128)(2,1)} %copy-done.8) | copy-start | bytes 18874372
  139.8 1.6 copy-start.12
  141.4 28.0 %copy-start.1 = (bf16[3,32,256]{2,1,0:T(8,128)(2,1)S(1)}, bf16[3,32,256]{2,1,0:T(8,128)(2,1)}, u32[]{:S(2)}) copy-start(bf16[3,32,256]{2,1,0:T(8,128)(2,1)} %video.3) | copy-start | bytes 147460
  146.7 34.1 %copy-start.3 = (bf16[3,16,256]{2,1,0:T(8,128)(2,1)S(1)}, bf16[3,16,256]{2,1,0:T(8,128)(2,1)}, u32[]{:S(2)}) copy-start(bf16[3,16,256]{2,1,0:T(8,128)(2,1)} %gloss.3) | copy-start | bytes 73732
  146.7 12.4 %collective-permute-start.8 = (bf16[400,256]{1,0:T(8,128)(2,1)S(1)}, bf16[400,256]{1,0:T(8,128)(2,1)S(1)}, u32[]{:S(2)}, u32[]{:S(2)}) collective-permute-start(bf16[400,256]{1,0:T(8,128)(2,1)S(1)} %get-tuple-element.43), channel_id=1, source_target_pairs={{0,272},{1,273},{2,274},{3,275},{4,276},{5,277},{6,278},{7,279},{8... | collective-permute-start | bytes 614408 | tf_op jit(solution)/shard_map/gloss_to_owner/ppermute | solution.py:421
  150.6 11.4 %collective-permute-start.9 = (bf16[400,256]{1,0:T(8,128)(2,1)S(1)}, bf16[400,256]{1,0:T(8,128)(2,1)S(1)}, u32[]{:S(2)}, u32[]{:S(2)}) collective-permute-start(bf16[400,256]{1,0:T(8,128)(2,1)S(1)} %get-tuple-element.44), channel_id=1, source_target_pairs={{0,16},{1,17},{2,18},{3,19},{4,20},{5,21},{6,22},{7,23},{8,24},{9,... | collective-permute-start | bytes 614408 | tf_op jit(solution)/shard_map/gloss_to_owner/ppermute | solution.py:421
  153.7 11.0 %collective-permute-start.10 = (bf16[400,256]{1,0:T(8,128)(2,1)S(1)}, bf16[400,256]{1,0:T(8,128)(2,1)S(1)}, u32[]{:S(2)}, u32[]{:S(2)}) collective-permute-start(bf16[400,256]{1,0:T(8,128)(2,1)S(1)} %get-tuple-element.45), channel_id=1, source_target_pairs={{0,256},{1,257},{2,258},{3,259},{4,260},{5,261},{6,262},{7,263},{8... | collective-permute-start | bytes 614408 | tf_op jit(solution)/shard_map/gloss_to_owner/ppermute | solution.py:421
  165.9 14.9 %all-to-all-start.4 = ((bf16[8,64,256]{2,1,0:T(8,128)(2,1)}), bf16[8,64,256]{2,1,0:T(8,128)(2,1)S(1)}, u32[]{:S(2)}, u32[]{:S(2)}) async-start(bf16[8,64,256]{2,1,0:T(8,128)(2,1)} %gloss_to_owner.1), calls=%async_computation.4 | async-start | bytes 524288 | tf_op jit(solution)/shard_map/gloss_to_owner/all_to_all | solution.py:424
  (5 other events, 3.4 us)

commit v2 on v1

--- a/solution.py
+++ b/solution.py
@@ -26,6 +26,7 @@
 GROWS = GLOSSES * LANES
 VOWN = FRAMES * OWN
 GOWN = GLOSSES * OWN
+SLOT = OWN * NY
 EXTRA = 16
 PAIRS = GLOSSES // 2
 
@@ -33,7 +34,15 @@
 Y_GROUPS = [[h * 16 + 2 * i + c for i in range(NY)] for h in range(2) for c in range(NCORE)]
 
 
-def params(limit_mb=40):
+def flat(x, z, y, core):
+    return ((x % 2) * NZ + z) * 32 + (x // 2) * 16 + 2 * y + core
+
+
+XY_GROUPS = [[flat(x, z, y, c) for x in range(NX) for y in range(NY)] for z in range(NZ) for c in range(NCORE)]
+ZC_GROUPS = [[flat(x, z, y, c) for c in range(NCORE) for z in range(NZ)] for x in range(NX) for y in range(NY)]
+
+
+def params(limit_mb=16):
     return pltpu.CompilerParams(vmem_limit_bytes=limit_mb * 1024 * 1024)
 
 
@@ -89,7 +98,18 @@
     return pltpu.VMEM((2, rows, LANES), F32)
 
 
-def units_kernel(fc, gc, video, gloss, v_out, g_out, v_scr, g_scr):
+def units_kernel(fc_in, gc_in, video_in, gloss_in, v_out, g_out, count_out, fc, gc, video, gloss, v_scr, g_scr, sems):
+    pairs = ((fc_in, fc), (gc_in, gc), (video_in, video), (gloss_in, gloss))
+    copies = [pltpu.make_async_copy(a, b, sems.at[i]) for i, (a, b) in enumerate(pairs)]
+    for copy in copies:
+        copy.start()
+    for copy in copies:
+        copy.wait()
+    row = iota((8, LANES), 0)
+    counts = jnp.zeros((8, LANES), jnp.int32)
+    for c in range(OWN):
+        counts = jnp.where(row == c, fc[c], jnp.where(row == OWN + c, gc[c], counts))
+    count_out[...] = counts
     for count, raw, scr, tokens in ((fc, video, v_scr, FRAMES), (gc, gloss, g_scr, GLOSSES)):
         row, lane = iota((tokens, WIDTH), 0), iota((tokens, WIDTH), 1)
         for c in range(OWN):
@@ -106,10 +126,12 @@
         g_out[i] = g
 
 
-def diagonal_kernel(fc, gc, v_ref, g_ref, dv, dg, logit_sum):
+def diagonal_kernel(count_ref, v_ref, g_ref, dv, dg, logit_sum):
     def pick(count, which):
         return jnp.where(which == 0, count[0], jnp.where(which == 1, count[1], count[2]))
 
+    fc = [count_ref[c : c + 1, 0:1] for c in range(OWN)]
+    gc = [count_ref[OWN + c : OWN + c + 1, 0:1] for c in range(OWN)]
     v, g = v_ref[0], g_ref[0]
     shape = (VOWN, GOWN)
     r, q = iota(shape, 0), iota(shape, 1)
@@ -141,7 +163,7 @@
 
 def forward_kernel(
     v_mine, v_twin, g0, g1, g2, g3, diag,
-    v_out, g_out, row_out, col_out, e_out, r_mine, r_twin, c_out,
+    v_out, g_out, row_out, col_out, e_out, r_out, c_out,
     v_scr, g_scr, frame_mask, gloss_mask, rows, cols,
 ):
     for t, ref in enumerate((v_mine, v_twin)):
@@ -216,12 +238,19 @@
     spread = jnp.broadcast_to(sums, (CLIPS_DEV, LANES))
     row_mine = jnp.sum(jnp.where(lane == clip, spread, 0.0), axis=0, keepdims=True)
     row_twin = jnp.sum(jnp.where(lane == swapped, spread, 0.0), axis=0, keepdims=True)
-    at_diag = iota((8, LANES), 1) == CLIPS_DEV
-    r_mine[...] = jnp.where(at_diag, diag[...], jnp.broadcast_to(row_mine, (8, LANES)))
-    r_twin[...] = jnp.where(at_diag, diag[...], jnp.broadcast_to(row_twin, (8, LANES)))
+    row8, lane8 = iota((8, LANES), 0), iota((8, LANES), 1)
+    r_rows = jnp.where(row8 == 1, row_twin, row_mine)
+    r_rows = jnp.where(lane8 == CLIPS_DEV, diag[...], r_rows)
+    for i in range(NZ * NCORE):
+        r_out[i] = r_rows
     c_row = jnp.broadcast_to(jnp.sum(e_pair, axis=0, keepdims=True), (8, LANES))
-    for i in range(NY):
-        c_out[i] = c_row
+    c_rows = c_row
+    for s in range(1, NX):
+        ahead = pltpu.roll(c_row, SLOT * s, 1)
+        behind = pltpu.roll(c_row, (SLOT * s - TEXTS_DEV) % LANES, 1)
+        c_rows = jnp.where(row8 == s, jnp.where(lane8 < SLOT * s, behind, ahead), c_rows)
+    for i in range(NX * NY):
+        c_out[i] = c_rows
 
 
 def weights_kernel(v_ref, g_ref, row_ref, col_ref, e_ref, p_out, av_out, ag_out):
@@ -250,21 +279,26 @@
     ag_out[...] = tn(weights, v_ref[...])
 
 
-def text_sums(q0, q1, q2, q3):
-    lane = iota((8, LANES), 1)
-    slot = OWN * NY
-    total = q0[...]
-    for s, q in enumerate((q1, q2, q3), start=1):
-        part = q[...]
-        ahead = pltpu.roll(part, slot * s, 1)
-        behind = pltpu.roll(part, (slot * s - TEXTS_DEV) % LANES, 1)
-        total = total + jnp.where(lane < slot * s, behind, ahead)
-    return jnp.where(lane < TEXTS_DEV, total, 0.0)
-
-
-def by_text_kernel(q0, q1, q2, q3, p_ref, g_ref, out):
+def text_sums(got):
+    x = 2 * lax.div(lax.axis_index("inner"), 16) + lax.div(lax.axis_index("outer"), NZ)
+    total = jnp.zeros((1, LANES), F32)
+    for s in range(NX):
+        base = lax.rem(x - s + NX, NX) * NY
+        part = got[base]
+        for i in range(1, NY):
+            part = part + got[base + i]
+        total = total + part[s : s + 1]
+    return jnp.where(iota((1, LANES), 1) < TEXTS_DEV, total, 0.0)
+
+
+def by_text_kernel(got, p_ref, g_ref, out, c_out):
     step = pl.program_id(0)
-    c_row = text_sums(q0, q1, q2, q3)
+
+    @pl.when(step == 0)
+    def _():
+        c_out[...] = jnp.broadcast_to(text_sums(got), (8, LANES))
+
+    c_row = c_out[...]
     inverse = jnp.where(c_row > 0.0, 1.0 / c_row, 0.0)
     col = jnp.broadcast_to(column_of(inverse, LANES), (LANES, WIDTH))
     scaled = g_ref[...].astype(F32) * jnp.concatenate([col, col], axis=0)
@@ -281,14 +315,19 @@
         out[...] = out[...] + part
 
 
-def clip_sums(z_ref):
-    total = z_ref[0]
-    for i in range(1, NZ):
-        total = total + z_ref[i]
-    return total
-
-
-def video_partial_kernel(z_ref, q0, q1, q2, q3, av_ref, bv_ref, mine, twin):
+def clip_sums(got):
+    core = lax.rem(lax.axis_index("inner"), NCORE)
+    total = jnp.zeros((1, LANES), F32)
+    for t in range(NCORE):
+        base = lax.rem(core + t, NCORE) * NZ
+        part = got[base]
+        for i in range(1, NZ):
+            part = part + got[base + i]
+        total = total + part[t : t + 1]
+    return jnp.broadcast_to(total, (8, LANES))
+
+
+def video_partial_kernel(z_ref, c_ref, av_ref, bv_ref, mine, twin):
     r_row = clip_sums(z_ref)
     inverse = jnp.broadcast_to(1.0 / column_of(r_row, CLIPS_DEV), (CLIPS_DEV, WIDTH))
     half = CLIPS_DEV // 2
@@ -300,20 +339,20 @@
             mine[pl.ds(f * half, half), :] = block[:half]
             blocks.append(block[half:])
         twin[pl.ds(pair * CLIPS_DEV, CLIPS_DEV), :] = jnp.concatenate(blocks, axis=0).astype(BF16)
-    c_row = text_sums(q0, q1, q2, q3)[0:1]
+    c_row = c_ref[0:1]
     logs = jnp.where(iota((1, LANES), 1) < TEXTS_DEV, jnp.log(jnp.where(c_row > 0.0, c_row, 1.0)), 0.0)
     total = pieces(jnp.sum(logs, axis=1, keepdims=True))
     mine[pl.ds(FRAMES * half, EXTRA), :] = total
     twin[pl.ds(FRAMES * half, EXTRA), :] = total.astype(BF16)
 
 
-def gloss_partial_kernel(z_ref, q0, q1, q2, q3, p_ref, v_ref, ag_ref, s0, s1, s2, s3, v_hi, v_low):
+def gloss_partial_kernel(z_ref, c_ref, p_ref, v_ref, ag_ref, s0, s1, s2, s3, v_hi, v_low):
     step = pl.program_id(0)
-    r_row = clip_sums(z_ref)
-    slot = OWN * NY
+    slot = SLOT
 
     @pl.when(step == 0)
     def _():
+        r_row = clip_sums(z_ref)
         inverse = jnp.broadcast_to(1.0 / column_of(r_row, CLIPS_DEV), (CLIPS_DEV, WIDTH))
         for f in range(FRAMES):
             at = pl.ds(f * CLIPS_DEV, CLIPS_DEV)
@@ -331,7 +370,7 @@
         for out in (s1, s2, s3):
             out[at, :] = total.astype(BF16)
 
-    c_row = text_sums(q0, q1, q2, q3)
+    c_row = c_ref[...]
     inverse = jnp.where(c_row > 0.0, 1.0 / c_row, 0.0)
     col = jnp.broadcast_to(column_of(inverse, LANES), (LANES, WIDTH))
     part = tn(p_ref[0], v_hi[...]) + tn(p_ref[0], v_low[...])
@@ -402,7 +441,7 @@
 
 
 def on_device(clips, video, gloss, frame_count, gloss_count):
-    vmem, smem = pl.BlockSpec(memory_space=pltpu.VMEM), pl.BlockSpec(memory_space=pltpu.SMEM)
+    vmem = pl.BlockSpec(memory_space=pltpu.VMEM)
     core_pairs = [(i, i ^ 1) for i in range(NX // 2 * NY * NCORE)]
 
     def x_shift(s):
@@ -410,8 +449,7 @@
         for x in range(NX):
             for z in range(NZ):
                 for rest in range(NY * NCORE):
-                    flat = [((a % 2) * NZ + z) * 32 + (a // 2) * 16 + rest for a in (x, (x + s) % NX)]
-                    pairs.append((flat[0], flat[1]))
+                    pairs.append((flat(x, z, 0, rest), flat((x + s) % NX, z, 0, rest)))
         return sorted(pairs)
 
     def to_core(a):
@@ -426,20 +464,35 @@
     def over_z(a):
         return lax.all_to_all(a, "outer", 0, 0, axis_index_groups=Z_GROUPS, tiled=True)
 
+    def over_groups(a, groups):
+        return lax.all_to_all(a, ("outer", "inner"), 0, 0, axis_index_groups=groups, tiled=True)
+
     with jax.named_scope("unit_tokens"):
-        v_own, g_own = pl.pallas_call(
+        v_own, g_own, counts = pl.pallas_call(
             units_kernel,
-            in_specs=[smem, smem, vmem, vmem],
-            out_shape=(shape(NZ, VOWN, WIDTH, dtype=BF16), shape(NY, GOWN, WIDTH, dtype=BF16)),
-            scratch_shapes=[two_halves(VOWN), two_halves(GOWN)],
+            in_specs=[pl.BlockSpec(memory_space=pltpu.HBM)] * 4,
+            out_shape=(
+                shape(NZ, VOWN, WIDTH, dtype=BF16),
+                shape(NY, GOWN, WIDTH, dtype=BF16),
+                shape(8, LANES, dtype=jnp.int32),
+            ),
+            scratch_shapes=[
+                pltpu.SMEM((OWN,), jnp.int32),
+                pltpu.SMEM((OWN,), jnp.int32),
+                pltpu.VMEM((OWN, FRAMES, WIDTH), BF16),
+                pltpu.VMEM((OWN, GLOSSES, WIDTH), BF16),
+                two_halves(VOWN),
+                two_halves(GOWN),
+                pltpu.SemaphoreType.DMA((4,)),
+            ],
             compiler_params=params(),
             cost_estimate=cost(2e5, 7e5),
         )(frame_count, gloss_count, video, gloss)
 
     with jax.named_scope("gather"):
-        g_mine = over_y(g_own)
+        g_mine, v_ready = lax.optimization_barrier((over_y(g_own), v_own))
         g_parts = [g_mine] + [to_x(g_mine, s) for s in range(1, NX)]
-        v_mine = over_z(v_own)
+        v_mine = over_z(v_ready)
         v_twin = to_core(v_mine)
 
     def first(rows):
@@ -452,15 +505,15 @@
         dv_diag, dg_diag, logit_sum = pl.pallas_call(
             diagonal_kernel,
             grid=(1,),
-            in_specs=[smem, smem, first(VOWN), first(GOWN)],
+            in_specs=[whole(8, LANES), first(VOWN), first(GOWN)],
             out_specs=(whole(VOWN, WIDTH), whole(GOWN, WIDTH), whole(8, LANES)),
             out_shape=(shape(VOWN, WIDTH), shape(GOWN, WIDTH), shape(8, LANES)),
             compiler_params=params(),
             cost_estimate=cost(2e7, 3e5),
-        )(frame_count, gloss_count, v_own, g_own)
+        )(counts, v_own, g_own)
 
     with jax.named_scope("forward"):
-        v_all, g_all, row_inv, col_inv, e_pair, r_mine, r_twin, c_part = pl.pallas_call(
+        v_all, g_all, row_inv, col_inv, e_pair, r_part, c_part = pl.pallas_call(
             forward_kernel,
             in_specs=[vmem] * 7,
             out_shape=(
@@ -469,9 +522,8 @@
                 shape(VROWS, LANES),
                 shape(GLOSSES, CLIPS_DEV, LANES),
                 shape(CLIPS_DEV, LANES),
-                shape(8, LANES),
-                shape(8, LANES),
-                shape(NY, 8, LANES),
+                shape(NZ * NCORE, 8, LANES),
+                shape(NX * NY, 8, LANES),
             ),
             scratch_shapes=[
                 pltpu.VMEM((NCORE, 2, NZ * VOWN, LANES), F32),
@@ -486,10 +538,8 @@
         )(v_mine, v_twin, *g_parts, logit_sum)
 
     with jax.named_scope("batch_sums"):
-        c_mine = jnp.sum(over_y(c_part), axis=0)
-        c_parts = [c_mine] + [to_x(c_mine, s) for s in range(1, NX)]
-        r_pair = r_mine + to_core(r_twin)
-        r_got = over_z(jnp.broadcast_to(r_pair[None], (NZ, 8, LANES)))
+        c_got, r_ready = lax.optimization_barrier((over_groups(c_part, XY_GROUPS), r_part))
+        r_got = over_groups(r_ready, ZC_GROUPS)
 
     def halves(rows):
         return pl.BlockSpec((rows, WIDTH), lambda i: (i, 0))
@@ -512,27 +562,26 @@
             cost_estimate=cost(6 * VROWS * GROWS * WIDTH, 16e6, VROWS * GROWS),
         )(v_all, g_all, row_inv, col_inv, e_pair)
 
-    part_spec = whole(8, LANES)
     with jax.named_scope("by_text"):
-        bv = pl.pallas_call(
+        bv, c_sums = pl.pallas_call(
             by_text_kernel,
             grid=(PAIRS,),
-            in_specs=[part_spec] * 4 + [p_spec, halves(2 * LANES)],
-            out_specs=whole(VROWS, WIDTH),
-            out_shape=shape(VROWS, WIDTH),
+            in_specs=[whole(NX * NY, 8, LANES), p_spec, halves(2 * LANES)],
+            out_specs=(whole(VROWS, WIDTH), whole(8, LANES)),
+            out_shape=(shape(VROWS, WIDTH), shape(8, LANES)),
             compiler_params=params(),
             cost_estimate=cost(4 * VROWS * GROWS * WIDTH, 9e6),
-        )(*c_parts, weights, g_all)
+        )(c_got, weights, g_all)
 
     with jax.named_scope("video_partial"):
         v_rows = FRAMES * CLIPS_DEV // 2 + EXTRA
         dv_mine, dv_twin = pl.pallas_call(
             video_partial_kernel,
-            in_specs=[vmem] * 7,
+            in_specs=[vmem] * 4,
             out_shape=(shape(v_rows, WIDTH), shape(v_rows, WIDTH, dtype=BF16)),
             compiler_params=params(),
             cost_estimate=cost(2e6, 5e6),
-        )(r_got, *c_parts, av, bv)
+        )(r_got, c_sums, av, bv)
     with jax.named_scope("video_to_owner"):
         dv_got = to_core(dv_twin)
         dv_send = pl.pallas_call(
@@ -546,17 +595,17 @@
         dv_parts = over_z(dv_send)
 
     with jax.named_scope("gloss_partial"):
-        g_rows = GLOSSES * OWN * NY + EXTRA
+        g_rows = GLOSSES * SLOT + EXTRA
         dg_slots = pl.pallas_call(
             gloss_partial_kernel,
             grid=(PAIRS,),
-            in_specs=[whole(NZ, 8, LANES)] + [part_spec] * 4 + [p_spec, whole(VROWS, WIDTH), halves(2 * LANES)],
+            in_specs=[whole(NZ * NCORE, 8, LANES), whole(8, LANES), p_spec, whole(VROWS, WIDTH), halves(2 * LANES)],
             out_specs=(whole(g_rows, WIDTH),) * NX,
             out_shape=(shape(g_rows, WIDTH),) + (shape(g_rows, WIDTH, dtype=BF16),) * (NX - 1),
             scratch_shapes=[pltpu.VMEM((VROWS, WIDTH), BF16), pltpu.VMEM((VROWS, WIDTH), BF16)],
             compiler_params=params(),
             cost_estimate=cost(4 * VROWS * GROWS * WIDTH, 9e6),
-        )(r_got, *c_parts, weights, v_all, ag)
+        )(r_got, c_sums, weights, v_all, ag)
     with jax.named_scope("gloss_to_owner"):
         dg_got = [to_x(dg_slots[s], -s) for s in range(1, NX)]
         dg_send = pl.pallas_call(

time: 183 us -> 173 us (0.945)
  blocking collectives: 23 us -> 38.4 us
  starting transfers between devices: 60.8 us -> 47.4 us
  waiting for transfers between devices: 37.3 us -> 29.3 us
  local copies, waits for them, and re-layouts: 21.3 us -> 19.2 us
    all_to_all x0 -> x1, blocking collectives: none -> 17.4 us  [over_y(): lax.all_to_all(a, 'inner', 0, 0, axis_index_groups=Y_GROUPS, tiled=True)]
    all_to_all x3 -> x1, waiting for transfers between devices: 24.5 us -> 10.6 us  [over_y(): lax.all_to_all(a, 'inner', 0, 0, axis_index_groups=Y_GROUPS, tiled=True)]
    all_to_all x0 -> x2, starting transfers between devices: none -> 8.74 us  [over_groups(): lax.all_to_all(a, ('outer', 'inner'), 0, 0, axis_index_groups=groups, til...]
    ppermute x9 -> x6, starting transfers between devices: 29.2 us -> 20.6 us  [to_x(): return lax.ppermute(a, ('outer', 'inner'), x_shift(s % NX))]
    all_to_all x3 -> x1, starting transfers between devices: 13.9 us -> 6.67 us  [over_y(): lax.all_to_all(a, 'inner', 0, 0, axis_index_groups=Y_GROUPS, tiled=True)]
    ppermute x9 -> x6, waiting for transfers between devices: 11.1 us -> 17.1 us  [to_x(): return lax.ppermute(a, ('outer', 'inner'), x_shift(s % NX))]
    all_to_all x2 -> x1, starting transfers between devices: 11.9 us -> 7.23 us  [over_z(): lax.all_to_all(a, 'outer', 0, 0, axis_index_groups=Z_GROUPS, tiled=True)]
    all_to_all x1, blocking collectives: 23 us -> 21 us  [over_z(): lax.all_to_all(a, 'outer', 0, 0, axis_index_groups=Z_GROUPS, tiled=True)]
  transfers between devices with their start and end apart: 17 -> 12, of which waited for: 9 -> 8; matrix products, arithmetic and copies ran while one was open for 0% -> 0% of each run, Pallas kernels for 15% -> 15%
where the time goes in v2:
time: 173 us; the launch traced here: 172 us
  starting transfers between devices  47.4 us (27%)
  blocking collectives  38.4 us (22%)
  Pallas kernels  36.5 us (21%)
  waiting for transfers between devices  29.3 us (17%)
  local copies, waits for them, and re-layouts  19.2 us (11%)
    all_to_all x1, blocking collectives, over_z(): lax.all_to_all(a, 'outer', 0, 0, axis_index_groups=Z_GROUPS, tiled=True)  21 us
    ppermute x6, starting transfers between devices, to_x(): return lax.ppermute(a, ('outer', 'inner'), x_shift(s % NX))  20.6 us
    unnamed x36, local copies, waits for them, and re-layouts  19.2 us
    all_to_all x1, blocking collectives, over_y(): lax.all_to_all(a, 'inner', 0, 0, axis_index_groups=Y_GROUPS, tiled=True)  17.4 us
    ppermute x6, waiting for transfers between devices, to_x(): return lax.ppermute(a, ('outer', 'inner'), x_shift(s % NX))  17.1 us
    pallas_call x1, Pallas kernels, on_device(): pl.pallas_call(weights_kernel, grid=(PAIRS,), in_specs=[whole(VROWS, WIDT...  12.1 us
    all_to_all x1, waiting for transfers between devices, over_y(): lax.all_to_all(a, 'inner', 0, 0, axis_index_groups=Y_GROUPS, tiled=True)  10.6 us
    all_to_all x2, starting transfers between devices, over_groups(): lax.all_to_all(a, ('outer', 'inner'), 0, 0, axis_index_groups=groups, til...  8.74 us
  transfers between devices with their start and end apart: 12, of which 8 were waited for; matrix products, arithmetic and copies ran while one was open for 0% of the time, Pallas kernels for 15%

profile of v2, /device:TPU:64, one launch (start us, length us, event | category | flops | bytes accessed | tf_op | source)
XLA Modules:
  0.0 171.6 jit_solution(9790397623725398086)
XLA Ops:
  4.2 17.4 %all_to_all.30.g0 = bf16[8,48,256]{2,1,0:T(8,128)(2,1)S(1)} all-to-all(bf16[8,48,256]{2,1,0:T(8,128)(2,1)S(1)} %get-tuple-element.35.g_ref), channel_id=1, replica_groups={{0,2,4,6,8,10,12,14},{1,3,5,7,9,11,13,15},{16,18,20,22,24,26,28,30},{17..., dimensions={0} | all-to-all | bytes 393216 | tf_op jit(solution)/shard_map/gather/all_to_all | solution.py:462
  21.6 21.0 %all_to_all.31.v_mine = bf16[8,96,256]{2,1,0:T(8,128)(2,1)S(1)} all-to-all(bf16[8,96,256]{2,1,0:T(8,128)(2,1)S(1)} %get-tuple-element.37.v_ref), channel_id=1, replica_groups={{0,32,64,96,128,160,192,224},{256,288,320,352,384,416,448,480},{1,33,65..., dimensions={0} | all-to-all | bytes 786432 | tf_op jit(solution)/shard_map/gather/all_to_all | solution.py:465
  42.6 1.9 %collective-permute-start = (bf16[8,96,256]{2,1,0:T(8,128)(2,1)S(1)}, bf16[8,96,256]{2,1,0:T(8,128)(2,1)S(1)}, u32[]{:S(2)}, u32[]{:S(2)}) collective-permute-start(bf16[8,96,256]{2,1,0:T(8,128)(2,1)S(1)} %all_to_all.31.v_mine), channel_id=1, source_target_pairs={{0,1},{1,0},{2,3},{3,2},{4,5},{5,4},{6,7},{7,6},{8,9},{9,8},{10,11... | collective-permute-start | bytes 1179656 | tf_op jit(solution)/shard_map/gather/ppermute | solution.py:456
  44.6 4.7 %collective-permute-start.3 = (bf16[8,48,256]{2,1,0:T(8,128)(2,1)S(1)}, bf16[8,48,256]{2,1,0:T(8,128)(2,1)S(1)}, u32[]{:S(2)}, u32[]{:S(2)}) collective-permute-start(bf16[8,48,256]{2,1,0:T(8,128)(2,1)S(1)} %all_to_all.30.g0), channel_id=1, source_target_pairs={{0,272},{1,273},{2,274},{3,275},{4,276},{5,277},{6,278},{7,279},{8... | collective-permute-start | bytes 589832 | tf_op jit(solution)/shard_map/gather/ppermute | solution.py:459
  49.2 2.7 %collective-permute-start.2 = (bf16[8,48,256]{2,1,0:T(8,128)(2,1)S(1)}, bf16[8,48,256]{2,1,0:T(8,128)(2,1)S(1)}, u32[]{:S(2)}, u32[]{:S(2)}) collective-permute-start(bf16[8,48,256]{2,1,0:T(8,128)(2,1)S(1)} %all_to_all.30.g0), channel_id=1, source_target_pairs={{0,16},{1,17},{2,18},{3,19},{4,20},{5,21},{6,22},{7,23},{8,24},{9,... | collective-permute-start | bytes 589832 | tf_op jit(solution)/shard_map/gather/ppermute | solution.py:459
  51.9 2.8 %collective-permute-start.1 = (bf16[8,48,256]{2,1,0:T(8,128)(2,1)S(1)}, bf16[8,48,256]{2,1,0:T(8,128)(2,1)S(1)}, u32[]{:S(2)}, u32[]{:S(2)}) collective-permute-start(bf16[8,48,256]{2,1,0:T(8,128)(2,1)S(1)} %all_to_all.30.g0), channel_id=1, source_target_pairs={{0,256},{1,257},{2,258},{3,259},{4,260},{5,261},{6,262},{7,263},{8... | collective-permute-start | bytes 589832 | tf_op jit(solution)/shard_map/gather/ppermute | solution.py:459
  55.4 2.9 %collective-permute-done.3.g3 = bf16[8,48,256]{2,1,0:T(8,128)(2,1)S(1)} collective-permute-done((bf16[8,48,256]{2,1,0:T(8,128)(2,1)S(1)}, bf16[8,48,256]{2,1,0:T(8,128)(2,1)S(1)}, u32[]{:S(2)}, u32[]{:S(2)}) %collective-permute-start.3) | collective-permute-done | bytes 196640 | tf_op jit(solution)/shard_map/gather/ppermute | solution.py:459
  58.3 2.1 %collective-permute-done.2.g2 = bf16[8,48,256]{2,1,0:T(8,128)(2,1)S(1)} collective-permute-done((bf16[8,48,256]{2,1,0:T(8,128)(2,1)S(1)}, bf16[8,48,256]{2,1,0:T(8,128)(2,1)S(1)}, u32[]{:S(2)}, u32[]{:S(2)}) %collective-permute-start.2) | collective-permute-done | bytes 196640 | tf_op jit(solution)/shard_map/gather/ppermute | solution.py:459
  60.4 3.5 %collective-permute-done.1.g1 = bf16[8,48,256]{2,1,0:T(8,128)(2,1)S(1)} collective-permute-done((bf16[8,48,256]{2,1,0:T(8,128)(2,1)S(1)}, bf16[8,48,256]{2,1,0:T(8,128)(2,1)S(1)}, u32[]{:S(2)}, u32[]{:S(2)}) %collective-permute-start.1) | collective-permute-done | bytes 196640 | tf_op jit(solution)/shard_map/gather/ppermute | solution.py:459
  63.9 7.1 %forward.1 = (bf16[1536,256]{1,0:T(8,128)(2,1)S(1)}, bf16[2048,256]{1,0:T(8,128)(2,1)S(1)}, f32[1536,128]{1,0:T(8,128)S(1)}, f32[16,48,128]{2,1,0:T(8,128)S(1)},...) custom-call(bf16[8,96,256]{2,1,0:T(8,128)(2,1)S(1)} %all_to_all.31.v_mine, ...), custom_call_target="tpu_custom_call" | custom-call | flops 1610612736 | bytes 8000000 | tf_op jit(solution)/shard_map/forward/pallas_call | solution.py:516
  72.7 4.0 %all-to-all-start.2 = ((f32[32,8,128]{2,1,0:T(8,128)}), f32[32,8,128]{2,1,0:T(8,128)S(1)}, u32[]{:S(2)}, u32[]{:S(2)}) async-start(f32[32,8,128]{2,1,0:T(8,128)} %get-tuple-element.41), calls=%async_computation.2 | async-start | bytes 262144 | tf_op jit(solution)/shard_map/batch_sums/all_to_all | solution.py:468
  78.9 12.1 %weights.1 = (bf16[8,1536,256]{2,1,0:T(8,128)(2,1)S(1)}, f32[1536,256]{1,0:T(8,128)S(1)}, f32[2048,256]{1,0:T(8,128)S(1)}) custom-call(bf16[1536,256]{1,0:T(8,128)(2,1)S(1)} %get-tuple-element.45.v_ref, bf16[2048,256]{1,0:T(8,128)(2,1)S(1)} %copy-done.14, f32[1536,128]{1,0:T(8,128)S(1)} %get-tuple-element.47.row_ref, f32[16,48,128]{2,1,0:T(8,128)S(1)} %copy-done.17, ...), custom_call_target="tpu_custom_call" | custom-call | flops 4831838208 | bytes 16000000 | tf_op jit(solution)/shard_map/weights/pallas_call | solution.py:549
  91.0 2.6 %copy-done.6 = bf16[8,1536,256]{2,1,0:T(8,128)(2,1)} copy-done((bf16[8,1536,256]{2,1,0:T(8,128)(2,1)}, bf16[8,1536,256]{2,1,0:T(8,128)(2,1)S(1)}, u32[]{:S(2)}) %copy-start.6) | copy-done | bytes 6291480
  93.7 1.4 copy-done.9
  95.1 4.7 %all-to-all-start.3 = ((f32[16,8,128]{2,1,0:T(8,128)}), f32[16,8,128]{2,1,0:T(8,128)S(1)}, u32[]{:S(2)}, u32[]{:S(2)}) async-start(f32[16,8,128]{2,1,0:T(8,128)} %get-tuple-element.43), calls=%async_computation.3 | async-start | bytes 131072 | tf_op jit(solution)/shard_map/batch_sums/all_to_all | solution.py:468
  99.8 2.8 %copy-done.7 = bf16[8,1536,256]{2,1,0:T(8,128)(2,1)S(1)} copy-done((bf16[8,1536,256]{2,1,0:T(8,128)(2,1)S(1)}, bf16[8,1536,256]{2,1,0:T(8,128)(2,1)}, u32[]{:S(2)}) %copy-start.7) | copy-done | bytes 6291480
  102.6 1.2 copy-done.15
  103.8 6.6 %by_text.1 = (f32[1536,256]{1,0:T(8,128)S(1)}, f32[8,128]{1,0:T(8,128)S(1)}) custom-call(f32[32,8,128]{2,1,0:T(8,128)S(1)} %all-to-all-done.2.got, bf16[8,1536,256]{2,1,0:T(8,128)(2,1)S(1)} %copy-done.7, bf16[2048,256]{1,0:T(8,128)(2,1)S(1)} %copy-done.15), custom_call_target="tpu_custom_call" | custom-call | flops 3221225472 | bytes 9000000 | tf_op jit(solution)/shard_map/by_text/pallas_call | solution.py:566
  110.7 2.2 %collective-permute-start.7 = (bf16[784,256]{1,0:T(8,128)(2,1)S(1)}, bf16[784,256]{1,0:T(8,128)(2,1)S(1)}, u32[]{:S(2)}, u32[]{:S(2)}) collective-permute-start(bf16[784,256]{1,0:T(8,128)(2,1)S(1)} %get-tuple-element.61), channel_id=1, source_target_pairs={{0,1},{1,0},{2,3},{3,2},{4,5},{5,4},{6,7},{7,6},{8,9},{9,8},{10,11... | collective-permute-start | bytes 1204232 | tf_op jit(solution)/shard_map/video_to_owner/ppermute | solution.py:456
  112.9 1.5 collective-permute-done.7.refs_1_
  115.6 7.2 %all-to-all-start.5 = ((bf16[8,112,256]{2,1,0:T(8,128)(2,1)}), bf16[8,112,256]{2,1,0:T(8,128)(2,1)S(1)}, u32[]{:S(2)}, u32[]{:S(2)}) async-start(bf16[8,112,256]{2,1,0:T(8,128)(2,1)} %video_to_owner.1), calls=%async_computation.5 | async-start | bytes 917504 | tf_op jit(solution)/shard_map/video_to_owner/all_to_all | solution.py:465
  122.9 2.8 %copy-done.8 = bf16[8,1536,256]{2,1,0:T(8,128)(2,1)S(1)} copy-done((bf16[8,1536,256]{2,1,0:T(8,128)(2,1)S(1)}, bf16[8,1536,256]{2,1,0:T(8,128)(2,1)}, u32[]{:S(2)}) %copy-start.8) | copy-done | bytes 6291480
  125.7 1.6 copy-done.10
  127.2 5.3 %gloss_partial.1 = (f32[400,256]{1,0:T(8,128)S(1)}, bf16[400,256]{1,0:T(8,128)(2,1)S(1)}, bf16[400,256]{1,0:T(8,128)(2,1)S(1)}, bf16[400,256]{1,0:T(8,128)(2,1)S(1)}) custom-call(f32[16,8,128]{2,1,0:T(8,128)S(1)} %all-to-all-done.3.z_ref, f32[8,128]{1,0:T(8,128)S(1)} %get-tuple-element.51.c_ref, bf16[8,1536,256]{2,1,0:T(8,128)(2,1)S(1)} %copy-done.8, ...), custom_call_target="tpu_custom_call" | custom-call | flops 3221225472 | bytes 9000000 | tf_op jit(solution)/shard_map/gloss_partial/pallas_call | solution.py:599
  132.5 5.0 %collective-permute-start.4 = (bf16[400,256]{1,0:T(8,128)(2,1)S(1)}, bf16[400,256]{1,0:T(8,128)(2,1)S(1)}, u32[]{:S(2)}, u32[]{:S(2)}) collective-permute-start(bf16[400,256]{1,0:T(8,128)(2,1)S(1)} %get-tuple-element.54), channel_id=1, source_target_pairs={{0,272},{1,273},{2,274},{3,275},{4,276},{5,277},{6,278},{7,279},{8... | collective-permute-start | bytes 614408 | tf_op jit(solution)/shard_map/gloss_to_owner/ppermute | solution.py:459
  137.5 2.7 %collective-permute-start.5 = (bf16[400,256]{1,0:T(8,128)(2,1)S(1)}, bf16[400,256]{1,0:T(8,128)(2,1)S(1)}, u32[]{:S(2)}, u32[]{:S(2)}) collective-permute-start(bf16[400,256]{1,0:T(8,128)(2,1)S(1)} %get-tuple-element.55), channel_id=1, source_target_pairs={{0,16},{1,17},{2,18},{3,19},{4,20},{5,21},{6,22},{7,23},{8,24},{9,... | collective-permute-start | bytes 614408 | tf_op jit(solution)/shard_map/gloss_to_owner/ppermute | solution.py:459
  140.2 2.8 %collective-permute-start.6 = (bf16[400,256]{1,0:T(8,128)(2,1)S(1)}, bf16[400,256]{1,0:T(8,128)(2,1)S(1)}, u32[]{:S(2)}, u32[]{:S(2)}) collective-permute-start(bf16[400,256]{1,0:T(8,128)(2,1)S(1)} %get-tuple-element.56), channel_id=1, source_target_pairs={{0,256},{1,257},{2,258},{3,259},{4,260},{5,261},{6,262},{7,263},{8... | collective-permute-start | bytes 614408 | tf_op jit(solution)/shard_map/gloss_to_owner/ppermute | solution.py:459
  143.0 3.0 %collective-permute-done.4.refs_1_ = bf16[400,256]{1,0:T(8,128)(2,1)S(1)} collective-permute-done((bf16[400,256]{1,0:T(8,128)(2,1)S(1)}, bf16[400,256]{1,0:T(8,128)(2,1)S(1)}, u32[]{:S(2)}, u32[]{:S(2)}) %collective-permute-start.4) | collective-permute-done | bytes 204832 | tf_op jit(solution)/shard_map/gloss_to_owner/ppermute | solution.py:459
  146.0 2.9 %collective-permute-done.5.refs_2_ = bf16[400,256]{1,0:T(8,128)(2,1)S(1)} collective-permute-done((bf16[400,256]{1,0:T(8,128)(2,1)S(1)}, bf16[400,256]{1,0:T(8,128)(2,1)S(1)}, u32[]{:S(2)}, u32[]{:S(2)}) %collective-permute-start.5) | collective-permute-done | bytes 204832 | tf_op jit(solution)/shard_map/gloss_to_owner/ppermute | solution.py:459
  148.9 2.7 %collective-permute-done.6.refs_3_ = bf16[400,256]{1,0:T(8,128)(2,1)S(1)} collective-permute-done((bf16[400,256]{1,0:T(8,128)(2,1)S(1)}, bf16[400,256]{1,0:T(8,128)(2,1)S(1)}, u32[]{:S(2)}, u32[]{:S(2)}) %collective-permute-start.6) | collective-permute-done | bytes 204832 | tf_op jit(solution)/shard_map/gloss_to_owner/ppermute | solution.py:459
  152.7 6.7 %all-to-all-start.4 = ((bf16[8,64,256]{2,1,0:T(8,128)(2,1)}), bf16[8,64,256]{2,1,0:T(8,128)(2,1)S(1)}, u32[]{:S(2)}, u32[]{:S(2)}) async-start(bf16[8,64,256]{2,1,0:T(8,128)(2,1)} %gloss_to_owner.1), calls=%async_computation.4 | async-start | bytes 524288 | tf_op jit(solution)/shard_map/gloss_to_owner/all_to_all | solution.py:462
  160.2 10.6 %all-to-all-done.4.got = bf16[8,64,256]{2,1,0:T(8,128)(2,1)S(1)} async-done(((bf16[8,64,256]{2,1,0:T(8,128)(2,1)}), bf16[8,64,256]{2,1,0:T(8,128)(2,1)S(1)}, u32[]{:S(2)}, u32[]{:S(2)}) %all-to-all-start.4) | async-done | bytes 262176 | tf_op jit(solution)/shard_map/gloss_to_owner/all_to_all | solution.py:462
  (41 shorter events, 12.2 us)
Async XLA Ops:
  0.6 0.8 copy-start
  1.4 0.7 copy-start.2
  2.2 0.7 copy-start.4
  2.8 0.7 copy-start.5
  42.6 21.2 %collective-permute-start = (bf16[8,96,256]{2,1,0:T(8,128)(2,1)S(1)}, bf16[8,96,256]{2,1,0:T(8,128)(2,1)S(1)}, u32[]{:S(2)}, u32[]{:S(2)}) collective-permute-start(bf16[8,96,256]{2,1,0:T(8,128)(2,1)S(1)} %all_to_all.31.v_mine), channel_id=1, source_target_pairs={{0,1},{1,0},{2,3},{3,2},{4,5},{5,4},{6,7},{7,6},{8,9},{9,8},{10,11... | collective-permute-start | bytes 1179656 | tf_op jit(solution)/shard_map/gather/ppermute | solution.py:456
  44.6 13.7 %collective-permute-start.3 = (bf16[8,48,256]{2,1,0:T(8,128)(2,1)S(1)}, bf16[8,48,256]{2,1,0:T(8,128)(2,1)S(1)}, u32[]{:S(2)}, u32[]{:S(2)}) collective-permute-start(bf16[8,48,256]{2,1,0:T(8,128)(2,1)S(1)} %all_to_all.30.g0), channel_id=1, source_target_pairs={{0,272},{1,273},{2,274},{3,275},{4,276},{5,277},{6,278},{7,279},{8... | collective-permute-start | bytes 589832 | tf_op jit(solution)/shard_map/gather/ppermute | solution.py:459
  49.2 11.1 %collective-permute-start.2 = (bf16[8,48,256]{2,1,0:T(8,128)(2,1)S(1)}, bf16[8,48,256]{2,1,0:T(8,128)(2,1)S(1)}, u32[]{:S(2)}, u32[]{:S(2)}) collective-permute-start(bf16[8,48,256]{2,1,0:T(8,128)(2,1)S(1)} %all_to_all.30.g0), channel_id=1, source_target_pairs={{0,16},{1,17},{2,18},{3,19},{4,20},{5,21},{6,22},{7,23},{8,24},{9,... | collective-permute-start | bytes 589832 | tf_op jit(solution)/shard_map/gather/ppermute | solution.py:459
  51.9 11.9 %collective-permute-start.1 = (bf16[8,48,256]{2,1,0:T(8,128)(2,1)S(1)}, bf16[8,48,256]{2,1,0:T(8,128)(2,1)S(1)}, u32[]{:S(2)}, u32[]{:S(2)}) collective-permute-start(bf16[8,48,256]{2,1,0:T(8,128)(2,1)S(1)} %all_to_all.30.g0), channel_id=1, source_target_pairs={{0,256},{1,257},{2,258},{3,259},{4,260},{5,261},{6,262},{7,263},{8... | collective-permute-start | bytes 589832 | tf_op jit(solution)/shard_map/gather/ppermute | solution.py:459
  71.0 1.0 copy-start.13
  72.0 0.7 copy-start.16
  72.7 18.3 %copy-start.11 = (bf16[1536,256]{1,0:T(8,128)(2,1)}, bf16[1536,256]{1,0:T(8,128)(2,1)S(1)}, u32[]{:S(2)}) copy-start(bf16[1536,256]{1,0:T(8,128)(2,1)S(1)} %get-tuple-element.45.v_ref) | copy-start | bytes 2359300
  72.7 22.4 %all-to-all-start.2 = ((f32[32,8,128]{2,1,0:T(8,128)}), f32[32,8,128]{2,1,0:T(8,128)S(1)}, u32[]{:S(2)}, u32[]{:S(2)}) async-start(f32[32,8,128]{2,1,0:T(8,128)} %get-tuple-element.41), calls=%async_computation.2 | async-start | bytes 262144 | tf_op jit(solution)/shard_map/batch_sums/all_to_all | solution.py:468
  76.7 1.2 copy-start.14
  78.0 1.0 copy-start.17
  91.0 2.7 %copy-start.6 = (bf16[8,1536,256]{2,1,0:T(8,128)(2,1)}, bf16[8,1536,256]{2,1,0:T(8,128)(2,1)S(1)}, u32[]{:S(2)}) copy-start(bf16[8,1536,256]{2,1,0:T(8,128)(2,1)S(1)} %get-tuple-element.50.p_ref) | copy-start | bytes 18874372
  93.7 1.4 copy-start.9
  95.1 15.4 %all-to-all-start.3 = ((f32[16,8,128]{2,1,0:T(8,128)}), f32[16,8,128]{2,1,0:T(8,128)S(1)}, u32[]{:S(2)}, u32[]{:S(2)}) async-start(f32[16,8,128]{2,1,0:T(8,128)} %get-tuple-element.43), calls=%async_computation.3 | async-start | bytes 131072 | tf_op jit(solution)/shard_map/batch_sums/all_to_all | solution.py:468
  99.8 2.8 %copy-start.7 = (bf16[8,1536,256]{2,1,0:T(8,128)(2,1)S(1)}, bf16[8,1536,256]{2,1,0:T(8,128)(2,1)}, u32[]{:S(2)}) copy-start(bf16[8,1536,256]{2,1,0:T(8,128)(2,1)} %copy-done.6) | copy-start | bytes 18874372
  102.6 1.2 copy-start.15
  110.7 12.2 %copy-start.12 = (bf16[1536,256]{1,0:T(8,128)(2,1)S(1)}, bf16[1536,256]{1,0:T(8,128)(2,1)}, u32[]{:S(2)}) copy-start(bf16[1536,256]{1,0:T(8,128)(2,1)} %copy-done.11) | copy-start | bytes 2359300
  110.7 3.8 %collective-permute-start.7 = (bf16[784,256]{1,0:T(8,128)(2,1)S(1)}, bf16[784,256]{1,0:T(8,128)(2,1)S(1)}, u32[]{:S(2)}, u32[]{:S(2)}) collective-permute-start(bf16[784,256]{1,0:T(8,128)(2,1)S(1)} %get-tuple-element.61), channel_id=1, source_target_pairs={{0,1},{1,0},{2,3},{3,2},{4,5},{5,4},{6,7},{7,6},{8,9},{9,8},{10,11... | collective-permute-start | bytes 1204232 | tf_op jit(solution)/shard_map/video_to_owner/ppermute | solution.py:456
  115.6 37.1 %all-to-all-start.5 = ((bf16[8,112,256]{2,1,0:T(8,128)(2,1)}), bf16[8,112,256]{2,1,0:T(8,128)(2,1)S(1)}, u32[]{:S(2)}, u32[]{:S(2)}) async-start(bf16[8,112,256]{2,1,0:T(8,128)(2,1)} %video_to_owner.1), calls=%async_computation.5 | async-start | bytes 917504 | tf_op jit(solution)/shard_map/video_to_owner/all_to_all | solution.py:465
  122.9 2.8 %copy-start.8 = (bf16[8,1536,256]{2,1,0:T(8,128)(2,1)S(1)}, bf16[8,1536,256]{2,1,0:T(8,128)(2,1)}, u32[]{:S(2)}) copy-start(bf16[8,1536,256]{2,1,0:T(8,128)(2,1)} %copy-done.6) | copy-start | bytes 18874372
  125.7 1.6 copy-start.10
  127.2 32.2 %copy-start.1 = (bf16[3,32,256]{2,1,0:T(8,128)(2,1)S(1)}, bf16[3,32,256]{2,1,0:T(8,128)(2,1)}, u32[]{:S(2)}) copy-start(bf16[3,32,256]{2,1,0:T(8,128)(2,1)} %video.1) | copy-start | bytes 147460
  132.5 38.3 %copy-start.3 = (bf16[3,16,256]{2,1,0:T(8,128)(2,1)S(1)}, bf16[3,16,256]{2,1,0:T(8,128)(2,1)}, u32[]{:S(2)}) copy-start(bf16[3,16,256]{2,1,0:T(8,128)(2,1)} %gloss.1) | copy-start | bytes 73732
  132.5 13.5 %collective-permute-start.4 = (bf16[400,256]{1,0:T(8,128)(2,1)S(1)}, bf16[400,256]{1,0:T(8,128)(2,1)S(1)}, u32[]{:S(2)}, u32[]{:S(2)}) collective-permute-start(bf16[400,256]{1,0:T(8,128)(2,1)S(1)} %get-tuple-element.54), channel_id=1, source_target_pairs={{0,272},{1,273},{2,274},{3,275},{4,276},{5,277},{6,278},{7,279},{8... | collective-permute-start | bytes 614408 | tf_op jit(solution)/shard_map/gloss_to_owner/ppermute | solution.py:459
  137.5 11.4 %collective-permute-start.5 = (bf16[400,256]{1,0:T(8,128)(2,1)S(1)}, bf16[400,256]{1,0:T(8,128)(2,1)S(1)}, u32[]{:S(2)}, u32[]{:S(2)}) collective-permute-start(bf16[400,256]{1,0:T(8,128)(2,1)S(1)} %get-tuple-element.55), channel_id=1, source_target_pairs={{0,16},{1,17},{2,18},{3,19},{4,20},{5,21},{6,22},{7,23},{8,24},{9,... | collective-permute-start | bytes 614408 | tf_op jit(solution)/shard_map/gloss_to_owner/ppermute | solution.py:459
  140.2 11.4 %collective-permute-start.6 = (bf16[400,256]{1,0:T(8,128)(2,1)S(1)}, bf16[400,256]{1,0:T(8,128)(2,1)S(1)}, u32[]{:S(2)}, u32[]{:S(2)}) collective-permute-start(bf16[400,256]{1,0:T(8,128)(2,1)S(1)} %get-tuple-element.56), channel_id=1, source_target_pairs={{0,256},{1,257},{2,258},{3,259},{4,260},{5,261},{6,262},{7,263},{8... | collective-permute-start | bytes 614408 | tf_op jit(solution)/shard_map/gloss_to_owner/ppermute | solution.py:459
  152.7 18.1 %all-to-all-start.4 = ((bf16[8,64,256]{2,1,0:T(8,128)(2,1)}), bf16[8,64,256]{2,1,0:T(8,128)(2,1)S(1)}, u32[]{:S(2)}, u32[]{:S(2)}) async-start(bf16[8,64,256]{2,1,0:T(8,128)(2,1)} %gloss_to_owner.1), calls=%async_computation.4 | async-start | bytes 524288 | tf_op jit(solution)/shard_map/gloss_to_owner/all_to_all | solution.py:462

commit v3 on v2

v3 whole, which is shorter than its diff:
```python
import functools
import math

import jax
import jax.numpy as jnp
from jax import lax
from jax.experimental import pallas as pl
from jax.experimental.pallas import tpu as pltpu
from jax.sharding import PartitionSpec as P

F32 = jnp.float32
BF16 = jnp.bfloat16
EPSILON = 1e-06
EXP_SCALE = 10.0 * math.log2(math.e)
MARK = 2.0
MARK_LIMIT = 1.5
FAR = -1e30

NZ, NY, NX, NCORE = 8, 8, 4, 2
OWN = 3
FRAMES, GLOSSES, WIDTH = 32, 16, 256
CLIPS_DEV = NZ * NCORE * OWN
TEXTS_DEV = NY * NX * OWN
LANES = 128
VROWS = FRAMES * CLIPS_DEV
GROWS = GLOSSES * LANES
VOWN = FRAMES * OWN
GOWN = GLOSSES * OWN
EXTRA = 16
PAIRS = GLOSSES // 2
QUADS = GLOSSES // 4
NXY, NZC = NX * NY, NZ * NCORE
CHUNK = VOWN + EXTRA


def flat(x, z, y, core):
    return ((x % 2) * NZ + z) * 32 + (x // 2) * 16 + 2 * y + core


Z_GROUPS = [[flat(x, z, y, c) for z in range(NZ)] for x in range(NX) for y in range(NY) for c in range(NCORE)]
CORE_GROUPS = [[flat(x, z, y, c) for c in range(NCORE)] for x in range(NX) for y in range(NY) for z in range(NZ)]
XY_GROUPS = [[flat(x, z, y, c) for x in range(NX) for y in range(NY)] for z in range(NZ) for c in range(NCORE)]
ZC_GROUPS = [[flat(x, z, y, c) for c in range(NCORE) for z in range(NZ)] for x in range(NX) for y in range(NY)]


def params(limit_mb=16):
    return pltpu.CompilerParams(vmem_limit_bytes=limit_mb * 1024 * 1024)


def cost(flops, nbytes, trans=0):
    return pl.CostEstimate(flops=int(flops), bytes_accessed=int(nbytes), transcendentals=int(trans))


def iota(shape, dim):
    return lax.broadcasted_iota(jnp.int32, shape, dim)


def nt(a, b, **kw):
    return lax.dot_general(a, b, (((1,), (1,)), ((), ())), preferred_element_type=F32, **kw)


def nn(a, b, **kw):
    return lax.dot_general(a, b, (((1,), (0,)), ((), ())), preferred_element_type=F32, **kw)


def tn(a, b, **kw):
    return lax.dot_general(a, b, (((0,), (0,)), ((), ())), preferred_element_type=F32, **kw)


def column_of(row, n):
    eye = iota((n, LANES), 0) == iota((n, LANES), 1)
    return jnp.sum(jnp.where(eye, jnp.broadcast_to(row[0:1], (n, LANES)), 0.0), axis=1, keepdims=True)


def pieces(value):
    lane = iota((EXTRA, WIDTH), 1)
    full = jnp.broadcast_to(value, (EXTRA, WIDTH))
    hi = full.astype(BF16).astype(F32)
    mid = (full - hi).astype(BF16).astype(F32)
    low = (full - hi - mid).astype(BF16).astype(F32)
    return jnp.where(lane == 0, hi, jnp.where(lane == 1, mid, jnp.where(lane == 2, low, 0.0)))


def unpiece(block):
    mine = (iota((EXTRA, WIDTH), 0) == 0) & (iota((EXTRA, WIDTH), 1) < 3)
    return jnp.sum(jnp.where(mine, block, 0.0), keepdims=True).reshape(1, 1)


def put(ref, at, value):
    ref[0, at, :] = value[:, :LANES]
    ref[1, at, :] = value[:, LANES:]


def get(ref, at):
    return jnp.concatenate([ref[0, at, :], ref[1, at, :]], axis=1)


def two_halves(rows):
    return pltpu.VMEM((2, rows, LANES), F32)


def units_kernel(fc_in, gc_in, video_in, gloss_in, v_out, g_out, count_out, fc, gc, video, gloss, v_scr, g_scr, sems):
    pairs = ((fc_in, fc), (gc_in, gc), (video_in, video), (gloss_in, gloss))
    copies = [pltpu.make_async_copy(a, b, sems.at[i]) for i, (a, b) in enumerate(pairs)]
    for copy in copies:
        copy.start()
    for copy in copies:
        copy.wait()
    row = iota((8, LANES), 0)
    counts = jnp.zeros((8, LANES), jnp.int32)
    for c in range(OWN):
        counts = jnp.where(row == c, fc[c], jnp.where(row == OWN + c, gc[c], counts))
    count_out[...] = counts
    for count, raw, scr, tokens in ((fc, video, v_scr, FRAMES), (gc, gloss, g_scr, GLOSSES)):
        row, lane = iota((tokens, WIDTH), 0), iota((tokens, WIDTH), 1)
        for c in range(OWN):
            x = raw[c].astype(F32)
            mean_sq = jnp.mean(x * x, axis=-1, keepdims=True) + EPSILON
            unit = x * (lax.rsqrt(mean_sq) / math.sqrt(WIDTH))
            mark = jnp.where(lane == 0, MARK, 0.0)
            put(scr, pl.ds(c, tokens, stride=OWN), jnp.where(row < count[c], unit, mark))
    v = get(v_scr, pl.ds(0, VOWN)).astype(BF16)
    g = get(g_scr, pl.ds(0, GOWN)).astype(BF16)
    v_out[...] = v
    for i in range(NXY):
        g_out[i] = g


def diagonal_kernel(count_ref, v_ref, g_ref, dv, dg, logit_sum):
    def pick(count, which):
        return jnp.where(which == 0, count[0], jnp.where(which == 1, count[1], count[2]))

    fc = [count_ref[c : c + 1, 0:1] for c in range(OWN)]
    gc = [count_ref[OWN + c : OWN + c + 1, 0:1] for c in range(OWN)]
    v, g = v_ref[...], g_ref[0]
    shape = (VOWN, GOWN)
    r, q = iota(shape, 0), iota(shape, 1)
    rc, qc = lax.rem(r, OWN), lax.rem(q, OWN)
    valid = (rc == qc) & (lax.div(r, OWN) < pick(fc, rc)) & (lax.div(q, OWN) < pick(gc, qc))
    e = jnp.where(valid, jnp.exp2(nt(v, g) * EXP_SCALE), 0.0)
    r1, q1 = iota((VOWN, 1), 0), iota((1, GOWN), 1)
    rc1, qc1 = lax.rem(r1, OWN), lax.rem(q1, OWN)
    frames_r, glosses_r = pick(fc, rc1), pick(gc, rc1)
    frames_q, glosses_q = pick(fc, qc1), pick(gc, qc1)
    row_ok = lax.div(r1, OWN) < frames_r
    col_ok = lax.div(q1, OWN) < glosses_q
    frames_r, glosses_r = frames_r.astype(F32), glosses_r.astype(F32)
    frames_q, glosses_q = frames_q.astype(F32), glosses_q.astype(F32)
    rows = jnp.where(row_ok, jnp.sum(e, axis=1, keepdims=True), 1.0)
    cols = jnp.where(col_ok, jnp.sum(e, axis=0, keepdims=True), 1.0)
    by_row = jnp.where(row_ok, jnp.log(rows / glosses_r) / frames_r, 0.0)
    by_col = jnp.where(col_ok, jnp.log(cols / frames_q) / glosses_q, 0.0)
    total = jnp.sum(by_row, axis=0, keepdims=True) + jnp.sum(by_col, axis=1, keepdims=True)
    logit_sum[...] = jnp.broadcast_to(0.5 * total, (8, LANES))
    weight = -5.0 * e * (1.0 / (rows * frames_r) + 1.0 / (cols * glosses_q))
    dv[...] = nn(weight, g.astype(F32), precision=lax.Precision.HIGHEST)
    dg[...] = tn(weight, v.astype(F32), precision=lax.Precision.HIGHEST)


def exp_scores(v, g):
    return jnp.exp2(nt(v, g) * EXP_SCALE)


def forward_kernel(
    v_got, g_got, diag,
    v_out, g_out, row_out, col_out, e_out, r_out, c_out,
    v_scr, g_scr, frame_mask, gloss_mask, rows, cols,
):
    put(v_scr, pl.ds(0, VROWS), v_got[...].astype(F32))
    for f in range(FRAMES):
        parts = [
            get(v_scr, pl.ds(k * NZ * VOWN + f * OWN + c, NZ, stride=VOWN)) for k in range(NCORE) for c in range(OWN)
        ]
        v_out[pl.ds(f * CLIPS_DEV, CLIPS_DEV), :] = jnp.concatenate(parts, axis=0).astype(BF16)
    put(g_scr, pl.ds(0, NXY * GOWN), g_got[...].reshape(NXY * GOWN, WIDTH).astype(F32))
    pad = jnp.where(iota((LANES - TEXTS_DEV, WIDTH), 1) == 0, MARK, 0.0)
    for g in range(GLOSSES):
        parts = [get(g_scr, pl.ds(x * NY * GOWN + g * OWN + c, NY, stride=GOWN)) for x in range(NX) for c in range(OWN)]
        g_out[pl.ds(g * LANES, LANES), :] = jnp.concatenate(parts + [pad], axis=0).astype(BF16)

    first = jnp.where(iota((WIDTH, LANES), 0) == 0, 1.0, 0.0).astype(BF16)
    frame_mask[...] = jnp.where(nn(v_out[...], first) < MARK_LIMIT, 1.0, 0.0)
    first_row = jnp.where(iota((16, WIDTH), 1) == 0, 1.0, 0.0).astype(BF16)
    for g in range(GLOSSES):
        gloss_mask[g] = jnp.where(nt(first_row, g_out[pl.ds(g * LANES, LANES), :])[0:8] < MARK_LIMIT, 1.0, 0.0)
    frames = jnp.zeros((CLIPS_DEV, LANES), F32)
    for f in range(FRAMES):
        frames = frames + frame_mask[pl.ds(f * CLIPS_DEV, CLIPS_DEV), :]
    glosses = gloss_mask[0]
    for g in range(1, GLOSSES):
        glosses = glosses + gloss_mask[g]
    glosses = jnp.maximum(glosses, 1.0)[0:1]

    rows[...] = jnp.zeros_like(rows)

    def two_glosses(p, _):
        e = exp_scores(v_out[...], g_out[pl.ds(pl.multiple_of(p * WIDTH, WIDTH), WIDTH), :])
        m0, m1 = gloss_mask[2 * p][0:1], gloss_mask[2 * p + 1][0:1]
        col0 = jnp.zeros((CLIPS_DEV, LANES), F32)
        col1 = jnp.zeros((CLIPS_DEV, LANES), F32)
        for f in range(FRAMES):
            at = pl.ds(f * CLIPS_DEV, CLIPS_DEV)
            block = e[f * CLIPS_DEV : (f + 1) * CLIPS_DEV]
            e0, e1 = block[:, :LANES], block[:, LANES:]
            mask = frame_mask[at, :]
            rows[at, :] = rows[at, :] + (e0 * m0 + e1 * m1)
            col0 = col0 + e0 * mask
            col1 = col1 + e1 * mask
        cols[2 * p] = col0
        cols[2 * p + 1] = col1
        return 0

    lax.fori_loop(0, PAIRS, two_glosses, 0)

    lane = iota((CLIPS_DEV, LANES), 1)
    real = lane < TEXTS_DEV
    video_part = jnp.zeros((CLIPS_DEV, LANES), F32)
    for f in range(FRAMES):
        at = pl.ds(f * CLIPS_DEV, CLIPS_DEV)
        mask = frame_mask[at, :]
        total = jnp.where(real, rows[at, :], 1.0)
        video_part = video_part + mask * jnp.log(total / glosses)
        row_out[at, :] = jnp.where(mask > 0.0, 1.0 / (total * frames), FAR)
    gloss_part = jnp.zeros((CLIPS_DEV, LANES), F32)
    for g in range(GLOSSES):
        mask = gloss_mask[g][0:1]
        total = cols[g]
        gloss_part = gloss_part + mask * jnp.log(total / frames)
        col_out[g] = jnp.where(mask > 0.0, 1.0 / (total * glosses), FAR)
    logits = 0.5 * (video_part / frames + gloss_part / glosses)
    e_pair = jnp.where(real, jnp.exp(logits), 0.0)
    e_out[...] = e_pair

    sums = jnp.sum(e_pair, axis=1, keepdims=True)
    across = lane == iota((CLIPS_DEV, LANES), 0)
    r_row = jnp.sum(jnp.where(across, jnp.broadcast_to(sums, (CLIPS_DEV, LANES)), 0.0), axis=0, keepdims=True)
    r_rows = jnp.where(iota((8, LANES), 1) == CLIPS_DEV, diag[...], r_row)
    for i in range(NZC):
        r_out[i] = r_rows
    c_out[...] = jnp.broadcast_to(jnp.sum(e_pair, axis=0, keepdims=True), (8, LANES))


def weights_kernel(v_ref, g_ref, row_ref, col_ref, e_ref, p_out, av_out, ag_out):
    p = pl.program_id(0)
    e = exp_scores(v_ref[...], g_ref[...])
    scale = 2.5 * e_ref[...]
    col0, col1 = col_ref[0], col_ref[1]
    for f in range(FRAMES):
        at = pl.ds(f * CLIPS_DEV, CLIPS_DEV)
        block = e[f * CLIPS_DEV : (f + 1) * CLIPS_DEV]
        row = row_ref[at, :]
        w0 = scale * block[:, :LANES] * jnp.maximum(row + col0, 0.0)
        w1 = scale * block[:, LANES:] * jnp.maximum(row + col1, 0.0)
        p_out[0, at, :] = jnp.concatenate([w0, w1], axis=1).astype(BF16)
    weights = p_out[0]
    part = nn(weights, g_ref[...])

    @pl.when(p == 0)
    def _():
        av_out[...] = part

    @pl.when(p > 0)
    def _():
        av_out[...] = av_out[...] + part

    ag_out[...] = tn(weights, v_ref[...])


def added(got):
    total = got[0]
    for i in range(1, got.shape[0]):
        total = total + got[i]
    return total


def row_sums_kernel(r_got, c_part, c_out, r_out):
    r_rows = added(r_got)
    r_out[...] = r_rows
    lane = iota((1, LANES), 1)
    logs = jnp.where(lane < CLIPS_DEV, jnp.log(jnp.where(lane < CLIPS_DEV, r_rows[0:1], 1.0)), 0.0)
    logs = logs - jnp.where(lane == CLIPS_DEV, 2.0 * r_rows[0:1], 0.0)
    total = jnp.sum(logs, axis=1, keepdims=True)
    message = jnp.where(iota((8, LANES), 1) == TEXTS_DEV, total, c_part[...])
    for i in range(NXY):
        c_out[i] = message


def inverse_texts(c_rows):
    real = iota((8, LANES), 1) < TEXTS_DEV
    inverse = jnp.where(real, 1.0 / jnp.where(real, c_rows, 1.0), 0.0)
    return jnp.broadcast_to(column_of(inverse, LANES), (LANES, WIDTH))


def by_clip_kernel(r_ref, p_ref, v_ref, out, v_hi, v_low):
    @pl.when(pl.program_id(0) == 0)
    def _():
        inverse = jnp.broadcast_to(1.0 / column_of(r_ref[...], CLIPS_DEV), (CLIPS_DEV, WIDTH))
        for f in range(FRAMES):
            at = pl.ds(f * CLIPS_DEV, CLIPS_DEV)
            scaled = v_ref[at, :].astype(F32) * inverse
            hi = scaled.astype(BF16)
            v_hi[at, :] = hi
            v_low[at, :] = (scaled - hi.astype(F32)).astype(BF16)

    out[...] = tn(p_ref[0], v_hi[...]) + tn(p_ref[0], v_low[...])


def gloss_send_kernel(c_got, ag_ref, bg_ref, out, c_out, scr):
    step = pl.program_id(0)

    @pl.when(step == 0)
    def _():
        c_out[...] = added(c_got)

    col = inverse_texts(c_out[...])
    for k in range(GLOSSES // QUADS):
        at = pl.ds(k * LANES, LANES)
        block = ag_ref[at, :] * col + bg_ref[at, :]
        row = (step * (GLOSSES // QUADS) + k) * OWN
        for x in range(NX):
            for c in range(OWN):
                first = (x * OWN + c) * NY
                put(scr, pl.ds(x * NY * GOWN + row + c, NY, stride=GOWN), block[first : first + NY])

    @pl.when(step == QUADS - 1)
    def _():
        out[...] = get(scr, pl.ds(0, NXY * GOWN)).astype(BF16).reshape(NXY, GOWN, WIDTH)


def clip_send_kernel(c_got, r_ref, p_ref, g_ref, av_ref, mine, twin, c_rows, total):
    step = pl.program_id(0)

    @pl.when(step == 0)
    def _():
        c_rows[...] = added(c_got)

    col = inverse_texts(c_rows[...])
    scaled = g_ref[...].astype(F32) * jnp.concatenate([col] * (GLOSSES // QUADS), axis=0)
    part = nn(p_ref[0], scaled.astype(BF16))

    @pl.when(step == 0)
    def _():
        total[...] = part

    @pl.when((step > 0) & (step < QUADS - 1))
    def _():
        total[...] = total[...] + part

    @pl.when(step == QUADS - 1)
    def _():
        core = lax.rem(lax.axis_index("inner"), NCORE)
        inverse = jnp.broadcast_to(1.0 / column_of(r_ref[...], CLIPS_DEV), (CLIPS_DEV, WIDTH))
        half = CLIPS_DEV // 2
        for pair in range(FRAMES // 2):
            others = []
            for f in (2 * pair, 2 * pair + 1):
                at = pl.ds(f * CLIPS_DEV, CLIPS_DEV)
                new = part[f * CLIPS_DEV : (f + 1) * CLIPS_DEV]
                block = av_ref[at, :] * inverse + (total[at, :] + new)
                low, high = block[:half], block[half:]
                mine[pl.ds(f * half, half), :] = jnp.where(core == 0, low, high)
                others.append(jnp.where(core == 0, high, low))
            twin[pl.ds(pair * CLIPS_DEV, CLIPS_DEV), :] = jnp.concatenate(others, axis=0).astype(BF16)
        real = iota((1, LANES), 1) < TEXTS_DEV
        logs = jnp.where(real, jnp.log(jnp.where(real, c_rows[0:1], 1.0)), 0.0)
        extra = pieces(jnp.sum(logs, axis=1, keepdims=True))
        mine[pl.ds(FRAMES * half, EXTRA), :] = extra
        twin[pl.ds(FRAMES * half, EXTRA), :] = extra.astype(BF16)


def z_bits():
    z = lax.rem(lax.axis_index("outer"), NZ)
    return lax.rem(z, 2), lax.rem(lax.div(z, 2), 2), lax.div(z, 4)


def clip_rows_kernel(mine, got, keep, send, scr):
    step = 2 * NZ
    for i in range(VOWN // 2):
        at = pl.ds(i * step, step)
        two = mine[at, :] + got[at, :].astype(F32)
        for k in range(2):
            put(scr, pl.ds(2 * i + k, NZ, stride=CHUNK), two[k * NZ : (k + 1) * NZ])
    at = pl.ds(VOWN * NZ, EXTRA)
    extra = pieces(unpiece(mine[at, :]) + unpiece(got[at, :].astype(F32)))
    for i in range(NZ):
        put(scr, pl.ds(i * CHUNK + VOWN, EXTRA), extra)
    bit = z_bits()[0]
    for i in range(NZ // 2):
        at = pl.ds(i * CHUNK, CHUNK)
        keep[at, :] = get(scr, pl.ds(pl.multiple_of((2 * i + bit) * CHUNK, CHUNK), CHUNK))
        send[at, :] = get(scr, pl.ds(pl.multiple_of((2 * i + 1 - bit) * CHUNK, CHUNK), CHUNK)).astype(BF16)


def joined(mine, got, owner):
    start = owner * CHUNK if isinstance(owner, int) else pl.multiple_of(owner * CHUNK, CHUNK)
    at = pl.ds(start, VOWN)
    tail = pl.ds(start + VOWN, EXTRA)
    extra = pieces(unpiece(mine[tail, :]) + unpiece(got[tail, :].astype(F32)))
    return mine[at, :] + got[at, :].astype(F32), extra


def halve_kernel(which, mine, got, keep, send):
    bit = z_bits()[which]
    for i in range(NZ // 2 ** (which + 1)):
        for out, chosen in ((keep, bit), (send, 1 - bit)):
            rows, extra = joined(mine, got, 2 * i + chosen)
            out[pl.ds(i * CHUNK, VOWN), :] = rows.astype(out.dtype)
            out[pl.ds(i * CHUNK + VOWN, EXTRA), :] = extra.astype(out.dtype)


def token_grads(total, scr, raw, out, tokens):
    put(scr, pl.ds(0, OWN * tokens), total)
    for c in range(OWN):
        x = raw[c].astype(F32)
        d = get(scr, pl.ds(c, tokens, stride=OWN))
        mean_sq = jnp.mean(x * x, axis=-1, keepdims=True) + EPSILON
        factor = lax.rsqrt(mean_sq) / math.sqrt(WIDTH)
        inner = jnp.sum(d * x, axis=-1, keepdims=True)
        out[c] = factor * d - factor * x * (inner / (WIDTH * mean_sq))


def video_grad_kernel(clips, mine, got, c_rows, diag, video, out, loss, scr):
    total, extra = joined(mine, got, 0)
    token_grads(total + diag[...], scr, video, out, FRAMES)
    row_part = c_rows[0:1, TEXTS_DEV : TEXTS_DEV + 1]
    loss[...] = (unpiece(extra) + row_part) * (0.5 / clips)


def gloss_grad_kernel(got, diag, gloss, out, scr):
    total = got[0].astype(F32)
    for i in range(1, NXY):
        total = total + got[i].astype(F32)
    token_grads(total + diag[...], scr, gloss, out, GLOSSES)


def shape(*dims, dtype=F32):
    return jax.ShapeDtypeStruct(dims, dtype)


def on_device(clips, video, gloss, frame_count, gloss_count):
    vmem = pl.BlockSpec(memory_space=pltpu.VMEM)
    over_all = ("outer", "inner")

    def to_core(a):
        return lax.ppermute(a, "inner", [(i, i ^ 1) for i in range(lax.axis_size("inner"))])

    def to_z(a, mask):
        return lax.ppermute(a, "outer", [(i, i ^ mask) for i in range(lax.axis_size("outer"))])

    def exchanged(a, groups):
        return lax.all_to_all(a, over_all, 0, 0, axis_index_groups=groups, tiled=True)

    def gathered(a, groups):
        return lax.all_gather(a, over_all, axis=0, axis_index_groups=groups, tiled=True)

    def in_hbm(*arrays):
        return [pltpu.with_memory_space_constraint(a, pltpu.HBM) for a in arrays]

    with jax.named_scope("unit_tokens"):
        v_own, g_own, counts = pl.pallas_call(
            units_kernel,
            in_specs=[pl.BlockSpec(memory_space=pltpu.HBM)] * 4,
            out_shape=(
                shape(VOWN, WIDTH, dtype=BF16),
                shape(NXY, GOWN, WIDTH, dtype=BF16),
                shape(8, LANES, dtype=jnp.int32),
            ),
            scratch_shapes=[
                pltpu.SMEM((OWN,), jnp.int32),
                pltpu.SMEM((OWN,), jnp.int32),
                pltpu.VMEM((OWN, FRAMES, WIDTH), BF16),
                pltpu.VMEM((OWN, GLOSSES, WIDTH), BF16),
                two_halves(VOWN),
                two_halves(GOWN),
                pltpu.SemaphoreType.DMA((4,)),
            ],
            compiler_params=params(),
            cost_estimate=cost(2e5, 7e5),
        )(*in_hbm(frame_count, gloss_count, video, gloss))

    with jax.named_scope("gather"):
        g_got = exchanged(g_own, XY_GROUPS)
        v_got = gathered(gathered(v_own, Z_GROUPS), CORE_GROUPS)

    def first(rows):
        return pl.BlockSpec((1, rows, WIDTH), lambda i: (0, 0, 0))

    def whole(*dims):
        return pl.BlockSpec(dims, lambda i: (0,) * len(dims))

    with jax.named_scope("diagonal"):
        dv_diag, dg_diag, logit_sum = pl.pallas_call(
            diagonal_kernel,
            grid=(1,),
            in_specs=[whole(8, LANES), whole(VOWN, WIDTH), first(GOWN)],
            out_specs=(whole(VOWN, WIDTH), whole(GOWN, WIDTH), whole(8, LANES)),
            out_shape=(shape(VOWN, WIDTH), shape(GOWN, WIDTH), shape(8, LANES)),
            compiler_params=params(),
            cost_estimate=cost(2e7, 3e5),
        )(counts, v_own, g_own)

    with jax.named_scope("forward"):
        v_all, g_all, row_inv, col_inv, e_pair, r_part, c_part = pl.pallas_call(
            forward_kernel,
            in_specs=[vmem] * 3,
            out_shape=(
                shape(VROWS, WIDTH, dtype=BF16),
                shape(GROWS, WIDTH, dtype=BF16),
                shape(VROWS, LANES),
                shape(GLOSSES, CLIPS_DEV, LANES),
                shape(CLIPS_DEV, LANES),
                shape(NZC, 8, LANES),
                shape(8, LANES),
            ),
            scratch_shapes=[
                two_halves(VROWS),
                two_halves(NXY * GOWN),
                pltpu.VMEM((VROWS, LANES), F32),
                pltpu.VMEM((GLOSSES, 8, LANES), F32),
                pltpu.VMEM((VROWS, LANES), F32),
                pltpu.VMEM((GLOSSES, CLIPS_DEV, LANES), F32),
            ],
            compiler_params=params(),
            cost_estimate=cost(2 * VROWS * GROWS * WIDTH, 8e6, VROWS * GROWS),
        )(v_got, g_got, logit_sum)

    with jax.named_scope("row_sums"):
        c_send, r_rows = pl.pallas_call(
            row_sums_kernel,
            in_specs=[vmem] * 2,
            out_shape=(shape(NXY, 8, LANES), shape(8, LANES)),
            compiler_params=params(),
            cost_estimate=cost(1e5, 3e5),
        )(exchanged(r_part, ZC_GROUPS), c_part)
    with jax.named_scope("column_sums"):
        c_got = exchanged(c_send, XY_GROUPS)

    def halves(rows):
        return pl.BlockSpec((rows, WIDTH), lambda i: (i, 0))

    p_spec = pl.BlockSpec((1, VROWS, 2 * WIDTH), lambda i: (i, 0, 0))
    with jax.named_scope("weights"):
        weights, av, ag = pl.pallas_call(
            weights_kernel,
            grid=(PAIRS,),
            in_specs=[
                whole(VROWS, WIDTH),
                halves(2 * LANES),
                whole(VROWS, LANES),
                pl.BlockSpec((2, CLIPS_DEV, LANES), lambda i: (i, 0, 0)),
                whole(CLIPS_DEV, LANES),
            ],
            out_specs=(
                pl.BlockSpec((1, VROWS, WIDTH), lambda i: (i // 2, 0, i % 2)),
                whole(VROWS, WIDTH),
                halves(2 * LANES),
            ),
            out_shape=(shape(QUADS, VROWS, 2 * WIDTH, dtype=BF16), shape(VROWS, WIDTH), shape(GROWS, WIDTH)),
            compiler_params=params(),
            cost_estimate=cost(6 * VROWS * GROWS * WIDTH, 16e6, VROWS * GROWS),
        )(*in_hbm(v_all, g_all, row_inv, col_inv), e_pair)

    with jax.named_scope("by_clip"):
        bg = pl.pallas_call(
            by_clip_kernel,
            grid=(QUADS,),
            in_specs=[whole(8, LANES), p_spec, whole(VROWS, WIDTH)],
            out_specs=halves(4 * LANES),
            out_shape=shape(GROWS, WIDTH),
            scratch_shapes=[pltpu.VMEM((VROWS, WIDTH), BF16), pltpu.VMEM((VROWS, WIDTH), BF16)],
            compiler_params=params(),
            cost_estimate=cost(4 * VROWS * GROWS * WIDTH, 9e6),
        )(r_rows, *in_hbm(weights, v_all))

    with jax.named_scope("gloss_send"):
        dg_send, c_rows = pl.pallas_call(
            gloss_send_kernel,
            grid=(QUADS,),
            in_specs=[whole(NXY, 8, LANES), halves(4 * LANES), halves(4 * LANES)],
            out_specs=(whole(NXY, GOWN, WIDTH), whole(8, LANES)),
            out_shape=(shape(NXY, GOWN, WIDTH, dtype=BF16), shape(8, LANES)),
            scratch_shapes=[two_halves(NXY * GOWN)],
            compiler_params=params(),
            cost_estimate=cost(2e6, 5e6),
        )(c_got, *in_hbm(ag, bg))
        dg_got = exchanged(dg_send, XY_GROUPS)

    with jax.named_scope("clip_send"):
        v_rows = FRAMES * CLIPS_DEV // 2 + EXTRA
        mine, twin = pl.pallas_call(
            clip_send_kernel,
            grid=(QUADS,),
            in_specs=[whole(NXY, 8, LANES), whole(8, LANES), p_spec, halves(4 * LANES), whole(VROWS, WIDTH)],
            out_specs=(whole(v_rows, WIDTH), whole(v_rows, WIDTH)),
            out_shape=(shape(v_rows, WIDTH), shape(v_rows, WIDTH, dtype=BF16)),
            scratch_shapes=[pltpu.VMEM((8, LANES), F32), pltpu.VMEM((VROWS, WIDTH), F32)],
            compiler_params=params(),
            cost_estimate=cost(2 * VROWS * GROWS * WIDTH, 1e7),
        )(c_got, r_rows, *in_hbm(weights, g_all), av)

    def kept_and_sent(owners):
        return (shape(owners * CHUNK, WIDTH), shape(owners * CHUNK, WIDTH, dtype=BF16))

    with jax.named_scope("clips_by_core"):
        mine, sent = pl.pallas_call(
            clip_rows_kernel,
            in_specs=[vmem] * 2,
            out_shape=kept_and_sent(NZ // 2),
            scratch_shapes=[two_halves(NZ * CHUNK)],
            compiler_params=params(),
            cost_estimate=cost(1e6, 2e6),
        )(mine, to_core(twin))
    for which, scope in ((1, "clips_by_z1"), (2, "clips_by_z2")):
        with jax.named_scope(scope):
            mine, sent = pl.pallas_call(
                functools.partial(halve_kernel, which),
                in_specs=[vmem] * 2,
                out_shape=kept_and_sent(NZ // 2 ** (which + 1)),
                compiler_params=params(),
                cost_estimate=cost(1e6, 1e6),
            )(mine, to_z(sent, 2 ** (which - 1)))

    with jax.named_scope("video_grad"):
        grad_video, loss = pl.pallas_call(
            functools.partial(video_grad_kernel, clips),
            in_specs=[vmem] * 5,
            out_shape=(shape(OWN, FRAMES, WIDTH), shape(1, 1)),
            scratch_shapes=[two_halves(VOWN)],
            compiler_params=params(),
            cost_estimate=cost(1e6, 1e6),
        )(mine, to_z(sent, NZ // 2), c_rows, dv_diag, video)
    with jax.named_scope("gloss_grad"):
        grad_gloss = pl.pallas_call(
            gloss_grad_kernel,
            in_specs=[vmem] * 3,
            out_shape=shape(OWN, GLOSSES, WIDTH),
            scratch_shapes=[two_halves(GOWN)],
            compiler_params=params(),
            cost_estimate=cost(1e6, 1e6),
        )(dg_got, dg_diag, gloss)
    return loss.reshape(()), grad_video, grad_gloss


def solution(mesh):
    clips = OWN * mesh.shape["outer"] * mesh.shape["inner"]
    over_all = ("outer", "inner")
    tokens, counts = P(over_all, None, None), P(over_all)
    return jax.shard_map(
        functools.partial(on_device, clips),
        mesh=mesh,
        in_specs=(tokens, tokens, counts, counts),
        out_specs=(P(), tokens, tokens),
        check_vma=False,
    )
```

time: 173 us -> 156 us (0.902)
  the two profiles are of different devices: /device:TPU:64 before, /device:TPU:2 now
where the time goes in v3:
time: 156 us; the launch traced here: 155 us
  starting transfers between devices  50 us (32%)
  Pallas kernels  44.1 us (28%)
  blocking collectives  33.7 us (22%)
  waiting for transfers between devices  17.4 us (11%)
  local copies, waits for them, and re-layouts  9 us (6%)
    all_gather x2, blocking collectives, gathered(): lax.all_gather(a, over_all, axis=0, axis_index_groups=groups, tiled=True)  33.7 us
    all_to_all x4, starting transfers between devices, exchanged(): lax.all_to_all(a, over_all, 0, 0, axis_index_groups=groups, tiled=True)  32.2 us
    ppermute x3, starting transfers between devices, to_z(): lax.ppermute(a, 'outer', [(i, i ^ mask) for i in range(lax.axis_size('out...  15.7 us
    pallas_call x1, Pallas kernels, on_device(): pl.pallas_call(weights_kernel, grid=(PAIRS,), in_specs=[whole(VROWS, WIDT...  14.2 us
    ppermute x3, waiting for transfers between devices, to_z(): lax.ppermute(a, 'outer', [(i, i ^ mask) for i in range(lax.axis_size('out...  13.9 us
    unnamed x18, local copies, waits for them, and re-layouts  9 us
    pallas_call x1, Pallas kernels, on_device(): pl.pallas_call(forward_kernel, in_specs=[vmem] * 3, out_shape=(shape(VROW...  7.05 us
    pallas_call x1, Pallas kernels, on_device(): pl.pallas_call(by_clip_kernel, grid=(QUADS,), in_specs=[whole(8, LANES),...  6.54 us
  transfers between devices with their start and end apart: 8, of which 5 were waited for; matrix products, arithmetic and copies ran while one was open for 0% of the time, Pallas kernels for 19%

profile of v3, /device:TPU:2, one launch (start us, length us, event | category | flops | bytes accessed | tf_op | source)
XLA Modules:
  0.0 154.9 jit_solution(6149302026791956609)
XLA Ops:
  0.6 1.9 %unit_tokens.1 = (bf16[96,256]{1,0:T(8,128)(2,1)S(1)}, bf16[32,48,256]{2,1,0:T(8,128)(2,1)}, s32[8,128]{1,0:T(8,128)S(1)}) custom-call(s32[3]{0:T(128)} %fc_in.1, s32[3]{0:T(128)} %gc_in.1, bf16[3,32,256]{2,1,0:T(8,128)(2,1)} %video.1, bf16[3,16,256]{2,1,0:T(8,128)(2,1)} %gloss.1), custom_call_target="tpu_custom_call" | custom-call | flops 200000 | bytes 700000 | tf_op jit(solution)/shard_map/unit_tokens/pallas_call | solution.py:460
  2.5 10.3 %all-to-all-start = ((bf16[32,48,256]{2,1,0:T(8,128)(2,1)}), bf16[32,48,256]{2,1,0:T(8,128)(2,1)S(1)}, u32[]{:S(2)}, u32[]{:S(2)}) async-start(bf16[32,48,256]{2,1,0:T(8,128)(2,1)} %get-tuple-element.34.g_ref), calls=%async_computation | async-start | bytes 1572864 | tf_op jit(solution)/shard_map/gather/all_to_all | solution.py:451
  12.8 1.3 diagonal.1
  14.1 31.4 %all_gather.6 = bf16[768,256]{1,0:T(8,128)(2,1)S(1)} all-gather(bf16[96,256]{1,0:T(8,128)(2,1)S(1)} %get-tuple-element.33.v_ref), channel_id=1, replica_groups={{0,32,64,96,128,160,192,224},{1,33,65,97,129,161,193,225},{2,34,66,98,1..., dimensions={0}, use_global_device_ids=true | all-gather | bytes 442368 | tf_op jit(solution)/shard_map/gather/all_gather | solution.py:454
  45.5 2.4 %all_gather.7.v_got = bf16[1536,256]{1,0:T(8,128)(2,1)S(1)} all-gather(bf16[768,256]{1,0:T(8,128)(2,1)S(1)} %all_gather.6), channel_id=1, replica_groups={{0,1},{32,33},{64,65},{96,97},{128,129},{160,161},{192,193},{224,225},{..., dimensions={0}, use_global_device_ids=true | all-gather | bytes 1179648 | tf_op jit(solution)/shard_map/gather/all_gather | solution.py:454
  47.9 7.0 %forward.1 = (bf16[1536,256]{1,0:T(8,128)(2,1)S(1)}, bf16[2048,256]{1,0:T(8,128)(2,1)S(1)}, f32[1536,128]{1,0:T(8,128)S(1)}, f32[16,48,128]{2,1,0:T(8,128)S(1)},...) custom-call(bf16[1536,256]{1,0:T(8,128)(2,1)S(1)} %all_gather.7.v_got, ...), custom_call_target="tpu_custom_call" | custom-call | flops 1610612736 | bytes 8000000 | tf_op jit(solution)/shard_map/forward/pallas_call | solution.py:503
  54.9 1.0 copy-done.3
  55.9 1.0 copy-done.6
  56.9 0.9 copy-done.7
  57.8 0.8 copy-done.8
  58.5 4.2 %all-to-all-start.1 = ((f32[16,8,128]{2,1,0:T(8,128)}), f32[16,8,128]{2,1,0:T(8,128)S(1)}, u32[]{:S(2)}, u32[]{:S(2)}) async-start(f32[16,8,128]{2,1,0:T(8,128)} %get-tuple-element.37), calls=%async_computation.1 | async-start | bytes 131072 | tf_op jit(solution)/shard_map/row_sums/all_to_all | solution.py:451
  62.7 14.2 %weights.1 = (bf16[4,1536,512]{2,1,0:T(8,128)(2,1)S(1)}, f32[1536,256]{1,0:T(8,128)S(1)}, f32[2048,256]{1,0:T(8,128)S(1)}) custom-call(bf16[1536,256]{1,0:T(8,128)(2,1)} %copy-done.6, bf16[2048,256]{1,0:T(8,128)(2,1)} %copy-done.3, f32[1536,128]{1,0:T(8,128)} %copy-done.7, f32[16,48,128]{2,1,0:T(8,128)} %copy-done.8, f32[48,128]{1,0:T(8,128)S(1)} %get-tuple-element.45.e_ref), custom_call_target="tpu_custom_call" | custom-call | flops 4831838208 | bytes 16000000 | tf_op jit(solution)/shard_map/weights/pallas_call | solution.py:543
  77.0 2.6 %copy-done = bf16[4,1536,512]{2,1,0:T(8,128)(2,1)} copy-done((bf16[4,1536,512]{2,1,0:T(8,128)(2,1)}, bf16[4,1536,512]{2,1,0:T(8,128)(2,1)S(1)}, u32[]{:S(2)}) %copy-start) | copy-done | bytes 6291480
  79.6 1.4 copy-done.1
  81.0 0.8 row_sums.1
  81.8 9.8 %all-to-all-start.2 = ((f32[32,8,128]{2,1,0:T(8,128)}), f32[32,8,128]{2,1,0:T(8,128)S(1)}, u32[]{:S(2)}, u32[]{:S(2)}) async-start(f32[32,8,128]{2,1,0:T(8,128)} %get-tuple-element.39), calls=%async_computation.2 | async-start | bytes 262144 | tf_op jit(solution)/shard_map/column_sums/all_to_all | solution.py:451
  91.5 6.5 %by_clip.1.bg_ref = f32[2048,256]{1,0:T(8,128)S(1)} custom-call(f32[8,128]{1,0:T(8,128)S(1)} %get-tuple-element.40.r_ref, bf16[4,1536,512]{2,1,0:T(8,128)(2,1)} %copy-done, bf16[1536,256]{1,0:T(8,128)(2,1)} %copy-done.6), custom_call_target="tpu_custom_call" | custom-call | flops 3221225472 | bytes 9000000 | tf_op jit(solution)/shard_map/by_clip/pallas_call | solution.py:564
  98.1 1.4 copy-done.2
  99.5 1.8 %all-to-all-done.2.c_got = f32[32,8,128]{2,1,0:T(8,128)S(1)} async-done(((f32[32,8,128]{2,1,0:T(8,128)}), f32[32,8,128]{2,1,0:T(8,128)S(1)}, u32[]{:S(2)}, u32[]{:S(2)}) %all-to-all-start.2) | async-done | bytes 131104 | tf_op jit(solution)/shard_map/column_sums/all_to_all | solution.py:451
  101.3 4.2 %gloss_send.1 = (bf16[32,48,256]{2,1,0:T(8,128)(2,1)}, f32[8,128]{1,0:T(8,128)S(1)}) custom-call(f32[32,8,128]{2,1,0:T(8,128)S(1)} %all-to-all-done.2.c_got, f32[2048,256]{1,0:T(8,128)} %copy-done.1, f32[2048,256]{1,0:T(8,128)} %copy-done.2), custom_call_target="tpu_custom_call" | custom-call | flops 2000000 | bytes 5000000 | tf_op jit(solution)/shard_map/gloss_send/pallas_call | solution.py:576
  105.5 8.0 %all-to-all-start.3 = ((bf16[32,48,256]{2,1,0:T(8,128)(2,1)}), bf16[32,48,256]{2,1,0:T(8,128)(2,1)S(1)}, u32[]{:S(2)}, u32[]{:S(2)}) async-start(bf16[32,48,256]{2,1,0:T(8,128)(2,1)} %get-tuple-element.61), calls=%async_computation.3 | async-start | bytes 1572864 | tf_op jit(solution)/shard_map/gloss_send/all_to_all | solution.py:451
  113.5 5.6 %clip_send.1 = (f32[784,256]{1,0:T(8,128)S(1)}, bf16[784,256]{1,0:T(8,128)(2,1)S(1)}) custom-call(f32[32,8,128]{2,1,0:T(8,128)S(1)} %all-to-all-done.2.c_got, f32[8,128]{1,0:T(8,128)S(1)} %get-tuple-element.40.r_ref, bf16[4,1536,512]{2,1,0:T(8,128)(2,1)} %copy-done, bf16[2048,256]{1,0:T(8,128)(2,1)} %copy-done.3, f32[1536,256]{1,0:T(8,128)S(1)} %get-tuple-element.47.av_ref), custom_call_target="tpu_custom_call" | custom-call | flops 1610612736 | bytes 10000000 | tf_op jit(solution)/shard_map/clip_send/pallas_call | solution.py:590
  119.1 2.1 %collective-permute-start = (bf16[784,256]{1,0:T(8,128)(2,1)S(1)}, bf16[784,256]{1,0:T(8,128)(2,1)S(1)}, u32[]{:S(2)}, u32[]{:S(2)}) collective-permute-start(bf16[784,256]{1,0:T(8,128)(2,1)S(1)} %get-tuple-element.49), channel_id=1, source_target_pairs={{0,1},{1,0},{2,3},{3,2},{4,5},{5,4},{6,7},{7,6},{8,9},{9,8},{10,11... | collective-permute-start | bytes 1204232 | tf_op jit(solution)/shard_map/clips_by_core/ppermute | solution.py:445
  121.2 1.7 %collective-permute-done.got = bf16[784,256]{1,0:T(8,128)(2,1)S(1)} collective-permute-done((bf16[784,256]{1,0:T(8,128)(2,1)S(1)}, bf16[784,256]{1,0:T(8,128)(2,1)S(1)}, u32[]{:S(2)}, u32[]{:S(2)}) %collective-permute-start) | collective-permute-done | bytes 401440 | tf_op jit(solution)/shard_map/clips_by_core/ppermute | solution.py:445
  123.3 3.8 %collective-permute-start.1 = (bf16[448,256]{1,0:T(8,128)(2,1)S(1)}, bf16[448,256]{1,0:T(8,128)(2,1)S(1)}, u32[]{:S(2)}, u32[]{:S(2)}) collective-permute-start(bf16[448,256]{1,0:T(8,128)(2,1)S(1)} %get-tuple-element.51), channel_id=1, source_target_pairs={{0,32},{32,0},{64,96},{96,64},{128,160},{160,128},{192,224},{224,1... | collective-permute-start | bytes 688136 | tf_op jit(solution)/shard_map/clips_by_z1/ppermute | solution.py:448
  127.2 5.9 %collective-permute-done.1.got = bf16[448,256]{1,0:T(8,128)(2,1)S(1)} collective-permute-done((bf16[448,256]{1,0:T(8,128)(2,1)S(1)}, bf16[448,256]{1,0:T(8,128)(2,1)S(1)}, u32[]{:S(2)}, u32[]{:S(2)}) %collective-permute-start.1) | collective-permute-done | bytes 229408 | tf_op jit(solution)/shard_map/clips_by_z1/ppermute | solution.py:448
  133.2 4.5 %collective-permute-start.2 = (bf16[224,256]{1,0:T(8,128)(2,1)S(1)}, bf16[224,256]{1,0:T(8,128)(2,1)S(1)}, u32[]{:S(2)}, u32[]{:S(2)}) collective-permute-start(bf16[224,256]{1,0:T(8,128)(2,1)S(1)} %get-tuple-element.53), channel_id=1, source_target_pairs={{0,64},{32,96},{64,0},{96,32},{128,192},{160,224},{192,128},{224,1... | collective-permute-start | bytes 344072 | tf_op jit(solution)/shard_map/clips_by_z2/ppermute | solution.py:448
  137.7 5.3 %collective-permute-done.2.got = bf16[224,256]{1,0:T(8,128)(2,1)S(1)} collective-permute-done((bf16[224,256]{1,0:T(8,128)(2,1)S(1)}, bf16[224,256]{1,0:T(8,128)(2,1)S(1)}, u32[]{:S(2)}, u32[]{:S(2)}) %collective-permute-start.2) | collective-permute-done | bytes 114720 | tf_op jit(solution)/shard_map/clips_by_z2/ppermute | solution.py:448
  143.2 7.3 %collective-permute-start.3 = (bf16[112,256]{1,0:T(8,128)(2,1)S(1)}, bf16[112,256]{1,0:T(8,128)(2,1)S(1)}, u32[]{:S(2)}, u32[]{:S(2)}) collective-permute-start(bf16[112,256]{1,0:T(8,128)(2,1)S(1)} %get-tuple-element.55), channel_id=1, source_target_pairs={{0,128},{32,160},{64,192},{96,224},{128,0},{160,32},{192,64},{224,... | collective-permute-start | bytes 172040 | tf_op jit(solution)/shard_map/video_grad/ppermute | solution.py:448
  150.5 2.7 %collective-permute-done.3.got = bf16[112,256]{1,0:T(8,128)(2,1)S(1)} collective-permute-done((bf16[112,256]{1,0:T(8,128)(2,1)S(1)}, bf16[112,256]{1,0:T(8,128)(2,1)S(1)}, u32[]{:S(2)}, u32[]{:S(2)}) %collective-permute-start.3) | collective-permute-done | bytes 57376 | tf_op jit(solution)/shard_map/video_grad/ppermute | solution.py:448
  153.2 0.9 video_grad.1
  154.1 0.8 gloss_grad.1
  (17 shorter events, 0.7 us)
Async XLA Ops:
  2.5 45.3 %all-to-all-start = ((bf16[32,48,256]{2,1,0:T(8,128)(2,1)}), bf16[32,48,256]{2,1,0:T(8,128)(2,1)S(1)}, u32[]{:S(2)}, u32[]{:S(2)}) async-start(bf16[32,48,256]{2,1,0:T(8,128)(2,1)} %get-tuple-element.34.g_ref), calls=%async_computation | async-start | bytes 1572864 | tf_op jit(solution)/shard_map/gather/all_to_all | solution.py:451
  54.9 1.0 copy-start.3
  55.9 1.0 copy-start.6
  56.9 0.9 copy-start.7
  57.8 0.8 copy-start.8
  58.5 22.5 %all-to-all-start.1 = ((f32[16,8,128]{2,1,0:T(8,128)}), f32[16,8,128]{2,1,0:T(8,128)S(1)}, u32[]{:S(2)}, u32[]{:S(2)}) async-start(f32[16,8,128]{2,1,0:T(8,128)} %get-tuple-element.37), calls=%async_computation.1 | async-start | bytes 131072 | tf_op jit(solution)/shard_map/row_sums/all_to_all | solution.py:451
  77.0 2.6 %copy-start = (bf16[4,1536,512]{2,1,0:T(8,128)(2,1)}, bf16[4,1536,512]{2,1,0:T(8,128)(2,1)S(1)}, u32[]{:S(2)}) copy-start(bf16[4,1536,512]{2,1,0:T(8,128)(2,1)S(1)} %get-tuple-element.46.p_ref) | copy-start | bytes 18874372
  79.6 1.4 copy-start.1
  81.8 19.5 %all-to-all-start.2 = ((f32[32,8,128]{2,1,0:T(8,128)}), f32[32,8,128]{2,1,0:T(8,128)S(1)}, u32[]{:S(2)}, u32[]{:S(2)}) async-start(f32[32,8,128]{2,1,0:T(8,128)} %get-tuple-element.39), calls=%async_computation.2 | async-start | bytes 262144 | tf_op jit(solution)/shard_map/column_sums/all_to_all | solution.py:451
  98.1 1.4 copy-start.2
  105.5 48.6 %all-to-all-start.3 = ((bf16[32,48,256]{2,1,0:T(8,128)(2,1)}), bf16[32,48,256]{2,1,0:T(8,128)(2,1)S(1)}, u32[]{:S(2)}, u32[]{:S(2)}) async-start(bf16[32,48,256]{2,1,0:T(8,128)(2,1)} %get-tuple-element.61), calls=%async_computation.3 | async-start | bytes 1572864 | tf_op jit(solution)/shard_map/gloss_send/all_to_all | solution.py:451
  119.1 34.1 %copy-start.4 = (bf16[3,32,256]{2,1,0:T(8,128)(2,1)S(1)}, bf16[3,32,256]{2,1,0:T(8,128)(2,1)}, u32[]{:S(2)}) copy-start(bf16[3,32,256]{2,1,0:T(8,128)(2,1)} %video.1) | copy-start | bytes 147460
  119.1 35.0 %copy-start.5 = (bf16[3,16,256]{2,1,0:T(8,128)(2,1)S(1)}, bf16[3,16,256]{2,1,0:T(8,128)(2,1)}, u32[]{:S(2)}) copy-start(bf16[3,16,256]{2,1,0:T(8,128)(2,1)} %gloss.1) | copy-start | bytes 73732
  119.1 3.8 %collective-permute-start = (bf16[784,256]{1,0:T(8,128)(2,1)S(1)}, bf16[784,256]{1,0:T(8,128)(2,1)S(1)}, u32[]{:S(2)}, u32[]{:S(2)}) collective-permute-start(bf16[784,256]{1,0:T(8,128)(2,1)S(1)} %get-tuple-element.49), channel_id=1, source_target_pairs={{0,1},{1,0},{2,3},{3,2},{4,5},{5,4},{6,7},{7,6},{8,9},{9,8},{10,11... | collective-permute-start | bytes 1204232 | tf_op jit(solution)/shard_map/clips_by_core/ppermute | solution.py:445
  123.3 9.7 %collective-permute-start.1 = (bf16[448,256]{1,0:T(8,128)(2,1)S(1)}, bf16[448,256]{1,0:T(8,128)(2,1)S(1)}, u32[]{:S(2)}, u32[]{:S(2)}) collective-permute-start(bf16[448,256]{1,0:T(8,128)(2,1)S(1)} %get-tuple-element.51), channel_id=1, source_target_pairs={{0,32},{32,0},{64,96},{96,64},{128,160},{160,128},{192,224},{224,1... | collective-permute-start | bytes 688136 | tf_op jit(solution)/shard_map/clips_by_z1/ppermute | solution.py:448
  133.2 9.8 %collective-permute-start.2 = (bf16[224,256]{1,0:T(8,128)(2,1)S(1)}, bf16[224,256]{1,0:T(8,128)(2,1)S(1)}, u32[]{:S(2)}, u32[]{:S(2)}) collective-permute-start(bf16[224,256]{1,0:T(8,128)(2,1)S(1)} %get-tuple-element.53), channel_id=1, source_target_pairs={{0,64},{32,96},{64,0},{96,32},{128,192},{160,224},{192,128},{224,1... | collective-permute-start | bytes 344072 | tf_op jit(solution)/shard_map/clips_by_z2/ppermute | solution.py:448
  143.2 10.0 %collective-permute-start.3 = (bf16[112,256]{1,0:T(8,128)(2,1)S(1)}, bf16[112,256]{1,0:T(8,128)(2,1)S(1)}, u32[]{:S(2)}, u32[]{:S(2)}) collective-permute-start(bf16[112,256]{1,0:T(8,128)(2,1)S(1)} %get-tuple-element.55), channel_id=1, source_target_pairs={{0,128},{32,160},{64,192},{96,224},{128,0},{160,32},{192,64},{224,... | collective-permute-start | bytes 172040 | tf_op jit(solution)/shard_map/video_grad/ppermute | solution.py:448

commit v4 on v3

--- a/solution.py
+++ b/solution.py
@@ -37,7 +37,17 @@
     return ((x % 2) * NZ + z) * 32 + (x // 2) * 16 + 2 * y + core
 
 
-Z_GROUPS = [[flat(x, z, y, c) for z in range(NZ)] for x in range(NX) for y in range(NY) for c in range(NCORE)]
+def z_pairs(mask):
+    return [
+        [flat(x, z, y, c), flat(x, z ^ mask, y, c)]
+        for x in range(NX)
+        for y in range(NY)
+        for c in range(NCORE)
+        for z in range(NZ)
+        if not z & mask
+    ]
+
+
 CORE_GROUPS = [[flat(x, z, y, c) for c in range(NCORE)] for x in range(NX) for y in range(NY) for z in range(NZ)]
 XY_GROUPS = [[flat(x, z, y, c) for x in range(NX) for y in range(NY)] for z in range(NZ) for c in range(NCORE)]
 ZC_GROUPS = [[flat(x, z, y, c) for c in range(NCORE) for z in range(NZ)] for x in range(NX) for y in range(NY)]
@@ -163,20 +173,25 @@
 
 def forward_kernel(
     v_got, g_got, diag,
-    v_out, g_out, row_out, col_out, e_out, r_out, c_out,
-    v_scr, g_scr, frame_mask, gloss_mask, rows, cols,
+    v_hbm, g_hbm, row_hbm, col_hbm, e_out, r_out, c_out,
+    v_out, g_out, row_out, col_out, v_scr, g_scr, frame_mask, gloss_mask, rows, cols, sems,
 ):
+    results = ((v_out, v_hbm), (g_out, g_hbm), (row_out, row_hbm), (col_out, col_hbm))
+    copies = [pltpu.make_async_copy(a, b, sems.at[i]) for i, (a, b) in enumerate(results)]
     put(v_scr, pl.ds(0, VROWS), v_got[...].astype(F32))
     for f in range(FRAMES):
         parts = [
             get(v_scr, pl.ds(k * NZ * VOWN + f * OWN + c, NZ, stride=VOWN)) for k in range(NCORE) for c in range(OWN)
         ]
         v_out[pl.ds(f * CLIPS_DEV, CLIPS_DEV), :] = jnp.concatenate(parts, axis=0).astype(BF16)
+    copies[0].start()
     put(g_scr, pl.ds(0, NXY * GOWN), g_got[...].reshape(NXY * GOWN, WIDTH).astype(F32))
     pad = jnp.where(iota((LANES - TEXTS_DEV, WIDTH), 1) == 0, MARK, 0.0)
     for g in range(GLOSSES):
         parts = [get(g_scr, pl.ds(x * NY * GOWN + g * OWN + c, NY, stride=GOWN)) for x in range(NX) for c in range(OWN)]
         g_out[pl.ds(g * LANES, LANES), :] = jnp.concatenate(parts + [pad], axis=0).astype(BF16)
+
+    copies[1].start()
 
     first = jnp.where(iota((WIDTH, LANES), 0) == 0, 1.0, 0.0).astype(BF16)
     frame_mask[...] = jnp.where(nn(v_out[...], first) < MARK_LIMIT, 1.0, 0.0)
@@ -221,12 +236,14 @@
         total = jnp.where(real, rows[at, :], 1.0)
         video_part = video_part + mask * jnp.log(total / glosses)
         row_out[at, :] = jnp.where(mask > 0.0, 1.0 / (total * frames), FAR)
+    copies[2].start()
     gloss_part = jnp.zeros((CLIPS_DEV, LANES), F32)
     for g in range(GLOSSES):
         mask = gloss_mask[g][0:1]
         total = cols[g]
         gloss_part = gloss_part + mask * jnp.log(total / frames)
         col_out[g] = jnp.where(mask > 0.0, 1.0 / (total * glosses), FAR)
+    copies[3].start()
     logits = 0.5 * (video_part / frames + gloss_part / glosses)
     e_pair = jnp.where(real, jnp.exp(logits), 0.0)
     e_out[...] = e_pair
@@ -238,9 +255,11 @@
     for i in range(NZC):
         r_out[i] = r_rows
     c_out[...] = jnp.broadcast_to(jnp.sum(e_pair, axis=0, keepdims=True), (8, LANES))
-
-
-def weights_kernel(v_ref, g_ref, row_ref, col_ref, e_ref, p_out, av_out, ag_out):
+    for copy in copies:
+        copy.wait()
+
+
+def weights_kernel(v_ref, g_ref, row_ref, col_ref, e_ref, p_out, av_out):
     p = pl.program_id(0)
     e = exp_scores(v_ref[...], g_ref[...])
     scale = 2.5 * e_ref[...]
@@ -263,8 +282,6 @@
     def _():
         av_out[...] = av_out[...] + part
 
-    ag_out[...] = tn(weights, v_ref[...])
-
 
 def added(got):
     total = got[0]
@@ -291,21 +308,20 @@
     return jnp.broadcast_to(column_of(inverse, LANES), (LANES, WIDTH))
 
 
-def by_clip_kernel(r_ref, p_ref, v_ref, out, v_hi, v_low):
+def by_clip_kernel(r_ref, p_ref, v_ref, out, both):
     @pl.when(pl.program_id(0) == 0)
     def _():
         inverse = jnp.broadcast_to(1.0 / column_of(r_ref[...], CLIPS_DEV), (CLIPS_DEV, WIDTH))
         for f in range(FRAMES):
             at = pl.ds(f * CLIPS_DEV, CLIPS_DEV)
-            scaled = v_ref[at, :].astype(F32) * inverse
-            hi = scaled.astype(BF16)
-            v_hi[at, :] = hi
-            v_low[at, :] = (scaled - hi.astype(F32)).astype(BF16)
-
-    out[...] = tn(p_ref[0], v_hi[...]) + tn(p_ref[0], v_low[...])
-
-
-def gloss_send_kernel(c_got, ag_ref, bg_ref, out, c_out, scr):
+            v = v_ref[at, :]
+            both[at, :WIDTH] = v
+            both[at, WIDTH:] = (v.astype(F32) * inverse).astype(BF16)
+
+    out[...] = tn(p_ref[0], both[...])
+
+
+def gloss_send_kernel(c_got, by_clip, out, c_out, scr):
     step = pl.program_id(0)
 
     @pl.when(step == 0)
@@ -315,7 +331,7 @@
     col = inverse_texts(c_out[...])
     for k in range(GLOSSES // QUADS):
         at = pl.ds(k * LANES, LANES)
-        block = ag_ref[at, :] * col + bg_ref[at, :]
+        block = by_clip[at, :WIDTH] * col + by_clip[at, WIDTH:]
         row = (step * (GLOSSES // QUADS) + k) * OWN
         for x in range(NX):
             for c in range(OWN):
@@ -387,8 +403,8 @@
     bit = z_bits()[0]
     for i in range(NZ // 2):
         at = pl.ds(i * CHUNK, CHUNK)
-        keep[at, :] = get(scr, pl.ds(pl.multiple_of((2 * i + bit) * CHUNK, CHUNK), CHUNK))
-        send[at, :] = get(scr, pl.ds(pl.multiple_of((2 * i + 1 - bit) * CHUNK, CHUNK), CHUNK)).astype(BF16)
+        keep[at, :] = get(scr, pl.ds(pl.multiple_of((NZ // 2 * bit + i) * CHUNK, CHUNK), CHUNK))
+        send[at, :] = get(scr, pl.ds(pl.multiple_of((NZ // 2 * (1 - bit) + i) * CHUNK, CHUNK), CHUNK)).astype(BF16)
 
 
 def joined(mine, got, owner):
@@ -401,9 +417,10 @@
 
 def halve_kernel(which, mine, got, keep, send):
     bit = z_bits()[which]
-    for i in range(NZ // 2 ** (which + 1)):
+    owners = NZ // 2 ** (which + 1)
+    for i in range(owners):
         for out, chosen in ((keep, bit), (send, 1 - bit)):
-            rows, extra = joined(mine, got, 2 * i + chosen)
+            rows, extra = joined(mine, got, owners * chosen + i)
             out[pl.ds(i * CHUNK, VOWN), :] = rows.astype(out.dtype)
             out[pl.ds(i * CHUNK + VOWN, EXTRA), :] = extra.astype(out.dtype)
 
@@ -480,7 +497,10 @@
 
     with jax.named_scope("gather"):
         g_got = exchanged(g_own, XY_GROUPS)
-        v_got = gathered(gathered(v_own, Z_GROUPS), CORE_GROUPS)
+        v_got = v_own
+        for mask in (4, 2, 1):
+            v_got = gathered(v_got, z_pairs(mask))
+        v_got = gathered(v_got, CORE_GROUPS)
 
     def first(rows):
         return pl.BlockSpec((1, rows, WIDTH), lambda i: (0, 0, 0))
@@ -503,22 +523,28 @@
         v_all, g_all, row_inv, col_inv, e_pair, r_part, c_part = pl.pallas_call(
             forward_kernel,
             in_specs=[vmem] * 3,
+            out_specs=[pl.BlockSpec(memory_space=pltpu.HBM)] * 4 + [vmem] * 3,
             out_shape=(
-                shape(VROWS, WIDTH, dtype=BF16),
-                shape(GROWS, WIDTH, dtype=BF16),
-                shape(VROWS, LANES),
-                shape(GLOSSES, CLIPS_DEV, LANES),
+                pltpu.HBM((VROWS, WIDTH), BF16),
+                pltpu.HBM((GROWS, WIDTH), BF16),
+                pltpu.HBM((VROWS, LANES), F32),
+                pltpu.HBM((GLOSSES, CLIPS_DEV, LANES), F32),
                 shape(CLIPS_DEV, LANES),
                 shape(NZC, 8, LANES),
                 shape(8, LANES),
             ),
             scratch_shapes=[
+                pltpu.VMEM((VROWS, WIDTH), BF16),
+                pltpu.VMEM((GROWS, WIDTH), BF16),
+                pltpu.VMEM((VROWS, LANES), F32),
+                pltpu.VMEM((GLOSSES, CLIPS_DEV, LANES), F32),
                 two_halves(VROWS),
                 two_halves(NXY * GOWN),
                 pltpu.VMEM((VROWS, LANES), F32),
                 pltpu.VMEM((GLOSSES, 8, LANES), F32),
                 pltpu.VMEM((VROWS, LANES), F32),
                 pltpu.VMEM((GLOSSES, CLIPS_DEV, LANES), F32),
+                pltpu.SemaphoreType.DMA((4,)),
             ],
             compiler_params=params(),
             cost_estimate=cost(2 * VROWS * GROWS * WIDTH, 8e6, VROWS * GROWS),
@@ -540,7 +566,7 @@
 
     p_spec = pl.BlockSpec((1, VROWS, 2 * WIDTH), lambda i: (i, 0, 0))
     with jax.named_scope("weights"):
-        weights, av, ag = pl.pallas_call(
+        weights, av = pl.pallas_call(
             weights_kernel,
             grid=(PAIRS,),
             in_specs=[
@@ -553,37 +579,23 @@
             out_specs=(
                 pl.BlockSpec((1, VROWS, WIDTH), lambda i: (i // 2, 0, i % 2)),
                 whole(VROWS, WIDTH),
-                halves(2 * LANES),
             ),
-            out_shape=(shape(QUADS, VROWS, 2 * WIDTH, dtype=BF16), shape(VROWS, WIDTH), shape(GROWS, WIDTH)),
-            compiler_params=params(),
-            cost_estimate=cost(6 * VROWS * GROWS * WIDTH, 16e6, VROWS * GROWS),
+            out_shape=(pltpu.HBM((QUADS, VROWS, 2 * WIDTH), BF16), shape(VROWS, WIDTH)),
+            compiler_params=params(),
+            cost_estimate=cost(4 * VROWS * GROWS * WIDTH, 12e6, VROWS * GROWS),
         )(*in_hbm(v_all, g_all, row_inv, col_inv), e_pair)
 
     with jax.named_scope("by_clip"):
-        bg = pl.pallas_call(
+        by_clip = pl.pallas_call(
             by_clip_kernel,
             grid=(QUADS,),
             in_specs=[whole(8, LANES), p_spec, whole(VROWS, WIDTH)],
-            out_specs=halves(4 * LANES),
-            out_shape=shape(GROWS, WIDTH),
-            scratch_shapes=[pltpu.VMEM((VROWS, WIDTH), BF16), pltpu.VMEM((VROWS, WIDTH), BF16)],
+            out_specs=pl.BlockSpec((4 * LANES, 2 * WIDTH), lambda i: (i, 0)),
+            out_shape=pltpu.HBM((GROWS, 2 * WIDTH), F32),
+            scratch_shapes=[pltpu.VMEM((VROWS, 2 * WIDTH), BF16)],
             compiler_params=params(),
             cost_estimate=cost(4 * VROWS * GROWS * WIDTH, 9e6),
         )(r_rows, *in_hbm(weights, v_all))
-
-    with jax.named_scope("gloss_send"):
-        dg_send, c_rows = pl.pallas_call(
-            gloss_send_kernel,
-            grid=(QUADS,),
-            in_specs=[whole(NXY, 8, LANES), halves(4 * LANES), halves(4 * LANES)],
-            out_specs=(whole(NXY, GOWN, WIDTH), whole(8, LANES)),
-            out_shape=(shape(NXY, GOWN, WIDTH, dtype=BF16), shape(8, LANES)),
-            scratch_shapes=[two_halves(NXY * GOWN)],
-            compiler_params=params(),
-            cost_estimate=cost(2e6, 5e6),
-        )(c_got, *in_hbm(ag, bg))
-        dg_got = exchanged(dg_send, XY_GROUPS)
 
     with jax.named_scope("clip_send"):
         v_rows = FRAMES * CLIPS_DEV // 2 + EXTRA
@@ -597,6 +609,20 @@
             compiler_params=params(),
             cost_estimate=cost(2 * VROWS * GROWS * WIDTH, 1e7),
         )(c_got, r_rows, *in_hbm(weights, g_all), av)
+
+    with jax.named_scope("gloss_send"):
+        twin, c_ready = lax.optimization_barrier((twin, c_got))
+        dg_send, c_rows = pl.pallas_call(
+            gloss_send_kernel,
+            grid=(QUADS,),
+            in_specs=[whole(NXY, 8, LANES), pl.BlockSpec((4 * LANES, 2 * WIDTH), lambda i: (i, 0))],
+            out_specs=(whole(NXY, GOWN, WIDTH), whole(8, LANES)),
+            out_shape=(shape(NXY, GOWN, WIDTH, dtype=BF16), shape(8, LANES)),
+            scratch_shapes=[two_halves(NXY * GOWN)],
+            compiler_params=params(),
+            cost_estimate=cost(2e6, 5e6),
+        )(c_ready, *in_hbm(by_clip))
+        dg_got = exchanged(dg_send, XY_GROUPS)
 
     def kept_and_sent(owners):
         return (shape(owners * CHUNK, WIDTH), shape(owners * CHUNK, WIDTH, dtype=BF16))

time: 156 us -> 143 us (0.917)
  local copies, waits for them, and re-layouts: 9 us -> 0.01 us
  blocking collectives: 33.7 us -> 27.2 us
  starting transfers between devices: 50 us -> 53.8 us
  Pallas kernels: 44.1 us -> 42.3 us
    unnamed x18 -> x4, local copies, waits for them, and re-layouts: 9 us -> 0.01 us
    all_gather x2 -> x4, blocking collectives: 33.7 us -> 27.2 us  [gathered(): lax.all_gather(a, over_all, axis=0, axis_index_groups=groups, tiled=True)]
    all_to_all x4, starting transfers between devices: 32.2 us -> 36.2 us  [exchanged(): lax.all_to_all(a, over_all, 0, 0, axis_index_groups=groups, tiled=True)]
    pallas_call x1, Pallas kernels: 14.2 us -> 10.3 us  [on_device(): pl.pallas_call(weights_kernel, grid=(PAIRS,), in_specs=[whole(VROWS, WIDT...]
  transfers between devices with their start and end apart: 8 -> 8, of which waited for: 5 -> 5; matrix products, arithmetic and copies ran while one was open for 0% -> 0% of each run, Pallas kernels for 19% -> 15%
where the time goes in v4:
time: 143 us; the launch traced here: 142 us
  starting transfers between devices  53.8 us (38%)
  Pallas kernels  42.3 us (30%)
  blocking collectives  27.2 us (19%)
  waiting for transfers between devices  17.4 us (12%)
    all_to_all x4, starting transfers between devices, exchanged(): lax.all_to_all(a, over_all, 0, 0, axis_index_groups=groups, tiled=True)  36.2 us
    all_gather x4, blocking collectives, gathered(): lax.all_gather(a, over_all, axis=0, axis_index_groups=groups, tiled=True)  27.2 us
    ppermute x3, starting transfers between devices, to_z(): lax.ppermute(a, 'outer', [(i, i ^ mask) for i in range(lax.axis_size('out...  15.7 us
    ppermute x3, waiting for transfers between devices, to_z(): lax.ppermute(a, 'outer', [(i, i ^ mask) for i in range(lax.axis_size('out...  13.8 us
    pallas_call x1, Pallas kernels, on_device(): pl.pallas_call(weights_kernel, grid=(PAIRS,), in_specs=[whole(VROWS, WIDT...  10.3 us
    pallas_call x1, Pallas kernels, on_device(): pl.pallas_call(forward_kernel, in_specs=[vmem] * 3, out_specs=[pl.BlockSp...  7.95 us
    pallas_call x1, Pallas kernels, on_device(): pl.pallas_call(by_clip_kernel, grid=(QUADS,), in_specs=[whole(8, LANES),...  7.77 us
    pallas_call x1, Pallas kernels, on_device(): pl.pallas_call(clip_send_kernel, grid=(QUADS,), in_specs=[whole(NXY, 8, L...  5.63 us
  transfers between devices with their start and end apart: 8, of which 5 were waited for; matrix products, arithmetic and copies ran while one was open for 0% of the time, Pallas kernels for 15%

profile of v4, /device:TPU:2, one launch (start us, length us, event | category | flops | bytes accessed | tf_op | source)
XLA Modules:
  0.0 141.6 jit_solution(14028407774262828893)
XLA Ops:
  0.6 1.9 %unit_tokens.1 = (bf16[96,256]{1,0:T(8,128)(2,1)S(1)}, bf16[32,48,256]{2,1,0:T(8,128)(2,1)}, s32[8,128]{1,0:T(8,128)S(1)}) custom-call(s32[3]{0:T(128)} %fc_in.1, s32[3]{0:T(128)} %gc_in.1, bf16[3,32,256]{2,1,0:T(8,128)(2,1)} %video.1, bf16[3,16,256]{2,1,0:T(8,128)(2,1)} %gloss.1), custom_call_target="tpu_custom_call" | custom-call | flops 200000 | bytes 700000 | tf_op jit(solution)/shard_map/unit_tokens/pallas_call | solution.py:477
  2.5 10.3 %all-to-all-start = ((bf16[32,48,256]{2,1,0:T(8,128)(2,1)}), bf16[32,48,256]{2,1,0:T(8,128)(2,1)S(1)}, u32[]{:S(2)}, u32[]{:S(2)}) async-start(bf16[32,48,256]{2,1,0:T(8,128)(2,1)} %get-tuple-element.35.g_ref), calls=%async_computation | async-start | bytes 1572864 | tf_op jit(solution)/shard_map/gather/all_to_all | solution.py:468
  12.8 1.3 diagonal.1
  14.1 11.8 %all_gather.12 = bf16[192,256]{1,0:T(8,128)(2,1)S(1)} all-gather(bf16[96,256]{1,0:T(8,128)(2,1)S(1)} %get-tuple-element.34.v_ref), channel_id=1, replica_groups={{0,128},{32,160},{64,192},{96,224},{1,129},{33,161},{65,193},{97,225},{..., dimensions={0}, use_global_device_ids=true | all-gather | bytes 147456 | tf_op jit(solution)/shard_map/gather/all_gather | solution.py:471
  25.9 6.4 %all_gather.13 = bf16[384,256]{1,0:T(8,128)(2,1)S(1)} all-gather(bf16[192,256]{1,0:T(8,128)(2,1)S(1)} %all_gather.12), channel_id=1, replica_groups={{0,64},{32,96},{128,192},{160,224},{1,65},{33,97},{129,193},{161,225},{..., dimensions={0}, use_global_device_ids=true | all-gather | bytes 294912 | tf_op jit(solution)/shard_map/gather/all_gather | solution.py:471
  32.3 6.7 %all_gather.14 = bf16[768,256]{1,0:T(8,128)(2,1)S(1)} all-gather(bf16[384,256]{1,0:T(8,128)(2,1)S(1)} %all_gather.13), channel_id=1, replica_groups={{0,32},{64,96},{128,160},{192,224},{1,33},{65,97},{129,161},{193,225},{..., dimensions={0}, use_global_device_ids=true | all-gather | bytes 589824 | tf_op jit(solution)/shard_map/gather/all_gather | solution.py:471
  39.0 2.4 %all_gather.15.v_got = bf16[1536,256]{1,0:T(8,128)(2,1)S(1)} all-gather(bf16[768,256]{1,0:T(8,128)(2,1)S(1)} %all_gather.14), channel_id=1, replica_groups={{0,1},{32,33},{64,65},{96,97},{128,129},{160,161},{192,193},{224,225},{..., dimensions={0}, use_global_device_ids=true | all-gather | bytes 1179648 | tf_op jit(solution)/shard_map/gather/all_gather | solution.py:471
  41.4 8.0 %forward.1 = (bf16[1536,256]{1,0:T(8,128)(2,1)}, bf16[2048,256]{1,0:T(8,128)(2,1)}, f32[1536,128]{1,0:T(8,128)}, f32[16,48,128]{2,1,0:T(8,128)}, f32[48,128]{1,0...) custom-call(bf16[1536,256]{1,0:T(8,128)(2,1)S(1)} %all_gather.15.v_got, ...), custom_call_target="tpu_custom_call" | custom-call | flops 1610612736 | bytes 8000000 | tf_op jit(solution)/shard_map/forward/pallas_call | solution.py:523
  49.3 8.3 %all-to-all-start.1 = ((f32[16,8,128]{2,1,0:T(8,128)}), f32[16,8,128]{2,1,0:T(8,128)S(1)}, u32[]{:S(2)}, u32[]{:S(2)}) async-start(f32[16,8,128]{2,1,0:T(8,128)} %get-tuple-element.38), calls=%async_computation.1 | async-start | bytes 131072 | tf_op jit(solution)/shard_map/row_sums/all_to_all | solution.py:468
  57.6 10.3 %weights.1 = (bf16[4,1536,512]{2,1,0:T(8,128)(2,1)}, f32[1536,256]{1,0:T(8,128)S(1)}) custom-call(bf16[1536,256]{1,0:T(8,128)(2,1)} %get-tuple-element.42.v_ref, bf16[2048,256]{1,0:T(8,128)(2,1)} %get-tuple-element.43.g_ref, f32[1536,128]{1,0:T(8,128)} %get-tuple-element.44.row_ref, f32[16,48,128]{2,1,0:T(8,128)} %get-tuple-element.45.col_ref, ...), custom_call_target="tpu_custom_call" | custom-call | flops 3221225472 | bytes 12000000 | tf_op jit(solution)/shard_map/weights/pallas_call | solution.py:569
  67.9 0.8 row_sums.1
  68.7 9.8 %all-to-all-start.2 = ((f32[32,8,128]{2,1,0:T(8,128)}), f32[32,8,128]{2,1,0:T(8,128)S(1)}, u32[]{:S(2)}, u32[]{:S(2)}) async-start(f32[32,8,128]{2,1,0:T(8,128)} %get-tuple-element.40), calls=%async_computation.2 | async-start | bytes 262144 | tf_op jit(solution)/shard_map/column_sums/all_to_all | solution.py:468
  78.5 7.8 %by_clip.1 = f32[2048,512]{1,0:T(8,128)} custom-call(f32[8,128]{1,0:T(8,128)S(1)} %get-tuple-element.41.r_ref, bf16[4,1536,512]{2,1,0:T(8,128)(2,1)} %get-tuple-element.47.p_ref, bf16[1536,256]{1,0:T(8,128)(2,1)} %get-tuple-element.42.v_ref), custom_call_target="tpu_custom_call" | custom-call | flops 3221225472 | bytes 9000000 | tf_op jit(solution)/shard_map/by_clip/pallas_call | solution.py:589
  86.2 1.9 %all-to-all-done.2.c_got = f32[32,8,128]{2,1,0:T(8,128)S(1)} async-done(((f32[32,8,128]{2,1,0:T(8,128)}), f32[32,8,128]{2,1,0:T(8,128)S(1)}, u32[]{:S(2)}, u32[]{:S(2)}) %all-to-all-start.2) | async-done | bytes 131104 | tf_op jit(solution)/shard_map/column_sums/all_to_all | solution.py:468
  88.2 5.6 %clip_send.1 = (f32[784,256]{1,0:T(8,128)S(1)}, bf16[784,256]{1,0:T(8,128)(2,1)S(1)}) custom-call(f32[32,8,128]{2,1,0:T(8,128)S(1)} %all-to-all-done.2.c_got, f32[8,128]{1,0:T(8,128)S(1)} %get-tuple-element.41.r_ref, bf16[4,1536,512]{2,1,0:T(8,128)(2,1)} %get-tuple-element.47.p_ref, bf16[2048,256]{1,0:T(8,128)(2,1)} %get-tuple-element.43.g_ref, ...), custom_call_target="tpu_custom_call" | custom-call | flops 1610612736 | bytes 10000000 | tf_op jit(solution)/shard_map/clip_send/pallas_call | solution.py:602
  93.8 0.0 copy-start
  93.8 0.0 copy-start.1
  93.8 4.3 %gloss_send.1 = (bf16[32,48,256]{2,1,0:T(8,128)(2,1)}, f32[8,128]{1,0:T(8,128)S(1)}) custom-call(f32[32,8,128]{2,1,0:T(8,128)S(1)} %all-to-all-done.2.c_got, f32[2048,512]{1,0:T(8,128)} %by_clip.1), custom_call_target="tpu_custom_call" | custom-call | flops 2000000 | bytes 5000000 | tf_op jit(solution)/shard_map/gloss_send/pallas_call | solution.py:615
  98.1 7.8 %all-to-all-start.3 = ((bf16[32,48,256]{2,1,0:T(8,128)(2,1)}), bf16[32,48,256]{2,1,0:T(8,128)(2,1)S(1)}, u32[]{:S(2)}, u32[]{:S(2)}) async-start(bf16[32,48,256]{2,1,0:T(8,128)(2,1)} %get-tuple-element.63), calls=%async_computation.3 | async-start | bytes 1572864 | tf_op jit(solution)/shard_map/gloss_send/all_to_all | solution.py:468
  106.0 1.9 %collective-permute-start = (bf16[784,256]{1,0:T(8,128)(2,1)S(1)}, bf16[784,256]{1,0:T(8,128)(2,1)S(1)}, u32[]{:S(2)}, u32[]{:S(2)}) collective-permute-start(bf16[784,256]{1,0:T(8,128)(2,1)S(1)} %get-tuple-element.51), channel_id=1, source_target_pairs={{0,1},{1,0},{2,3},{3,2},{4,5},{5,4},{6,7},{7,6},{8,9},{9,8},{10,11... | collective-permute-start | bytes 1204232 | tf_op jit(solution)/shard_map/clips_by_core/ppermute | solution.py:462
  107.9 1.7 %collective-permute-done.got = bf16[784,256]{1,0:T(8,128)(2,1)S(1)} collective-permute-done((bf16[784,256]{1,0:T(8,128)(2,1)S(1)}, bf16[784,256]{1,0:T(8,128)(2,1)S(1)}, u32[]{:S(2)}, u32[]{:S(2)}) %collective-permute-start) | collective-permute-done | bytes 401440 | tf_op jit(solution)/shard_map/clips_by_core/ppermute | solution.py:462
  109.6 0.4 clips_by_core.1
  110.0 3.8 %collective-permute-start.1 = (bf16[448,256]{1,0:T(8,128)(2,1)S(1)}, bf16[448,256]{1,0:T(8,128)(2,1)S(1)}, u32[]{:S(2)}, u32[]{:S(2)}) collective-permute-start(bf16[448,256]{1,0:T(8,128)(2,1)S(1)} %get-tuple-element.53), channel_id=1, source_target_pairs={{0,32},{32,0},{64,96},{96,64},{128,160},{160,128},{192,224},{224,1... | collective-permute-start | bytes 688136 | tf_op jit(solution)/shard_map/clips_by_z1/ppermute | solution.py:465
  113.8 5.9 %collective-permute-done.1.got = bf16[448,256]{1,0:T(8,128)(2,1)S(1)} collective-permute-done((bf16[448,256]{1,0:T(8,128)(2,1)S(1)}, bf16[448,256]{1,0:T(8,128)(2,1)S(1)}, u32[]{:S(2)}, u32[]{:S(2)}) %collective-permute-start.1) | collective-permute-done | bytes 229408 | tf_op jit(solution)/shard_map/clips_by_z1/ppermute | solution.py:465
  119.7 0.2 clips_by_z1.1
  119.9 4.5 %collective-permute-start.2 = (bf16[224,256]{1,0:T(8,128)(2,1)S(1)}, bf16[224,256]{1,0:T(8,128)(2,1)S(1)}, u32[]{:S(2)}, u32[]{:S(2)}) collective-permute-start(bf16[224,256]{1,0:T(8,128)(2,1)S(1)} %get-tuple-element.55), channel_id=1, source_target_pairs={{0,64},{32,96},{64,0},{96,32},{128,192},{160,224},{192,128},{224,1... | collective-permute-start | bytes 344072 | tf_op jit(solution)/shard_map/clips_by_z2/ppermute | solution.py:465
  124.4 5.3 %collective-permute-done.2.got = bf16[224,256]{1,0:T(8,128)(2,1)S(1)} collective-permute-done((bf16[224,256]{1,0:T(8,128)(2,1)S(1)}, bf16[224,256]{1,0:T(8,128)(2,1)S(1)}, u32[]{:S(2)}, u32[]{:S(2)}) %collective-permute-start.2) | collective-permute-done | bytes 114720 | tf_op jit(solution)/shard_map/clips_by_z2/ppermute | solution.py:465
  129.7 0.2 clips_by_z2.1
  129.9 7.3 %collective-permute-start.3 = (bf16[112,256]{1,0:T(8,128)(2,1)S(1)}, bf16[112,256]{1,0:T(8,128)(2,1)S(1)}, u32[]{:S(2)}, u32[]{:S(2)}) collective-permute-start(bf16[112,256]{1,0:T(8,128)(2,1)S(1)} %get-tuple-element.57), channel_id=1, source_target_pairs={{0,128},{32,160},{64,192},{96,224},{128,0},{160,32},{192,64},{224,... | collective-permute-start | bytes 172040 | tf_op jit(solution)/shard_map/video_grad/ppermute | solution.py:465
  137.2 2.6 %collective-permute-done.3.got = bf16[112,256]{1,0:T(8,128)(2,1)S(1)} collective-permute-done((bf16[112,256]{1,0:T(8,128)(2,1)S(1)}, bf16[112,256]{1,0:T(8,128)(2,1)S(1)}, u32[]{:S(2)}, u32[]{:S(2)}) %collective-permute-start.3) | collective-permute-done | bytes 57376 | tf_op jit(solution)/shard_map/video_grad/ppermute | solution.py:465
  139.9 0.9 video_grad.1
  140.7 0.8 gloss_grad.1
  (5 shorter events, 0.0 us)
Async XLA Ops:
  2.5 38.9 %all-to-all-start = ((bf16[32,48,256]{2,1,0:T(8,128)(2,1)}), bf16[32,48,256]{2,1,0:T(8,128)(2,1)S(1)}, u32[]{:S(2)}, u32[]{:S(2)}) async-start(bf16[32,48,256]{2,1,0:T(8,128)(2,1)} %get-tuple-element.35.g_ref), calls=%async_computation | async-start | bytes 1572864 | tf_op jit(solution)/shard_map/gather/all_to_all | solution.py:468
  49.3 18.6 %all-to-all-start.1 = ((f32[16,8,128]{2,1,0:T(8,128)}), f32[16,8,128]{2,1,0:T(8,128)S(1)}, u32[]{:S(2)}, u32[]{:S(2)}) async-start(f32[16,8,128]{2,1,0:T(8,128)} %get-tuple-element.38), calls=%async_computation.1 | async-start | bytes 131072 | tf_op jit(solution)/shard_map/row_sums/all_to_all | solution.py:468
  68.7 19.5 %all-to-all-start.2 = ((f32[32,8,128]{2,1,0:T(8,128)}), f32[32,8,128]{2,1,0:T(8,128)S(1)}, u32[]{:S(2)}, u32[]{:S(2)}) async-start(f32[32,8,128]{2,1,0:T(8,128)} %get-tuple-element.40), calls=%async_computation.2 | async-start | bytes 262144 | tf_op jit(solution)/shard_map/column_sums/all_to_all | solution.py:468
  93.8 46.0 %copy-start = (bf16[3,32,256]{2,1,0:T(8,128)(2,1)S(1)}, bf16[3,32,256]{2,1,0:T(8,128)(2,1)}, u32[]{:S(2)}) copy-start(bf16[3,32,256]{2,1,0:T(8,128)(2,1)} %video.1) | copy-start | bytes 147460
  93.8 46.9 %copy-start.1 = (bf16[3,16,256]{2,1,0:T(8,128)(2,1)S(1)}, bf16[3,16,256]{2,1,0:T(8,128)(2,1)}, u32[]{:S(2)}) copy-start(bf16[3,16,256]{2,1,0:T(8,128)(2,1)} %gloss.1) | copy-start | bytes 73732
  98.1 42.6 %all-to-all-start.3 = ((bf16[32,48,256]{2,1,0:T(8,128)(2,1)}), bf16[32,48,256]{2,1,0:T(8,128)(2,1)S(1)}, u32[]{:S(2)}, u32[]{:S(2)}) async-start(bf16[32,48,256]{2,1,0:T(8,128)(2,1)} %get-tuple-element.63), calls=%async_computation.3 | async-start | bytes 1572864 | tf_op jit(solution)/shard_map/gloss_send/all_to_all | solution.py:468
  106.0 3.6 %collective-permute-start = (bf16[784,256]{1,0:T(8,128)(2,1)S(1)}, bf16[784,256]{1,0:T(8,128)(2,1)S(1)}, u32[]{:S(2)}, u32[]{:S(2)}) collective-permute-start(bf16[784,256]{1,0:T(8,128)(2,1)S(1)} %get-tuple-element.51), channel_id=1, source_target_pairs={{0,1},{1,0},{2,3},{3,2},{4,5},{5,4},{6,7},{7,6},{8,9},{9,8},{10,11... | collective-permute-start | bytes 1204232 | tf_op jit(solution)/shard_map/clips_by_core/ppermute | solution.py:462
  110.0 9.7 %collective-permute-start.1 = (bf16[448,256]{1,0:T(8,128)(2,1)S(1)}, bf16[448,256]{1,0:T(8,128)(2,1)S(1)}, u32[]{:S(2)}, u32[]{:S(2)}) collective-permute-start(bf16[448,256]{1,0:T(8,128)(2,1)S(1)} %get-tuple-element.53), channel_id=1, source_target_pairs={{0,32},{32,0},{64,96},{96,64},{128,160},{160,128},{192,224},{224,1... | collective-permute-start | bytes 688136 | tf_op jit(solution)/shard_map/clips_by_z1/ppermute | solution.py:465
  119.9 9.8 %collective-permute-start.2 = (bf16[224,256]{1,0:T(8,128)(2,1)S(1)}, bf16[224,256]{1,0:T(8,128)(2,1)S(1)}, u32[]{:S(2)}, u32[]{:S(2)}) collective-permute-start(bf16[224,256]{1,0:T(8,128)(2,1)S(1)} %get-tuple-element.55), channel_id=1, source_target_pairs={{0,64},{32,96},{64,0},{96,32},{128,192},{160,224},{192,128},{224,1... | collective-permute-start | bytes 344072 | tf_op jit(solution)/shard_map/clips_by_z2/ppermute | solution.py:465
  129.9 10.0 %collective-permute-start.3 = (bf16[112,256]{1,0:T(8,128)(2,1)S(1)}, bf16[112,256]{1,0:T(8,128)(2,1)S(1)}, u32[]{:S(2)}, u32[]{:S(2)}) collective-permute-start(bf16[112,256]{1,0:T(8,128)(2,1)S(1)} %get-tuple-element.57), channel_id=1, source_target_pairs={{0,128},{32,160},{64,192},{96,224},{128,0},{160,32},{192,64},{224,... | collective-permute-start | bytes 172040 | tf_op jit(solution)/shard_map/video_grad/ppermute | solution.py:465

commit v5 on v4

--- a/solution.py
+++ b/solution.py
@@ -30,8 +30,6 @@
 PAIRS = GLOSSES // 2
 QUADS = GLOSSES // 4
 NXY, NZC = NX * NY, NZ * NCORE
-CHUNK = VOWN + EXTRA
-
 
 def flat(x, z, y, core):
     return ((x % 2) * NZ + z) * 32 + (x // 2) * 16 + 2 * y + core
@@ -79,7 +77,7 @@
 
 def column_of(row, n):
     eye = iota((n, LANES), 0) == iota((n, LANES), 1)
-    return jnp.sum(jnp.where(eye, jnp.broadcast_to(row[0:1], (n, LANES)), 0.0), axis=1, keepdims=True)
+    return jnp.sum(jnp.where(eye, jnp.broadcast_to(row, (n, LANES)), 0.0), axis=1, keepdims=True)
 
 
 def pieces(value):
@@ -161,7 +159,7 @@
     by_row = jnp.where(row_ok, jnp.log(rows / glosses_r) / frames_r, 0.0)
     by_col = jnp.where(col_ok, jnp.log(cols / frames_q) / glosses_q, 0.0)
     total = jnp.sum(by_row, axis=0, keepdims=True) + jnp.sum(by_col, axis=1, keepdims=True)
-    logit_sum[...] = jnp.broadcast_to(0.5 * total, (8, LANES))
+    logit_sum[...] = jnp.broadcast_to(0.5 * total, (1, LANES))
     weight = -5.0 * e * (1.0 / (rows * frames_r) + 1.0 / (cols * glosses_q))
     dv[...] = nn(weight, g.astype(F32), precision=lax.Precision.HIGHEST)
     dg[...] = tn(weight, v.astype(F32), precision=lax.Precision.HIGHEST)
@@ -251,16 +249,15 @@
     sums = jnp.sum(e_pair, axis=1, keepdims=True)
     across = lane == iota((CLIPS_DEV, LANES), 0)
     r_row = jnp.sum(jnp.where(across, jnp.broadcast_to(sums, (CLIPS_DEV, LANES)), 0.0), axis=0, keepdims=True)
-    r_rows = jnp.where(iota((8, LANES), 1) == CLIPS_DEV, diag[...], r_row)
+    r_row = jnp.where(iota((1, LANES), 1) == CLIPS_DEV, diag[...], r_row)
     for i in range(NZC):
-        r_out[i] = r_rows
-    c_out[...] = jnp.broadcast_to(jnp.sum(e_pair, axis=0, keepdims=True), (8, LANES))
+        r_out[i] = r_row
+    c_out[...] = jnp.sum(e_pair, axis=0, keepdims=True)
     for copy in copies:
         copy.wait()
 
 
-def weights_kernel(v_ref, g_ref, row_ref, col_ref, e_ref, p_out, av_out):
-    p = pl.program_id(0)
+def weights_kernel(v_ref, g_ref, row_ref, col_ref, e_ref, p_out):
     e = exp_scores(v_ref[...], g_ref[...])
     scale = 2.5 * e_ref[...]
     col0, col1 = col_ref[0], col_ref[1]
@@ -271,17 +268,6 @@
         w0 = scale * block[:, :LANES] * jnp.maximum(row + col0, 0.0)
         w1 = scale * block[:, LANES:] * jnp.maximum(row + col1, 0.0)
         p_out[0, at, :] = jnp.concatenate([w0, w1], axis=1).astype(BF16)
-    weights = p_out[0]
-    part = nn(weights, g_ref[...])
-
-    @pl.when(p == 0)
-    def _():
-        av_out[...] = part
-
-    @pl.when(p > 0)
-    def _():
-        av_out[...] = av_out[...] + part
-
 
 def added(got):
     total = got[0]
@@ -291,25 +277,27 @@
 
 
 def row_sums_kernel(r_got, c_part, c_out, r_out):
-    r_rows = added(r_got)
-    r_out[...] = r_rows
+    r_row = added(r_got)
+    r_out[...] = r_row
     lane = iota((1, LANES), 1)
-    logs = jnp.where(lane < CLIPS_DEV, jnp.log(jnp.where(lane < CLIPS_DEV, r_rows[0:1], 1.0)), 0.0)
-    logs = logs - jnp.where(lane == CLIPS_DEV, 2.0 * r_rows[0:1], 0.0)
+    logs = jnp.where(lane < CLIPS_DEV, jnp.log(jnp.where(lane < CLIPS_DEV, r_row, 1.0)), 0.0)
+    logs = logs - jnp.where(lane == CLIPS_DEV, 2.0 * r_row, 0.0)
     total = jnp.sum(logs, axis=1, keepdims=True)
-    message = jnp.where(iota((8, LANES), 1) == TEXTS_DEV, total, c_part[...])
+    message = jnp.where(lane == TEXTS_DEV, total, c_part[...])
     for i in range(NXY):
         c_out[i] = message
 
 
-def inverse_texts(c_rows):
-    real = iota((8, LANES), 1) < TEXTS_DEV
-    inverse = jnp.where(real, 1.0 / jnp.where(real, c_rows, 1.0), 0.0)
+def inverse_texts(c_row):
+    real = iota((1, LANES), 1) < TEXTS_DEV
+    inverse = jnp.where(real, 1.0 / jnp.where(real, c_row, 1.0), 0.0)
     return jnp.broadcast_to(column_of(inverse, LANES), (LANES, WIDTH))
 
 
-def by_clip_kernel(r_ref, p_ref, v_ref, out, both):
-    @pl.when(pl.program_id(0) == 0)
+def by_clip_kernel(r_ref, p_ref, v_ref, g_ref, out, av_out, both):
+    step = pl.program_id(0)
+
+    @pl.when(step == 0)
     def _():
         inverse = jnp.broadcast_to(1.0 / column_of(r_ref[...], CLIPS_DEV), (CLIPS_DEV, WIDTH))
         for f in range(FRAMES):
@@ -319,6 +307,15 @@
             both[at, WIDTH:] = (v.astype(F32) * inverse).astype(BF16)
 
     out[...] = tn(p_ref[0], both[...])
+    part = nn(p_ref[0], g_ref[...])
+
+    @pl.when(step == 0)
+    def _():
+        av_out[...] = part
+
+    @pl.when(step > 0)
+    def _():
+        av_out[...] = av_out[...] + part
 
 
 def gloss_send_kernel(c_got, by_clip, out, c_out, scr):
@@ -343,14 +340,14 @@
         out[...] = get(scr, pl.ds(0, NXY * GOWN)).astype(BF16).reshape(NXY, GOWN, WIDTH)
 
 
-def clip_send_kernel(c_got, r_ref, p_ref, g_ref, av_ref, mine, twin, c_rows, total):
+def clip_send_kernel(c_got, r_ref, p_ref, g_ref, av_ref, mine, twin, c_row, total):
     step = pl.program_id(0)
 
     @pl.when(step == 0)
     def _():
-        c_rows[...] = added(c_got)
-
-    col = inverse_texts(c_rows[...])
+        c_row[...] = added(c_got)
+
+    col = inverse_texts(c_row[...])
     scaled = g_ref[...].astype(F32) * jnp.concatenate([col] * (GLOSSES // QUADS), axis=0)
     part = nn(p_ref[0], scaled.astype(BF16))
 
@@ -378,7 +375,7 @@
                 others.append(jnp.where(core == 0, high, low))
             twin[pl.ds(pair * CLIPS_DEV, CLIPS_DEV), :] = jnp.concatenate(others, axis=0).astype(BF16)
         real = iota((1, LANES), 1) < TEXTS_DEV
-        logs = jnp.where(real, jnp.log(jnp.where(real, c_rows[0:1], 1.0)), 0.0)
+        logs = jnp.where(real, jnp.log(jnp.where(real, c_row[...], 1.0)), 0.0)
         extra = pieces(jnp.sum(logs, axis=1, keepdims=True))
         mine[pl.ds(FRAMES * half, EXTRA), :] = extra
         twin[pl.ds(FRAMES * half, EXTRA), :] = extra.astype(BF16)
@@ -395,34 +392,31 @@
         at = pl.ds(i * step, step)
         two = mine[at, :] + got[at, :].astype(F32)
         for k in range(2):
-            put(scr, pl.ds(2 * i + k, NZ, stride=CHUNK), two[k * NZ : (k + 1) * NZ])
-    at = pl.ds(VOWN * NZ, EXTRA)
-    extra = pieces(unpiece(mine[at, :]) + unpiece(got[at, :].astype(F32)))
-    for i in range(NZ):
-        put(scr, pl.ds(i * CHUNK + VOWN, EXTRA), extra)
+            put(scr, pl.ds(2 * i + k, NZ, stride=VOWN), two[k * NZ : (k + 1) * NZ])
     bit = z_bits()[0]
-    for i in range(NZ // 2):
-        at = pl.ds(i * CHUNK, CHUNK)
-        keep[at, :] = get(scr, pl.ds(pl.multiple_of((NZ // 2 * bit + i) * CHUNK, CHUNK), CHUNK))
-        send[at, :] = get(scr, pl.ds(pl.multiple_of((NZ // 2 * (1 - bit) + i) * CHUNK, CHUNK), CHUNK)).astype(BF16)
-
-
-def joined(mine, got, owner):
-    start = owner * CHUNK if isinstance(owner, int) else pl.multiple_of(owner * CHUNK, CHUNK)
-    at = pl.ds(start, VOWN)
-    tail = pl.ds(start + VOWN, EXTRA)
-    extra = pieces(unpiece(mine[tail, :]) + unpiece(got[tail, :].astype(F32)))
-    return mine[at, :] + got[at, :].astype(F32), extra
+    owners = NZ // 2
+    for i in range(owners):
+        at = pl.ds(i * VOWN, VOWN)
+        keep[at, :] = get(scr, pl.ds(pl.multiple_of((owners * bit + i) * VOWN, VOWN), VOWN))
+        send[at, :] = get(scr, pl.ds(pl.multiple_of((owners * (1 - bit) + i) * VOWN, VOWN), VOWN)).astype(BF16)
+    extra = loss_rows(mine, got, NZ)
+    keep[pl.ds(owners * VOWN, EXTRA), :] = extra
+    send[pl.ds(owners * VOWN, EXTRA), :] = extra.astype(BF16)
+
+
+def loss_rows(mine, got, owners):
+    tail = pl.ds(owners * VOWN, EXTRA)
+    return pieces(unpiece(mine[tail, :]) + unpiece(got[tail, :].astype(F32)))
 
 
 def halve_kernel(which, mine, got, keep, send):
     bit = z_bits()[which]
     owners = NZ // 2 ** (which + 1)
-    for i in range(owners):
-        for out, chosen in ((keep, bit), (send, 1 - bit)):
-            rows, extra = joined(mine, got, owners * chosen + i)
-            out[pl.ds(i * CHUNK, VOWN), :] = rows.astype(out.dtype)
-            out[pl.ds(i * CHUNK + VOWN, EXTRA), :] = extra.astype(out.dtype)
+    extra = loss_rows(mine, got, 2 * owners)
+    for out, chosen in ((keep, bit), (send, 1 - bit)):
+        half = pl.ds(pl.multiple_of(chosen * owners * VOWN, VOWN), owners * VOWN)
+        out[pl.ds(0, owners * VOWN), :] = (mine[half, :] + got[half, :].astype(F32)).astype(out.dtype)
+        out[pl.ds(owners * VOWN, EXTRA), :] = extra.astype(out.dtype)
 
 
 def token_grads(total, scr, raw, out, tokens):
@@ -436,11 +430,12 @@
         out[c] = factor * d - factor * x * (inner / (WIDTH * mean_sq))
 
 
-def video_grad_kernel(clips, mine, got, c_rows, diag, video, out, loss, scr):
-    total, extra = joined(mine, got, 0)
+def video_grad_kernel(clips, mine, got, c_row, diag, video, out, loss, scr):
+    at = pl.ds(0, VOWN)
+    total = mine[at, :] + got[at, :].astype(F32)
     token_grads(total + diag[...], scr, video, out, FRAMES)
-    row_part = c_rows[0:1, TEXTS_DEV : TEXTS_DEV + 1]
-    loss[...] = (unpiece(extra) + row_part) * (0.5 / clips)
+    row_part = c_row[:, TEXTS_DEV : TEXTS_DEV + 1]
+    loss[...] = (unpiece(loss_rows(mine, got, 1)) + row_part) * (0.5 / clips)
 
 
 def gloss_grad_kernel(got, diag, gloss, out, scr):
@@ -513,8 +508,8 @@
             diagonal_kernel,
             grid=(1,),
             in_specs=[whole(8, LANES), whole(VOWN, WIDTH), first(GOWN)],
-            out_specs=(whole(VOWN, WIDTH), whole(GOWN, WIDTH), whole(8, LANES)),
-            out_shape=(shape(VOWN, WIDTH), shape(GOWN, WIDTH), shape(8, LANES)),
+            out_specs=(whole(VOWN, WIDTH), whole(GOWN, WIDTH), whole(1, LANES)),
+            out_shape=(shape(VOWN, WIDTH), shape(GOWN, WIDTH), shape(1, LANES)),
             compiler_params=params(),
             cost_estimate=cost(2e7, 3e5),
         )(counts, v_own, g_own)
@@ -530,8 +525,8 @@
                 pltpu.HBM((VROWS, LANES), F32),
                 pltpu.HBM((GLOSSES, CLIPS_DEV, LANES), F32),
                 shape(CLIPS_DEV, LANES),
-                shape(NZC, 8, LANES),
-                shape(8, LANES),
+                shape(NZC, 1, LANES),
+                shape(1, LANES),
             ),
             scratch_shapes=[
                 pltpu.VMEM((VROWS, WIDTH), BF16),
@@ -551,10 +546,10 @@
         )(v_got, g_got, logit_sum)
 
     with jax.named_scope("row_sums"):
-        c_send, r_rows = pl.pallas_call(
+        c_send, r_row = pl.pallas_call(
             row_sums_kernel,
             in_specs=[vmem] * 2,
-            out_shape=(shape(NXY, 8, LANES), shape(8, LANES)),
+            out_shape=(shape(NXY, 1, LANES), shape(1, LANES)),
             compiler_params=params(),
             cost_estimate=cost(1e5, 3e5),
         )(exchanged(r_part, ZC_GROUPS), c_part)
@@ -566,7 +561,7 @@
 
     p_spec = pl.BlockSpec((1, VROWS, 2 * WIDTH), lambda i: (i, 0, 0))
     with jax.named_scope("weights"):
-        weights, av = pl.pallas_call(
+        weights = pl.pallas_call(
             weights_kernel,
             grid=(PAIRS,),
             in_specs=[
@@ -576,66 +571,64 @@
                 pl.BlockSpec((2, CLIPS_DEV, LANES), lambda i: (i, 0, 0)),
                 whole(CLIPS_DEV, LANES),
             ],
-            out_specs=(
-                pl.BlockSpec((1, VROWS, WIDTH), lambda i: (i // 2, 0, i % 2)),
-                whole(VROWS, WIDTH),
-            ),
-            out_shape=(pltpu.HBM((QUADS, VROWS, 2 * WIDTH), BF16), shape(VROWS, WIDTH)),
-            compiler_params=params(),
-            cost_estimate=cost(4 * VROWS * GROWS * WIDTH, 12e6, VROWS * GROWS),
+            out_specs=pl.BlockSpec((1, VROWS, WIDTH), lambda i: (i // 2, 0, i % 2)),
+            out_shape=pltpu.HBM((QUADS, VROWS, 2 * WIDTH), BF16),
+            compiler_params=params(),
+            cost_estimate=cost(2 * VROWS * GROWS * WIDTH, 12e6, VROWS * GROWS),
         )(*in_hbm(v_all, g_all, row_inv, col_inv), e_pair)
 
     with jax.named_scope("by_clip"):
-        by_clip = pl.pallas_call(
+        by_clip, av = pl.pallas_call(
             by_clip_kernel,
             grid=(QUADS,),
-            in_specs=[whole(8, LANES), p_spec, whole(VROWS, WIDTH)],
-            out_specs=pl.BlockSpec((4 * LANES, 2 * WIDTH), lambda i: (i, 0)),
-            out_shape=pltpu.HBM((GROWS, 2 * WIDTH), F32),
+            in_specs=[whole(1, LANES), p_spec, whole(VROWS, WIDTH), halves(4 * LANES)],
+            out_specs=(pl.BlockSpec((4 * LANES, 2 * WIDTH), lambda i: (i, 0)), whole(VROWS, WIDTH)),
+            out_shape=(pltpu.HBM((GROWS, 2 * WIDTH), F32), shape(VROWS, WIDTH)),
             scratch_shapes=[pltpu.VMEM((VROWS, 2 * WIDTH), BF16)],
             compiler_params=params(),
-            cost_estimate=cost(4 * VROWS * GROWS * WIDTH, 9e6),
-        )(r_rows, *in_hbm(weights, v_all))
+            cost_estimate=cost(6 * VROWS * GROWS * WIDTH, 14e6),
+        )(r_row, *in_hbm(weights, v_all, g_all))
 
     with jax.named_scope("clip_send"):
         v_rows = FRAMES * CLIPS_DEV // 2 + EXTRA
         mine, twin = pl.pallas_call(
             clip_send_kernel,
             grid=(QUADS,),
-            in_specs=[whole(NXY, 8, LANES), whole(8, LANES), p_spec, halves(4 * LANES), whole(VROWS, WIDTH)],
+            in_specs=[whole(NXY, 1, LANES), whole(1, LANES), p_spec, halves(4 * LANES), whole(VROWS, WIDTH)],
             out_specs=(whole(v_rows, WIDTH), whole(v_rows, WIDTH)),
             out_shape=(shape(v_rows, WIDTH), shape(v_rows, WIDTH, dtype=BF16)),
-            scratch_shapes=[pltpu.VMEM((8, LANES), F32), pltpu.VMEM((VROWS, WIDTH), F32)],
+            scratch_shapes=[pltpu.VMEM((1, LANES), F32), pltpu.VMEM((VROWS, WIDTH), F32)],
             compiler_params=params(),
             cost_estimate=cost(2 * VROWS * GROWS * WIDTH, 1e7),
-        )(c_got, r_rows, *in_hbm(weights, g_all), av)
-
-    with jax.named_scope("gloss_send"):
-        twin, c_ready = lax.optimization_barrier((twin, c_got))
-        dg_send, c_rows = pl.pallas_call(
-            gloss_send_kernel,
-            grid=(QUADS,),
-            in_specs=[whole(NXY, 8, LANES), pl.BlockSpec((4 * LANES, 2 * WIDTH), lambda i: (i, 0))],
-            out_specs=(whole(NXY, GOWN, WIDTH), whole(8, LANES)),
-            out_shape=(shape(NXY, GOWN, WIDTH, dtype=BF16), shape(8, LANES)),
-            scratch_shapes=[two_halves(NXY * GOWN)],
-            compiler_params=params(),
-            cost_estimate=cost(2e6, 5e6),
-        )(c_ready, *in_hbm(by_clip))
-        dg_got = exchanged(dg_send, XY_GROUPS)
+        )(c_got, r_row, *in_hbm(weights, g_all), av)
 
     def kept_and_sent(owners):
-        return (shape(owners * CHUNK, WIDTH), shape(owners * CHUNK, WIDTH, dtype=BF16))
+        rows = owners * VOWN + EXTRA
+        return (shape(rows, WIDTH), shape(rows, WIDTH, dtype=BF16))
 
     with jax.named_scope("clips_by_core"):
         mine, sent = pl.pallas_call(
             clip_rows_kernel,
             in_specs=[vmem] * 2,
             out_shape=kept_and_sent(NZ // 2),
-            scratch_shapes=[two_halves(NZ * CHUNK)],
+            scratch_shapes=[two_halves(NZ * VOWN)],
             compiler_params=params(),
             cost_estimate=cost(1e6, 2e6),
         )(mine, to_core(twin))
+    with jax.named_scope("gloss_send"):
+        sent, c_ready = lax.optimization_barrier((sent, c_got))
+        dg_send, c_row = pl.pallas_call(
+            gloss_send_kernel,
+            grid=(QUADS,),
+            in_specs=[whole(NXY, 1, LANES), pl.BlockSpec((4 * LANES, 2 * WIDTH), lambda i: (i, 0))],
+            out_specs=(whole(NXY, GOWN, WIDTH), whole(1, LANES)),
+            out_shape=(shape(NXY, GOWN, WIDTH, dtype=BF16), shape(1, LANES)),
+            scratch_shapes=[two_halves(NXY * GOWN)],
+            compiler_params=params(),
+            cost_estimate=cost(2e6, 5e6),
+        )(c_ready, *in_hbm(by_clip))
+        dg_got = exchanged(dg_send, XY_GROUPS)
+
     for which, scope in ((1, "clips_by_z1"), (2, "clips_by_z2")):
         with jax.named_scope(scope):
             mine, sent = pl.pallas_call(
@@ -654,7 +647,7 @@
             scratch_shapes=[two_halves(VOWN)],
             compiler_params=params(),
             cost_estimate=cost(1e6, 1e6),
-        )(mine, to_z(sent, NZ // 2), c_rows, dv_diag, video)
+        )(mine, to_z(sent, NZ // 2), c_row, dv_diag, video)
     with jax.named_scope("gloss_grad"):
         grad_gloss = pl.pallas_call(
             gloss_grad_kernel,

time: 143 us -> 141 us (0.986)
  waiting for transfers between devices: 17.4 us -> 13.4 us
  starting transfers between devices: 53.8 us -> 55.9 us
    ppermute x3, waiting for transfers between devices: 13.8 us -> 11.7 us  [to_z(): lax.ppermute(a, 'outer', [(i, i ^ mask) for i in range(lax.axis_size('out...]
    all_to_all x4, starting transfers between devices: 36.2 us -> 38.2 us  [exchanged(): lax.all_to_all(a, over_all, 0, 0, axis_index_groups=groups, tiled=True)]
    all_to_all x4, waiting for transfers between devices: 1.95 us -> 0.01 us  [exchanged(): lax.all_to_all(a, over_all, 0, 0, axis_index_groups=groups, tiled=True)]
    pallas_call x3, Pallas kernels: 17.7 us -> 19.3 us  [the longest x1 9.44 us: on_device(): pl.pallas_call(by_clip_kernel, grid=(QUADS,), in_specs=[whole(1, LANES),...]
  transfers between devices with their start and end apart: 8 -> 8, of which waited for: 5 -> 4; matrix products, arithmetic and copies ran while one was open for 0% -> 0% of each run, Pallas kernels for 15% -> 15%
where the time goes in v5:
time: 141 us; the launch traced here: 140 us
  starting transfers between devices  55.9 us (40%)
  Pallas kernels  42.9 us (30%)
  blocking collectives  27.3 us (19%)
  waiting for transfers between devices  13.4 us (10%)
    all_to_all x4, starting transfers between devices, exchanged(): lax.all_to_all(a, over_all, 0, 0, axis_index_groups=groups, tiled=True)  38.2 us
    all_gather x4, blocking collectives, gathered(): lax.all_gather(a, over_all, axis=0, axis_index_groups=groups, tiled=True)  27.3 us
    ppermute x3, starting transfers between devices, to_z(): lax.ppermute(a, 'outer', [(i, i ^ mask) for i in range(lax.axis_size('out...  15.7 us
    ppermute x3, waiting for transfers between devices, to_z(): lax.ppermute(a, 'outer', [(i, i ^ mask) for i in range(lax.axis_size('out...  11.7 us
    pallas_call x1, Pallas kernels, on_device(): pl.pallas_call(by_clip_kernel, grid=(QUADS,), in_specs=[whole(1, LANES),...  9.44 us
    pallas_call x1, Pallas kernels, on_device(): pl.pallas_call(weights_kernel, grid=(PAIRS,), in_specs=[whole(VROWS, WIDT...  8.94 us
    pallas_call x1, Pallas kernels, on_device(): pl.pallas_call(forward_kernel, in_specs=[vmem] * 3, out_specs=[pl.BlockSp...  7.92 us
    pallas_call x1, Pallas kernels, on_device(): pl.pallas_call(clip_send_kernel, grid=(QUADS,), in_specs=[whole(NXY, 1, L...  5.62 us
  transfers between devices with their start and end apart: 8, of which 4 were waited for; matrix products, arithmetic and copies ran while one was open for 0% of the time, Pallas kernels for 15%

profile of v5, /device:TPU:2, one launch (start us, length us, event | category | flops | bytes accessed | tf_op | source)
XLA Modules:
  0.0 140.2 jit_solution(5849677306059996400)
XLA Ops:
  0.6 1.9 %unit_tokens.1 = (bf16[96,256]{1,0:T(8,128)(2,1)S(1)}, bf16[32,48,256]{2,1,0:T(8,128)(2,1)}, s32[8,128]{1,0:T(8,128)S(1)}) custom-call(s32[3]{0:T(128)} %fc_in.1, s32[3]{0:T(128)} %gc_in.1, bf16[3,32,256]{2,1,0:T(8,128)(2,1)} %video.1, bf16[3,16,256]{2,1,0:T(8,128)(2,1)} %gloss.1), custom_call_target="tpu_custom_call" | custom-call | flops 200000 | bytes 700000 | tf_op jit(solution)/shard_map/unit_tokens/pallas_call | solution.py:472
  2.5 10.3 %all-to-all-start = ((bf16[32,48,256]{2,1,0:T(8,128)(2,1)}), bf16[32,48,256]{2,1,0:T(8,128)(2,1)S(1)}, u32[]{:S(2)}, u32[]{:S(2)}) async-start(bf16[32,48,256]{2,1,0:T(8,128)(2,1)} %get-tuple-element.35.g_ref), calls=%async_computation | async-start | bytes 1572864 | tf_op jit(solution)/shard_map/gather/all_to_all | solution.py:463
  12.8 1.3 diagonal.1
  14.1 11.8 %all_gather.12 = bf16[192,256]{1,0:T(8,128)(2,1)S(1)} all-gather(bf16[96,256]{1,0:T(8,128)(2,1)S(1)} %get-tuple-element.34.v_ref), channel_id=1, replica_groups={{0,128},{32,160},{64,192},{96,224},{1,129},{33,161},{65,193},{97,225},{..., dimensions={0}, use_global_device_ids=true | all-gather | bytes 147456 | tf_op jit(solution)/shard_map/gather/all_gather | solution.py:466
  25.9 6.4 %all_gather.13 = bf16[384,256]{1,0:T(8,128)(2,1)S(1)} all-gather(bf16[192,256]{1,0:T(8,128)(2,1)S(1)} %all_gather.12), channel_id=1, replica_groups={{0,64},{32,96},{128,192},{160,224},{1,65},{33,97},{129,193},{161,225},{..., dimensions={0}, use_global_device_ids=true | all-gather | bytes 294912 | tf_op jit(solution)/shard_map/gather/all_gather | solution.py:466
  32.3 6.7 %all_gather.14 = bf16[768,256]{1,0:T(8,128)(2,1)S(1)} all-gather(bf16[384,256]{1,0:T(8,128)(2,1)S(1)} %all_gather.13), channel_id=1, replica_groups={{0,32},{64,96},{128,160},{192,224},{1,33},{65,97},{129,161},{193,225},{..., dimensions={0}, use_global_device_ids=true | all-gather | bytes 589824 | tf_op jit(solution)/shard_map/gather/all_gather | solution.py:466
  39.0 2.4 %all_gather.15.v_got = bf16[1536,256]{1,0:T(8,128)(2,1)S(1)} all-gather(bf16[768,256]{1,0:T(8,128)(2,1)S(1)} %all_gather.14), channel_id=1, replica_groups={{0,1},{32,33},{64,65},{96,97},{128,129},{160,161},{192,193},{224,225},{..., dimensions={0}, use_global_device_ids=true | all-gather | bytes 1179648 | tf_op jit(solution)/shard_map/gather/all_gather | solution.py:466
  41.4 7.9 %forward.1 = (bf16[1536,256]{1,0:T(8,128)(2,1)}, bf16[2048,256]{1,0:T(8,128)(2,1)}, f32[1536,128]{1,0:T(8,128)}, f32[16,48,128]{2,1,0:T(8,128)}, f32[48,128]{1,0...) custom-call(bf16[1536,256]{1,0:T(8,128)(2,1)S(1)} %all_gather.15.v_got, ...), custom_call_target="tpu_custom_call" | custom-call | flops 1610612736 | bytes 8000000 | tf_op jit(solution)/shard_map/forward/pallas_call | solution.py:518
  49.3 8.3 %all-to-all-start.1 = ((f32[16,1,128]{2,1,0:T(1,128)}), f32[16,1,128]{2,1,0:T(1,128)S(1)}, u32[]{:S(2)}, u32[]{:S(2)}) async-start(f32[16,1,128]{2,1,0:T(1,128)} %get-tuple-element.38), calls=%async_computation.1 | async-start | bytes 16384 | tf_op jit(solution)/shard_map/row_sums/all_to_all | solution.py:463
  57.6 8.9 %weights.1.p_ref = bf16[4,1536,512]{2,1,0:T(8,128)(2,1)} custom-call(bf16[1536,256]{1,0:T(8,128)(2,1)} %get-tuple-element.42.v_ref, bf16[2048,256]{1,0:T(8,128)(2,1)} %get-tuple-element.43.g_ref, f32[1536,128]{1,0:T(8,128)} %get-tuple-element.44.row_ref, f32[16,48,128]{2,1,0:T(8,128)} %get-tuple-element.45.col_ref, f32[48,128]{1,0:T(8,128)S(1)} %get-tuple-element.46.e_ref), custom_call_target="tpu_custom_call" | custom-call | flops 1610612736 | bytes 12000000 | tf_op jit(solution)/shard_map/weights/pallas_call | solution.py:564
  66.5 0.0 all-to-all-done.1.r_got
  66.5 0.7 row_sums.1
  67.3 9.8 %all-to-all-start.2 = ((f32[32,1,128]{2,1,0:T(1,128)}), f32[32,1,128]{2,1,0:T(1,128)S(1)}, u32[]{:S(2)}, u32[]{:S(2)}) async-start(f32[32,1,128]{2,1,0:T(1,128)} %get-tuple-element.40), calls=%async_computation.2 | async-start | bytes 32768 | tf_op jit(solution)/shard_map/column_sums/all_to_all | solution.py:463
  77.1 9.4 %by_clip.1 = (f32[2048,512]{1,0:T(8,128)}, f32[1536,256]{1,0:T(8,128)S(1)}) custom-call(f32[1,128]{1,0:T(1,128)S(1)} %get-tuple-element.41.r_ref, bf16[4,1536,512]{2,1,0:T(8,128)(2,1)} %weights.1.p_ref, bf16[1536,256]{1,0:T(8,128)(2,1)} %get-tuple-element.42.v_ref, bf16[2048,256]{1,0:T(8,128)(2,1)} %get-tuple-element.43.g_ref), custom_call_target="tpu_custom_call" | custom-call | flops 4831838208 | bytes 14000000 | tf_op jit(solution)/shard_map/by_clip/pallas_call | solution.py:581
  86.5 5.6 %clip_send.1 = (f32[784,256]{1,0:T(8,128)S(1)}, bf16[784,256]{1,0:T(8,128)(2,1)S(1)}) custom-call(f32[32,1,128]{2,1,0:T(1,128)S(1)} %all-to-all-done.2.c_got, f32[1,128]{1,0:T(1,128)S(1)} %get-tuple-element.41.r_ref, bf16[4,1536,512]{2,1,0:T(8,128)(2,1)} %weights.1.p_ref, bf16[2048,256]{1,0:T(8,128)(2,1)} %get-tuple-element.43.g_ref, ...), custom_call_target="tpu_custom_call" | custom-call | flops 1610612736 | bytes 10000000 | tf_op jit(solution)/shard_map/clip_send/pallas_call | solution.py:594
  92.1 0.0 copy-start
  92.1 0.0 copy-start.1
  92.2 2.1 %collective-permute-start = (bf16[784,256]{1,0:T(8,128)(2,1)S(1)}, bf16[784,256]{1,0:T(8,128)(2,1)S(1)}, u32[]{:S(2)}, u32[]{:S(2)}) collective-permute-start(bf16[784,256]{1,0:T(8,128)(2,1)S(1)} %get-tuple-element.49), channel_id=1, source_target_pairs={{0,1},{1,0},{2,3},{3,2},{4,5},{5,4},{6,7},{7,6},{8,9},{9,8},{10,11... | collective-permute-start | bytes 1204232 | tf_op jit(solution)/shard_map/clips_by_core/ppermute | solution.py:457
  94.2 1.7 %collective-permute-done.got = bf16[784,256]{1,0:T(8,128)(2,1)S(1)} collective-permute-done((bf16[784,256]{1,0:T(8,128)(2,1)S(1)}, bf16[784,256]{1,0:T(8,128)(2,1)S(1)}, u32[]{:S(2)}, u32[]{:S(2)}) %collective-permute-start) | collective-permute-done | bytes 401440 | tf_op jit(solution)/shard_map/clips_by_core/ppermute | solution.py:457
  95.9 0.8 clips_by_core.1
  96.7 4.3 %gloss_send.1 = (bf16[32,48,256]{2,1,0:T(8,128)(2,1)}, f32[1,128]{1,0:T(1,128)S(1)}) custom-call(f32[32,1,128]{2,1,0:T(1,128)S(1)} %all-to-all-done.2.c_got, f32[2048,512]{1,0:T(8,128)} %get-tuple-element.58.by_clip), custom_call_target="tpu_custom_call" | custom-call | flops 2000000 | bytes 5000000 | tf_op jit(solution)/shard_map/gloss_send/pallas_call | solution.py:620
  101.0 9.8 %all-to-all-start.3 = ((bf16[32,48,256]{2,1,0:T(8,128)(2,1)}), bf16[32,48,256]{2,1,0:T(8,128)(2,1)S(1)}, u32[]{:S(2)}, u32[]{:S(2)}) async-start(bf16[32,48,256]{2,1,0:T(8,128)(2,1)} %get-tuple-element.63), calls=%async_computation.3 | async-start | bytes 1572864 | tf_op jit(solution)/shard_map/gloss_send/all_to_all | solution.py:463
  110.8 3.8 %collective-permute-start.1 = (bf16[400,256]{1,0:T(8,128)(2,1)S(1)}, bf16[400,256]{1,0:T(8,128)(2,1)S(1)}, u32[]{:S(2)}, u32[]{:S(2)}) collective-permute-start(bf16[400,256]{1,0:T(8,128)(2,1)S(1)} %get-tuple-element.52), channel_id=1, source_target_pairs={{0,32},{32,0},{64,96},{96,64},{128,160},{160,128},{192,224},{224,1... | collective-permute-start | bytes 614408 | tf_op jit(solution)/shard_map/clips_by_z1/ppermute | solution.py:460
  114.6 4.8 %collective-permute-done.1.got = bf16[400,256]{1,0:T(8,128)(2,1)S(1)} collective-permute-done((bf16[400,256]{1,0:T(8,128)(2,1)S(1)}, bf16[400,256]{1,0:T(8,128)(2,1)S(1)}, u32[]{:S(2)}, u32[]{:S(2)}) %collective-permute-start.1) | collective-permute-done | bytes 204832 | tf_op jit(solution)/shard_map/clips_by_z1/ppermute | solution.py:460
  119.4 0.1 clips_by_z1.1
  119.6 4.6 %collective-permute-start.2 = (bf16[208,256]{1,0:T(8,128)(2,1)S(1)}, bf16[208,256]{1,0:T(8,128)(2,1)S(1)}, u32[]{:S(2)}, u32[]{:S(2)}) collective-permute-start(bf16[208,256]{1,0:T(8,128)(2,1)S(1)} %get-tuple-element.54), channel_id=1, source_target_pairs={{0,64},{32,96},{64,0},{96,32},{128,192},{160,224},{192,128},{224,1... | collective-permute-start | bytes 319496 | tf_op jit(solution)/shard_map/clips_by_z2/ppermute | solution.py:460
  124.1 4.3 %collective-permute-done.2.got = bf16[208,256]{1,0:T(8,128)(2,1)S(1)} collective-permute-done((bf16[208,256]{1,0:T(8,128)(2,1)S(1)}, bf16[208,256]{1,0:T(8,128)(2,1)S(1)}, u32[]{:S(2)}, u32[]{:S(2)}) %collective-permute-start.2) | collective-permute-done | bytes 106528 | tf_op jit(solution)/shard_map/clips_by_z2/ppermute | solution.py:460
  128.4 0.1 clips_by_z2.1
  128.5 7.4 %collective-permute-start.3 = (bf16[112,256]{1,0:T(8,128)(2,1)S(1)}, bf16[112,256]{1,0:T(8,128)(2,1)S(1)}, u32[]{:S(2)}, u32[]{:S(2)}) collective-permute-start(bf16[112,256]{1,0:T(8,128)(2,1)S(1)} %get-tuple-element.56), channel_id=1, source_target_pairs={{0,128},{32,160},{64,192},{96,224},{128,0},{160,32},{192,64},{224,... | collective-permute-start | bytes 172040 | tf_op jit(solution)/shard_map/video_grad/ppermute | solution.py:460
  135.9 2.6 %collective-permute-done.3.got = bf16[112,256]{1,0:T(8,128)(2,1)S(1)} collective-permute-done((bf16[112,256]{1,0:T(8,128)(2,1)S(1)}, bf16[112,256]{1,0:T(8,128)(2,1)S(1)}, u32[]{:S(2)}, u32[]{:S(2)}) %collective-permute-start.3) | collective-permute-done | bytes 57376 | tf_op jit(solution)/shard_map/video_grad/ppermute | solution.py:460
  138.5 0.9 video_grad.1
  139.4 0.8 gloss_grad.1
  (5 shorter events, 0.0 us)
Async XLA Ops:
  2.5 38.9 %all-to-all-start = ((bf16[32,48,256]{2,1,0:T(8,128)(2,1)}), bf16[32,48,256]{2,1,0:T(8,128)(2,1)S(1)}, u32[]{:S(2)}, u32[]{:S(2)}) async-start(bf16[32,48,256]{2,1,0:T(8,128)(2,1)} %get-tuple-element.35.g_ref), calls=%async_computation | async-start | bytes 1572864 | tf_op jit(solution)/shard_map/gather/all_to_all | solution.py:463
  49.3 17.2 %all-to-all-start.1 = ((f32[16,1,128]{2,1,0:T(1,128)}), f32[16,1,128]{2,1,0:T(1,128)S(1)}, u32[]{:S(2)}, u32[]{:S(2)}) async-start(f32[16,1,128]{2,1,0:T(1,128)} %get-tuple-element.38), calls=%async_computation.1 | async-start | bytes 16384 | tf_op jit(solution)/shard_map/row_sums/all_to_all | solution.py:463
  67.3 19.2 %all-to-all-start.2 = ((f32[32,1,128]{2,1,0:T(1,128)}), f32[32,1,128]{2,1,0:T(1,128)S(1)}, u32[]{:S(2)}, u32[]{:S(2)}) async-start(f32[32,1,128]{2,1,0:T(1,128)} %get-tuple-element.40), calls=%async_computation.2 | async-start | bytes 32768 | tf_op jit(solution)/shard_map/column_sums/all_to_all | solution.py:463
  92.1 46.4 %copy-start = (bf16[3,32,256]{2,1,0:T(8,128)(2,1)S(1)}, bf16[3,32,256]{2,1,0:T(8,128)(2,1)}, u32[]{:S(2)}) copy-start(bf16[3,32,256]{2,1,0:T(8,128)(2,1)} %video.1) | copy-start | bytes 147460
  92.1 47.3 %copy-start.1 = (bf16[3,16,256]{2,1,0:T(8,128)(2,1)S(1)}, bf16[3,16,256]{2,1,0:T(8,128)(2,1)}, u32[]{:S(2)}) copy-start(bf16[3,16,256]{2,1,0:T(8,128)(2,1)} %gloss.1) | copy-start | bytes 73732
  92.2 3.8 %collective-permute-start = (bf16[784,256]{1,0:T(8,128)(2,1)S(1)}, bf16[784,256]{1,0:T(8,128)(2,1)S(1)}, u32[]{:S(2)}, u32[]{:S(2)}) collective-permute-start(bf16[784,256]{1,0:T(8,128)(2,1)S(1)} %get-tuple-element.49), channel_id=1, source_target_pairs={{0,1},{1,0},{2,3},{3,2},{4,5},{5,4},{6,7},{7,6},{8,9},{9,8},{10,11... | collective-permute-start | bytes 1204232 | tf_op jit(solution)/shard_map/clips_by_core/ppermute | solution.py:457
  101.0 38.4 %all-to-all-start.3 = ((bf16[32,48,256]{2,1,0:T(8,128)(2,1)}), bf16[32,48,256]{2,1,0:T(8,128)(2,1)S(1)}, u32[]{:S(2)}, u32[]{:S(2)}) async-start(bf16[32,48,256]{2,1,0:T(8,128)(2,1)} %get-tuple-element.63), calls=%async_computation.3 | async-start | bytes 1572864 | tf_op jit(solution)/shard_map/gloss_send/all_to_all | solution.py:463
  110.8 8.6 %collective-permute-start.1 = (bf16[400,256]{1,0:T(8,128)(2,1)S(1)}, bf16[400,256]{1,0:T(8,128)(2,1)S(1)}, u32[]{:S(2)}, u32[]{:S(2)}) collective-permute-start(bf16[400,256]{1,0:T(8,128)(2,1)S(1)} %get-tuple-element.52), channel_id=1, source_target_pairs={{0,32},{32,0},{64,96},{96,64},{128,160},{160,128},{192,224},{224,1... | collective-permute-start | bytes 614408 | tf_op jit(solution)/shard_map/clips_by_z1/ppermute | solution.py:460
  119.6 8.8 %collective-permute-start.2 = (bf16[208,256]{1,0:T(8,128)(2,1)S(1)}, bf16[208,256]{1,0:T(8,128)(2,1)S(1)}, u32[]{:S(2)}, u32[]{:S(2)}) collective-permute-start(bf16[208,256]{1,0:T(8,128)(2,1)S(1)} %get-tuple-element.54), channel_id=1, source_target_pairs={{0,64},{32,96},{64,0},{96,32},{128,192},{160,224},{192,128},{224,1... | collective-permute-start | bytes 319496 | tf_op jit(solution)/shard_map/clips_by_z2/ppermute | solution.py:460
  128.5 10.0 %collective-permute-start.3 = (bf16[112,256]{1,0:T(8,128)(2,1)S(1)}, bf16[112,256]{1,0:T(8,128)(2,1)S(1)}, u32[]{:S(2)}, u32[]{:S(2)}) collective-permute-start(bf16[112,256]{1,0:T(8,128)(2,1)S(1)} %get-tuple-element.56), channel_id=1, source_target_pairs={{0,128},{32,160},{64,192},{96,224},{128,0},{160,32},{192,64},{224,... | collective-permute-start | bytes 172040 | tf_op jit(solution)/shard_map/video_grad/ppermute | solution.py:460

commit v6 on v5

--- a/solution.py
+++ b/solution.py
@@ -35,17 +35,18 @@
     return ((x % 2) * NZ + z) * 32 + (x // 2) * 16 + 2 * y + core
 
 
-def z_pairs(mask):
+def z_groups(masks):
     return [
-        [flat(x, z, y, c), flat(x, z ^ mask, y, c)]
+        [flat(x, z ^ mask, y, c) for mask in masks]
         for x in range(NX)
         for y in range(NY)
         for c in range(NCORE)
         for z in range(NZ)
-        if not z & mask
+        if not z & masks[-1] and not z & masks[len(masks) // 2]
     ]
 
 
+Z_QUADS, Z_PAIRS = z_groups((0, 2, 4, 6)), z_groups((0, 1))
 CORE_GROUPS = [[flat(x, z, y, c) for c in range(NCORE)] for x in range(NX) for y in range(NY) for z in range(NZ)]
 XY_GROUPS = [[flat(x, z, y, c) for x in range(NX) for y in range(NY)] for z in range(NZ) for c in range(NCORE)]
 ZC_GROUPS = [[flat(x, z, y, c) for c in range(NCORE) for z in range(NZ)] for x in range(NX) for y in range(NY)]
@@ -381,9 +382,8 @@
         twin[pl.ds(FRAMES * half, EXTRA), :] = extra.astype(BF16)
 
 
-def z_bits():
-    z = lax.rem(lax.axis_index("outer"), NZ)
-    return lax.rem(z, 2), lax.rem(lax.div(z, 2), 2), lax.div(z, 4)
+def own_z():
+    return lax.rem(lax.axis_index("outer"), NZ)
 
 
 def clip_rows_kernel(mine, got, keep, send, scr):
@@ -393,7 +393,7 @@
         two = mine[at, :] + got[at, :].astype(F32)
         for k in range(2):
             put(scr, pl.ds(2 * i + k, NZ, stride=VOWN), two[k * NZ : (k + 1) * NZ])
-    bit = z_bits()[0]
+    bit = lax.rem(own_z(), 2)
     owners = NZ // 2
     for i in range(owners):
         at = pl.ds(i * VOWN, VOWN)
@@ -409,14 +409,13 @@
     return pieces(unpiece(mine[tail, :]) + unpiece(got[tail, :].astype(F32)))
 
 
-def halve_kernel(which, mine, got, keep, send):
-    bit = z_bits()[which]
-    owners = NZ // 2 ** (which + 1)
-    extra = loss_rows(mine, got, 2 * owners)
-    for out, chosen in ((keep, bit), (send, 1 - bit)):
-        half = pl.ds(pl.multiple_of(chosen * owners * VOWN, VOWN), owners * VOWN)
-        out[pl.ds(0, owners * VOWN), :] = (mine[half, :] + got[half, :].astype(F32)).astype(out.dtype)
-        out[pl.ds(owners * VOWN, EXTRA), :] = extra.astype(out.dtype)
+def quarter_kernel(mine, got, keep, *sends):
+    own = lax.div(own_z(), 2)
+    extra = loss_rows(mine, got, NZ // 2)
+    for out, owner in zip((keep, *sends), (own, own ^ 1, own ^ 2, own ^ 3), strict=True):
+        at = pl.ds(pl.multiple_of(owner * VOWN, VOWN), VOWN)
+        out[pl.ds(0, VOWN), :] = (mine[at, :] + got[at, :].astype(F32)).astype(out.dtype)
+        out[pl.ds(VOWN, EXTRA), :] = extra.astype(out.dtype)
 
 
 def token_grads(total, scr, raw, out, tokens):
@@ -430,12 +429,17 @@
         out[c] = factor * d - factor * x * (inner / (WIDTH * mean_sq))
 
 
-def video_grad_kernel(clips, mine, got, c_row, diag, video, out, loss, scr):
+def video_grad_kernel(clips, mine, got1, got2, got3, c_row, diag, video, out, loss, scr):
     at = pl.ds(0, VOWN)
-    total = mine[at, :] + got[at, :].astype(F32)
+    total = mine[at, :]
+    for got in (got1, got2, got3):
+        total = total + got[at, :].astype(F32)
     token_grads(total + diag[...], scr, video, out, FRAMES)
     row_part = c_row[:, TEXTS_DEV : TEXTS_DEV + 1]
-    loss[...] = (unpiece(loss_rows(mine, got, 1)) + row_part) * (0.5 / clips)
+    tail = pl.ds(VOWN, EXTRA)
+    near = unpiece(mine[tail, :]) + unpiece(got1[tail, :].astype(F32))
+    far = unpiece(got2[tail, :].astype(F32)) + unpiece(got3[tail, :].astype(F32))
+    loss[...] = (near + far + row_part) * (0.5 / clips)
 
 
 def gloss_grad_kernel(got, diag, gloss, out, scr):
@@ -492,9 +496,7 @@
 
     with jax.named_scope("gather"):
         g_got = exchanged(g_own, XY_GROUPS)
-        v_got = v_own
-        for mask in (4, 2, 1):
-            v_got = gathered(v_got, z_pairs(mask))
+        v_got = gathered(gathered(v_own, Z_QUADS), Z_PAIRS)
         v_got = gathered(v_got, CORE_GROUPS)
 
     def first(rows):
@@ -602,21 +604,8 @@
             cost_estimate=cost(2 * VROWS * GROWS * WIDTH, 1e7),
         )(c_got, r_row, *in_hbm(weights, g_all), av)
 
-    def kept_and_sent(owners):
-        rows = owners * VOWN + EXTRA
-        return (shape(rows, WIDTH), shape(rows, WIDTH, dtype=BF16))
-
-    with jax.named_scope("clips_by_core"):
-        mine, sent = pl.pallas_call(
-            clip_rows_kernel,
-            in_specs=[vmem] * 2,
-            out_shape=kept_and_sent(NZ // 2),
-            scratch_shapes=[two_halves(NZ * VOWN)],
-            compiler_params=params(),
-            cost_estimate=cost(1e6, 2e6),
-        )(mine, to_core(twin))
     with jax.named_scope("gloss_send"):
-        sent, c_ready = lax.optimization_barrier((sent, c_got))
+        twin, c_ready = lax.optimization_barrier((twin, c_got))
         dg_send, c_row = pl.pallas_call(
             gloss_send_kernel,
             grid=(QUADS,),
@@ -629,25 +618,37 @@
         )(c_ready, *in_hbm(by_clip))
         dg_got = exchanged(dg_send, XY_GROUPS)
 
-    for which, scope in ((1, "clips_by_z1"), (2, "clips_by_z2")):
-        with jax.named_scope(scope):
-            mine, sent = pl.pallas_call(
-                functools.partial(halve_kernel, which),
-                in_specs=[vmem] * 2,
-                out_shape=kept_and_sent(NZ // 2 ** (which + 1)),
-                compiler_params=params(),
-                cost_estimate=cost(1e6, 1e6),
-            )(mine, to_z(sent, 2 ** (which - 1)))
+    def kept_and_sent(owners):
+        rows = owners * VOWN + EXTRA
+        return (shape(rows, WIDTH), shape(rows, WIDTH, dtype=BF16))
+
+    with jax.named_scope("clips_by_core"):
+        mine, sent = pl.pallas_call(
+            clip_rows_kernel,
+            in_specs=[vmem] * 2,
+            out_shape=kept_and_sent(NZ // 2),
+            scratch_shapes=[two_halves(NZ * VOWN)],
+            compiler_params=params(),
+            cost_estimate=cost(1e6, 2e6),
+        )(mine, to_core(twin))
+    with jax.named_scope("clips_by_z"):
+        mine, *sent = pl.pallas_call(
+            quarter_kernel,
+            in_specs=[vmem] * 2,
+            out_shape=kept_and_sent(1) + kept_and_sent(1)[1:] * 2,
+            compiler_params=params(),
+            cost_estimate=cost(1e6, 1e6),
+        )(mine, to_z(sent, 1))
 
     with jax.named_scope("video_grad"):
         grad_video, loss = pl.pallas_call(
             functools.partial(video_grad_kernel, clips),
-            in_specs=[vmem] * 5,
+            in_specs=[vmem] * 7,
             out_shape=(shape(OWN, FRAMES, WIDTH), shape(1, 1)),
             scratch_shapes=[two_halves(VOWN)],
             compiler_params=params(),
             cost_estimate=cost(1e6, 1e6),
-        )(mine, to_z(sent, NZ // 2), c_row, dv_diag, video)
+        )(mine, *[to_z(a, 2 * m) for m, a in enumerate(sent, start=1)], c_row, dv_diag, video)
     with jax.named_scope("gloss_grad"):
         grad_gloss = pl.pallas_call(
             gloss_grad_kernel,

time: 141 us -> 139 us (0.986)
  starting transfers between devices: 55.9 us -> 53.4 us
    all_to_all x4, starting transfers between devices: 38.2 us -> 35.4 us  [exchanged(): lax.all_to_all(a, over_all, 0, 0, axis_index_groups=groups, tiled=True)]
    all_gather x4 -> x3, blocking collectives: 27.3 us -> 28.2 us  [gathered(): lax.all_gather(a, over_all, axis=0, axis_index_groups=groups, tiled=True)]
    ppermute x3 -> x4, waiting for transfers between devices: 11.7 us -> 11.3 us  [to_z(): lax.ppermute(a, 'outer', [(i, i ^ mask) for i in range(lax.axis_size('out...]
    ppermute x3 -> x4, starting transfers between devices: 15.7 us -> 16 us  [to_z(): lax.ppermute(a, 'outer', [(i, i ^ mask) for i in range(lax.axis_size('out...]
  transfers between devices with their start and end apart: 8 -> 9, of which waited for: 4 -> 4; matrix products, arithmetic and copies ran while one was open for 0% -> 0% of each run, Pallas kernels for 15% -> 16%
where the time goes in v6:
time: 139 us; the launch traced here: 138 us
  starting transfers between devices  53.4 us (38%)
  Pallas kernels  42.7 us (31%)
  blocking collectives  28.2 us (20%)
  waiting for transfers between devices  13 us (9%)
    all_to_all x4, starting transfers between devices, exchanged(): lax.all_to_all(a, over_all, 0, 0, axis_index_groups=groups, tiled=True)  35.4 us
    all_gather x3, blocking collectives, gathered(): lax.all_gather(a, over_all, axis=0, axis_index_groups=groups, tiled=True)  28.2 us
    ppermute x4, starting transfers between devices, to_z(): lax.ppermute(a, 'outer', [(i, i ^ mask) for i in range(lax.axis_size('out...  16 us
    ppermute x4, waiting for transfers between devices, to_z(): lax.ppermute(a, 'outer', [(i, i ^ mask) for i in range(lax.axis_size('out...  11.3 us
    pallas_call x1, Pallas kernels, on_device(): pl.pallas_call(by_clip_kernel, grid=(QUADS,), in_specs=[whole(1, LANES),...  9.45 us
    pallas_call x1, Pallas kernels, on_device(): pl.pallas_call(weights_kernel, grid=(PAIRS,), in_specs=[whole(VROWS, WIDT...  8.95 us
    pallas_call x1, Pallas kernels, on_device(): pl.pallas_call(forward_kernel, in_specs=[vmem] * 3, out_specs=[pl.BlockSp...  7.92 us
    pallas_call x1, Pallas kernels, on_device(): pl.pallas_call(clip_send_kernel, grid=(QUADS,), in_specs=[whole(NXY, 1, L...  5.63 us
  transfers between devices with their start and end apart: 9, of which 4 were waited for; matrix products, arithmetic and copies ran while one was open for 0% of the time, Pallas kernels for 16%

profile of v6, /device:TPU:2, one launch (start us, length us, event | category | flops | bytes accessed | tf_op | source)
XLA Modules:
  0.0 138.0 jit_solution(7670686128011512397)
XLA Ops:
  0.6 1.9 %unit_tokens.1 = (bf16[96,256]{1,0:T(8,128)(2,1)S(1)}, bf16[32,48,256]{2,1,0:T(8,128)(2,1)}, s32[8,128]{1,0:T(8,128)S(1)}) custom-call(s32[3]{0:T(128)} %fc_in.1, s32[3]{0:T(128)} %gc_in.1, bf16[3,32,256]{2,1,0:T(8,128)(2,1)} %video.1, bf16[3,16,256]{2,1,0:T(8,128)(2,1)} %gloss.1), custom_call_target="tpu_custom_call" | custom-call | flops 200000 | bytes 700000 | tf_op jit(solution)/shard_map/unit_tokens/pallas_call | solution.py:476
  2.5 10.3 %all-to-all-start = ((bf16[32,48,256]{2,1,0:T(8,128)(2,1)}), bf16[32,48,256]{2,1,0:T(8,128)(2,1)S(1)}, u32[]{:S(2)}, u32[]{:S(2)}) async-start(bf16[32,48,256]{2,1,0:T(8,128)(2,1)} %get-tuple-element.35.g_ref), calls=%async_computation | async-start | bytes 1572864 | tf_op jit(solution)/shard_map/gather/all_to_all | solution.py:467
  12.8 1.3 diagonal.1
  14.1 19.5 %all_gather.9 = bf16[384,256]{1,0:T(8,128)(2,1)S(1)} all-gather(bf16[96,256]{1,0:T(8,128)(2,1)S(1)} %get-tuple-element.34.v_ref), channel_id=1, replica_groups={{0,64,128,192},{32,96,160,224},{1,65,129,193},{33,97,161,225},{2,66,130..., dimensions={0}, use_global_device_ids=true | all-gather | bytes 245760 | tf_op jit(solution)/shard_map/gather/all_gather | solution.py:470
  33.6 6.3 %all_gather.10 = bf16[768,256]{1,0:T(8,128)(2,1)S(1)} all-gather(bf16[384,256]{1,0:T(8,128)(2,1)S(1)} %all_gather.9), channel_id=1, replica_groups={{0,32},{64,96},{128,160},{192,224},{1,33},{65,97},{129,161},{193,225},{..., dimensions={0}, use_global_device_ids=true | all-gather | bytes 589824 | tf_op jit(solution)/shard_map/gather/all_gather | solution.py:470
  39.9 2.4 %all_gather.11.v_got = bf16[1536,256]{1,0:T(8,128)(2,1)S(1)} all-gather(bf16[768,256]{1,0:T(8,128)(2,1)S(1)} %all_gather.10), channel_id=1, replica_groups={{0,1},{32,33},{64,65},{96,97},{128,129},{160,161},{192,193},{224,225},{..., dimensions={0}, use_global_device_ids=true | all-gather | bytes 1179648 | tf_op jit(solution)/shard_map/gather/all_gather | solution.py:470
  42.3 0.0 all-to-all-done.g_got
  42.3 7.9 %forward.1 = (bf16[1536,256]{1,0:T(8,128)(2,1)}, bf16[2048,256]{1,0:T(8,128)(2,1)}, f32[1536,128]{1,0:T(8,128)}, f32[16,48,128]{2,1,0:T(8,128)}, f32[48,128]{1,0...) custom-call(bf16[1536,256]{1,0:T(8,128)(2,1)S(1)} %all_gather.11.v_got, ...), custom_call_target="tpu_custom_call" | custom-call | flops 1610612736 | bytes 8000000 | tf_op jit(solution)/shard_map/forward/pallas_call | solution.py:520
  50.2 5.5 %all-to-all-start.1 = ((f32[16,1,128]{2,1,0:T(1,128)}), f32[16,1,128]{2,1,0:T(1,128)S(1)}, u32[]{:S(2)}, u32[]{:S(2)}) async-start(f32[16,1,128]{2,1,0:T(1,128)} %get-tuple-element.38), calls=%async_computation.1 | async-start | bytes 16384 | tf_op jit(solution)/shard_map/row_sums/all_to_all | solution.py:467
  55.7 8.9 %weights.1.p_ref = bf16[4,1536,512]{2,1,0:T(8,128)(2,1)} custom-call(bf16[1536,256]{1,0:T(8,128)(2,1)} %get-tuple-element.42.v_ref, bf16[2048,256]{1,0:T(8,128)(2,1)} %get-tuple-element.43.g_ref, f32[1536,128]{1,0:T(8,128)} %get-tuple-element.44.row_ref, f32[16,48,128]{2,1,0:T(8,128)} %get-tuple-element.45.col_ref, f32[48,128]{1,0:T(8,128)S(1)} %get-tuple-element.46.e_ref), custom_call_target="tpu_custom_call" | custom-call | flops 1610612736 | bytes 12000000 | tf_op jit(solution)/shard_map/weights/pallas_call | solution.py:566
  64.7 0.0 all-to-all-done.1.r_got
  64.7 0.7 row_sums.1
  65.4 9.9 %all-to-all-start.2 = ((f32[32,1,128]{2,1,0:T(1,128)}), f32[32,1,128]{2,1,0:T(1,128)S(1)}, u32[]{:S(2)}, u32[]{:S(2)}) async-start(f32[32,1,128]{2,1,0:T(1,128)} %get-tuple-element.40), calls=%async_computation.2 | async-start | bytes 32768 | tf_op jit(solution)/shard_map/column_sums/all_to_all | solution.py:467
  75.3 9.5 %by_clip.1 = (f32[2048,512]{1,0:T(8,128)}, f32[1536,256]{1,0:T(8,128)S(1)}) custom-call(f32[1,128]{1,0:T(1,128)S(1)} %get-tuple-element.41.r_ref, bf16[4,1536,512]{2,1,0:T(8,128)(2,1)} %weights.1.p_ref, bf16[1536,256]{1,0:T(8,128)(2,1)} %get-tuple-element.42.v_ref, bf16[2048,256]{1,0:T(8,128)(2,1)} %get-tuple-element.43.g_ref), custom_call_target="tpu_custom_call" | custom-call | flops 4831838208 | bytes 14000000 | tf_op jit(solution)/shard_map/by_clip/pallas_call | solution.py:583
  84.7 5.6 %clip_send.1 = (f32[784,256]{1,0:T(8,128)S(1)}, bf16[784,256]{1,0:T(8,128)(2,1)S(1)}) custom-call(f32[32,1,128]{2,1,0:T(1,128)S(1)} %all-to-all-done.2.c_got, f32[1,128]{1,0:T(1,128)S(1)} %get-tuple-element.41.r_ref, bf16[4,1536,512]{2,1,0:T(8,128)(2,1)} %weights.1.p_ref, bf16[2048,256]{1,0:T(8,128)(2,1)} %get-tuple-element.43.g_ref, ...), custom_call_target="tpu_custom_call" | custom-call | flops 1610612736 | bytes 10000000 | tf_op jit(solution)/shard_map/clip_send/pallas_call | solution.py:596
  90.4 0.0 copy-start
  90.4 0.0 copy-start.1
  90.4 4.3 %gloss_send.1 = (bf16[32,48,256]{2,1,0:T(8,128)(2,1)}, f32[1,128]{1,0:T(1,128)S(1)}) custom-call(f32[32,1,128]{2,1,0:T(1,128)S(1)} %all-to-all-done.2.c_got, f32[2048,512]{1,0:T(8,128)} %get-tuple-element.58.by_clip), custom_call_target="tpu_custom_call" | custom-call | flops 2000000 | bytes 5000000 | tf_op jit(solution)/shard_map/gloss_send/pallas_call | solution.py:609
  94.7 9.8 %all-to-all-start.3 = ((bf16[32,48,256]{2,1,0:T(8,128)(2,1)}), bf16[32,48,256]{2,1,0:T(8,128)(2,1)S(1)}, u32[]{:S(2)}, u32[]{:S(2)}) async-start(bf16[32,48,256]{2,1,0:T(8,128)(2,1)} %get-tuple-element.63), calls=%async_computation.3 | async-start | bytes 1572864 | tf_op jit(solution)/shard_map/gloss_send/all_to_all | solution.py:467
  104.5 1.9 %collective-permute-start = (bf16[784,256]{1,0:T(8,128)(2,1)S(1)}, bf16[784,256]{1,0:T(8,128)(2,1)S(1)}, u32[]{:S(2)}, u32[]{:S(2)}) collective-permute-start(bf16[784,256]{1,0:T(8,128)(2,1)S(1)} %get-tuple-element.50), channel_id=1, source_target_pairs={{0,1},{1,0},{2,3},{3,2},{4,5},{5,4},{6,7},{7,6},{8,9},{9,8},{10,11... | collective-permute-start | bytes 1204232 | tf_op jit(solution)/shard_map/clips_by_core/ppermute | solution.py:461
  106.4 1.7 %collective-permute-done.got = bf16[784,256]{1,0:T(8,128)(2,1)S(1)} collective-permute-done((bf16[784,256]{1,0:T(8,128)(2,1)S(1)}, bf16[784,256]{1,0:T(8,128)(2,1)S(1)}, u32[]{:S(2)}, u32[]{:S(2)}) %collective-permute-start) | collective-permute-done | bytes 401440 | tf_op jit(solution)/shard_map/clips_by_core/ppermute | solution.py:461
  108.1 0.8 clips_by_core.1
  108.9 3.8 %collective-permute-start.1 = (bf16[400,256]{1,0:T(8,128)(2,1)S(1)}, bf16[400,256]{1,0:T(8,128)(2,1)S(1)}, u32[]{:S(2)}, u32[]{:S(2)}) collective-permute-start(bf16[400,256]{1,0:T(8,128)(2,1)S(1)} %get-tuple-element.52), channel_id=1, source_target_pairs={{0,32},{32,0},{64,96},{96,64},{128,160},{160,128},{192,224},{224,1... | collective-permute-start | bytes 614408 | tf_op jit(solution)/shard_map/clips_by_z/ppermute | solution.py:464
  112.7 5.4 %collective-permute-done.1.got = bf16[400,256]{1,0:T(8,128)(2,1)S(1)} collective-permute-done((bf16[400,256]{1,0:T(8,128)(2,1)S(1)}, bf16[400,256]{1,0:T(8,128)(2,1)S(1)}, u32[]{:S(2)}, u32[]{:S(2)}) %collective-permute-start.1) | collective-permute-done | bytes 204832 | tf_op jit(solution)/shard_map/clips_by_z/ppermute | solution.py:464
  118.1 0.1 clips_by_z.1
  118.2 4.6 %collective-permute-start.2 = (bf16[112,256]{1,0:T(8,128)(2,1)S(1)}, bf16[112,256]{1,0:T(8,128)(2,1)S(1)}, u32[]{:S(2)}, u32[]{:S(2)}) collective-permute-start(bf16[112,256]{1,0:T(8,128)(2,1)S(1)} %get-tuple-element.54), channel_id=1, source_target_pairs={{0,64},{32,96},{64,0},{96,32},{128,192},{160,224},{192,128},{224,1... | collective-permute-start | bytes 172040 | tf_op jit(solution)/shard_map/video_grad/ppermute | solution.py:464
  122.8 5.5 %collective-permute-start.3 = (bf16[112,256]{1,0:T(8,128)(2,1)S(1)}, bf16[112,256]{1,0:T(8,128)(2,1)S(1)}, u32[]{:S(2)}, u32[]{:S(2)}) collective-permute-start(bf16[112,256]{1,0:T(8,128)(2,1)S(1)} %get-tuple-element.55), channel_id=1, source_target_pairs={{0,128},{32,160},{64,192},{96,224},{128,0},{160,32},{192,64},{224,... | collective-permute-start | bytes 172040 | tf_op jit(solution)/shard_map/video_grad/ppermute | solution.py:464
  128.2 2.2 %collective-permute-start.4 = (bf16[112,256]{1,0:T(8,128)(2,1)S(1)}, bf16[112,256]{1,0:T(8,128)(2,1)S(1)}, u32[]{:S(2)}, u32[]{:S(2)}) collective-permute-start(bf16[112,256]{1,0:T(8,128)(2,1)S(1)} %get-tuple-element.56), channel_id=1, source_target_pairs={{0,192},{32,224},{64,128},{96,160},{128,64},{160,96},{192,0},{224,... | collective-permute-start | bytes 172040 | tf_op jit(solution)/shard_map/video_grad/ppermute | solution.py:464
  130.5 2.3 %collective-permute-done.3.got2 = bf16[112,256]{1,0:T(8,128)(2,1)S(1)} collective-permute-done((bf16[112,256]{1,0:T(8,128)(2,1)S(1)}, bf16[112,256]{1,0:T(8,128)(2,1)S(1)}, u32[]{:S(2)}, u32[]{:S(2)}) %collective-permute-start.3) | collective-permute-done | bytes 57376 | tf_op jit(solution)/shard_map/video_grad/ppermute | solution.py:464
  132.8 3.7 %collective-permute-done.4.got3 = bf16[112,256]{1,0:T(8,128)(2,1)S(1)} collective-permute-done((bf16[112,256]{1,0:T(8,128)(2,1)S(1)}, bf16[112,256]{1,0:T(8,128)(2,1)S(1)}, u32[]{:S(2)}, u32[]{:S(2)}) %collective-permute-start.4) | collective-permute-done | bytes 57376 | tf_op jit(solution)/shard_map/video_grad/ppermute | solution.py:464
  136.4 0.8 video_grad.1
  137.2 0.8 gloss_grad.1
  (5 shorter events, 0.0 us)
Async XLA Ops:
  2.5 39.8 %all-to-all-start = ((bf16[32,48,256]{2,1,0:T(8,128)(2,1)}), bf16[32,48,256]{2,1,0:T(8,128)(2,1)S(1)}, u32[]{:S(2)}, u32[]{:S(2)}) async-start(bf16[32,48,256]{2,1,0:T(8,128)(2,1)} %get-tuple-element.35.g_ref), calls=%async_computation | async-start | bytes 1572864 | tf_op jit(solution)/shard_map/gather/all_to_all | solution.py:467
  50.2 14.5 %all-to-all-start.1 = ((f32[16,1,128]{2,1,0:T(1,128)}), f32[16,1,128]{2,1,0:T(1,128)S(1)}, u32[]{:S(2)}, u32[]{:S(2)}) async-start(f32[16,1,128]{2,1,0:T(1,128)} %get-tuple-element.38), calls=%async_computation.1 | async-start | bytes 16384 | tf_op jit(solution)/shard_map/row_sums/all_to_all | solution.py:467
  65.4 19.3 %all-to-all-start.2 = ((f32[32,1,128]{2,1,0:T(1,128)}), f32[32,1,128]{2,1,0:T(1,128)S(1)}, u32[]{:S(2)}, u32[]{:S(2)}) async-start(f32[32,1,128]{2,1,0:T(1,128)} %get-tuple-element.40), calls=%async_computation.2 | async-start | bytes 32768 | tf_op jit(solution)/shard_map/column_sums/all_to_all | solution.py:467
  90.4 46.1 %copy-start = (bf16[3,32,256]{2,1,0:T(8,128)(2,1)S(1)}, bf16[3,32,256]{2,1,0:T(8,128)(2,1)}, u32[]{:S(2)}) copy-start(bf16[3,32,256]{2,1,0:T(8,128)(2,1)} %video.1) | copy-start | bytes 147460
  90.4 46.8 %copy-start.1 = (bf16[3,16,256]{2,1,0:T(8,128)(2,1)S(1)}, bf16[3,16,256]{2,1,0:T(8,128)(2,1)}, u32[]{:S(2)}) copy-start(bf16[3,16,256]{2,1,0:T(8,128)(2,1)} %gloss.1) | copy-start | bytes 73732
  94.7 42.5 %all-to-all-start.3 = ((bf16[32,48,256]{2,1,0:T(8,128)(2,1)}), bf16[32,48,256]{2,1,0:T(8,128)(2,1)S(1)}, u32[]{:S(2)}, u32[]{:S(2)}) async-start(bf16[32,48,256]{2,1,0:T(8,128)(2,1)} %get-tuple-element.63), calls=%async_computation.3 | async-start | bytes 1572864 | tf_op jit(solution)/shard_map/gloss_send/all_to_all | solution.py:467
  104.5 3.6 %collective-permute-start = (bf16[784,256]{1,0:T(8,128)(2,1)S(1)}, bf16[784,256]{1,0:T(8,128)(2,1)S(1)}, u32[]{:S(2)}, u32[]{:S(2)}) collective-permute-start(bf16[784,256]{1,0:T(8,128)(2,1)S(1)} %get-tuple-element.50), channel_id=1, source_target_pairs={{0,1},{1,0},{2,3},{3,2},{4,5},{5,4},{6,7},{7,6},{8,9},{9,8},{10,11... | collective-permute-start | bytes 1204232 | tf_op jit(solution)/shard_map/clips_by_core/ppermute | solution.py:461
  108.9 9.2 %collective-permute-start.1 = (bf16[400,256]{1,0:T(8,128)(2,1)S(1)}, bf16[400,256]{1,0:T(8,128)(2,1)S(1)}, u32[]{:S(2)}, u32[]{:S(2)}) collective-permute-start(bf16[400,256]{1,0:T(8,128)(2,1)S(1)} %get-tuple-element.52), channel_id=1, source_target_pairs={{0,32},{32,0},{64,96},{96,64},{128,160},{160,128},{192,224},{224,1... | collective-permute-start | bytes 614408 | tf_op jit(solution)/shard_map/clips_by_z/ppermute | solution.py:464
  118.2 12.2 %collective-permute-start.2 = (bf16[112,256]{1,0:T(8,128)(2,1)S(1)}, bf16[112,256]{1,0:T(8,128)(2,1)S(1)}, u32[]{:S(2)}, u32[]{:S(2)}) collective-permute-start(bf16[112,256]{1,0:T(8,128)(2,1)S(1)} %get-tuple-element.54), channel_id=1, source_target_pairs={{0,64},{32,96},{64,0},{96,32},{128,192},{160,224},{192,128},{224,1... | collective-permute-start | bytes 172040 | tf_op jit(solution)/shard_map/video_grad/ppermute | solution.py:464
  122.8 10.0 %collective-permute-start.3 = (bf16[112,256]{1,0:T(8,128)(2,1)S(1)}, bf16[112,256]{1,0:T(8,128)(2,1)S(1)}, u32[]{:S(2)}, u32[]{:S(2)}) collective-permute-start(bf16[112,256]{1,0:T(8,128)(2,1)S(1)} %get-tuple-element.55), channel_id=1, source_target_pairs={{0,128},{32,160},{64,192},{96,224},{128,0},{160,32},{192,64},{224,... | collective-permute-start | bytes 172040 | tf_op jit(solution)/shard_map/video_grad/ppermute | solution.py:464
  128.2 8.2 %collective-permute-start.4 = (bf16[112,256]{1,0:T(8,128)(2,1)S(1)}, bf16[112,256]{1,0:T(8,128)(2,1)S(1)}, u32[]{:S(2)}, u32[]{:S(2)}) collective-permute-start(bf16[112,256]{1,0:T(8,128)(2,1)S(1)} %get-tuple-element.56), channel_id=1, source_target_pairs={{0,192},{32,224},{64,128},{96,160},{128,64},{160,96},{192,0},{224,... | collective-permute-start | bytes 172040 | tf_op jit(solution)/shard_map/video_grad/ppermute | solution.py:464

commit v7 on v6

--- a/solution.py
+++ b/solution.py
@@ -52,7 +52,7 @@
 ZC_GROUPS = [[flat(x, z, y, c) for c in range(NCORE) for z in range(NZ)] for x in range(NX) for y in range(NY)]
 
 
-def params(limit_mb=16):
+def params(limit_mb=20):
     return pltpu.CompilerParams(vmem_limit_bytes=limit_mb * 1024 * 1024)
 
 
@@ -108,7 +108,7 @@
     return pltpu.VMEM((2, rows, LANES), F32)
 
 
-def units_kernel(fc_in, gc_in, video_in, gloss_in, v_out, g_out, count_out, fc, gc, video, gloss, v_scr, g_scr, sems):
+def units_kernel(fc_in, gc_in, video_in, gloss_in, v_out, g_out, g_one, count_out, fc, gc, video, gloss, v_scr, g_scr, sems):
     pairs = ((fc_in, fc), (gc_in, gc), (video_in, video), (gloss_in, gloss))
     copies = [pltpu.make_async_copy(a, b, sems.at[i]) for i, (a, b) in enumerate(pairs)]
     for copy in copies:
@@ -131,17 +131,18 @@
     v = get(v_scr, pl.ds(0, VOWN)).astype(BF16)
     g = get(g_scr, pl.ds(0, GOWN)).astype(BF16)
     v_out[...] = v
+    g_one[...] = g
     for i in range(NXY):
         g_out[i] = g
 
 
-def diagonal_kernel(count_ref, v_ref, g_ref, dv, dg, logit_sum):
+def diagonal_kernel(count_ref, v_ref, g_ref, dv, dg):
     def pick(count, which):
         return jnp.where(which == 0, count[0], jnp.where(which == 1, count[1], count[2]))
 
     fc = [count_ref[c : c + 1, 0:1] for c in range(OWN)]
     gc = [count_ref[OWN + c : OWN + c + 1, 0:1] for c in range(OWN)]
-    v, g = v_ref[...], g_ref[0]
+    v, g = v_ref[...], g_ref[...]
     shape = (VOWN, GOWN)
     r, q = iota(shape, 0), iota(shape, 1)
     rc, qc = lax.rem(r, OWN), lax.rem(q, OWN)
@@ -149,18 +150,12 @@
     e = jnp.where(valid, jnp.exp2(nt(v, g) * EXP_SCALE), 0.0)
     r1, q1 = iota((VOWN, 1), 0), iota((1, GOWN), 1)
     rc1, qc1 = lax.rem(r1, OWN), lax.rem(q1, OWN)
-    frames_r, glosses_r = pick(fc, rc1), pick(gc, rc1)
-    frames_q, glosses_q = pick(fc, qc1), pick(gc, qc1)
+    frames_r, glosses_q = pick(fc, rc1), pick(gc, qc1)
     row_ok = lax.div(r1, OWN) < frames_r
     col_ok = lax.div(q1, OWN) < glosses_q
-    frames_r, glosses_r = frames_r.astype(F32), glosses_r.astype(F32)
-    frames_q, glosses_q = frames_q.astype(F32), glosses_q.astype(F32)
+    frames_r, glosses_q = frames_r.astype(F32), glosses_q.astype(F32)
     rows = jnp.where(row_ok, jnp.sum(e, axis=1, keepdims=True), 1.0)
     cols = jnp.where(col_ok, jnp.sum(e, axis=0, keepdims=True), 1.0)
-    by_row = jnp.where(row_ok, jnp.log(rows / glosses_r) / frames_r, 0.0)
-    by_col = jnp.where(col_ok, jnp.log(cols / frames_q) / glosses_q, 0.0)
-    total = jnp.sum(by_row, axis=0, keepdims=True) + jnp.sum(by_col, axis=1, keepdims=True)
-    logit_sum[...] = jnp.broadcast_to(0.5 * total, (1, LANES))
     weight = -5.0 * e * (1.0 / (rows * frames_r) + 1.0 / (cols * glosses_q))
     dv[...] = nn(weight, g.astype(F32), precision=lax.Precision.HIGHEST)
     dg[...] = tn(weight, v.astype(F32), precision=lax.Precision.HIGHEST)
@@ -171,11 +166,11 @@
 
 
 def forward_kernel(
-    v_got, g_got, diag,
-    v_hbm, g_hbm, row_hbm, col_hbm, e_out, r_out, c_out,
-    v_out, g_out, row_out, col_out, v_scr, g_scr, frame_mask, gloss_mask, rows, cols, sems,
+    v_got, g_got,
+    v_hbm, g_hbm, row_out, col_out, e_out, r_out, c_out,
+    v_out, g_out, v_scr, g_scr, frame_mask, gloss_mask, rows, cols, sems,
 ):
-    results = ((v_out, v_hbm), (g_out, g_hbm), (row_out, row_hbm), (col_out, col_hbm))
+    results = ((v_out, v_hbm), (g_out, g_hbm))
     copies = [pltpu.make_async_copy(a, b, sems.at[i]) for i, (a, b) in enumerate(results)]
     put(v_scr, pl.ds(0, VROWS), v_got[...].astype(F32))
     for f in range(FRAMES):
@@ -224,7 +219,7 @@
         cols[2 * p + 1] = col1
         return 0
 
-    lax.fori_loop(0, PAIRS, two_glosses, 0)
+    lax.fori_loop(0, PAIRS, two_glosses, 0, unroll=2)
 
     lane = iota((CLIPS_DEV, LANES), 1)
     real = lane < TEXTS_DEV
@@ -235,14 +230,12 @@
         total = jnp.where(real, rows[at, :], 1.0)
         video_part = video_part + mask * jnp.log(total / glosses)
         row_out[at, :] = jnp.where(mask > 0.0, 1.0 / (total * frames), FAR)
-    copies[2].start()
     gloss_part = jnp.zeros((CLIPS_DEV, LANES), F32)
     for g in range(GLOSSES):
         mask = gloss_mask[g][0:1]
         total = cols[g]
         gloss_part = gloss_part + mask * jnp.log(total / frames)
         col_out[g] = jnp.where(mask > 0.0, 1.0 / (total * glosses), FAR)
-    copies[3].start()
     logits = 0.5 * (video_part / frames + gloss_part / glosses)
     e_pair = jnp.where(real, jnp.exp(logits), 0.0)
     e_out[...] = e_pair
@@ -250,7 +243,16 @@
     sums = jnp.sum(e_pair, axis=1, keepdims=True)
     across = lane == iota((CLIPS_DEV, LANES), 0)
     r_row = jnp.sum(jnp.where(across, jnp.broadcast_to(sums, (CLIPS_DEV, LANES)), 0.0), axis=0, keepdims=True)
-    r_row = jnp.where(iota((1, LANES), 1) == CLIPS_DEV, diag[...], r_row)
+    inner, outer = lax.axis_index("inner"), lax.axis_index("outer")
+    z, core = lax.rem(outer, NZ), lax.rem(inner, NCORE)
+    x, y = 2 * lax.div(inner, 16) + lax.div(outer, NZ), lax.rem(lax.div(inner, NCORE), NY)
+    clip0 = core * OWN * NZ + lax.rem(z, 2) * (NZ // 2) + lax.div(z, 2)
+    text0 = x * OWN * NY + y
+    own = jnp.zeros((CLIPS_DEV, LANES), jnp.bool_)
+    for c in range(OWN):
+        own = own | ((iota((CLIPS_DEV, LANES), 0) == clip0 + c * NZ) & (lane == text0 + c * NY))
+    diag = jnp.sum(jnp.where(own, logits, 0.0), keepdims=True).reshape(1, 1)
+    r_row = jnp.where(iota((1, LANES), 1) == CLIPS_DEV, diag, r_row)
     for i in range(NZC):
         r_out[i] = r_row
     c_out[...] = jnp.sum(e_pair, axis=0, keepdims=True)
@@ -307,7 +309,7 @@
             both[at, :WIDTH] = v
             both[at, WIDTH:] = (v.astype(F32) * inverse).astype(BF16)
 
-    out[...] = tn(p_ref[0], both[...])
+    out[...] = tn(p_ref[0], both[...]).reshape(GLOSSES // QUADS, LANES, 2 * WIDTH)
     part = nn(p_ref[0], g_ref[...])
 
     @pl.when(step == 0)
@@ -319,67 +321,68 @@
         av_out[...] = av_out[...] + part
 
 
-def gloss_send_kernel(c_got, by_clip, out, c_out, scr):
-    step = pl.program_id(0)
-
-    @pl.when(step == 0)
-    def _():
-        c_out[...] = added(c_got)
-
-    col = inverse_texts(c_out[...])
-    for k in range(GLOSSES // QUADS):
-        at = pl.ds(k * LANES, LANES)
-        block = by_clip[at, :WIDTH] * col + by_clip[at, WIDTH:]
-        row = (step * (GLOSSES // QUADS) + k) * OWN
-        for x in range(NX):
-            for c in range(OWN):
-                first = (x * OWN + c) * NY
-                put(scr, pl.ds(x * NY * GOWN + row + c, NY, stride=GOWN), block[first : first + NY])
-
-    @pl.when(step == QUADS - 1)
-    def _():
-        out[...] = get(scr, pl.ds(0, NXY * GOWN)).astype(BF16).reshape(NXY, GOWN, WIDTH)
-
-
-def clip_send_kernel(c_got, r_ref, p_ref, g_ref, av_ref, mine, twin, c_row, total):
-    step = pl.program_id(0)
-
-    @pl.when(step == 0)
-    def _():
-        c_row[...] = added(c_got)
-
-    col = inverse_texts(c_row[...])
-    scaled = g_ref[...].astype(F32) * jnp.concatenate([col] * (GLOSSES // QUADS), axis=0)
-    part = nn(p_ref[0], scaled.astype(BF16))
-
-    @pl.when(step == 0)
-    def _():
-        total[...] = part
-
-    @pl.when((step > 0) & (step < QUADS - 1))
-    def _():
-        total[...] = total[...] + part
-
-    @pl.when(step == QUADS - 1)
-    def _():
-        core = lax.rem(lax.axis_index("inner"), NCORE)
-        inverse = jnp.broadcast_to(1.0 / column_of(r_ref[...], CLIPS_DEV), (CLIPS_DEV, WIDTH))
-        half = CLIPS_DEV // 2
-        for pair in range(FRAMES // 2):
-            others = []
-            for f in (2 * pair, 2 * pair + 1):
-                at = pl.ds(f * CLIPS_DEV, CLIPS_DEV)
-                new = part[f * CLIPS_DEV : (f + 1) * CLIPS_DEV]
-                block = av_ref[at, :] * inverse + (total[at, :] + new)
-                low, high = block[:half], block[half:]
-                mine[pl.ds(f * half, half), :] = jnp.where(core == 0, low, high)
-                others.append(jnp.where(core == 0, high, low))
-            twin[pl.ds(pair * CLIPS_DEV, CLIPS_DEV), :] = jnp.concatenate(others, axis=0).astype(BF16)
-        real = iota((1, LANES), 1) < TEXTS_DEV
-        logs = jnp.where(real, jnp.log(jnp.where(real, c_row[...], 1.0)), 0.0)
-        extra = pieces(jnp.sum(logs, axis=1, keepdims=True))
-        mine[pl.ds(FRAMES * half, EXTRA), :] = extra
-        twin[pl.ds(FRAMES * half, EXTRA), :] = extra.astype(BF16)
+def started(copies):
+    for copy in copies:
+        copy.start()
+    return copies
+
+
+def gloss_send_kernel(c_got, by_clip, out, c_out, held, scr, sems):
+    many = GLOSSES // QUADS
+    copies = started(
+        [
+            pltpu.make_async_copy(by_clip.at[pl.ds(q * many, many), pl.ds(0, TEXTS_DEV)], held.at[q], sems.at[q])
+            for q in range(QUADS)
+        ]
+    )
+    c_out[...] = added(c_got)
+    col = inverse_texts(c_out[...])[:TEXTS_DEV]
+    for q, copy in enumerate(copies):
+        copy.wait()
+        for k in range(many):
+            block = held[q, k, :, :WIDTH] * col + held[q, k, :, WIDTH:]
+            row = (q * many + k) * OWN
+            for x in range(NX):
+                for c in range(OWN):
+                    first = (x * OWN + c) * NY
+                    put(scr, pl.ds(x * NY * GOWN + row + c, NY, stride=GOWN), block[first : first + NY])
+    out[...] = get(scr, pl.ds(0, NXY * GOWN)).astype(BF16).reshape(NXY, GOWN, WIDTH)
+
+
+def clip_send_kernel(c_got, r_ref, p_hbm, g_hbm, av_ref, mine, twin, held, g_held, total, sems):
+    g_copy = pltpu.make_async_copy(g_hbm, g_held, sems.at[QUADS])
+    copies = [pltpu.make_async_copy(p_hbm.at[q], held.at[q], sems.at[q]) for q in range(QUADS)]
+    started([g_copy, *copies])
+    c_row = added(c_got)
+    col = inverse_texts(c_row)
+    cols = jnp.concatenate([col] * (GLOSSES // QUADS), axis=0)
+    core = lax.rem(lax.axis_index("inner"), NCORE)
+    inverse = jnp.broadcast_to(1.0 / column_of(r_ref[...], CLIPS_DEV), (CLIPS_DEV, WIDTH))
+    half = CLIPS_DEV // 2
+    g_copy.wait()
+    for q, copy in enumerate(copies):
+        scaled = (g_held[pl.ds(q * 4 * LANES, 4 * LANES), :].astype(F32) * cols).astype(BF16)
+        copy.wait()
+        part = nn(held[q], scaled)
+        if q == 0:
+            total[...] = part
+        elif q < QUADS - 1:
+            total[...] = total[...] + part
+    for pair in range(FRAMES // 2):
+        others = []
+        for f in (2 * pair, 2 * pair + 1):
+            at = pl.ds(f * CLIPS_DEV, CLIPS_DEV)
+            new = part[f * CLIPS_DEV : (f + 1) * CLIPS_DEV]
+            block = av_ref[at, :] * inverse + (total[at, :] + new)
+            low, high = block[:half], block[half:]
+            mine[pl.ds(f * half, half), :] = jnp.where(core == 0, low, high)
+            others.append(jnp.where(core == 0, high, low))
+        twin[pl.ds(pair * CLIPS_DEV, CLIPS_DEV), :] = jnp.concatenate(others, axis=0).astype(BF16)
+    real = iota((1, LANES), 1) < TEXTS_DEV
+    logs = jnp.where(real, jnp.log(jnp.where(real, c_row, 1.0)), 0.0)
+    extra = pieces(jnp.sum(logs, axis=1, keepdims=True))
+    mine[pl.ds(FRAMES * half, EXTRA), :] = extra
+    twin[pl.ds(FRAMES * half, EXTRA), :] = extra.astype(BF16)
 
 
 def own_z():
@@ -454,7 +457,7 @@
 
 
 def on_device(clips, video, gloss, frame_count, gloss_count):
-    vmem = pl.BlockSpec(memory_space=pltpu.VMEM)
+    vmem, hbm = pl.BlockSpec(memory_space=pltpu.VMEM), pl.BlockSpec(memory_space=pltpu.HBM)
     over_all = ("outer", "inner")
 
     def to_core(a):
@@ -473,12 +476,13 @@
         return [pltpu.with_memory_space_constraint(a, pltpu.HBM) for a in arrays]
 
     with jax.named_scope("unit_tokens"):
-        v_own, g_own, counts = pl.pallas_call(
+        v_own, g_send, g_own, counts = pl.pallas_call(
             units_kernel,
-            in_specs=[pl.BlockSpec(memory_space=pltpu.HBM)] * 4,
+            in_specs=[hbm] * 4,
             out_shape=(
                 shape(VOWN, WIDTH, dtype=BF16),
                 shape(NXY, GOWN, WIDTH, dtype=BF16),
+                shape(GOWN, WIDTH, dtype=BF16),
                 shape(8, LANES, dtype=jnp.int32),
             ),
             scratch_shapes=[
@@ -495,37 +499,23 @@
         )(*in_hbm(frame_count, gloss_count, video, gloss))
 
     with jax.named_scope("gather"):
-        g_got = exchanged(g_own, XY_GROUPS)
+        g_got = exchanged(g_send, XY_GROUPS)
         v_got = gathered(gathered(v_own, Z_QUADS), Z_PAIRS)
         v_got = gathered(v_got, CORE_GROUPS)
 
-    def first(rows):
-        return pl.BlockSpec((1, rows, WIDTH), lambda i: (0, 0, 0))
-
     def whole(*dims):
         return pl.BlockSpec(dims, lambda i: (0,) * len(dims))
-
-    with jax.named_scope("diagonal"):
-        dv_diag, dg_diag, logit_sum = pl.pallas_call(
-            diagonal_kernel,
-            grid=(1,),
-            in_specs=[whole(8, LANES), whole(VOWN, WIDTH), first(GOWN)],
-            out_specs=(whole(VOWN, WIDTH), whole(GOWN, WIDTH), whole(1, LANES)),
-            out_shape=(shape(VOWN, WIDTH), shape(GOWN, WIDTH), shape(1, LANES)),
-            compiler_params=params(),
-            cost_estimate=cost(2e7, 3e5),
-        )(counts, v_own, g_own)
 
     with jax.named_scope("forward"):
         v_all, g_all, row_inv, col_inv, e_pair, r_part, c_part = pl.pallas_call(
             forward_kernel,
-            in_specs=[vmem] * 3,
-            out_specs=[pl.BlockSpec(memory_space=pltpu.HBM)] * 4 + [vmem] * 3,
+            in_specs=[vmem] * 2,
+            out_specs=[hbm] * 2 + [vmem] * 5,
             out_shape=(
                 pltpu.HBM((VROWS, WIDTH), BF16),
                 pltpu.HBM((GROWS, WIDTH), BF16),
-                pltpu.HBM((VROWS, LANES), F32),
-                pltpu.HBM((GLOSSES, CLIPS_DEV, LANES), F32),
+                shape(VROWS, LANES),
+                shape(GLOSSES, CLIPS_DEV, LANES),
                 shape(CLIPS_DEV, LANES),
                 shape(NZC, 1, LANES),
                 shape(1, LANES),
@@ -533,19 +523,17 @@
             scratch_shapes=[
                 pltpu.VMEM((VROWS, WIDTH), BF16),
                 pltpu.VMEM((GROWS, WIDTH), BF16),
-                pltpu.VMEM((VROWS, LANES), F32),
-                pltpu.VMEM((GLOSSES, CLIPS_DEV, LANES), F32),
                 two_halves(VROWS),
                 two_halves(NXY * GOWN),
                 pltpu.VMEM((VROWS, LANES), F32),
                 pltpu.VMEM((GLOSSES, 8, LANES), F32),
                 pltpu.VMEM((VROWS, LANES), F32),
                 pltpu.VMEM((GLOSSES, CLIPS_DEV, LANES), F32),
-                pltpu.SemaphoreType.DMA((4,)),
+                pltpu.SemaphoreType.DMA((2,)),
             ],
             compiler_params=params(),
             cost_estimate=cost(2 * VROWS * GROWS * WIDTH, 8e6, VROWS * GROWS),
-        )(v_got, g_got, logit_sum)
+        )(v_got, g_got)
 
     with jax.named_scope("row_sums"):
         c_send, r_row = pl.pallas_call(
@@ -577,15 +565,15 @@
             out_shape=pltpu.HBM((QUADS, VROWS, 2 * WIDTH), BF16),
             compiler_params=params(),
             cost_estimate=cost(2 * VROWS * GROWS * WIDTH, 12e6, VROWS * GROWS),
-        )(*in_hbm(v_all, g_all, row_inv, col_inv), e_pair)
+        )(*in_hbm(v_all, g_all), row_inv, col_inv, e_pair)
 
     with jax.named_scope("by_clip"):
         by_clip, av = pl.pallas_call(
             by_clip_kernel,
             grid=(QUADS,),
             in_specs=[whole(1, LANES), p_spec, whole(VROWS, WIDTH), halves(4 * LANES)],
-            out_specs=(pl.BlockSpec((4 * LANES, 2 * WIDTH), lambda i: (i, 0)), whole(VROWS, WIDTH)),
-            out_shape=(pltpu.HBM((GROWS, 2 * WIDTH), F32), shape(VROWS, WIDTH)),
+            out_specs=(pl.BlockSpec((GLOSSES // QUADS, LANES, 2 * WIDTH), lambda i: (i, 0, 0)), whole(VROWS, WIDTH)),
+            out_shape=(pltpu.HBM((GLOSSES, LANES, 2 * WIDTH), F32), shape(VROWS, WIDTH)),
             scratch_shapes=[pltpu.VMEM((VROWS, 2 * WIDTH), BF16)],
             compiler_params=params(),
             cost_estimate=cost(6 * VROWS * GROWS * WIDTH, 14e6),
@@ -595,11 +583,14 @@
         v_rows = FRAMES * CLIPS_DEV // 2 + EXTRA
         mine, twin = pl.pallas_call(
             clip_send_kernel,
-            grid=(QUADS,),
-            in_specs=[whole(NXY, 1, LANES), whole(1, LANES), p_spec, halves(4 * LANES), whole(VROWS, WIDTH)],
-            out_specs=(whole(v_rows, WIDTH), whole(v_rows, WIDTH)),
+            in_specs=[vmem, vmem, hbm, hbm, vmem],
             out_shape=(shape(v_rows, WIDTH), shape(v_rows, WIDTH, dtype=BF16)),
-            scratch_shapes=[pltpu.VMEM((1, LANES), F32), pltpu.VMEM((VROWS, WIDTH), F32)],
+            scratch_shapes=[
+                pltpu.VMEM((QUADS, VROWS, 2 * WIDTH), BF16),
+                pltpu.VMEM((GROWS, WIDTH), BF16),
+                pltpu.VMEM((VROWS, WIDTH), F32),
+                pltpu.SemaphoreType.DMA((QUADS + 1,)),
+            ],
             compiler_params=params(),
             cost_estimate=cost(2 * VROWS * GROWS * WIDTH, 1e7),
         )(c_got, r_row, *in_hbm(weights, g_all), av)
@@ -608,11 +599,13 @@
         twin, c_ready = lax.optimization_barrier((twin, c_got))
         dg_send, c_row = pl.pallas_call(
             gloss_send_kernel,
-            grid=(QUADS,),
-            in_specs=[whole(NXY, 1, LANES), pl.BlockSpec((4 * LANES, 2 * WIDTH), lambda i: (i, 0))],
-            out_specs=(whole(NXY, GOWN, WIDTH), whole(1, LANES)),
+            in_specs=[vmem, hbm],
             out_shape=(shape(NXY, GOWN, WIDTH, dtype=BF16), shape(1, LANES)),
-            scratch_shapes=[two_halves(NXY * GOWN)],
+            scratch_shapes=[
+                pltpu.VMEM((QUADS, GLOSSES // QUADS, TEXTS_DEV, 2 * WIDTH), F32),
+                two_halves(NXY * GOWN),
+                pltpu.SemaphoreType.DMA((QUADS,)),
+            ],
             compiler_params=params(),
             cost_estimate=cost(2e6, 5e6),
         )(c_ready, *in_hbm(by_clip))
@@ -637,8 +630,18 @@
             in_specs=[vmem] * 2,
             out_shape=kept_and_sent(1) + kept_and_sent(1)[1:] * 2,
             compiler_params=params(),
-            cost_estimate=cost(1e6, 1e6),
+            cost_estimate=cost(3e10, 1e6),
         )(mine, to_z(sent, 1))
+
+    with jax.named_scope("diagonal"):
+        mine, v_own, g_own, counts = lax.optimization_barrier((mine, v_own, g_own, counts))
+        dv_diag, dg_diag = pl.pallas_call(
+            diagonal_kernel,
+            in_specs=[vmem] * 3,
+            out_shape=(shape(VOWN, WIDTH), shape(GOWN, WIDTH)),
+            compiler_params=params(),
+            cost_estimate=cost(2e7, 3e5),
+        )(counts, v_own, g_own)
 
     with jax.named_scope("video_grad"):
         grad_video, loss = pl.pallas_call(

time: 139 us -> 133 us (0.957)
  the two profiles are of different devices: /device:TPU:2 before, /device:TPU:8 now
where the time goes in v7:
time: 133 us; the launch traced here: 132 us
  starting transfers between devices  53.3 us (40%)
  Pallas kernels  39 us (29%)
  blocking collectives  28.2 us (21%)
  waiting for transfers between devices  11.1 us (8%)
    all_to_all x4, starting transfers between devices, exchanged(): lax.all_to_all(a, over_all, 0, 0, axis_index_groups=groups, tiled=True)  35.3 us
    all_gather x3, blocking collectives, gathered(): lax.all_gather(a, over_all, axis=0, axis_index_groups=groups, tiled=True)  28.2 us
    ppermute x4, starting transfers between devices, to_z(): lax.ppermute(a, 'outer', [(i, i ^ mask) for i in range(lax.axis_size('out...  16.1 us
    pallas_call x1, Pallas kernels, on_device(): pl.pallas_call(by_clip_kernel, grid=(QUADS,), in_specs=[whole(1, LANES),...  9.44 us
    pallas_call x1, Pallas kernels, on_device(): pl.pallas_call(weights_kernel, grid=(PAIRS,), in_specs=[whole(VROWS, WIDT...  8.58 us
    pallas_call x1, Pallas kernels, on_device(): pl.pallas_call(forward_kernel, in_specs=[vmem] * 2, out_specs=[hbm] * 2 +...  6.58 us
    pallas_call x1, Pallas kernels, on_device(): pl.pallas_call(clip_send_kernel, in_specs=[vmem, vmem, hbm, hbm, vmem], o...  5.72 us
    all_to_all x4, waiting for transfers between devices, exchanged(): lax.all_to_all(a, over_all, 0, 0, axis_index_groups=groups, tiled=True)  5.13 us
  transfers between devices with their start and end apart: 9, of which 4 were waited for; matrix products, arithmetic and copies ran while one was open for 0% of the time, Pallas kernels for 17%

profile of v7, /device:TPU:8, one launch (start us, length us, event | category | flops | bytes accessed | tf_op | source)
XLA Modules:
  0.0 132.4 jit_solution(16477589454666892714)
XLA Ops:
  0.6 1.9 %unit_tokens.1 = (bf16[96,256]{1,0:T(8,128)(2,1)S(1)}, bf16[32,48,256]{2,1,0:T(8,128)(2,1)}, bf16[48,256]{1,0:T(8,128)(2,1)S(1)}, s32[8,128]{1,0:T(8,128)S(1)}) custom-call(s32[3]{0:T(128)} %fc_in.1, s32[3]{0:T(128)} %gc_in.1, bf16[3,32,256]{2,1,0:T(8,128)(2,1)} %video.1, bf16[3,16,256]{2,1,0:T(8,128)(2,1)} %gloss.1), custom_call_target="tpu_custom_call" | custom-call | flops 200000 | bytes 700000 | tf_op jit(solution)/shard_map/unit_tokens/pallas_call | solution.py:479
  2.5 10.2 %all-to-all-start = ((bf16[32,48,256]{2,1,0:T(8,128)(2,1)}), bf16[32,48,256]{2,1,0:T(8,128)(2,1)S(1)}, u32[]{:S(2)}, u32[]{:S(2)}) async-start(bf16[32,48,256]{2,1,0:T(8,128)(2,1)} %get-tuple-element.39), calls=%async_computation | async-start | bytes 1572864 | tf_op jit(solution)/shard_map/gather/all_to_all | solution.py:470
  12.7 19.5 %all_gather.9 = bf16[384,256]{1,0:T(8,128)(2,1)S(1)} all-gather(bf16[96,256]{1,0:T(8,128)(2,1)S(1)} %get-tuple-element.66.v_ref), channel_id=1, replica_groups={{0,64,128,192},{32,96,160,224},{1,65,129,193},{33,97,161,225},{2,66,130..., dimensions={0}, use_global_device_ids=true | all-gather | bytes 245760 | tf_op jit(solution)/shard_map/gather/all_gather | solution.py:473
  32.2 6.3 %all_gather.10 = bf16[768,256]{1,0:T(8,128)(2,1)S(1)} all-gather(bf16[384,256]{1,0:T(8,128)(2,1)S(1)} %all_gather.9), channel_id=1, replica_groups={{0,32},{64,96},{128,160},{192,224},{1,33},{65,97},{129,161},{193,225},{..., dimensions={0}, use_global_device_ids=true | all-gather | bytes 589824 | tf_op jit(solution)/shard_map/gather/all_gather | solution.py:473
  38.5 2.4 %all_gather.11.v_got = bf16[1536,256]{1,0:T(8,128)(2,1)S(1)} all-gather(bf16[768,256]{1,0:T(8,128)(2,1)S(1)} %all_gather.10), channel_id=1, replica_groups={{0,1},{32,33},{64,65},{96,97},{128,129},{160,161},{192,193},{224,225},{..., dimensions={0}, use_global_device_ids=true | all-gather | bytes 1179648 | tf_op jit(solution)/shard_map/gather/all_gather | solution.py:473
  40.9 6.6 %forward.1 = (bf16[1536,256]{1,0:T(8,128)(2,1)}, bf16[2048,256]{1,0:T(8,128)(2,1)}, f32[1536,128]{1,0:T(8,128)S(1)}, f32[16,48,128]{2,1,0:T(8,128)S(1)}, f32[48,...) custom-call(bf16[1536,256]{1,0:T(8,128)(2,1)S(1)} %all_gather.11.v_got, ...), custom_call_target="tpu_custom_call" | custom-call | flops 1610612736 | bytes 8000000 | tf_op jit(solution)/shard_map/forward/pallas_call | solution.py:510
  47.5 5.5 %all-to-all-start.1 = ((f32[16,1,128]{2,1,0:T(1,128)}), f32[16,1,128]{2,1,0:T(1,128)S(1)}, u32[]{:S(2)}, u32[]{:S(2)}) async-start(f32[16,1,128]{2,1,0:T(1,128)} %get-tuple-element.40), calls=%async_computation.1 | async-start | bytes 16384 | tf_op jit(solution)/shard_map/row_sums/all_to_all | solution.py:470
  53.0 8.6 %weights.1.p_ref.p_hbm = bf16[4,1536,512]{2,1,0:T(8,128)(2,1)} custom-call(bf16[1536,256]{1,0:T(8,128)(2,1)} %get-tuple-element.44.v_ref, bf16[2048,256]{1,0:T(8,128)(2,1)} %get-tuple-element.45.g_ref.g_hbm, f32[1536,128]{1,0:T(8,128)S(1)} %get-tuple-element.46.row_ref, f32[16,48,128]{2,1,0:T(8,128)S(1)} %get-tuple-element.47.col_ref, ...), custom_call_target="tpu_custom_call" | custom-call | flops 1610612736 | bytes 12000000 | tf_op jit(solution)/shard_map/weights/pallas_call | solution.py:554
  61.5 0.7 row_sums.1
  62.3 9.9 %all-to-all-start.2 = ((f32[32,1,128]{2,1,0:T(1,128)}), f32[32,1,128]{2,1,0:T(1,128)S(1)}, u32[]{:S(2)}, u32[]{:S(2)}) async-start(f32[32,1,128]{2,1,0:T(1,128)} %get-tuple-element.42), calls=%async_computation.2 | async-start | bytes 32768 | tf_op jit(solution)/shard_map/column_sums/all_to_all | solution.py:470
  72.1 9.4 %by_clip.1 = (f32[16,128,512]{2,1,0:T(8,128)}, f32[1536,256]{1,0:T(8,128)S(1)}) custom-call(f32[1,128]{1,0:T(1,128)S(1)} %get-tuple-element.43.r_ref, bf16[4,1536,512]{2,1,0:T(8,128)(2,1)} %weights.1.p_ref.p_hbm, bf16[1536,256]{1,0:T(8,128)(2,1)} %get-tuple-element.44.v_ref, bf16[2048,256]{1,0:T(8,128)(2,1)} %get-tuple-element.45.g_ref.g_hbm), custom_call_target="tpu_custom_call" | custom-call | flops 4831838208 | bytes 14000000 | tf_op jit(solution)/shard_map/by_clip/pallas_call | solution.py:571
  81.6 0.0 all-to-all-done.2.c_got
  81.6 5.7 %clip_send.1 = (f32[784,256]{1,0:T(8,128)S(1)}, bf16[784,256]{1,0:T(8,128)(2,1)S(1)}) custom-call(f32[32,1,128]{2,1,0:T(1,128)S(1)} %all-to-all-done.2.c_got, f32[1,128]{1,0:T(1,128)S(1)} %get-tuple-element.43.r_ref, bf16[4,1536,512]{2,1,0:T(8,128)(2,1)} %weights.1.p_ref.p_hbm, bf16[2048,256]{1,0:T(8,128)(2,1)} %get-tuple-element.45.g_ref.g_hbm, ...), custom_call_target="tpu_custom_call" | custom-call | flops 1610612736 | bytes 10000000 | tf_op jit(solution)/shard_map/clip_send/pallas_call | solution.py:584
  87.3 1.9 %collective-permute-start = (bf16[784,256]{1,0:T(8,128)(2,1)S(1)}, bf16[784,256]{1,0:T(8,128)(2,1)S(1)}, u32[]{:S(2)}, u32[]{:S(2)}) collective-permute-start(bf16[784,256]{1,0:T(8,128)(2,1)S(1)} %get-tuple-element.52), channel_id=1, source_target_pairs={{0,1},{1,0},{2,3},{3,2},{4,5},{5,4},{6,7},{7,6},{8,9},{9,8},{10,11... | collective-permute-start | bytes 1204232 | tf_op jit(solution)/shard_map/clips_by_core/ppermute | solution.py:464
  89.3 1.7 %collective-permute-done.got = bf16[784,256]{1,0:T(8,128)(2,1)S(1)} collective-permute-done((bf16[784,256]{1,0:T(8,128)(2,1)S(1)}, bf16[784,256]{1,0:T(8,128)(2,1)S(1)}, u32[]{:S(2)}, u32[]{:S(2)}) %collective-permute-start) | collective-permute-done | bytes 401440 | tf_op jit(solution)/shard_map/clips_by_core/ppermute | solution.py:464
  91.0 0.8 clips_by_core.1
  91.7 3.9 %collective-permute-start.1 = (bf16[400,256]{1,0:T(8,128)(2,1)S(1)}, bf16[400,256]{1,0:T(8,128)(2,1)S(1)}, u32[]{:S(2)}, u32[]{:S(2)}) collective-permute-start(bf16[400,256]{1,0:T(8,128)(2,1)S(1)} %get-tuple-element.54), channel_id=1, source_target_pairs={{0,32},{32,0},{64,96},{96,64},{128,160},{160,128},{192,224},{224,1... | collective-permute-start | bytes 614408 | tf_op jit(solution)/shard_map/clips_by_z/ppermute | solution.py:467
  95.6 3.0 %gloss_send.1 = (bf16[32,48,256]{2,1,0:T(8,128)(2,1)}, f32[1,128]{1,0:T(1,128)S(1)}) custom-call(f32[32,1,128]{2,1,0:T(1,128)S(1)} %all-to-all-done.2.c_got, f32[16,128,512]{2,1,0:T(8,128)} %get-tuple-element.63.by_clip), custom_call_target="tpu_custom_call" | custom-call | flops 2000000 | bytes 5000000 | tf_op jit(solution)/shard_map/gloss_send/pallas_call | solution.py:600
  98.6 9.8 %all-to-all-start.3 = ((bf16[32,48,256]{2,1,0:T(8,128)(2,1)}), bf16[32,48,256]{2,1,0:T(8,128)(2,1)S(1)}, u32[]{:S(2)}, u32[]{:S(2)}) async-start(bf16[32,48,256]{2,1,0:T(8,128)(2,1)} %get-tuple-element.71), calls=%async_computation.3 | async-start | bytes 1572864 | tf_op jit(solution)/shard_map/gloss_send/all_to_all | solution.py:470
  108.4 0.0 collective-permute-done.1.got
  108.4 0.0 copy-start
  108.4 0.0 copy-start.1
  108.4 0.1 clips_by_z.1
  108.6 4.3 %collective-permute-start.2 = (bf16[112,256]{1,0:T(8,128)(2,1)S(1)}, bf16[112,256]{1,0:T(8,128)(2,1)S(1)}, u32[]{:S(2)}, u32[]{:S(2)}) collective-permute-start(bf16[112,256]{1,0:T(8,128)(2,1)S(1)} %get-tuple-element.59), channel_id=1, source_target_pairs={{0,64},{32,96},{64,0},{96,32},{128,192},{160,224},{192,128},{224,1... | collective-permute-start | bytes 172040 | tf_op jit(solution)/shard_map/video_grad/ppermute | solution.py:467
  112.9 4.6 %collective-permute-start.3 = (bf16[112,256]{1,0:T(8,128)(2,1)S(1)}, bf16[112,256]{1,0:T(8,128)(2,1)S(1)}, u32[]{:S(2)}, u32[]{:S(2)}) collective-permute-start(bf16[112,256]{1,0:T(8,128)(2,1)S(1)} %get-tuple-element.60), channel_id=1, source_target_pairs={{0,128},{32,160},{64,192},{96,224},{128,0},{160,32},{192,64},{224,... | collective-permute-start | bytes 172040 | tf_op jit(solution)/shard_map/video_grad/ppermute | solution.py:467
  117.4 3.4 %collective-permute-start.4 = (bf16[112,256]{1,0:T(8,128)(2,1)S(1)}, bf16[112,256]{1,0:T(8,128)(2,1)S(1)}, u32[]{:S(2)}, u32[]{:S(2)}) collective-permute-start(bf16[112,256]{1,0:T(8,128)(2,1)S(1)} %get-tuple-element.61), channel_id=1, source_target_pairs={{0,192},{32,224},{64,128},{96,160},{128,64},{160,96},{192,0},{224,... | collective-permute-start | bytes 172040 | tf_op jit(solution)/shard_map/video_grad/ppermute | solution.py:467
  120.8 0.6 diagonal.1
  121.4 1.6 %collective-permute-done.3.got2 = bf16[112,256]{1,0:T(8,128)(2,1)S(1)} collective-permute-done((bf16[112,256]{1,0:T(8,128)(2,1)S(1)}, bf16[112,256]{1,0:T(8,128)(2,1)S(1)}, u32[]{:S(2)}, u32[]{:S(2)}) %collective-permute-start.3) | collective-permute-done | bytes 57376 | tf_op jit(solution)/shard_map/video_grad/ppermute | solution.py:467
  123.0 2.7 %collective-permute-done.4.got3 = bf16[112,256]{1,0:T(8,128)(2,1)S(1)} collective-permute-done((bf16[112,256]{1,0:T(8,128)(2,1)S(1)}, bf16[112,256]{1,0:T(8,128)(2,1)S(1)}, u32[]{:S(2)}, u32[]{:S(2)}) %collective-permute-start.4) | collective-permute-done | bytes 57376 | tf_op jit(solution)/shard_map/video_grad/ppermute | solution.py:467
  125.7 0.8 video_grad.1
  126.5 5.1 %all-to-all-done.3.got = bf16[32,48,256]{2,1,0:T(8,128)(2,1)S(1)} async-done(((bf16[32,48,256]{2,1,0:T(8,128)(2,1)}), bf16[32,48,256]{2,1,0:T(8,128)(2,1)S(1)}, u32[]{:S(2)}, u32[]{:S(2)}) %all-to-all-start.3) | async-done | bytes 786464 | tf_op jit(solution)/shard_map/gloss_send/all_to_all | solution.py:470
  131.6 0.8 gloss_grad.1
  (5 shorter events, 0.0 us)
Async XLA Ops:
  2.5 38.4 %all-to-all-start = ((bf16[32,48,256]{2,1,0:T(8,128)(2,1)}), bf16[32,48,256]{2,1,0:T(8,128)(2,1)S(1)}, u32[]{:S(2)}, u32[]{:S(2)}) async-start(bf16[32,48,256]{2,1,0:T(8,128)(2,1)} %get-tuple-element.39), calls=%async_computation | async-start | bytes 1572864 | tf_op jit(solution)/shard_map/gather/all_to_all | solution.py:470
  47.5 14.1 %all-to-all-start.1 = ((f32[16,1,128]{2,1,0:T(1,128)}), f32[16,1,128]{2,1,0:T(1,128)S(1)}, u32[]{:S(2)}, u32[]{:S(2)}) async-start(f32[16,1,128]{2,1,0:T(1,128)} %get-tuple-element.40), calls=%async_computation.1 | async-start | bytes 16384 | tf_op jit(solution)/shard_map/row_sums/all_to_all | solution.py:470
  62.3 19.3 %all-to-all-start.2 = ((f32[32,1,128]{2,1,0:T(1,128)}), f32[32,1,128]{2,1,0:T(1,128)S(1)}, u32[]{:S(2)}, u32[]{:S(2)}) async-start(f32[32,1,128]{2,1,0:T(1,128)} %get-tuple-element.42), calls=%async_computation.2 | async-start | bytes 32768 | tf_op jit(solution)/shard_map/column_sums/all_to_all | solution.py:470
  87.3 3.6 %collective-permute-start = (bf16[784,256]{1,0:T(8,128)(2,1)S(1)}, bf16[784,256]{1,0:T(8,128)(2,1)S(1)}, u32[]{:S(2)}, u32[]{:S(2)}) collective-permute-start(bf16[784,256]{1,0:T(8,128)(2,1)S(1)} %get-tuple-element.52), channel_id=1, source_target_pairs={{0,1},{1,0},{2,3},{3,2},{4,5},{5,4},{6,7},{7,6},{8,9},{9,8},{10,11... | collective-permute-start | bytes 1204232 | tf_op jit(solution)/shard_map/clips_by_core/ppermute | solution.py:464
  91.7 16.7 %collective-permute-start.1 = (bf16[400,256]{1,0:T(8,128)(2,1)S(1)}, bf16[400,256]{1,0:T(8,128)(2,1)S(1)}, u32[]{:S(2)}, u32[]{:S(2)}) collective-permute-start(bf16[400,256]{1,0:T(8,128)(2,1)S(1)} %get-tuple-element.54), channel_id=1, source_target_pairs={{0,32},{32,0},{64,96},{96,64},{128,160},{160,128},{192,224},{224,1... | collective-permute-start | bytes 614408 | tf_op jit(solution)/shard_map/clips_by_z/ppermute | solution.py:467
  98.6 33.0 %all-to-all-start.3 = ((bf16[32,48,256]{2,1,0:T(8,128)(2,1)}), bf16[32,48,256]{2,1,0:T(8,128)(2,1)S(1)}, u32[]{:S(2)}, u32[]{:S(2)}) async-start(bf16[32,48,256]{2,1,0:T(8,128)(2,1)} %get-tuple-element.71), calls=%async_computation.3 | async-start | bytes 1572864 | tf_op jit(solution)/shard_map/gloss_send/all_to_all | solution.py:470
  108.4 17.3 %copy-start = (bf16[3,32,256]{2,1,0:T(8,128)(2,1)S(1)}, bf16[3,32,256]{2,1,0:T(8,128)(2,1)}, u32[]{:S(2)}) copy-start(bf16[3,32,256]{2,1,0:T(8,128)(2,1)} %video.1) | copy-start | bytes 147460
  108.4 23.2 %copy-start.1 = (bf16[3,16,256]{2,1,0:T(8,128)(2,1)S(1)}, bf16[3,16,256]{2,1,0:T(8,128)(2,1)}, u32[]{:S(2)}) copy-start(bf16[3,16,256]{2,1,0:T(8,128)(2,1)} %gloss.1) | copy-start | bytes 73732
  108.6 12.9 %collective-permute-start.2 = (bf16[112,256]{1,0:T(8,128)(2,1)S(1)}, bf16[112,256]{1,0:T(8,128)(2,1)S(1)}, u32[]{:S(2)}, u32[]{:S(2)}) collective-permute-start(bf16[112,256]{1,0:T(8,128)(2,1)S(1)} %get-tuple-element.59), channel_id=1, source_target_pairs={{0,64},{32,96},{64,0},{96,32},{128,192},{160,224},{192,128},{224,1... | collective-permute-start | bytes 172040 | tf_op jit(solution)/shard_map/video_grad/ppermute | solution.py:467
  112.9 10.1 %collective-permute-start.3 = (bf16[112,256]{1,0:T(8,128)(2,1)S(1)}, bf16[112,256]{1,0:T(8,128)(2,1)S(1)}, u32[]{:S(2)}, u32[]{:S(2)}) collective-permute-start(bf16[112,256]{1,0:T(8,128)(2,1)S(1)} %get-tuple-element.60), channel_id=1, source_target_pairs={{0,128},{32,160},{64,192},{96,224},{128,0},{160,32},{192,64},{224,... | collective-permute-start | bytes 172040 | tf_op jit(solution)/shard_map/video_grad/ppermute | solution.py:467
  117.4 8.2 %collective-permute-start.4 = (bf16[112,256]{1,0:T(8,128)(2,1)S(1)}, bf16[112,256]{1,0:T(8,128)(2,1)S(1)}, u32[]{:S(2)}, u32[]{:S(2)}) collective-permute-start(bf16[112,256]{1,0:T(8,128)(2,1)S(1)} %get-tuple-element.61), channel_id=1, source_target_pairs={{0,192},{32,224},{64,128},{96,160},{128,64},{160,96},{192,0},{224,... | collective-permute-start | bytes 172040 | tf_op jit(solution)/shard_map/video_grad/ppermute | solution.py:467

commit v8 on v7

--- a/solution.py
+++ b/solution.py
@@ -23,12 +23,13 @@
 TEXTS_DEV = NY * NX * OWN
 LANES = 128
 VROWS = FRAMES * CLIPS_DEV
-GROWS = GLOSSES * LANES
+GROWS = GLOSSES * TEXTS_DEV
 VOWN = FRAMES * OWN
 GOWN = GLOSSES * OWN
 EXTRA = 16
-PAIRS = GLOSSES // 2
 QUADS = GLOSSES // 4
+TILES = GROWS // LANES
+HALF = GROWS // 2
 NXY, NZC = NX * NY, NZ * NCORE
 
 def flat(x, z, y, core):
@@ -52,7 +53,7 @@
 ZC_GROUPS = [[flat(x, z, y, c) for c in range(NCORE) for z in range(NZ)] for x in range(NX) for y in range(NY)]
 
 
-def params(limit_mb=20):
+def params(limit_mb=32):
     return pltpu.CompilerParams(vmem_limit_bytes=limit_mb * 1024 * 1024)
 
 
@@ -79,6 +80,19 @@
 def column_of(row, n):
     eye = iota((n, LANES), 0) == iota((n, LANES), 1)
     return jnp.sum(jnp.where(eye, jnp.broadcast_to(row, (n, LANES)), 0.0), axis=1, keepdims=True)
+
+
+def packed(x):
+    lane = iota(x.shape, 1)
+    a, b, c = (pltpu.roll(x, shift, 1) for shift in (96, 64, 32))
+    return jnp.where(lane < 96, x, a), jnp.where(lane < 64, a, b), jnp.where(lane < 32, b, c)
+
+
+def unpacked_sum(t0, t1, t2):
+    lane = iota(t0.shape, 1)
+    second = pltpu.roll(jnp.where(lane >= 96, t0, t1), 32, 1)
+    third = pltpu.roll(jnp.where(lane >= 64, t1, t2), 64, 1)
+    return (t0 + second) + (third + pltpu.roll(t2, 96, 1))
 
 
 def pieces(value):
@@ -180,63 +194,64 @@
         v_out[pl.ds(f * CLIPS_DEV, CLIPS_DEV), :] = jnp.concatenate(parts, axis=0).astype(BF16)
     copies[0].start()
     put(g_scr, pl.ds(0, NXY * GOWN), g_got[...].reshape(NXY * GOWN, WIDTH).astype(F32))
-    pad = jnp.where(iota((LANES - TEXTS_DEV, WIDTH), 1) == 0, MARK, 0.0)
     for g in range(GLOSSES):
         parts = [get(g_scr, pl.ds(x * NY * GOWN + g * OWN + c, NY, stride=GOWN)) for x in range(NX) for c in range(OWN)]
-        g_out[pl.ds(g * LANES, LANES), :] = jnp.concatenate(parts + [pad], axis=0).astype(BF16)
-
+        g_out[pl.ds(g * TEXTS_DEV, TEXTS_DEV), :] = jnp.concatenate(parts, axis=0).astype(BF16)
     copies[1].start()
 
     first = jnp.where(iota((WIDTH, LANES), 0) == 0, 1.0, 0.0).astype(BF16)
     frame_mask[...] = jnp.where(nn(v_out[...], first) < MARK_LIMIT, 1.0, 0.0)
     first_row = jnp.where(iota((16, WIDTH), 1) == 0, 1.0, 0.0).astype(BF16)
-    for g in range(GLOSSES):
-        gloss_mask[g] = jnp.where(nt(first_row, g_out[pl.ds(g * LANES, LANES), :])[0:8] < MARK_LIMIT, 1.0, 0.0)
+    for t in range(TILES):
+        found = nt(first_row, g_out[pl.ds(t * LANES, LANES), :])[0:1]
+        gloss_mask[t] = jnp.where(found < MARK_LIMIT, 1.0, 0.0)
     frames = jnp.zeros((CLIPS_DEV, LANES), F32)
     for f in range(FRAMES):
         frames = frames + frame_mask[pl.ds(f * CLIPS_DEV, CLIPS_DEV), :]
-    glosses = gloss_mask[0]
-    for g in range(1, GLOSSES):
-        glosses = glosses + gloss_mask[g]
-    glosses = jnp.maximum(glosses, 1.0)[0:1]
-
-    rows[...] = jnp.zeros_like(rows)
-
-    def two_glosses(p, _):
-        e = exp_scores(v_out[...], g_out[pl.ds(pl.multiple_of(p * WIDTH, WIDTH), WIDTH), :])
-        m0, m1 = gloss_mask[2 * p][0:1], gloss_mask[2 * p + 1][0:1]
-        col0 = jnp.zeros((CLIPS_DEV, LANES), F32)
-        col1 = jnp.zeros((CLIPS_DEV, LANES), F32)
+    by_tile = []
+    for t in range(3):
+        by_tile.append(gloss_mask[t] + gloss_mask[t + 3] + gloss_mask[t + 6] + gloss_mask[t + 9])
+    lane = iota((CLIPS_DEV, LANES), 1)
+    real = lane < TEXTS_DEV
+    counts = unpacked_sum(*[jnp.broadcast_to(t, (8, LANES)) for t in by_tile])
+    glosses = jnp.where(real[0:8], counts, 1.0)
+    packed_glosses = [t[0:1] for t in packed(glosses)]
+    glosses = glosses[0:1]
+
+    for half in range(2):
+        e = exp_scores(v_out[...], g_out[pl.ds(half * HALF, HALF), :])
+        tiles = range(half * TILES // 2, (half + 1) * TILES // 2)
+        masks = [gloss_mask[t] for t in tiles]
+        sums = [jnp.zeros((CLIPS_DEV, LANES), F32) for _ in tiles]
         for f in range(FRAMES):
             at = pl.ds(f * CLIPS_DEV, CLIPS_DEV)
+            mask = frame_mask[at, :]
             block = e[f * CLIPS_DEV : (f + 1) * CLIPS_DEV]
-            e0, e1 = block[:, :LANES], block[:, LANES:]
-            mask = frame_mask[at, :]
-            rows[at, :] = rows[at, :] + (e0 * m0 + e1 * m1)
-            col0 = col0 + e0 * mask
-            col1 = col1 + e1 * mask
-        cols[2 * p] = col0
-        cols[2 * p + 1] = col1
-        return 0
-
-    lax.fori_loop(0, PAIRS, two_glosses, 0, unroll=2)
-
-    lane = iota((CLIPS_DEV, LANES), 1)
-    real = lane < TEXTS_DEV
+            parts = [block[:, k * LANES : (k + 1) * LANES] for k in range(TILES // 2)]
+            sums = [total + part * mask for total, part in zip(sums, parts, strict=True)]
+            for k in range(3):
+                part = parts[k] * masks[k] + parts[k + 3] * masks[k + 3]
+                rows[at, pl.ds(k * LANES, LANES)] = part if half == 0 else rows[at, pl.ds(k * LANES, LANES)] + part
+        for k, t in enumerate(tiles):
+            cols[t] = sums[k]
+
     video_part = jnp.zeros((CLIPS_DEV, LANES), F32)
     for f in range(FRAMES):
         at = pl.ds(f * CLIPS_DEV, CLIPS_DEV)
         mask = frame_mask[at, :]
-        total = jnp.where(real, rows[at, :], 1.0)
-        video_part = video_part + mask * jnp.log(total / glosses)
+        total = unpacked_sum(*[rows[at, pl.ds(k * LANES, LANES)] for k in range(3)])
+        total = jnp.where(real, total, 1.0)
+        video_part = video_part + mask * jnp.log(total)
         row_out[at, :] = jnp.where(mask > 0.0, 1.0 / (total * frames), FAR)
-    gloss_part = jnp.zeros((CLIPS_DEV, LANES), F32)
-    for g in range(GLOSSES):
-        mask = gloss_mask[g][0:1]
-        total = cols[g]
-        gloss_part = gloss_part + mask * jnp.log(total / frames)
-        col_out[g] = jnp.where(mask > 0.0, 1.0 / (total * glosses), FAR)
-    logits = 0.5 * (video_part / frames + gloss_part / glosses)
+    video_part = video_part / frames - jnp.log(glosses)
+    gloss_parts = [jnp.zeros((CLIPS_DEV, LANES), F32)] * 3
+    for t in range(TILES):
+        mask = gloss_mask[t]
+        total = cols[t]
+        gloss_parts[t % 3] = gloss_parts[t % 3] + mask * jnp.log(total)
+        col_out[t] = jnp.where(mask > 0.0, 1.0 / (total * packed_glosses[t % 3]), FAR)
+    gloss_part = unpacked_sum(*gloss_parts) / glosses - jnp.log(frames)
+    logits = 0.5 * (video_part + gloss_part)
     e_pair = jnp.where(real, jnp.exp(logits), 0.0)
     e_out[...] = e_pair
 
@@ -260,17 +275,36 @@
         copy.wait()
 
 
-def weights_kernel(v_ref, g_ref, row_ref, col_ref, e_ref, p_out):
-    e = exp_scores(v_ref[...], g_ref[...])
-    scale = 2.5 * e_ref[...]
-    col0, col1 = col_ref[0], col_ref[1]
-    for f in range(FRAMES):
-        at = pl.ds(f * CLIPS_DEV, CLIPS_DEV)
-        block = e[f * CLIPS_DEV : (f + 1) * CLIPS_DEV]
-        row = row_ref[at, :]
-        w0 = scale * block[:, :LANES] * jnp.maximum(row + col0, 0.0)
-        w1 = scale * block[:, LANES:] * jnp.maximum(row + col1, 0.0)
-        p_out[0, at, :] = jnp.concatenate([w0, w1], axis=1).astype(BF16)
+def started(copies):
+    for copy in copies:
+        copy.start()
+    return copies
+
+
+def halves_of(p):
+    return [(r, h, p.at[h, pl.ds(r * VROWS // 2, VROWS // 2)]) for r in range(2) for h in range(2)]
+
+
+def weights_kernel(v_hbm, g_hbm, row_ref, col_ref, e_ref, p_hbm, v, g, p, sems):
+    loads = started([pltpu.make_async_copy(a, b, sems.at[i]) for i, (a, b) in enumerate(((v_hbm, v), (g_hbm, g)))])
+    scales = packed(2.5 * e_ref[...])
+    for load in loads:
+        load.wait()
+    stores = []
+    for (r, h, out), (_, _, here) in zip(halves_of(p_hbm), halves_of(p), strict=True):
+        e = exp_scores(v[pl.ds(r * VROWS // 2, VROWS // 2), :], g[pl.ds(h * HALF, HALF), :])
+        for f in range(FRAMES // 2):
+            row = packed(row_ref[pl.ds((r * FRAMES // 2 + f) * CLIPS_DEV, CLIPS_DEV), :])
+            block = e[f * CLIPS_DEV : (f + 1) * CLIPS_DEV]
+            parts = []
+            for k in range(TILES // 2):
+                share = jnp.maximum(row[k % 3] + col_ref[h * TILES // 2 + k], 0.0)
+                parts.append(scales[k % 3] * block[:, k * LANES : (k + 1) * LANES] * share)
+            here[pl.ds(f * CLIPS_DEV, CLIPS_DEV), :] = jnp.concatenate(parts, axis=1).astype(BF16)
+        stores += started([pltpu.make_async_copy(here, out, sems.at[2 + 2 * r + h])])
+    for store in stores:
+        store.wait()
+
 
 def added(got):
     total = got[0]
@@ -292,9 +326,7 @@
 
 
 def inverse_texts(c_row):
-    real = iota((1, LANES), 1) < TEXTS_DEV
-    inverse = jnp.where(real, 1.0 / jnp.where(real, c_row, 1.0), 0.0)
-    return jnp.broadcast_to(column_of(inverse, LANES), (LANES, WIDTH))
+    return jnp.broadcast_to(1.0 / column_of(c_row, TEXTS_DEV), (TEXTS_DEV, WIDTH))
 
 
 def by_clip_kernel(r_ref, p_ref, v_ref, g_ref, out, av_out, both):
@@ -309,7 +341,7 @@
             both[at, :WIDTH] = v
             both[at, WIDTH:] = (v.astype(F32) * inverse).astype(BF16)
 
-    out[...] = tn(p_ref[0], both[...]).reshape(GLOSSES // QUADS, LANES, 2 * WIDTH)
+    out[...] = tn(p_ref[0], both[...]).reshape(GLOSSES // 2, TEXTS_DEV, 2 * WIDTH)
     part = nn(p_ref[0], g_ref[...])
 
     @pl.when(step == 0)
@@ -319,29 +351,24 @@
     @pl.when(step > 0)
     def _():
         av_out[...] = av_out[...] + part
-
-
-def started(copies):
-    for copy in copies:
-        copy.start()
-    return copies
 
 
 def gloss_send_kernel(c_got, by_clip, out, c_out, held, scr, sems):
     many = GLOSSES // QUADS
     copies = started(
         [
-            pltpu.make_async_copy(by_clip.at[pl.ds(q * many, many), pl.ds(0, TEXTS_DEV)], held.at[q], sems.at[q])
+            pltpu.make_async_copy(by_clip.at[pl.ds(q * many, many)], held.at[pl.ds(q * many, many)], sems.at[q])
             for q in range(QUADS)
         ]
     )
     c_out[...] = added(c_got)
-    col = inverse_texts(c_out[...])[:TEXTS_DEV]
+    col = inverse_texts(c_out[...])
     for q, copy in enumerate(copies):
         copy.wait()
         for k in range(many):
-            block = held[q, k, :, :WIDTH] * col + held[q, k, :, WIDTH:]
-            row = (q * many + k) * OWN
+            g = q * many + k
+            block = held[g, :, :WIDTH] * col + held[g, :, WIDTH:]
+            row = g * OWN
             for x in range(NX):
                 for c in range(OWN):
                     first = (x * OWN + c) * NY
@@ -349,35 +376,37 @@
     out[...] = get(scr, pl.ds(0, NXY * GOWN)).astype(BF16).reshape(NXY, GOWN, WIDTH)
 
 
-def clip_send_kernel(c_got, r_ref, p_hbm, g_hbm, av_ref, mine, twin, held, g_held, total, sems):
-    g_copy = pltpu.make_async_copy(g_hbm, g_held, sems.at[QUADS])
-    copies = [pltpu.make_async_copy(p_hbm.at[q], held.at[q], sems.at[q]) for q in range(QUADS)]
+def clip_send_kernel(c_got, r_ref, p_hbm, g_hbm, av_ref, mine, twin, p, g, g_by_text, sems):
+    g_copy = pltpu.make_async_copy(g_hbm, g, sems.at[4])
+    copies = []
+    for (r, h, theirs), (_, _, here) in zip(halves_of(p_hbm), halves_of(p), strict=True):
+        copies.append(pltpu.make_async_copy(theirs, here, sems.at[2 * r + h]))
     started([g_copy, *copies])
     c_row = added(c_got)
     col = inverse_texts(c_row)
-    cols = jnp.concatenate([col] * (GLOSSES // QUADS), axis=0)
     core = lax.rem(lax.axis_index("inner"), NCORE)
     inverse = jnp.broadcast_to(1.0 / column_of(r_ref[...], CLIPS_DEV), (CLIPS_DEV, WIDTH))
     half = CLIPS_DEV // 2
     g_copy.wait()
-    for q, copy in enumerate(copies):
-        scaled = (g_held[pl.ds(q * 4 * LANES, 4 * LANES), :].astype(F32) * cols).astype(BF16)
-        copy.wait()
-        part = nn(held[q], scaled)
-        if q == 0:
-            total[...] = part
-        elif q < QUADS - 1:
-            total[...] = total[...] + part
-    for pair in range(FRAMES // 2):
-        others = []
-        for f in (2 * pair, 2 * pair + 1):
-            at = pl.ds(f * CLIPS_DEV, CLIPS_DEV)
-            new = part[f * CLIPS_DEV : (f + 1) * CLIPS_DEV]
-            block = av_ref[at, :] * inverse + (total[at, :] + new)
-            low, high = block[:half], block[half:]
-            mine[pl.ds(f * half, half), :] = jnp.where(core == 0, low, high)
-            others.append(jnp.where(core == 0, high, low))
-        twin[pl.ds(pair * CLIPS_DEV, CLIPS_DEV), :] = jnp.concatenate(others, axis=0).astype(BF16)
+    for i in range(GLOSSES):
+        at = pl.ds(i * TEXTS_DEV, TEXTS_DEV)
+        g_by_text[at, :] = (g[at, :].astype(F32) * col).astype(BF16)
+    for r in range(2):
+        copies[2 * r].wait()
+        copies[2 * r + 1].wait()
+        at = pl.ds(r * VROWS // 2, VROWS // 2)
+        part = nn(p[0, at, :], g_by_text[pl.ds(0, HALF), :]) + nn(p[1, at, :], g_by_text[pl.ds(HALF, HALF), :])
+        for pair in range(FRAMES // 4):
+            others = []
+            for f in (2 * pair, 2 * pair + 1):
+                full = r * FRAMES // 2 + f
+                new = part[f * CLIPS_DEV : (f + 1) * CLIPS_DEV]
+                block = av_ref[pl.ds(full * CLIPS_DEV, CLIPS_DEV), :] * inverse + new
+                low, high = block[:half], block[half:]
+                mine[pl.ds(full * half, half), :] = jnp.where(core == 0, low, high)
+                others.append(jnp.where(core == 0, high, low))
+            at = pl.ds((r * FRAMES // 4 + pair) * CLIPS_DEV, CLIPS_DEV)
+            twin[at, :] = jnp.concatenate(others, axis=0).astype(BF16)
     real = iota((1, LANES), 1) < TEXTS_DEV
     logs = jnp.where(real, jnp.log(jnp.where(real, c_row, 1.0)), 0.0)
     extra = pieces(jnp.sum(logs, axis=1, keepdims=True))
@@ -515,7 +544,7 @@
                 pltpu.HBM((VROWS, WIDTH), BF16),
                 pltpu.HBM((GROWS, WIDTH), BF16),
                 shape(VROWS, LANES),
-                shape(GLOSSES, CLIPS_DEV, LANES),
+                shape(TILES, CLIPS_DEV, LANES),
                 shape(CLIPS_DEV, LANES),
                 shape(NZC, 1, LANES),
                 shape(1, LANES),
@@ -526,9 +555,9 @@
                 two_halves(VROWS),
                 two_halves(NXY * GOWN),
                 pltpu.VMEM((VROWS, LANES), F32),
-                pltpu.VMEM((GLOSSES, 8, LANES), F32),
-                pltpu.VMEM((VROWS, LANES), F32),
-                pltpu.VMEM((GLOSSES, CLIPS_DEV, LANES), F32),
+                pltpu.VMEM((TILES, 1, LANES), F32),
+                pltpu.VMEM((VROWS, 3 * LANES), F32),
+                pltpu.VMEM((TILES, CLIPS_DEV, LANES), F32),
                 pltpu.SemaphoreType.DMA((2,)),
             ],
             compiler_params=params(),
@@ -546,23 +575,18 @@
     with jax.named_scope("column_sums"):
         c_got = exchanged(c_send, XY_GROUPS)
 
-    def halves(rows):
-        return pl.BlockSpec((rows, WIDTH), lambda i: (i, 0))
-
-    p_spec = pl.BlockSpec((1, VROWS, 2 * WIDTH), lambda i: (i, 0, 0))
     with jax.named_scope("weights"):
         weights = pl.pallas_call(
             weights_kernel,
-            grid=(PAIRS,),
-            in_specs=[
-                whole(VROWS, WIDTH),
-                halves(2 * LANES),
-                whole(VROWS, LANES),
-                pl.BlockSpec((2, CLIPS_DEV, LANES), lambda i: (i, 0, 0)),
-                whole(CLIPS_DEV, LANES),
+            in_specs=[hbm, hbm, vmem, vmem, vmem],
+            out_specs=hbm,
+            out_shape=pltpu.HBM((2, VROWS, HALF), BF16),
+            scratch_shapes=[
+                pltpu.VMEM((VROWS, WIDTH), BF16),
+                pltpu.VMEM((GROWS, WIDTH), BF16),
+                pltpu.VMEM((2, VROWS, HALF), BF16),
+                pltpu.SemaphoreType.DMA((6,)),
             ],
-            out_specs=pl.BlockSpec((1, VROWS, WIDTH), lambda i: (i // 2, 0, i % 2)),
-            out_shape=pltpu.HBM((QUADS, VROWS, 2 * WIDTH), BF16),
             compiler_params=params(),
             cost_estimate=cost(2 * VROWS * GROWS * WIDTH, 12e6, VROWS * GROWS),
         )(*in_hbm(v_all, g_all), row_inv, col_inv, e_pair)
@@ -570,10 +594,18 @@
     with jax.named_scope("by_clip"):
         by_clip, av = pl.pallas_call(
             by_clip_kernel,
-            grid=(QUADS,),
-            in_specs=[whole(1, LANES), p_spec, whole(VROWS, WIDTH), halves(4 * LANES)],
-            out_specs=(pl.BlockSpec((GLOSSES // QUADS, LANES, 2 * WIDTH), lambda i: (i, 0, 0)), whole(VROWS, WIDTH)),
-            out_shape=(pltpu.HBM((GLOSSES, LANES, 2 * WIDTH), F32), shape(VROWS, WIDTH)),
+            grid=(2,),
+            in_specs=[
+                whole(1, LANES),
+                pl.BlockSpec((1, VROWS, HALF), lambda i: (i, 0, 0)),
+                whole(VROWS, WIDTH),
+                pl.BlockSpec((HALF, WIDTH), lambda i: (i, 0)),
+            ],
+            out_specs=(
+                pl.BlockSpec((GLOSSES // 2, TEXTS_DEV, 2 * WIDTH), lambda i: (i, 0, 0)),
+                whole(VROWS, WIDTH),
+            ),
+            out_shape=(pltpu.HBM((GLOSSES, TEXTS_DEV, 2 * WIDTH), F32), shape(VROWS, WIDTH)),
             scratch_shapes=[pltpu.VMEM((VROWS, 2 * WIDTH), BF16)],
             compiler_params=params(),
             cost_estimate=cost(6 * VROWS * GROWS * WIDTH, 14e6),
@@ -586,10 +618,10 @@
             in_specs=[vmem, vmem, hbm, hbm, vmem],
             out_shape=(shape(v_rows, WIDTH), shape(v_rows, WIDTH, dtype=BF16)),
             scratch_shapes=[
-                pltpu.VMEM((QUADS, VROWS, 2 * WIDTH), BF16),
+                pltpu.VMEM((2, VROWS, HALF), BF16),
                 pltpu.VMEM((GROWS, WIDTH), BF16),
-                pltpu.VMEM((VROWS, WIDTH), F32),
-                pltpu.SemaphoreType.DMA((QUADS + 1,)),
+                pltpu.VMEM((GROWS, WIDTH), BF16),
+                pltpu.SemaphoreType.DMA((5,)),
             ],
             compiler_params=params(),
             cost_estimate=cost(2 * VROWS * GROWS * WIDTH, 1e7),
@@ -602,7 +634,7 @@
             in_specs=[vmem, hbm],
             out_shape=(shape(NXY, GOWN, WIDTH, dtype=BF16), shape(1, LANES)),
             scratch_shapes=[
-                pltpu.VMEM((QUADS, GLOSSES // QUADS, TEXTS_DEV, 2 * WIDTH), F32),
+                pltpu.VMEM((GLOSSES, TEXTS_DEV, 2 * WIDTH), F32),
                 two_halves(NXY * GOWN),
                 pltpu.SemaphoreType.DMA((QUADS,)),
             ],
@@ -630,7 +662,7 @@
             in_specs=[vmem] * 2,
             out_shape=kept_and_sent(1) + kept_and_sent(1)[1:] * 2,
             compiler_params=params(),
-            cost_estimate=cost(3e10, 1e6),
+            cost_estimate=cost(1e10, 1e6),
         )(mine, to_z(sent, 1))
 
     with jax.named_scope("diagonal"):

time: 133 us -> 126 us (0.947)
  the two profiles are of different devices: /device:TPU:8 before, /device:TPU:2 now
where the time goes in v8:
time: 126 us; the launch traced here: 125 us
  starting transfers between devices  51.3 us (41%)
  Pallas kernels  32.4 us (26%)
  blocking collectives  28.2 us (22%)
  waiting for transfers between devices  12.7 us (10%)
    all_to_all x4, starting transfers between devices, exchanged(): lax.all_to_all(a, over_all, 0, 0, axis_index_groups=groups, tiled=True)  34.6 us
    all_gather x3, blocking collectives, gathered(): lax.all_gather(a, over_all, axis=0, axis_index_groups=groups, tiled=True)  28.2 us
    ppermute x4, starting transfers between devices, to_z(): lax.ppermute(a, 'outer', [(i, i ^ mask) for i in range(lax.axis_size('out...  14.7 us
    ppermute x4, waiting for transfers between devices, to_z(): lax.ppermute(a, 'outer', [(i, i ^ mask) for i in range(lax.axis_size('out...  9.68 us
    pallas_call x1, Pallas kernels, on_device(): pl.pallas_call(by_clip_kernel, grid=(2,), in_specs=[whole(1, LANES), pl.B...  7.71 us
    pallas_call x1, Pallas kernels, on_device(): pl.pallas_call(forward_kernel, in_specs=[vmem] * 2, out_specs=[hbm] * 2 +...  6.07 us
    pallas_call x1, Pallas kernels, on_device(): pl.pallas_call(weights_kernel, in_specs=[hbm, hbm, vmem, vmem, vmem], out...  5.32 us
    pallas_call x1, Pallas kernels, on_device(): pl.pallas_call(clip_send_kernel, in_specs=[vmem, vmem, hbm, hbm, vmem], o...  4.65 us
  transfers between devices with their start and end apart: 9, of which 4 were waited for; matrix products, arithmetic and copies ran while one was open for 0% of the time, Pallas kernels for 15%

profile of v8, /device:TPU:2, one launch (start us, length us, event | category | flops | bytes accessed | tf_op | source)
XLA Modules:
  0.0 125.3 jit_solution(7420878729989677255)
XLA Ops:
  0.6 1.9 %unit_tokens.1 = (bf16[96,256]{1,0:T(8,128)(2,1)S(1)}, bf16[32,48,256]{2,1,0:T(8,128)(2,1)}, bf16[48,256]{1,0:T(8,128)(2,1)S(1)}, s32[8,128]{1,0:T(8,128)S(1)}) custom-call(s32[3]{0:T(128)} %fc_in.1, s32[3]{0:T(128)} %gc_in.1, bf16[3,32,256]{2,1,0:T(8,128)(2,1)} %video.1, bf16[3,16,256]{2,1,0:T(8,128)(2,1)} %gloss.1), custom_call_target="tpu_custom_call" | custom-call | flops 200000 | bytes 700000 | tf_op jit(solution)/shard_map/unit_tokens/pallas_call | solution.py:508
  2.5 10.3 %all-to-all-start = ((bf16[32,48,256]{2,1,0:T(8,128)(2,1)}), bf16[32,48,256]{2,1,0:T(8,128)(2,1)S(1)}, u32[]{:S(2)}, u32[]{:S(2)}) async-start(bf16[32,48,256]{2,1,0:T(8,128)(2,1)} %get-tuple-element.39), calls=%async_computation | async-start | bytes 1572864 | tf_op jit(solution)/shard_map/gather/all_to_all | solution.py:499
  12.8 19.5 %all_gather.9 = bf16[384,256]{1,0:T(8,128)(2,1)S(1)} all-gather(bf16[96,256]{1,0:T(8,128)(2,1)S(1)} %get-tuple-element.66.v_ref), channel_id=1, replica_groups={{0,64,128,192},{32,96,160,224},{1,65,129,193},{33,97,161,225},{2,66,130..., dimensions={0}, use_global_device_ids=true | all-gather | bytes 245760 | tf_op jit(solution)/shard_map/gather/all_gather | solution.py:502
  32.3 6.3 %all_gather.10 = bf16[768,256]{1,0:T(8,128)(2,1)S(1)} all-gather(bf16[384,256]{1,0:T(8,128)(2,1)S(1)} %all_gather.9), channel_id=1, replica_groups={{0,32},{64,96},{128,160},{192,224},{1,33},{65,97},{129,161},{193,225},{..., dimensions={0}, use_global_device_ids=true | all-gather | bytes 589824 | tf_op jit(solution)/shard_map/gather/all_gather | solution.py:502
  38.6 2.4 %all_gather.11.v_got = bf16[1536,256]{1,0:T(8,128)(2,1)S(1)} all-gather(bf16[768,256]{1,0:T(8,128)(2,1)S(1)} %all_gather.10), channel_id=1, replica_groups={{0,1},{32,33},{64,65},{96,97},{128,129},{160,161},{192,193},{224,225},{..., dimensions={0}, use_global_device_ids=true | all-gather | bytes 1179648 | tf_op jit(solution)/shard_map/gather/all_gather | solution.py:502
  40.9 0.0 all-to-all-done.g_got
  41.0 6.1 %forward.1 = (bf16[1536,256]{1,0:T(8,128)(2,1)}, bf16[1536,256]{1,0:T(8,128)(2,1)}, f32[1536,128]{1,0:T(8,128)S(1)}, f32[12,48,128]{2,1,0:T(8,128)S(1)}, f32[48,...) custom-call(bf16[1536,256]{1,0:T(8,128)(2,1)S(1)} %all_gather.11.v_got, ...), custom_call_target="tpu_custom_call" | custom-call | flops 1207959552 | bytes 8000000 | tf_op jit(solution)/shard_map/forward/pallas_call | solution.py:539
  47.0 5.5 %all-to-all-start.1 = ((f32[16,1,128]{2,1,0:T(1,128)}), f32[16,1,128]{2,1,0:T(1,128)S(1)}, u32[]{:S(2)}, u32[]{:S(2)}) async-start(f32[16,1,128]{2,1,0:T(1,128)} %get-tuple-element.40), calls=%async_computation.1 | async-start | bytes 16384 | tf_op jit(solution)/shard_map/row_sums/all_to_all | solution.py:499
  52.5 5.3 %weights.1.p_ref.p_hbm = bf16[2,1536,768]{2,1,0:T(8,128)(2,1)} custom-call(bf16[1536,256]{1,0:T(8,128)(2,1)} %get-tuple-element.44.v_hbm.v_ref, bf16[1536,256]{1,0:T(8,128)(2,1)} %get-tuple-element.45.g_hbm.g_ref, f32[1536,128]{1,0:T(8,128)S(1)} %get-tuple-element.46.row_ref, f32[12,48,128]{2,1,0:T(8,128)S(1)} %get-tuple-element.47.col_ref, ...), custom_call_target="tpu_custom_call" | custom-call | flops 1207959552 | bytes 12000000 | tf_op jit(solution)/shard_map/weights/pallas_call | solution.py:579
  57.8 2.2 %all-to-all-done.1.r_got = f32[16,1,128]{2,1,0:T(1,128)S(1)} async-done(((f32[16,1,128]{2,1,0:T(1,128)}), f32[16,1,128]{2,1,0:T(1,128)S(1)}, u32[]{:S(2)}, u32[]{:S(2)}) %all-to-all-start.1) | async-done | bytes 8224 | tf_op jit(solution)/shard_map/row_sums/all_to_all | solution.py:499
  60.0 0.7 row_sums.1
  60.7 9.9 %all-to-all-start.2 = ((f32[32,1,128]{2,1,0:T(1,128)}), f32[32,1,128]{2,1,0:T(1,128)S(1)}, u32[]{:S(2)}, u32[]{:S(2)}) async-start(f32[32,1,128]{2,1,0:T(1,128)} %get-tuple-element.42), calls=%async_computation.2 | async-start | bytes 32768 | tf_op jit(solution)/shard_map/column_sums/all_to_all | solution.py:499
  70.6 7.7 %by_clip.1 = (f32[16,96,512]{2,1,0:T(8,128)}, f32[1536,256]{1,0:T(8,128)S(1)}) custom-call(f32[1,128]{1,0:T(1,128)S(1)} %get-tuple-element.43.r_ref, bf16[2,1536,768]{2,1,0:T(8,128)(2,1)} %weights.1.p_ref.p_hbm, bf16[1536,256]{1,0:T(8,128)(2,1)} %get-tuple-element.44.v_hbm.v_ref, bf16[1536,256]{1,0:T(8,128)(2,1)} %get-tuple-element.45.g_hbm.g_ref), custom_call_target="tpu_custom_call" | custom-call | flops 3623878656 | bytes 14000000 | tf_op jit(solution)/shard_map/by_clip/pallas_call | solution.py:595
  78.4 0.8 all-to-all-done.2.c_got
  79.2 4.6 %clip_send.1 = (f32[784,256]{1,0:T(8,128)S(1)}, bf16[784,256]{1,0:T(8,128)(2,1)S(1)}) custom-call(f32[32,1,128]{2,1,0:T(1,128)S(1)} %all-to-all-done.2.c_got, f32[1,128]{1,0:T(1,128)S(1)} %get-tuple-element.43.r_ref, bf16[2,1536,768]{2,1,0:T(8,128)(2,1)} %weights.1.p_ref.p_hbm, bf16[1536,256]{1,0:T(8,128)(2,1)} %get-tuple-element.45.g_hbm.g_ref, ...), custom_call_target="tpu_custom_call" | custom-call | flops 1207959552 | bytes 10000000 | tf_op jit(solution)/shard_map/clip_send/pallas_call | solution.py:616
  83.8 1.9 %collective-permute-start = (bf16[784,256]{1,0:T(8,128)(2,1)S(1)}, bf16[784,256]{1,0:T(8,128)(2,1)S(1)}, u32[]{:S(2)}, u32[]{:S(2)}) collective-permute-start(bf16[784,256]{1,0:T(8,128)(2,1)S(1)} %get-tuple-element.52), channel_id=1, source_target_pairs={{0,1},{1,0},{2,3},{3,2},{4,5},{5,4},{6,7},{7,6},{8,9},{9,8},{10,11... | collective-permute-start | bytes 1204232 | tf_op jit(solution)/shard_map/clips_by_core/ppermute | solution.py:493
  85.8 3.0 %gloss_send.1 = (bf16[32,48,256]{2,1,0:T(8,128)(2,1)}, f32[1,128]{1,0:T(1,128)S(1)}) custom-call(f32[32,1,128]{2,1,0:T(1,128)S(1)} %all-to-all-done.2.c_got, f32[16,96,512]{2,1,0:T(8,128)} %get-tuple-element.63.by_clip), custom_call_target="tpu_custom_call" | custom-call | flops 2000000 | bytes 5000000 | tf_op jit(solution)/shard_map/gloss_send/pallas_call | solution.py:632
  88.8 9.0 %all-to-all-start.3 = ((bf16[32,48,256]{2,1,0:T(8,128)(2,1)}), bf16[32,48,256]{2,1,0:T(8,128)(2,1)S(1)}, u32[]{:S(2)}, u32[]{:S(2)}) async-start(bf16[32,48,256]{2,1,0:T(8,128)(2,1)} %get-tuple-element.71), calls=%async_computation.3 | async-start | bytes 1572864 | tf_op jit(solution)/shard_map/gloss_send/all_to_all | solution.py:499
  97.8 0.0 collective-permute-done.got
  97.8 0.7 clips_by_core.1
  98.5 2.5 %collective-permute-start.1 = (bf16[400,256]{1,0:T(8,128)(2,1)S(1)}, bf16[400,256]{1,0:T(8,128)(2,1)S(1)}, u32[]{:S(2)}, u32[]{:S(2)}) collective-permute-start(bf16[400,256]{1,0:T(8,128)(2,1)S(1)} %get-tuple-element.54), channel_id=1, source_target_pairs={{0,32},{32,0},{64,96},{96,64},{128,160},{160,128},{192,224},{224,1... | collective-permute-start | bytes 614408 | tf_op jit(solution)/shard_map/clips_by_z/ppermute | solution.py:496
  101.0 6.3 %collective-permute-done.1.got = bf16[400,256]{1,0:T(8,128)(2,1)S(1)} collective-permute-done((bf16[400,256]{1,0:T(8,128)(2,1)S(1)}, bf16[400,256]{1,0:T(8,128)(2,1)S(1)}, u32[]{:S(2)}, u32[]{:S(2)}) %collective-permute-start.1) | collective-permute-done | bytes 204832 | tf_op jit(solution)/shard_map/clips_by_z/ppermute | solution.py:496
  107.3 0.1 clips_by_z.1
  107.5 2.6 %collective-permute-start.2 = (bf16[112,256]{1,0:T(8,128)(2,1)S(1)}, bf16[112,256]{1,0:T(8,128)(2,1)S(1)}, u32[]{:S(2)}, u32[]{:S(2)}) collective-permute-start(bf16[112,256]{1,0:T(8,128)(2,1)S(1)} %get-tuple-element.59), channel_id=1, source_target_pairs={{0,64},{32,96},{64,0},{96,32},{128,192},{160,224},{192,128},{224,1... | collective-permute-start | bytes 172040 | tf_op jit(solution)/shard_map/video_grad/ppermute | solution.py:496
  110.1 5.5 %collective-permute-start.3 = (bf16[112,256]{1,0:T(8,128)(2,1)S(1)}, bf16[112,256]{1,0:T(8,128)(2,1)S(1)}, u32[]{:S(2)}, u32[]{:S(2)}) collective-permute-start(bf16[112,256]{1,0:T(8,128)(2,1)S(1)} %get-tuple-element.60), channel_id=1, source_target_pairs={{0,128},{32,160},{64,192},{96,224},{128,0},{160,32},{192,64},{224,... | collective-permute-start | bytes 172040 | tf_op jit(solution)/shard_map/video_grad/ppermute | solution.py:496
  115.5 4.2 %collective-permute-start.4 = (bf16[112,256]{1,0:T(8,128)(2,1)S(1)}, bf16[112,256]{1,0:T(8,128)(2,1)S(1)}, u32[]{:S(2)}, u32[]{:S(2)}) collective-permute-start(bf16[112,256]{1,0:T(8,128)(2,1)S(1)} %get-tuple-element.61), channel_id=1, source_target_pairs={{0,192},{32,224},{64,128},{96,160},{128,64},{160,96},{192,0},{224,... | collective-permute-start | bytes 172040 | tf_op jit(solution)/shard_map/video_grad/ppermute | solution.py:496
  119.7 0.6 diagonal.1
  120.3 0.0 collective-permute-done.2.got1
  120.3 0.0 collective-permute-done.3.got2
  120.3 3.4 %collective-permute-done.4.got3 = bf16[112,256]{1,0:T(8,128)(2,1)S(1)} collective-permute-done((bf16[112,256]{1,0:T(8,128)(2,1)S(1)}, bf16[112,256]{1,0:T(8,128)(2,1)S(1)}, u32[]{:S(2)}, u32[]{:S(2)}) %collective-permute-start.4) | collective-permute-done | bytes 57376 | tf_op jit(solution)/shard_map/video_grad/ppermute | solution.py:496
  123.7 0.8 video_grad.1
  124.5 0.8 gloss_grad.1
  (5 shorter events, 0.0 us)
Async XLA Ops:
  2.5 38.4 %all-to-all-start = ((bf16[32,48,256]{2,1,0:T(8,128)(2,1)}), bf16[32,48,256]{2,1,0:T(8,128)(2,1)S(1)}, u32[]{:S(2)}, u32[]{:S(2)}) async-start(bf16[32,48,256]{2,1,0:T(8,128)(2,1)} %get-tuple-element.39), calls=%async_computation | async-start | bytes 1572864 | tf_op jit(solution)/shard_map/gather/all_to_all | solution.py:499
  47.0 13.0 %all-to-all-start.1 = ((f32[16,1,128]{2,1,0:T(1,128)}), f32[16,1,128]{2,1,0:T(1,128)S(1)}, u32[]{:S(2)}, u32[]{:S(2)}) async-start(f32[16,1,128]{2,1,0:T(1,128)} %get-tuple-element.40), calls=%async_computation.1 | async-start | bytes 16384 | tf_op jit(solution)/shard_map/row_sums/all_to_all | solution.py:499
  60.7 18.4 %all-to-all-start.2 = ((f32[32,1,128]{2,1,0:T(1,128)}), f32[32,1,128]{2,1,0:T(1,128)S(1)}, u32[]{:S(2)}, u32[]{:S(2)}) async-start(f32[32,1,128]{2,1,0:T(1,128)} %get-tuple-element.42), calls=%async_computation.2 | async-start | bytes 32768 | tf_op jit(solution)/shard_map/column_sums/all_to_all | solution.py:499
  83.8 13.9 %collective-permute-start = (bf16[784,256]{1,0:T(8,128)(2,1)S(1)}, bf16[784,256]{1,0:T(8,128)(2,1)S(1)}, u32[]{:S(2)}, u32[]{:S(2)}) collective-permute-start(bf16[784,256]{1,0:T(8,128)(2,1)S(1)} %get-tuple-element.52), channel_id=1, source_target_pairs={{0,1},{1,0},{2,3},{3,2},{4,5},{5,4},{6,7},{7,6},{8,9},{9,8},{10,11... | collective-permute-start | bytes 1204232 | tf_op jit(solution)/shard_map/clips_by_core/ppermute | solution.py:493
  88.8 35.7 %all-to-all-start.3 = ((bf16[32,48,256]{2,1,0:T(8,128)(2,1)}), bf16[32,48,256]{2,1,0:T(8,128)(2,1)S(1)}, u32[]{:S(2)}, u32[]{:S(2)}) async-start(bf16[32,48,256]{2,1,0:T(8,128)(2,1)} %get-tuple-element.71), calls=%async_computation.3 | async-start | bytes 1572864 | tf_op jit(solution)/shard_map/gloss_send/all_to_all | solution.py:499
  98.5 8.8 %collective-permute-start.1 = (bf16[400,256]{1,0:T(8,128)(2,1)S(1)}, bf16[400,256]{1,0:T(8,128)(2,1)S(1)}, u32[]{:S(2)}, u32[]{:S(2)}) collective-permute-start(bf16[400,256]{1,0:T(8,128)(2,1)S(1)} %get-tuple-element.54), channel_id=1, source_target_pairs={{0,32},{32,0},{64,96},{96,64},{128,160},{160,128},{192,224},{224,1... | collective-permute-start | bytes 614408 | tf_op jit(solution)/shard_map/clips_by_z/ppermute | solution.py:496
  107.3 16.4 %copy-start = (bf16[3,32,256]{2,1,0:T(8,128)(2,1)S(1)}, bf16[3,32,256]{2,1,0:T(8,128)(2,1)}, u32[]{:S(2)}) copy-start(bf16[3,32,256]{2,1,0:T(8,128)(2,1)} %video.1) | copy-start | bytes 147460
  107.3 17.2 %copy-start.1 = (bf16[3,16,256]{2,1,0:T(8,128)(2,1)S(1)}, bf16[3,16,256]{2,1,0:T(8,128)(2,1)}, u32[]{:S(2)}) copy-start(bf16[3,16,256]{2,1,0:T(8,128)(2,1)} %gloss.1) | copy-start | bytes 73732
  107.5 12.9 %collective-permute-start.2 = (bf16[112,256]{1,0:T(8,128)(2,1)S(1)}, bf16[112,256]{1,0:T(8,128)(2,1)S(1)}, u32[]{:S(2)}, u32[]{:S(2)}) collective-permute-start(bf16[112,256]{1,0:T(8,128)(2,1)S(1)} %get-tuple-element.59), channel_id=1, source_target_pairs={{0,64},{32,96},{64,0},{96,32},{128,192},{160,224},{192,128},{224,1... | collective-permute-start | bytes 172040 | tf_op jit(solution)/shard_map/video_grad/ppermute | solution.py:496
  110.1 10.3 %collective-permute-start.3 = (bf16[112,256]{1,0:T(8,128)(2,1)S(1)}, bf16[112,256]{1,0:T(8,128)(2,1)S(1)}, u32[]{:S(2)}, u32[]{:S(2)}) collective-permute-start(bf16[112,256]{1,0:T(8,128)(2,1)S(1)} %get-tuple-element.60), channel_id=1, source_target_pairs={{0,128},{32,160},{64,192},{96,224},{128,0},{160,32},{192,64},{224,... | collective-permute-start | bytes 172040 | tf_op jit(solution)/shard_map/video_grad/ppermute | solution.py:496
  115.5 8.2 %collective-permute-start.4 = (bf16[112,256]{1,0:T(8,128)(2,1)S(1)}, bf16[112,256]{1,0:T(8,128)(2,1)S(1)}, u32[]{:S(2)}, u32[]{:S(2)}) collective-permute-start(bf16[112,256]{1,0:T(8,128)(2,1)S(1)} %get-tuple-element.61), channel_id=1, source_target_pairs={{0,192},{32,224},{64,128},{96,160},{128,64},{160,96},{192,0},{224,... | collective-permute-start | bytes 172040 | tf_op jit(solution)/shard_map/video_grad/ppermute | solution.py:496

commit v9 on v8

--- a/solution.py
+++ b/solution.py
@@ -27,6 +27,7 @@
 VOWN = FRAMES * OWN
 GOWN = GLOSSES * OWN
 EXTRA = 16
+V_PITCH, G_PITCH = VOWN + 8, GOWN + 8
 QUADS = GLOSSES // 4
 TILES = GROWS // LANES
 HALF = GROWS // 2
@@ -186,16 +187,20 @@
 ):
     results = ((v_out, v_hbm), (g_out, g_hbm))
     copies = [pltpu.make_async_copy(a, b, sems.at[i]) for i, (a, b) in enumerate(results)]
-    put(v_scr, pl.ds(0, VROWS), v_got[...].astype(F32))
+    for i in range(NZC):
+        put(v_scr, pl.ds(i * V_PITCH, VOWN), v_got[pl.ds(i * VOWN, VOWN), :].astype(F32))
     for f in range(FRAMES):
         parts = [
-            get(v_scr, pl.ds(k * NZ * VOWN + f * OWN + c, NZ, stride=VOWN)) for k in range(NCORE) for c in range(OWN)
+            get(v_scr, pl.ds(k * NZ * V_PITCH + f * OWN + c, NZ, stride=V_PITCH)) for k in range(NCORE) for c in range(OWN)
         ]
         v_out[pl.ds(f * CLIPS_DEV, CLIPS_DEV), :] = jnp.concatenate(parts, axis=0).astype(BF16)
     copies[0].start()
-    put(g_scr, pl.ds(0, NXY * GOWN), g_got[...].reshape(NXY * GOWN, WIDTH).astype(F32))
+    for i in range(NXY):
+        put(g_scr, pl.ds(i * G_PITCH, GOWN), g_got[i].astype(F32))
     for g in range(GLOSSES):
-        parts = [get(g_scr, pl.ds(x * NY * GOWN + g * OWN + c, NY, stride=GOWN)) for x in range(NX) for c in range(OWN)]
+        parts = [
+            get(g_scr, pl.ds(x * NY * G_PITCH + g * OWN + c, NY, stride=G_PITCH)) for x in range(NX) for c in range(OWN)
+        ]
         g_out[pl.ds(g * TEXTS_DEV, TEXTS_DEV), :] = jnp.concatenate(parts, axis=0).astype(BF16)
     copies[1].start()
 
@@ -372,22 +377,21 @@
             for x in range(NX):
                 for c in range(OWN):
                     first = (x * OWN + c) * NY
-                    put(scr, pl.ds(x * NY * GOWN + row + c, NY, stride=GOWN), block[first : first + NY])
-    out[...] = get(scr, pl.ds(0, NXY * GOWN)).astype(BF16).reshape(NXY, GOWN, WIDTH)
-
-
-def clip_send_kernel(c_got, r_ref, p_hbm, g_hbm, av_ref, mine, twin, p, g, g_by_text, sems):
-    g_copy = pltpu.make_async_copy(g_hbm, g, sems.at[4])
+                    put(scr, pl.ds(x * NY * G_PITCH + row + c, NY, stride=G_PITCH), block[first : first + NY])
+    for i in range(NXY):
+        out[i] = get(scr, pl.ds(i * G_PITCH, GOWN)).astype(BF16)
+
+
+def clip_send_kernel(c_got, r_ref, p_hbm, g, av_ref, mine, twin, p, g_by_text, sems):
     copies = []
     for (r, h, theirs), (_, _, here) in zip(halves_of(p_hbm), halves_of(p), strict=True):
         copies.append(pltpu.make_async_copy(theirs, here, sems.at[2 * r + h]))
-    started([g_copy, *copies])
+    started(copies)
     c_row = added(c_got)
     col = inverse_texts(c_row)
     core = lax.rem(lax.axis_index("inner"), NCORE)
     inverse = jnp.broadcast_to(1.0 / column_of(r_ref[...], CLIPS_DEV), (CLIPS_DEV, WIDTH))
     half = CLIPS_DEV // 2
-    g_copy.wait()
     for i in range(GLOSSES):
         at = pl.ds(i * TEXTS_DEV, TEXTS_DEV)
         g_by_text[at, :] = (g[at, :].astype(F32) * col).astype(BF16)
@@ -424,13 +428,13 @@
         at = pl.ds(i * step, step)
         two = mine[at, :] + got[at, :].astype(F32)
         for k in range(2):
-            put(scr, pl.ds(2 * i + k, NZ, stride=VOWN), two[k * NZ : (k + 1) * NZ])
+            put(scr, pl.ds(2 * i + k, NZ, stride=V_PITCH), two[k * NZ : (k + 1) * NZ])
     bit = lax.rem(own_z(), 2)
     owners = NZ // 2
     for i in range(owners):
         at = pl.ds(i * VOWN, VOWN)
-        keep[at, :] = get(scr, pl.ds(pl.multiple_of((owners * bit + i) * VOWN, VOWN), VOWN))
-        send[at, :] = get(scr, pl.ds(pl.multiple_of((owners * (1 - bit) + i) * VOWN, VOWN), VOWN)).astype(BF16)
+        keep[at, :] = get(scr, pl.ds(pl.multiple_of((owners * bit + i) * V_PITCH, 8), VOWN))
+        send[at, :] = get(scr, pl.ds(pl.multiple_of((owners * (1 - bit) + i) * V_PITCH, 8), VOWN)).astype(BF16)
     extra = loss_rows(mine, got, NZ)
     keep[pl.ds(owners * VOWN, EXTRA), :] = extra
     send[pl.ds(owners * VOWN, EXTRA), :] = extra.astype(BF16)
@@ -552,8 +556,8 @@
             scratch_shapes=[
                 pltpu.VMEM((VROWS, WIDTH), BF16),
                 pltpu.VMEM((GROWS, WIDTH), BF16),
-                two_halves(VROWS),
-                two_halves(NXY * GOWN),
+                two_halves(NZC * V_PITCH),
+                two_halves(NXY * G_PITCH),
                 pltpu.VMEM((VROWS, LANES), F32),
                 pltpu.VMEM((TILES, 1, LANES), F32),
                 pltpu.VMEM((VROWS, 3 * LANES), F32),
@@ -615,17 +619,16 @@
         v_rows = FRAMES * CLIPS_DEV // 2 + EXTRA
         mine, twin = pl.pallas_call(
             clip_send_kernel,
-            in_specs=[vmem, vmem, hbm, hbm, vmem],
+            in_specs=[vmem, vmem, hbm, vmem, vmem],
             out_shape=(shape(v_rows, WIDTH), shape(v_rows, WIDTH, dtype=BF16)),
             scratch_shapes=[
                 pltpu.VMEM((2, VROWS, HALF), BF16),
                 pltpu.VMEM((GROWS, WIDTH), BF16),
-                pltpu.VMEM((GROWS, WIDTH), BF16),
-                pltpu.SemaphoreType.DMA((5,)),
+                pltpu.SemaphoreType.DMA((4,)),
             ],
             compiler_params=params(),
             cost_estimate=cost(2 * VROWS * GROWS * WIDTH, 1e7),
-        )(c_got, r_row, *in_hbm(weights, g_all), av)
+        )(c_got, r_row, *in_hbm(weights), g_all, av)
 
     with jax.named_scope("gloss_send"):
         twin, c_ready = lax.optimization_barrier((twin, c_got))
@@ -635,7 +638,7 @@
             out_shape=(shape(NXY, GOWN, WIDTH, dtype=BF16), shape(1, LANES)),
             scratch_shapes=[
                 pltpu.VMEM((GLOSSES, TEXTS_DEV, 2 * WIDTH), F32),
-                two_halves(NXY * GOWN),
+                two_halves(NXY * G_PITCH),
                 pltpu.SemaphoreType.DMA((QUADS,)),
             ],
             compiler_params=params(),
@@ -652,7 +655,7 @@
             clip_rows_kernel,
             in_specs=[vmem] * 2,
             out_shape=kept_and_sent(NZ // 2),
-            scratch_shapes=[two_halves(NZ * VOWN)],
+            scratch_shapes=[two_halves(NZ * V_PITCH)],
             compiler_params=params(),
             cost_estimate=cost(1e6, 2e6),
         )(mine, to_core(twin))
@@ -675,6 +678,17 @@
             cost_estimate=cost(2e7, 3e5),
         )(counts, v_own, g_own)
 
+    with jax.named_scope("gloss_grad"):
+        grad_gloss = pl.pallas_call(
+            gloss_grad_kernel,
+            in_specs=[vmem] * 3,
+            out_shape=shape(OWN, GLOSSES, WIDTH),
+            scratch_shapes=[two_halves(GOWN)],
+            compiler_params=params(),
+            cost_estimate=cost(1e6, 1e6),
+        )(dg_got, dg_diag, gloss)
+    mine, grad_gloss = lax.optimization_barrier((mine, grad_gloss))
+
     with jax.named_scope("video_grad"):
         grad_video, loss = pl.pallas_call(
             functools.partial(video_grad_kernel, clips),
@@ -684,15 +698,6 @@
             compiler_params=params(),
             cost_estimate=cost(1e6, 1e6),
         )(mine, *[to_z(a, 2 * m) for m, a in enumerate(sent, start=1)], c_row, dv_diag, video)
-    with jax.named_scope("gloss_grad"):
-        grad_gloss = pl.pallas_call(
-            gloss_grad_kernel,
-            in_specs=[vmem] * 3,
-            out_shape=shape(OWN, GLOSSES, WIDTH),
-            scratch_shapes=[two_halves(GOWN)],
-            compiler_params=params(),
-            cost_estimate=cost(1e6, 1e6),
-        )(dg_got, dg_diag, gloss)
     return loss.reshape(()), grad_video, grad_gloss
 
 

time: 126 us -> 125 us (level)
  no operation moved by 1% of the time
where the time goes in v9:
time: 125 us; the launch traced here: 124 us
  starting transfers between devices  51.6 us (41%)
  Pallas kernels  31.9 us (26%)
  blocking collectives  28.2 us (23%)
  waiting for transfers between devices  11.5 us (9%)
    all_to_all x4, starting transfers between devices, exchanged(): lax.all_to_all(a, over_all, 0, 0, axis_index_groups=groups, tiled=True)  35 us
    all_gather x3, blocking collectives, gathered(): lax.all_gather(a, over_all, axis=0, axis_index_groups=groups, tiled=True)  28.2 us
    ppermute x4, starting transfers between devices, to_z(): lax.ppermute(a, 'outer', [(i, i ^ mask) for i in range(lax.axis_size('out...  14.7 us
    ppermute x4, waiting for transfers between devices, to_z(): lax.ppermute(a, 'outer', [(i, i ^ mask) for i in range(lax.axis_size('out...  8.85 us
    pallas_call x1, Pallas kernels, on_device(): pl.pallas_call(by_clip_kernel, grid=(2,), in_specs=[whole(1, LANES), pl.B...  8.04 us
    pallas_call x1, Pallas kernels, on_device(): pl.pallas_call(weights_kernel, in_specs=[hbm, hbm, vmem, vmem, vmem], out...  5.31 us
    pallas_call x1, Pallas kernels, on_device(): pl.pallas_call(forward_kernel, in_specs=[vmem] * 2, out_specs=[hbm] * 2 +...  5.25 us
    pallas_call x1, Pallas kernels, on_device(): pl.pallas_call(clip_send_kernel, in_specs=[vmem, vmem, hbm, vmem, vmem],...  5.21 us
  transfers between devices with their start and end apart: 9, of which 4 were waited for; matrix products, arithmetic and copies ran while one was open for 0% of the time, Pallas kernels for 15%

profile of v9, /device:TPU:2, one launch (start us, length us, event | category | flops | bytes accessed | tf_op | source)
XLA Modules:
  0.0 124.0 jit_solution(16056741170358782583)
XLA Ops:
  0.6 1.9 %unit_tokens.1 = (bf16[96,256]{1,0:T(8,128)(2,1)S(1)}, bf16[32,48,256]{2,1,0:T(8,128)(2,1)}, bf16[48,256]{1,0:T(8,128)(2,1)S(1)}, s32[8,128]{1,0:T(8,128)S(1)}) custom-call(s32[3]{0:T(128)} %fc_in.1, s32[3]{0:T(128)} %gc_in.1, bf16[3,32,256]{2,1,0:T(8,128)(2,1)} %video.1, bf16[3,16,256]{2,1,0:T(8,128)(2,1)} %gloss.1), custom_call_target="tpu_custom_call" | custom-call | flops 200000 | bytes 700000 | tf_op jit(solution)/shard_map/unit_tokens/pallas_call | solution.py:512
  2.5 10.3 %all-to-all-start = ((bf16[32,48,256]{2,1,0:T(8,128)(2,1)}), bf16[32,48,256]{2,1,0:T(8,128)(2,1)S(1)}, u32[]{:S(2)}, u32[]{:S(2)}) async-start(bf16[32,48,256]{2,1,0:T(8,128)(2,1)} %get-tuple-element.41), calls=%async_computation | async-start | bytes 1572864 | tf_op jit(solution)/shard_map/gather/all_to_all | solution.py:503
  12.8 19.5 %all_gather.9 = bf16[384,256]{1,0:T(8,128)(2,1)S(1)} all-gather(bf16[96,256]{1,0:T(8,128)(2,1)S(1)} %get-tuple-element.65.v_ref), channel_id=1, replica_groups={{0,64,128,192},{32,96,160,224},{1,65,129,193},{33,97,161,225},{2,66,130..., dimensions={0}, use_global_device_ids=true | all-gather | bytes 245760 | tf_op jit(solution)/shard_map/gather/all_gather | solution.py:506
  32.2 6.3 %all_gather.10 = bf16[768,256]{1,0:T(8,128)(2,1)S(1)} all-gather(bf16[384,256]{1,0:T(8,128)(2,1)S(1)} %all_gather.9), channel_id=1, replica_groups={{0,32},{64,96},{128,160},{192,224},{1,33},{65,97},{129,161},{193,225},{..., dimensions={0}, use_global_device_ids=true | all-gather | bytes 589824 | tf_op jit(solution)/shard_map/gather/all_gather | solution.py:506
  38.6 2.4 %all_gather.11.v_got = bf16[1536,256]{1,0:T(8,128)(2,1)S(1)} all-gather(bf16[768,256]{1,0:T(8,128)(2,1)S(1)} %all_gather.10), channel_id=1, replica_groups={{0,1},{32,33},{64,65},{96,97},{128,129},{160,161},{192,193},{224,225},{..., dimensions={0}, use_global_device_ids=true | all-gather | bytes 1179648 | tf_op jit(solution)/shard_map/gather/all_gather | solution.py:506
  40.9 0.0 all-to-all-done.g_got
  40.9 5.2 %forward.1 = (bf16[1536,256]{1,0:T(8,128)(2,1)}, bf16[1536,256]{1,0:T(8,128)(2,1)}, f32[1536,128]{1,0:T(8,128)S(1)}, f32[12,48,128]{2,1,0:T(8,128)S(1)}, f32[48,...) custom-call(bf16[1536,256]{1,0:T(8,128)(2,1)S(1)} %all_gather.11.v_got, ...), custom_call_target="tpu_custom_call" | custom-call | flops 1207959552 | bytes 8000000 | tf_op jit(solution)/shard_map/forward/pallas_call | solution.py:543
  46.2 5.5 %all-to-all-start.1 = ((f32[16,1,128]{2,1,0:T(1,128)}), f32[16,1,128]{2,1,0:T(1,128)S(1)}, u32[]{:S(2)}, u32[]{:S(2)}) async-start(f32[16,1,128]{2,1,0:T(1,128)} %get-tuple-element.42), calls=%async_computation.1 | async-start | bytes 16384 | tf_op jit(solution)/shard_map/row_sums/all_to_all | solution.py:503
  51.7 5.3 %weights.1.p_ref.p_hbm = bf16[2,1536,768]{2,1,0:T(8,128)(2,1)} custom-call(bf16[1536,256]{1,0:T(8,128)(2,1)} %get-tuple-element.46.v_hbm.v_ref, bf16[1536,256]{1,0:T(8,128)(2,1)} %get-tuple-element.47.g_hbm.g_ref.g, f32[1536,128]{1,0:T(8,128)S(1)} %get-tuple-element.48.row_ref, f32[12,48,128]{2,1,0:T(8,128)S(1)} %get-tuple-element.49.col_ref, ...), custom_call_target="tpu_custom_call" | custom-call | flops 1207959552 | bytes 12000000 | tf_op jit(solution)/shard_map/weights/pallas_call | solution.py:583
  57.0 2.2 %all-to-all-done.1.r_got = f32[16,1,128]{2,1,0:T(1,128)S(1)} async-done(((f32[16,1,128]{2,1,0:T(1,128)}), f32[16,1,128]{2,1,0:T(1,128)S(1)}, u32[]{:S(2)}, u32[]{:S(2)}) %all-to-all-start.1) | async-done | bytes 8224 | tf_op jit(solution)/shard_map/row_sums/all_to_all | solution.py:503
  59.2 0.7 row_sums.1
  59.9 9.9 %all-to-all-start.2 = ((f32[32,1,128]{2,1,0:T(1,128)}), f32[32,1,128]{2,1,0:T(1,128)S(1)}, u32[]{:S(2)}, u32[]{:S(2)}) async-start(f32[32,1,128]{2,1,0:T(1,128)} %get-tuple-element.44), calls=%async_computation.2 | async-start | bytes 32768 | tf_op jit(solution)/shard_map/column_sums/all_to_all | solution.py:503
  69.8 8.0 %by_clip.1 = (f32[16,96,512]{2,1,0:T(8,128)}, f32[1536,256]{1,0:T(8,128)S(1)}) custom-call(f32[1,128]{1,0:T(1,128)S(1)} %get-tuple-element.45.r_ref, bf16[2,1536,768]{2,1,0:T(8,128)(2,1)} %weights.1.p_ref.p_hbm, bf16[1536,256]{1,0:T(8,128)(2,1)} %get-tuple-element.46.v_hbm.v_ref, bf16[1536,256]{1,0:T(8,128)(2,1)} %get-tuple-element.47.g_hbm.g_ref.g), custom_call_target="tpu_custom_call" | custom-call | flops 3623878656 | bytes 14000000 | tf_op jit(solution)/shard_map/by_clip/pallas_call | solution.py:599
  77.9 0.5 all-to-all-done.2.c_got
  78.4 5.2 %clip_send.1 = (f32[784,256]{1,0:T(8,128)S(1)}, bf16[784,256]{1,0:T(8,128)(2,1)}) custom-call(f32[32,1,128]{2,1,0:T(1,128)S(1)} %all-to-all-done.2.c_got, f32[1,128]{1,0:T(1,128)S(1)} %get-tuple-element.45.r_ref, bf16[2,1536,768]{2,1,0:T(8,128)(2,1)} %weights.1.p_ref.p_hbm, bf16[1536,256]{1,0:T(8,128)(2,1)S(1)} %copy-done, ...), custom_call_target="tpu_custom_call" | custom-call | flops 1207959552 | bytes 10000000 | tf_op jit(solution)/shard_map/clip_send/pallas_call | solution.py:620
  83.6 1.9 %collective-permute-start = (bf16[784,256]{1,0:T(8,128)(2,1)}, bf16[784,256]{1,0:T(8,128)(2,1)S(1)}, u32[]{:S(2)}, u32[]{:S(2)}) collective-permute-start(bf16[784,256]{1,0:T(8,128)(2,1)} %get-tuple-element.54), channel_id=1, source_target_pairs={{0,1},{1,0},{2,3},{3,2},{4,5},{5,4},{6,7},{7,6},{8,9},{9,8},{10,11... | collective-permute-start | bytes 1204232 | tf_op jit(solution)/shard_map/clips_by_core/ppermute | solution.py:497
  85.5 2.9 %gloss_send.1 = (bf16[32,48,256]{2,1,0:T(8,128)(2,1)}, f32[1,128]{1,0:T(1,128)S(1)}) custom-call(f32[32,1,128]{2,1,0:T(1,128)S(1)} %all-to-all-done.2.c_got, f32[16,96,512]{2,1,0:T(8,128)} %get-tuple-element.62.by_clip), custom_call_target="tpu_custom_call" | custom-call | flops 2000000 | bytes 5000000 | tf_op jit(solution)/shard_map/gloss_send/pallas_call | solution.py:635
  88.5 9.3 %all-to-all-start.3 = ((bf16[32,48,256]{2,1,0:T(8,128)(2,1)}), bf16[32,48,256]{2,1,0:T(8,128)(2,1)S(1)}, u32[]{:S(2)}, u32[]{:S(2)}) async-start(bf16[32,48,256]{2,1,0:T(8,128)(2,1)} %get-tuple-element.63), calls=%async_computation.3 | async-start | bytes 1572864 | tf_op jit(solution)/shard_map/gloss_send/all_to_all | solution.py:503
  97.8 0.0 collective-permute-done.got
  97.8 0.2 clips_by_core.1
  98.0 2.5 %collective-permute-start.1 = (bf16[400,256]{1,0:T(8,128)(2,1)S(1)}, bf16[400,256]{1,0:T(8,128)(2,1)S(1)}, u32[]{:S(2)}, u32[]{:S(2)}) collective-permute-start(bf16[400,256]{1,0:T(8,128)(2,1)S(1)} %get-tuple-element.56), channel_id=1, source_target_pairs={{0,32},{32,0},{64,96},{96,64},{128,160},{160,128},{192,224},{224,1... | collective-permute-start | bytes 614408 | tf_op jit(solution)/shard_map/clips_by_z/ppermute | solution.py:500
  100.5 6.3 %collective-permute-done.1.got = bf16[400,256]{1,0:T(8,128)(2,1)S(1)} collective-permute-done((bf16[400,256]{1,0:T(8,128)(2,1)S(1)}, bf16[400,256]{1,0:T(8,128)(2,1)S(1)}, u32[]{:S(2)}, u32[]{:S(2)}) %collective-permute-start.1) | collective-permute-done | bytes 204832 | tf_op jit(solution)/shard_map/clips_by_z/ppermute | solution.py:500
  106.8 0.1 clips_by_z.1
  107.0 2.6 %collective-permute-start.2 = (bf16[112,256]{1,0:T(8,128)(2,1)S(1)}, bf16[112,256]{1,0:T(8,128)(2,1)S(1)}, u32[]{:S(2)}, u32[]{:S(2)}) collective-permute-start(bf16[112,256]{1,0:T(8,128)(2,1)S(1)} %get-tuple-element.69), channel_id=1, source_target_pairs={{0,64},{32,96},{64,0},{96,32},{128,192},{160,224},{192,128},{224,1... | collective-permute-start | bytes 172040 | tf_op jit(solution)/shard_map/video_grad/ppermute | solution.py:500
  109.5 5.5 %collective-permute-start.3 = (bf16[112,256]{1,0:T(8,128)(2,1)S(1)}, bf16[112,256]{1,0:T(8,128)(2,1)S(1)}, u32[]{:S(2)}, u32[]{:S(2)}) collective-permute-start(bf16[112,256]{1,0:T(8,128)(2,1)S(1)} %get-tuple-element.70), channel_id=1, source_target_pairs={{0,128},{32,160},{64,192},{96,224},{128,0},{160,32},{192,64},{224,... | collective-permute-start | bytes 172040 | tf_op jit(solution)/shard_map/video_grad/ppermute | solution.py:500
  115.0 4.2 %collective-permute-start.4 = (bf16[112,256]{1,0:T(8,128)(2,1)S(1)}, bf16[112,256]{1,0:T(8,128)(2,1)S(1)}, u32[]{:S(2)}, u32[]{:S(2)}) collective-permute-start(bf16[112,256]{1,0:T(8,128)(2,1)S(1)} %get-tuple-element.71), channel_id=1, source_target_pairs={{0,192},{32,224},{64,128},{96,160},{128,64},{160,96},{192,0},{224,... | collective-permute-start | bytes 172040 | tf_op jit(solution)/shard_map/video_grad/ppermute | solution.py:500
  119.2 0.6 diagonal.1
  119.8 0.0 all-to-all-done.3.got
  119.8 0.8 gloss_grad.1
  120.7 0.0 collective-permute-done.2.got1
  120.7 2.5 %collective-permute-done.4.got3 = bf16[112,256]{1,0:T(8,128)(2,1)S(1)} collective-permute-done((bf16[112,256]{1,0:T(8,128)(2,1)S(1)}, bf16[112,256]{1,0:T(8,128)(2,1)S(1)}, u32[]{:S(2)}, u32[]{:S(2)}) %collective-permute-start.4) | collective-permute-done | bytes 57376 | tf_op jit(solution)/shard_map/video_grad/ppermute | solution.py:500
  123.2 0.8 video_grad.1
  (7 shorter events, 0.0 us)
Async XLA Ops:
  2.5 38.4 %all-to-all-start = ((bf16[32,48,256]{2,1,0:T(8,128)(2,1)}), bf16[32,48,256]{2,1,0:T(8,128)(2,1)S(1)}, u32[]{:S(2)}, u32[]{:S(2)}) async-start(bf16[32,48,256]{2,1,0:T(8,128)(2,1)} %get-tuple-element.41), calls=%async_computation | async-start | bytes 1572864 | tf_op jit(solution)/shard_map/gather/all_to_all | solution.py:503
  46.2 13.0 %all-to-all-start.1 = ((f32[16,1,128]{2,1,0:T(1,128)}), f32[16,1,128]{2,1,0:T(1,128)S(1)}, u32[]{:S(2)}, u32[]{:S(2)}) async-start(f32[16,1,128]{2,1,0:T(1,128)} %get-tuple-element.42), calls=%async_computation.1 | async-start | bytes 16384 | tf_op jit(solution)/shard_map/row_sums/all_to_all | solution.py:503
  59.9 18.4 %all-to-all-start.2 = ((f32[32,1,128]{2,1,0:T(1,128)}), f32[32,1,128]{2,1,0:T(1,128)S(1)}, u32[]{:S(2)}, u32[]{:S(2)}) async-start(f32[32,1,128]{2,1,0:T(1,128)} %get-tuple-element.44), calls=%async_computation.2 | async-start | bytes 32768 | tf_op jit(solution)/shard_map/column_sums/all_to_all | solution.py:503
  69.8 8.5 %copy-start = (bf16[1536,256]{1,0:T(8,128)(2,1)S(1)}, bf16[1536,256]{1,0:T(8,128)(2,1)}, u32[]{:S(2)}) copy-start(bf16[1536,256]{1,0:T(8,128)(2,1)} %get-tuple-element.47.g_hbm.g_ref.g) | copy-start | bytes 2359300
  83.6 14.2 %collective-permute-start = (bf16[784,256]{1,0:T(8,128)(2,1)}, bf16[784,256]{1,0:T(8,128)(2,1)S(1)}, u32[]{:S(2)}, u32[]{:S(2)}) collective-permute-start(bf16[784,256]{1,0:T(8,128)(2,1)} %get-tuple-element.54), channel_id=1, source_target_pairs={{0,1},{1,0},{2,3},{3,2},{4,5},{5,4},{6,7},{7,6},{8,9},{9,8},{10,11... | collective-permute-start | bytes 1204232 | tf_op jit(solution)/shard_map/clips_by_core/ppermute | solution.py:497
  88.5 31.4 %all-to-all-start.3 = ((bf16[32,48,256]{2,1,0:T(8,128)(2,1)}), bf16[32,48,256]{2,1,0:T(8,128)(2,1)S(1)}, u32[]{:S(2)}, u32[]{:S(2)}) async-start(bf16[32,48,256]{2,1,0:T(8,128)(2,1)} %get-tuple-element.63), calls=%async_computation.3 | async-start | bytes 1572864 | tf_op jit(solution)/shard_map/gloss_send/all_to_all | solution.py:503
  98.0 8.8 %collective-permute-start.1 = (bf16[400,256]{1,0:T(8,128)(2,1)S(1)}, bf16[400,256]{1,0:T(8,128)(2,1)S(1)}, u32[]{:S(2)}, u32[]{:S(2)}) collective-permute-start(bf16[400,256]{1,0:T(8,128)(2,1)S(1)} %get-tuple-element.56), channel_id=1, source_target_pairs={{0,32},{32,0},{64,96},{96,64},{128,160},{160,128},{192,224},{224,1... | collective-permute-start | bytes 614408 | tf_op jit(solution)/shard_map/clips_by_z/ppermute | solution.py:500
  106.8 13.0 %copy-start.2 = (bf16[3,16,256]{2,1,0:T(8,128)(2,1)S(1)}, bf16[3,16,256]{2,1,0:T(8,128)(2,1)}, u32[]{:S(2)}) copy-start(bf16[3,16,256]{2,1,0:T(8,128)(2,1)} %gloss.1) | copy-start | bytes 73732
  106.8 16.4 %copy-start.1 = (bf16[3,32,256]{2,1,0:T(8,128)(2,1)S(1)}, bf16[3,32,256]{2,1,0:T(8,128)(2,1)}, u32[]{:S(2)}) copy-start(bf16[3,32,256]{2,1,0:T(8,128)(2,1)} %video.1) | copy-start | bytes 147460
  107.0 13.7 %collective-permute-start.2 = (bf16[112,256]{1,0:T(8,128)(2,1)S(1)}, bf16[112,256]{1,0:T(8,128)(2,1)S(1)}, u32[]{:S(2)}, u32[]{:S(2)}) collective-permute-start(bf16[112,256]{1,0:T(8,128)(2,1)S(1)} %get-tuple-element.69), channel_id=1, source_target_pairs={{0,64},{32,96},{64,0},{96,32},{128,192},{160,224},{192,128},{224,1... | collective-permute-start | bytes 172040 | tf_op jit(solution)/shard_map/video_grad/ppermute | solution.py:500
  109.5 11.1 %collective-permute-start.3 = (bf16[112,256]{1,0:T(8,128)(2,1)S(1)}, bf16[112,256]{1,0:T(8,128)(2,1)S(1)}, u32[]{:S(2)}, u32[]{:S(2)}) collective-permute-start(bf16[112,256]{1,0:T(8,128)(2,1)S(1)} %get-tuple-element.70), channel_id=1, source_target_pairs={{0,128},{32,160},{64,192},{96,224},{128,0},{160,32},{192,64},{224,... | collective-permute-start | bytes 172040 | tf_op jit(solution)/shard_map/video_grad/ppermute | solution.py:500
  115.0 8.2 %collective-permute-start.4 = (bf16[112,256]{1,0:T(8,128)(2,1)S(1)}, bf16[112,256]{1,0:T(8,128)(2,1)S(1)}, u32[]{:S(2)}, u32[]{:S(2)}) collective-permute-start(bf16[112,256]{1,0:T(8,128)(2,1)S(1)} %get-tuple-element.71), channel_id=1, source_target_pairs={{0,192},{32,224},{64,128},{96,160},{128,64},{160,96},{192,0},{224,... | collective-permute-start | bytes 172040 | tf_op jit(solution)/shard_map/video_grad/ppermute | solution.py:500

commit v10 on v9

--- a/solution.py
+++ b/solution.py
@@ -51,6 +51,12 @@
 Z_QUADS, Z_PAIRS = z_groups((0, 2, 4, 6)), z_groups((0, 1))
 CORE_GROUPS = [[flat(x, z, y, c) for c in range(NCORE)] for x in range(NX) for y in range(NY) for z in range(NZ)]
 XY_GROUPS = [[flat(x, z, y, c) for x in range(NX) for y in range(NY)] for z in range(NZ) for c in range(NCORE)]
+HALF_GROUPS = [
+    [flat(2 * hi + lo, z, y, c) for hi in range(NX // 2) for y in range(NY)]
+    for lo in range(2)
+    for z in range(NZ)
+    for c in range(NCORE)
+]
 ZC_GROUPS = [[flat(x, z, y, c) for c in range(NCORE) for z in range(NZ)] for x in range(NX) for y in range(NY)]
 
 
@@ -318,15 +324,15 @@
     return total
 
 
-def row_sums_kernel(r_got, c_part, c_out, r_out):
+def row_sums_kernel(r_got, c_part, c_near, c_out, r_out):
     r_row = added(r_got)
     r_out[...] = r_row
     lane = iota((1, LANES), 1)
     logs = jnp.where(lane < CLIPS_DEV, jnp.log(jnp.where(lane < CLIPS_DEV, r_row, 1.0)), 0.0)
     logs = logs - jnp.where(lane == CLIPS_DEV, 2.0 * r_row, 0.0)
     total = jnp.sum(logs, axis=1, keepdims=True)
-    message = jnp.where(lane == TEXTS_DEV, total, c_part[...])
-    for i in range(NXY):
+    message = jnp.where(lane == TEXTS_DEV, total, c_part[...] + c_near[...])
+    for i in range(NXY // 2):
         c_out[i] = message
 
 
@@ -382,16 +388,18 @@
         out[i] = get(scr, pl.ds(i * G_PITCH, GOWN)).astype(BF16)
 
 
-def clip_send_kernel(c_got, r_ref, p_hbm, g, av_ref, mine, twin, p, g_by_text, sems):
+def clip_send_kernel(c_got, r_ref, p_hbm, g_hbm, av_ref, mine, twin, p, g, g_by_text, sems):
+    g_copy = pltpu.make_async_copy(g_hbm, g, sems.at[4])
     copies = []
     for (r, h, theirs), (_, _, here) in zip(halves_of(p_hbm), halves_of(p), strict=True):
         copies.append(pltpu.make_async_copy(theirs, here, sems.at[2 * r + h]))
-    started(copies)
+    started([g_copy, *copies])
     c_row = added(c_got)
     col = inverse_texts(c_row)
     core = lax.rem(lax.axis_index("inner"), NCORE)
     inverse = jnp.broadcast_to(1.0 / column_of(r_ref[...], CLIPS_DEV), (CLIPS_DEV, WIDTH))
     half = CLIPS_DEV // 2
+    g_copy.wait()
     for i in range(GLOSSES):
         at = pl.ds(i * TEXTS_DEV, TEXTS_DEV)
         g_by_text[at, :] = (g[at, :].astype(F32) * col).astype(BF16)
@@ -465,13 +473,14 @@
         out[c] = factor * d - factor * x * (inner / (WIDTH * mean_sq))
 
 
-def video_grad_kernel(clips, mine, got1, got2, got3, c_row, diag, video, out, loss, scr):
+def video_grad_kernel(clips, mine, got1, got2, got3, c_row, c_near, diag, video, out, loss, scr):
     at = pl.ds(0, VOWN)
     total = mine[at, :]
     for got in (got1, got2, got3):
         total = total + got[at, :].astype(F32)
     token_grads(total + diag[...], scr, video, out, FRAMES)
-    row_part = c_row[:, TEXTS_DEV : TEXTS_DEV + 1]
+    at_sum = pl.ds(TEXTS_DEV, 1)
+    row_part = c_row[:, at_sum] + c_near[:, at_sum]
     tail = pl.ds(VOWN, EXTRA)
     near = unpiece(mine[tail, :]) + unpiece(got1[tail, :].astype(F32))
     far = unpiece(got2[tail, :].astype(F32)) + unpiece(got3[tail, :].astype(F32))
@@ -498,6 +507,9 @@
 
     def to_z(a, mask):
         return lax.ppermute(a, "outer", [(i, i ^ mask) for i in range(lax.axis_size("outer"))])
+
+    def to_near_x(a):
+        return lax.ppermute(a, "outer", [(i, i ^ NZ) for i in range(lax.axis_size("outer"))])
 
     def exchanged(a, groups):
         return lax.all_to_all(a, over_all, 0, 0, axis_index_groups=groups, tiled=True)
@@ -571,13 +583,13 @@
     with jax.named_scope("row_sums"):
         c_send, r_row = pl.pallas_call(
             row_sums_kernel,
-            in_specs=[vmem] * 2,
-            out_shape=(shape(NXY, 1, LANES), shape(1, LANES)),
+            in_specs=[vmem] * 3,
+            out_shape=(shape(NXY // 2, 1, LANES), shape(1, LANES)),
             compiler_params=params(),
             cost_estimate=cost(1e5, 3e5),
-        )(exchanged(r_part, ZC_GROUPS), c_part)
+        )(exchanged(r_part, ZC_GROUPS), c_part, to_near_x(c_part))
     with jax.named_scope("column_sums"):
-        c_got = exchanged(c_send, XY_GROUPS)
+        c_got = exchanged(c_send, HALF_GROUPS)
 
     with jax.named_scope("weights"):
         weights = pl.pallas_call(
@@ -619,16 +631,17 @@
         v_rows = FRAMES * CLIPS_DEV // 2 + EXTRA
         mine, twin = pl.pallas_call(
             clip_send_kernel,
-            in_specs=[vmem, vmem, hbm, vmem, vmem],
+            in_specs=[vmem, vmem, hbm, hbm, vmem],
             out_shape=(shape(v_rows, WIDTH), shape(v_rows, WIDTH, dtype=BF16)),
             scratch_shapes=[
                 pltpu.VMEM((2, VROWS, HALF), BF16),
                 pltpu.VMEM((GROWS, WIDTH), BF16),
-                pltpu.SemaphoreType.DMA((4,)),
+                pltpu.VMEM((GROWS, WIDTH), BF16),
+                pltpu.SemaphoreType.DMA((5,)),
             ],
             compiler_params=params(),
             cost_estimate=cost(2 * VROWS * GROWS * WIDTH, 1e7),
-        )(c_got, r_row, *in_hbm(weights), g_all, av)
+        )(c_got, r_row, *in_hbm(weights, g_all), av)
 
     with jax.named_scope("gloss_send"):
         twin, c_ready = lax.optimization_barrier((twin, c_got))
@@ -692,12 +705,12 @@
     with jax.named_scope("video_grad"):
         grad_video, loss = pl.pallas_call(
             functools.partial(video_grad_kernel, clips),
-            in_specs=[vmem] * 7,
+            in_specs=[vmem] * 8,
             out_shape=(shape(OWN, FRAMES, WIDTH), shape(1, 1)),
             scratch_shapes=[two_halves(VOWN)],
             compiler_params=params(),
             cost_estimate=cost(1e6, 1e6),
-        )(mine, *[to_z(a, 2 * m) for m, a in enumerate(sent, start=1)], c_row, dv_diag, video)
+        )(mine, *[to_z(a, 2 * m) for m, a in enumerate(sent, start=1)], c_row, to_near_x(c_row), dv_diag, video)
     return loss.reshape(()), grad_video, grad_gloss
 
 

time: 125 us -> 127 us (1.016)
  starting transfers between devices: 51.6 us -> 56.6 us
  waiting for transfers between devices: 11.5 us -> 9.44 us
    ppermute x0 -> x2, starting transfers between devices: none -> 4.72 us  [to_near_x(): lax.ppermute(a, 'outer', [(i, i ^ NZ) for i in range(lax.axis_size('outer...]
    ppermute x4, waiting for transfers between devices: 8.85 us -> 5.71 us  [to_z(): lax.ppermute(a, 'outer', [(i, i ^ mask) for i in range(lax.axis_size('out...]
    ppermute x0 -> x2, waiting for transfers between devices: none -> 1.56 us  [to_near_x(): lax.ppermute(a, 'outer', [(i, i ^ NZ) for i in range(lax.axis_size('outer...]
    ppermute x4, starting transfers between devices: 14.7 us -> 16 us  [to_z(): lax.ppermute(a, 'outer', [(i, i ^ mask) for i in range(lax.axis_size('out...]
  transfers between devices with their start and end apart: 9 -> 11, of which waited for: 4 -> 4; matrix products, arithmetic and copies ran while one was open for 0% -> 0% of each run, Pallas kernels for 15% -> 14%
where the time goes in v10:
time: 127 us; the launch traced here: 126 us
  starting transfers between devices  56.6 us (45%)
  Pallas kernels  31 us (24%)
  blocking collectives  28.2 us (22%)
  waiting for transfers between devices  9.44 us (7%)
    all_to_all x4, starting transfers between devices, exchanged(): lax.all_to_all(a, over_all, 0, 0, axis_index_groups=groups, tiled=True)  33.9 us
    all_gather x3, blocking collectives, gathered(): lax.all_gather(a, over_all, axis=0, axis_index_groups=groups, tiled=True)  28.2 us
    ppermute x4, starting transfers between devices, to_z(): lax.ppermute(a, 'outer', [(i, i ^ mask) for i in range(lax.axis_size('out...  16 us
    pallas_call x1, Pallas kernels, on_device(): pl.pallas_call(by_clip_kernel, grid=(2,), in_specs=[whole(1, LANES), pl.B...  7.72 us
    ppermute x4, waiting for transfers between devices, to_z(): lax.ppermute(a, 'outer', [(i, i ^ mask) for i in range(lax.axis_size('out...  5.71 us
    pallas_call x1, Pallas kernels, on_device(): pl.pallas_call(weights_kernel, in_specs=[hbm, hbm, vmem, vmem, vmem], out...  5.32 us
    pallas_call x1, Pallas kernels, on_device(): pl.pallas_call(forward_kernel, in_specs=[vmem] * 2, out_specs=[hbm] * 2 +...  5.24 us
    ppermute x2, starting transfers between devices, to_near_x(): lax.ppermute(a, 'outer', [(i, i ^ NZ) for i in range(lax.axis_size('outer...  4.72 us
  transfers between devices with their start and end apart: 11, of which 4 were waited for; matrix products, arithmetic and copies ran while one was open for 0% of the time, Pallas kernels for 14%

profile of v10, /device:TPU:2, one launch (start us, length us, event | category | flops | bytes accessed | tf_op | source)
XLA Modules:
  0.0 126.0 jit_solution(12096445440363133629)
XLA Ops:
  0.6 1.9 %unit_tokens.1 = (bf16[96,256]{1,0:T(8,128)(2,1)S(1)}, bf16[32,48,256]{2,1,0:T(8,128)(2,1)}, bf16[48,256]{1,0:T(8,128)(2,1)S(1)}, s32[8,128]{1,0:T(8,128)S(1)}) custom-call(s32[3]{0:T(128)} %fc_in.1, s32[3]{0:T(128)} %gc_in.1, bf16[3,32,256]{2,1,0:T(8,128)(2,1)} %video.1, bf16[3,16,256]{2,1,0:T(8,128)(2,1)} %gloss.1), custom_call_target="tpu_custom_call" | custom-call | flops 200000 | bytes 700000 | tf_op jit(solution)/shard_map/unit_tokens/pallas_call | solution.py:524
  2.5 10.3 %all-to-all-start = ((bf16[32,48,256]{2,1,0:T(8,128)(2,1)}), bf16[32,48,256]{2,1,0:T(8,128)(2,1)S(1)}, u32[]{:S(2)}, u32[]{:S(2)}) async-start(bf16[32,48,256]{2,1,0:T(8,128)(2,1)} %get-tuple-element.41), calls=%async_computation | async-start | bytes 1572864 | tf_op jit(solution)/shard_map/gather/all_to_all | solution.py:515
  12.8 19.5 %all_gather.9 = bf16[384,256]{1,0:T(8,128)(2,1)S(1)} all-gather(bf16[96,256]{1,0:T(8,128)(2,1)S(1)} %get-tuple-element.65.v_ref), channel_id=1, replica_groups={{0,64,128,192},{32,96,160,224},{1,65,129,193},{33,97,161,225},{2,66,130..., dimensions={0}, use_global_device_ids=true | all-gather | bytes 245760 | tf_op jit(solution)/shard_map/gather/all_gather | solution.py:518
  32.3 6.3 %all_gather.10 = bf16[768,256]{1,0:T(8,128)(2,1)S(1)} all-gather(bf16[384,256]{1,0:T(8,128)(2,1)S(1)} %all_gather.9), channel_id=1, replica_groups={{0,32},{64,96},{128,160},{192,224},{1,33},{65,97},{129,161},{193,225},{..., dimensions={0}, use_global_device_ids=true | all-gather | bytes 589824 | tf_op jit(solution)/shard_map/gather/all_gather | solution.py:518
  38.6 2.4 %all_gather.11.v_got = bf16[1536,256]{1,0:T(8,128)(2,1)S(1)} all-gather(bf16[768,256]{1,0:T(8,128)(2,1)S(1)} %all_gather.10), channel_id=1, replica_groups={{0,1},{32,33},{64,65},{96,97},{128,129},{160,161},{192,193},{224,225},{..., dimensions={0}, use_global_device_ids=true | all-gather | bytes 1179648 | tf_op jit(solution)/shard_map/gather/all_gather | solution.py:518
  41.0 0.0 all-to-all-done.g_got
  41.0 5.2 %forward.1 = (bf16[1536,256]{1,0:T(8,128)(2,1)}, bf16[1536,256]{1,0:T(8,128)(2,1)}, f32[1536,128]{1,0:T(8,128)S(1)}, f32[12,48,128]{2,1,0:T(8,128)S(1)}, f32[48,...) custom-call(bf16[1536,256]{1,0:T(8,128)(2,1)S(1)} %all_gather.11.v_got, ...), custom_call_target="tpu_custom_call" | custom-call | flops 1207959552 | bytes 8000000 | tf_op jit(solution)/shard_map/forward/pallas_call | solution.py:555
  46.2 5.5 %all-to-all-start.1 = ((f32[16,1,128]{2,1,0:T(1,128)}), f32[16,1,128]{2,1,0:T(1,128)S(1)}, u32[]{:S(2)}, u32[]{:S(2)}) async-start(f32[16,1,128]{2,1,0:T(1,128)} %get-tuple-element.42), calls=%async_computation.1 | async-start | bytes 16384 | tf_op jit(solution)/shard_map/row_sums/all_to_all | solution.py:515
  51.7 2.3 %collective-permute-start = (f32[1,128]{1,0:T(1,128)S(1)}, f32[1,128]{1,0:T(1,128)S(1)}, u32[]{:S(2)}, u32[]{:S(2)}) collective-permute-start(f32[1,128]{1,0:T(1,128)S(1)} %get-tuple-element.43.c_part), channel_id=1, source_target_pairs={{0,256},{32,288},{64,320},{96,352},{128,384},{160,416},{192,448},{... | collective-permute-start | bytes 1544 | tf_op jit(solution)/shard_map/row_sums/ppermute | solution.py:512
  54.0 5.3 %weights.1.p_ref.p_hbm = bf16[2,1536,768]{2,1,0:T(8,128)(2,1)} custom-call(bf16[1536,256]{1,0:T(8,128)(2,1)} %get-tuple-element.46.v_hbm.v_ref, bf16[1536,256]{1,0:T(8,128)(2,1)} %get-tuple-element.47.g_hbm.g_ref, f32[1536,128]{1,0:T(8,128)S(1)} %get-tuple-element.48.row_ref, f32[12,48,128]{2,1,0:T(8,128)S(1)} %get-tuple-element.49.col_ref, ...), custom_call_target="tpu_custom_call" | custom-call | flops 1207959552 | bytes 12000000 | tf_op jit(solution)/shard_map/weights/pallas_call | solution.py:595
  59.3 0.0 collective-permute-done.c_near
  59.4 0.7 row_sums.1
  60.1 8.9 %all-to-all-start.2 = ((f32[16,1,128]{2,1,0:T(1,128)}), f32[16,1,128]{2,1,0:T(1,128)S(1)}, u32[]{:S(2)}, u32[]{:S(2)}) async-start(f32[16,1,128]{2,1,0:T(1,128)} %get-tuple-element.44), calls=%async_computation.2 | async-start | bytes 16384 | tf_op jit(solution)/shard_map/column_sums/all_to_all | solution.py:515
  68.9 7.7 %by_clip.1 = (f32[16,96,512]{2,1,0:T(8,128)}, f32[1536,256]{1,0:T(8,128)S(1)}) custom-call(f32[1,128]{1,0:T(1,128)S(1)} %get-tuple-element.45.r_ref, bf16[2,1536,768]{2,1,0:T(8,128)(2,1)} %weights.1.p_ref.p_hbm, bf16[1536,256]{1,0:T(8,128)(2,1)} %get-tuple-element.46.v_hbm.v_ref, bf16[1536,256]{1,0:T(8,128)(2,1)} %get-tuple-element.47.g_hbm.g_ref), custom_call_target="tpu_custom_call" | custom-call | flops 3623878656 | bytes 14000000 | tf_op jit(solution)/shard_map/by_clip/pallas_call | solution.py:611
  76.6 2.2 %all-to-all-done.2.c_got = f32[16,1,128]{2,1,0:T(1,128)S(1)} async-done(((f32[16,1,128]{2,1,0:T(1,128)}), f32[16,1,128]{2,1,0:T(1,128)S(1)}, u32[]{:S(2)}, u32[]{:S(2)}) %all-to-all-start.2) | async-done | bytes 8224 | tf_op jit(solution)/shard_map/column_sums/all_to_all | solution.py:515
  78.8 4.6 %clip_send.1 = (f32[784,256]{1,0:T(8,128)S(1)}, bf16[784,256]{1,0:T(8,128)(2,1)S(1)}) custom-call(f32[16,1,128]{2,1,0:T(1,128)S(1)} %all-to-all-done.2.c_got, f32[1,128]{1,0:T(1,128)S(1)} %get-tuple-element.45.r_ref, bf16[2,1536,768]{2,1,0:T(8,128)(2,1)} %weights.1.p_ref.p_hbm, bf16[1536,256]{1,0:T(8,128)(2,1)} %get-tuple-element.47.g_hbm.g_ref, ...), custom_call_target="tpu_custom_call" | custom-call | flops 1207959552 | bytes 10000000 | tf_op jit(solution)/shard_map/clip_send/pallas_call | solution.py:632
  83.5 1.9 %collective-permute-start.1 = (bf16[784,256]{1,0:T(8,128)(2,1)S(1)}, bf16[784,256]{1,0:T(8,128)(2,1)S(1)}, u32[]{:S(2)}, u32[]{:S(2)}) collective-permute-start(bf16[784,256]{1,0:T(8,128)(2,1)S(1)} %get-tuple-element.54), channel_id=1, source_target_pairs={{0,1},{1,0},{2,3},{3,2},{4,5},{5,4},{6,7},{7,6},{8,9},{9,8},{10,11... | collective-permute-start | bytes 1204232 | tf_op jit(solution)/shard_map/clips_by_core/ppermute | solution.py:506
  85.4 2.9 %gloss_send.1 = (bf16[32,48,256]{2,1,0:T(8,128)(2,1)}, f32[1,128]{1,0:T(1,128)S(1)}) custom-call(f32[16,1,128]{2,1,0:T(1,128)S(1)} %all-to-all-done.2.c_got, f32[16,96,512]{2,1,0:T(8,128)} %get-tuple-element.62.by_clip), custom_call_target="tpu_custom_call" | custom-call | flops 2000000 | bytes 5000000 | tf_op jit(solution)/shard_map/gloss_send/pallas_call | solution.py:648
  88.3 9.3 %all-to-all-start.3 = ((bf16[32,48,256]{2,1,0:T(8,128)(2,1)}), bf16[32,48,256]{2,1,0:T(8,128)(2,1)S(1)}, u32[]{:S(2)}, u32[]{:S(2)}) async-start(bf16[32,48,256]{2,1,0:T(8,128)(2,1)} %get-tuple-element.63), calls=%async_computation.3 | async-start | bytes 1572864 | tf_op jit(solution)/shard_map/gloss_send/all_to_all | solution.py:515
  97.6 0.2 clips_by_core.1
  97.9 3.8 %collective-permute-start.2 = (bf16[400,256]{1,0:T(8,128)(2,1)S(1)}, bf16[400,256]{1,0:T(8,128)(2,1)S(1)}, u32[]{:S(2)}, u32[]{:S(2)}) collective-permute-start(bf16[400,256]{1,0:T(8,128)(2,1)S(1)} %get-tuple-element.56), channel_id=1, source_target_pairs={{0,32},{32,0},{64,96},{96,64},{128,160},{160,128},{192,224},{224,1... | collective-permute-start | bytes 614408 | tf_op jit(solution)/shard_map/clips_by_z/ppermute | solution.py:509
  101.7 5.2 %collective-permute-done.2.got = bf16[400,256]{1,0:T(8,128)(2,1)S(1)} collective-permute-done((bf16[400,256]{1,0:T(8,128)(2,1)S(1)}, bf16[400,256]{1,0:T(8,128)(2,1)S(1)}, u32[]{:S(2)}, u32[]{:S(2)}) %collective-permute-start.2) | collective-permute-done | bytes 204832 | tf_op jit(solution)/shard_map/clips_by_z/ppermute | solution.py:509
  106.9 0.1 clips_by_z.1
  107.0 4.5 %collective-permute-start.3 = (bf16[112,256]{1,0:T(8,128)(2,1)S(1)}, bf16[112,256]{1,0:T(8,128)(2,1)S(1)}, u32[]{:S(2)}, u32[]{:S(2)}) collective-permute-start(bf16[112,256]{1,0:T(8,128)(2,1)S(1)} %get-tuple-element.69), channel_id=1, source_target_pairs={{0,64},{32,96},{64,0},{96,32},{128,192},{160,224},{192,128},{224,1... | collective-permute-start | bytes 172040 | tf_op jit(solution)/shard_map/video_grad/ppermute | solution.py:509
  111.5 5.5 %collective-permute-start.4 = (bf16[112,256]{1,0:T(8,128)(2,1)S(1)}, bf16[112,256]{1,0:T(8,128)(2,1)S(1)}, u32[]{:S(2)}, u32[]{:S(2)}) collective-permute-start(bf16[112,256]{1,0:T(8,128)(2,1)S(1)} %get-tuple-element.70), channel_id=1, source_target_pairs={{0,128},{32,160},{64,192},{96,224},{128,0},{160,32},{192,64},{224,... | collective-permute-start | bytes 172040 | tf_op jit(solution)/shard_map/video_grad/ppermute | solution.py:509
  117.0 2.2 %collective-permute-start.5 = (bf16[112,256]{1,0:T(8,128)(2,1)S(1)}, bf16[112,256]{1,0:T(8,128)(2,1)S(1)}, u32[]{:S(2)}, u32[]{:S(2)}) collective-permute-start(bf16[112,256]{1,0:T(8,128)(2,1)S(1)} %get-tuple-element.71), channel_id=1, source_target_pairs={{0,192},{32,224},{64,128},{96,160},{128,64},{160,96},{192,0},{224,... | collective-permute-start | bytes 172040 | tf_op jit(solution)/shard_map/video_grad/ppermute | solution.py:509
  119.2 2.4 %collective-permute-start.6 = (f32[1,128]{1,0:T(1,128)S(1)}, f32[1,128]{1,0:T(1,128)S(1)}, u32[]{:S(2)}, u32[]{:S(2)}) collective-permute-start(f32[1,128]{1,0:T(1,128)S(1)} %get-tuple-element.72.c_row), channel_id=1, source_target_pairs={{0,256},{32,288},{64,320},{96,352},{128,384},{160,416},{192,448},{... | collective-permute-start | bytes 1544 | tf_op jit(solution)/shard_map/video_grad/ppermute | solution.py:512
  121.7 0.6 diagonal.1
  122.3 0.8 gloss_grad.1
  123.1 1.6 %collective-permute-done.6.c_near = f32[1,128]{1,0:T(1,128)S(1)} collective-permute-done((f32[1,128]{1,0:T(1,128)S(1)}, f32[1,128]{1,0:T(1,128)S(1)}, u32[]{:S(2)}, u32[]{:S(2)}) %collective-permute-start.6) | collective-permute-done | bytes 544 | tf_op jit(solution)/shard_map/video_grad/ppermute | solution.py:512
  124.7 0.5 collective-permute-done.5.got3
  125.2 0.8 video_grad.1
  (9 shorter events, 0.0 us)
Async XLA Ops:
  2.5 38.4 %all-to-all-start = ((bf16[32,48,256]{2,1,0:T(8,128)(2,1)}), bf16[32,48,256]{2,1,0:T(8,128)(2,1)S(1)}, u32[]{:S(2)}, u32[]{:S(2)}) async-start(bf16[32,48,256]{2,1,0:T(8,128)(2,1)} %get-tuple-element.41), calls=%async_computation | async-start | bytes 1572864 | tf_op jit(solution)/shard_map/gather/all_to_all | solution.py:515
  46.2 13.1 %all-to-all-start.1 = ((f32[16,1,128]{2,1,0:T(1,128)}), f32[16,1,128]{2,1,0:T(1,128)S(1)}, u32[]{:S(2)}, u32[]{:S(2)}) async-start(f32[16,1,128]{2,1,0:T(1,128)} %get-tuple-element.42), calls=%async_computation.1 | async-start | bytes 16384 | tf_op jit(solution)/shard_map/row_sums/all_to_all | solution.py:515
  51.7 7.6 %collective-permute-start = (f32[1,128]{1,0:T(1,128)S(1)}, f32[1,128]{1,0:T(1,128)S(1)}, u32[]{:S(2)}, u32[]{:S(2)}) collective-permute-start(f32[1,128]{1,0:T(1,128)S(1)} %get-tuple-element.43.c_part), channel_id=1, source_target_pairs={{0,256},{32,288},{64,320},{96,352},{128,384},{160,416},{192,448},{... | collective-permute-start | bytes 1544 | tf_op jit(solution)/shard_map/row_sums/ppermute | solution.py:512
  60.1 18.7 %all-to-all-start.2 = ((f32[16,1,128]{2,1,0:T(1,128)}), f32[16,1,128]{2,1,0:T(1,128)S(1)}, u32[]{:S(2)}, u32[]{:S(2)}) async-start(f32[16,1,128]{2,1,0:T(1,128)} %get-tuple-element.44), calls=%async_computation.2 | async-start | bytes 16384 | tf_op jit(solution)/shard_map/column_sums/all_to_all | solution.py:515
  83.5 14.2 %collective-permute-start.1 = (bf16[784,256]{1,0:T(8,128)(2,1)S(1)}, bf16[784,256]{1,0:T(8,128)(2,1)S(1)}, u32[]{:S(2)}, u32[]{:S(2)}) collective-permute-start(bf16[784,256]{1,0:T(8,128)(2,1)S(1)} %get-tuple-element.54), channel_id=1, source_target_pairs={{0,1},{1,0},{2,3},{3,2},{4,5},{5,4},{6,7},{7,6},{8,9},{9,8},{10,11... | collective-permute-start | bytes 1204232 | tf_op jit(solution)/shard_map/clips_by_core/ppermute | solution.py:506
  88.3 33.9 %all-to-all-start.3 = ((bf16[32,48,256]{2,1,0:T(8,128)(2,1)}), bf16[32,48,256]{2,1,0:T(8,128)(2,1)S(1)}, u32[]{:S(2)}, u32[]{:S(2)}) async-start(bf16[32,48,256]{2,1,0:T(8,128)(2,1)} %get-tuple-element.63), calls=%async_computation.3 | async-start | bytes 1572864 | tf_op jit(solution)/shard_map/gloss_send/all_to_all | solution.py:515
  97.9 9.0 %collective-permute-start.2 = (bf16[400,256]{1,0:T(8,128)(2,1)S(1)}, bf16[400,256]{1,0:T(8,128)(2,1)S(1)}, u32[]{:S(2)}, u32[]{:S(2)}) collective-permute-start(bf16[400,256]{1,0:T(8,128)(2,1)S(1)} %get-tuple-element.56), channel_id=1, source_target_pairs={{0,32},{32,0},{64,96},{96,64},{128,160},{160,128},{192,224},{224,1... | collective-permute-start | bytes 614408 | tf_op jit(solution)/shard_map/clips_by_z/ppermute | solution.py:509
  106.9 15.4 %copy-start.1 = (bf16[3,16,256]{2,1,0:T(8,128)(2,1)S(1)}, bf16[3,16,256]{2,1,0:T(8,128)(2,1)}, u32[]{:S(2)}) copy-start(bf16[3,16,256]{2,1,0:T(8,128)(2,1)} %gloss.1) | copy-start | bytes 73732
  106.9 18.4 %copy-start = (bf16[3,32,256]{2,1,0:T(8,128)(2,1)S(1)}, bf16[3,32,256]{2,1,0:T(8,128)(2,1)}, u32[]{:S(2)}) copy-start(bf16[3,32,256]{2,1,0:T(8,128)(2,1)} %video.1) | copy-start | bytes 147460
  107.0 17.7 %collective-permute-start.3 = (bf16[112,256]{1,0:T(8,128)(2,1)S(1)}, bf16[112,256]{1,0:T(8,128)(2,1)S(1)}, u32[]{:S(2)}, u32[]{:S(2)}) collective-permute-start(bf16[112,256]{1,0:T(8,128)(2,1)S(1)} %get-tuple-element.69), channel_id=1, source_target_pairs={{0,64},{32,96},{64,0},{96,32},{128,192},{160,224},{192,128},{224,1... | collective-permute-start | bytes 172040 | tf_op jit(solution)/shard_map/video_grad/ppermute | solution.py:509
  111.5 13.1 %collective-permute-start.4 = (bf16[112,256]{1,0:T(8,128)(2,1)S(1)}, bf16[112,256]{1,0:T(8,128)(2,1)S(1)}, u32[]{:S(2)}, u32[]{:S(2)}) collective-permute-start(bf16[112,256]{1,0:T(8,128)(2,1)S(1)} %get-tuple-element.70), channel_id=1, source_target_pairs={{0,128},{32,160},{64,192},{96,224},{128,0},{160,32},{192,64},{224,... | collective-permute-start | bytes 172040 | tf_op jit(solution)/shard_map/video_grad/ppermute | solution.py:509
  117.0 8.2 %collective-permute-start.5 = (bf16[112,256]{1,0:T(8,128)(2,1)S(1)}, bf16[112,256]{1,0:T(8,128)(2,1)S(1)}, u32[]{:S(2)}, u32[]{:S(2)}) collective-permute-start(bf16[112,256]{1,0:T(8,128)(2,1)S(1)} %get-tuple-element.71), channel_id=1, source_target_pairs={{0,192},{32,224},{64,128},{96,160},{128,64},{160,96},{192,0},{224,... | collective-permute-start | bytes 172040 | tf_op jit(solution)/shard_map/video_grad/ppermute | solution.py:509
  119.2 5.4 %collective-permute-start.6 = (f32[1,128]{1,0:T(1,128)S(1)}, f32[1,128]{1,0:T(1,128)S(1)}, u32[]{:S(2)}, u32[]{:S(2)}) collective-permute-start(f32[1,128]{1,0:T(1,128)S(1)} %get-tuple-element.72.c_row), channel_id=1, source_target_pairs={{0,256},{32,288},{64,320},{96,352},{128,384},{160,416},{192,448},{... | collective-permute-start | bytes 1544 | tf_op jit(solution)/shard_map/video_grad/ppermute | solution.py:512

commit v11 on v9

--- a/solution.py
+++ b/solution.py
@@ -246,7 +246,9 @@
         mask = frame_mask[at, :]
         total = unpacked_sum(*[rows[at, pl.ds(k * LANES, LANES)] for k in range(3)])
         total = jnp.where(real, total, 1.0)
-        video_part = video_part + mask * jnp.log(total)
+        product = jnp.where(mask > 0.0, total, 1.0) * (1.0 if f % 4 == 0 else product)
+        if f % 4 == 3:
+            video_part = video_part + jnp.log(product)
         row_out[at, :] = jnp.where(mask > 0.0, 1.0 / (total * frames), FAR)
     video_part = video_part / frames - jnp.log(glosses)
     gloss_parts = [jnp.zeros((CLIPS_DEV, LANES), F32)] * 3
@@ -291,12 +293,15 @@
 
 
 def weights_kernel(v_hbm, g_hbm, row_ref, col_ref, e_ref, p_hbm, v, g, p, sems):
-    loads = started([pltpu.make_async_copy(a, b, sems.at[i]) for i, (a, b) in enumerate(((v_hbm, v), (g_hbm, g)))])
+    firsts = [pl.ds(0, VROWS // 2), pl.ds(VROWS // 2, VROWS // 2)]
+    order = ((v_hbm, v, 0), (g_hbm, g, 0), (g_hbm, g, 1), (v_hbm, v, 1))
+    loads = started([pltpu.make_async_copy(a.at[firsts[i]], b.at[firsts[i]], sems.at[k]) for k, (a, b, i) in enumerate(order)])
     scales = packed(2.5 * e_ref[...])
-    for load in loads:
-        load.wait()
     stores = []
     for (r, h, out), (_, _, here) in zip(halves_of(p_hbm), halves_of(p), strict=True):
+        for load in loads[: 2 if r + h == 0 else 1]:
+            load.wait()
+        loads = loads[2 if r + h == 0 else 1 :]
         e = exp_scores(v[pl.ds(r * VROWS // 2, VROWS // 2), :], g[pl.ds(h * HALF, HALF), :])
         for f in range(FRAMES // 2):
             row = packed(row_ref[pl.ds((r * FRAMES // 2 + f) * CLIPS_DEV, CLIPS_DEV), :])
@@ -306,7 +311,9 @@
                 share = jnp.maximum(row[k % 3] + col_ref[h * TILES // 2 + k], 0.0)
                 parts.append(scales[k % 3] * block[:, k * LANES : (k + 1) * LANES] * share)
             here[pl.ds(f * CLIPS_DEV, CLIPS_DEV), :] = jnp.concatenate(parts, axis=1).astype(BF16)
-        stores += started([pltpu.make_async_copy(here, out, sems.at[2 + 2 * r + h])])
+            if f % 8 == 7:
+                at = pl.ds((f - 7) * CLIPS_DEV, 8 * CLIPS_DEV)
+                stores += started([pltpu.make_async_copy(here.at[at], out.at[at], sems.at[4 + 4 * r + 2 * h + f // 8])])
     for store in stores:
         store.wait()
 
@@ -382,16 +389,18 @@
         out[i] = get(scr, pl.ds(i * G_PITCH, GOWN)).astype(BF16)
 
 
-def clip_send_kernel(c_got, r_ref, p_hbm, g, av_ref, mine, twin, p, g_by_text, sems):
+def clip_send_kernel(c_got, r_ref, p_hbm, g_hbm, av_ref, mine, twin, p, g, g_by_text, sems):
+    g_copy = pltpu.make_async_copy(g_hbm, g, sems.at[4])
     copies = []
     for (r, h, theirs), (_, _, here) in zip(halves_of(p_hbm), halves_of(p), strict=True):
         copies.append(pltpu.make_async_copy(theirs, here, sems.at[2 * r + h]))
-    started(copies)
+    started([g_copy, *copies])
     c_row = added(c_got)
     col = inverse_texts(c_row)
     core = lax.rem(lax.axis_index("inner"), NCORE)
     inverse = jnp.broadcast_to(1.0 / column_of(r_ref[...], CLIPS_DEV), (CLIPS_DEV, WIDTH))
     half = CLIPS_DEV // 2
+    g_copy.wait()
     for i in range(GLOSSES):
         at = pl.ds(i * TEXTS_DEV, TEXTS_DEV)
         g_by_text[at, :] = (g[at, :].astype(F32) * col).astype(BF16)
@@ -589,7 +598,7 @@
                 pltpu.VMEM((VROWS, WIDTH), BF16),
                 pltpu.VMEM((GROWS, WIDTH), BF16),
                 pltpu.VMEM((2, VROWS, HALF), BF16),
-                pltpu.SemaphoreType.DMA((6,)),
+                pltpu.SemaphoreType.DMA((12,)),
             ],
             compiler_params=params(),
             cost_estimate=cost(2 * VROWS * GROWS * WIDTH, 12e6, VROWS * GROWS),
@@ -619,16 +628,17 @@
         v_rows = FRAMES * CLIPS_DEV // 2 + EXTRA
         mine, twin = pl.pallas_call(
             clip_send_kernel,
-            in_specs=[vmem, vmem, hbm, vmem, vmem],
+            in_specs=[vmem, vmem, hbm, hbm, vmem],
             out_shape=(shape(v_rows, WIDTH), shape(v_rows, WIDTH, dtype=BF16)),
             scratch_shapes=[
                 pltpu.VMEM((2, VROWS, HALF), BF16),
                 pltpu.VMEM((GROWS, WIDTH), BF16),
-                pltpu.SemaphoreType.DMA((4,)),
+                pltpu.VMEM((GROWS, WIDTH), BF16),
+                pltpu.SemaphoreType.DMA((5,)),
             ],
             compiler_params=params(),
             cost_estimate=cost(2 * VROWS * GROWS * WIDTH, 1e7),
-        )(c_got, r_row, *in_hbm(weights), g_all, av)
+        )(c_got, r_row, *in_hbm(weights, g_all), av)
 
     with jax.named_scope("gloss_send"):
         twin, c_ready = lax.optimization_barrier((twin, c_got))

time: 125 us -> 123 us (0.984)
  transfers between devices with their start and end apart: 9 -> 9, of which waited for: 4 -> 4; matrix products, arithmetic and copies ran while one was open for 0% -> 0% of each run, Pallas kernels for 15% -> 14%
where the time goes in v11:
time: 123 us
  starting transfers between devices  51.3 us (42%)
  Pallas kernels  30.7 us (25%)
  blocking collectives  28.2 us (23%)
  waiting for transfers between devices  11.9 us (10%)
    all_to_all x4, starting transfers between devices, exchanged(): lax.all_to_all(a, over_all, 0, 0, axis_index_groups=groups, tiled=True)  34.6 us
    all_gather x3, blocking collectives, gathered(): lax.all_gather(a, over_all, axis=0, axis_index_groups=groups, tiled=True)  28.2 us
    ppermute x4, starting transfers between devices, to_z(): lax.ppermute(a, 'outer', [(i, i ^ mask) for i in range(lax.axis_size('out...  14.7 us
    ppermute x4, waiting for transfers between devices, to_z(): lax.ppermute(a, 'outer', [(i, i ^ mask) for i in range(lax.axis_size('out...  8.71 us
    pallas_call x1, Pallas kernels, on_device(): pl.pallas_call(by_clip_kernel, grid=(2,), in_specs=[whole(1, LANES), pl.B...  7.71 us
    pallas_call x1, Pallas kernels, on_device(): pl.pallas_call(weights_kernel, in_specs=[hbm, hbm, vmem, vmem, vmem], out...  5.18 us
    pallas_call x1, Pallas kernels, on_device(): pl.pallas_call(forward_kernel, in_specs=[vmem] * 2, out_specs=[hbm] * 2 +...  5.09 us
    pallas_call x1, Pallas kernels, on_device(): pl.pallas_call(clip_send_kernel, in_specs=[vmem, vmem, hbm, hbm, vmem], o...  4.65 us
  transfers between devices with their start and end apart: 9, of which 4 were waited for; matrix products, arithmetic and copies ran while one was open for 0% of the time, Pallas kernels for 14%

profile of v11, /device:TPU:2, one launch (start us, length us, event | category | flops | bytes accessed | tf_op | source)
XLA Modules:
  0.0 122.8 jit_solution(17373527987010813897)
XLA Ops:
  0.6 1.9 %unit_tokens.1 = (bf16[96,256]{1,0:T(8,128)(2,1)S(1)}, bf16[32,48,256]{2,1,0:T(8,128)(2,1)}, bf16[48,256]{1,0:T(8,128)(2,1)S(1)}, s32[8,128]{1,0:T(8,128)S(1)}) custom-call(s32[3]{0:T(128)} %fc_in.1, s32[3]{0:T(128)} %gc_in.1, bf16[3,32,256]{2,1,0:T(8,128)(2,1)} %video.1, bf16[3,16,256]{2,1,0:T(8,128)(2,1)} %gloss.1), custom_call_target="tpu_custom_call" | custom-call | flops 200000 | bytes 700000 | tf_op jit(solution)/shard_map/unit_tokens/pallas_call | solution.py:521
  2.5 10.3 %all-to-all-start = ((bf16[32,48,256]{2,1,0:T(8,128)(2,1)}), bf16[32,48,256]{2,1,0:T(8,128)(2,1)S(1)}, u32[]{:S(2)}, u32[]{:S(2)}) async-start(bf16[32,48,256]{2,1,0:T(8,128)(2,1)} %get-tuple-element.41), calls=%async_computation | async-start | bytes 1572864 | tf_op jit(solution)/shard_map/gather/all_to_all | solution.py:512
  12.8 19.5 %all_gather.9 = bf16[384,256]{1,0:T(8,128)(2,1)S(1)} all-gather(bf16[96,256]{1,0:T(8,128)(2,1)S(1)} %get-tuple-element.65.v_ref), channel_id=1, replica_groups={{0,64,128,192},{32,96,160,224},{1,65,129,193},{33,97,161,225},{2,66,130..., dimensions={0}, use_global_device_ids=true | all-gather | bytes 245760 | tf_op jit(solution)/shard_map/gather/all_gather | solution.py:515
  32.3 6.3 %all_gather.10 = bf16[768,256]{1,0:T(8,128)(2,1)S(1)} all-gather(bf16[384,256]{1,0:T(8,128)(2,1)S(1)} %all_gather.9), channel_id=1, replica_groups={{0,32},{64,96},{128,160},{192,224},{1,33},{65,97},{129,161},{193,225},{..., dimensions={0}, use_global_device_ids=true | all-gather | bytes 589824 | tf_op jit(solution)/shard_map/gather/all_gather | solution.py:515
  38.6 2.4 %all_gather.11.v_got = bf16[1536,256]{1,0:T(8,128)(2,1)S(1)} all-gather(bf16[768,256]{1,0:T(8,128)(2,1)S(1)} %all_gather.10), channel_id=1, replica_groups={{0,1},{32,33},{64,65},{96,97},{128,129},{160,161},{192,193},{224,225},{..., dimensions={0}, use_global_device_ids=true | all-gather | bytes 1179648 | tf_op jit(solution)/shard_map/gather/all_gather | solution.py:515
  40.9 0.0 all-to-all-done.g_got
  41.0 5.1 %forward.1 = (bf16[1536,256]{1,0:T(8,128)(2,1)}, bf16[1536,256]{1,0:T(8,128)(2,1)}, f32[1536,128]{1,0:T(8,128)S(1)}, f32[12,48,128]{2,1,0:T(8,128)S(1)}, f32[48,...) custom-call(bf16[1536,256]{1,0:T(8,128)(2,1)S(1)} %all_gather.11.v_got, ...), custom_call_target="tpu_custom_call" | custom-call | flops 1207959552 | bytes 8000000 | tf_op jit(solution)/shard_map/forward/pallas_call | solution.py:552
  46.0 5.5 %all-to-all-start.1 = ((f32[16,1,128]{2,1,0:T(1,128)}), f32[16,1,128]{2,1,0:T(1,128)S(1)}, u32[]{:S(2)}, u32[]{:S(2)}) async-start(f32[16,1,128]{2,1,0:T(1,128)} %get-tuple-element.42), calls=%async_computation.1 | async-start | bytes 16384 | tf_op jit(solution)/shard_map/row_sums/all_to_all | solution.py:512
  51.5 5.2 %weights.1.p_ref.p_hbm = bf16[2,1536,768]{2,1,0:T(8,128)(2,1)} custom-call(bf16[1536,256]{1,0:T(8,128)(2,1)} %get-tuple-element.46.v_hbm.v_ref, bf16[1536,256]{1,0:T(8,128)(2,1)} %get-tuple-element.47.g_hbm.g_ref, f32[1536,128]{1,0:T(8,128)S(1)} %get-tuple-element.48.row_ref, f32[12,48,128]{2,1,0:T(8,128)S(1)} %get-tuple-element.49.col_ref, ...), custom_call_target="tpu_custom_call" | custom-call | flops 1207959552 | bytes 12000000 | tf_op jit(solution)/shard_map/weights/pallas_call | solution.py:592
  56.7 2.3 %all-to-all-done.1.r_got = f32[16,1,128]{2,1,0:T(1,128)S(1)} async-done(((f32[16,1,128]{2,1,0:T(1,128)}), f32[16,1,128]{2,1,0:T(1,128)S(1)}, u32[]{:S(2)}, u32[]{:S(2)}) %all-to-all-start.1) | async-done | bytes 8224 | tf_op jit(solution)/shard_map/row_sums/all_to_all | solution.py:512
  59.0 0.7 row_sums.1
  59.8 9.9 %all-to-all-start.2 = ((f32[32,1,128]{2,1,0:T(1,128)}), f32[32,1,128]{2,1,0:T(1,128)S(1)}, u32[]{:S(2)}, u32[]{:S(2)}) async-start(f32[32,1,128]{2,1,0:T(1,128)} %get-tuple-element.44), calls=%async_computation.2 | async-start | bytes 32768 | tf_op jit(solution)/shard_map/column_sums/all_to_all | solution.py:512
  69.7 7.7 %by_clip.1 = (f32[16,96,512]{2,1,0:T(8,128)}, f32[1536,256]{1,0:T(8,128)S(1)}) custom-call(f32[1,128]{1,0:T(1,128)S(1)} %get-tuple-element.45.r_ref, bf16[2,1536,768]{2,1,0:T(8,128)(2,1)} %weights.1.p_ref.p_hbm, bf16[1536,256]{1,0:T(8,128)(2,1)} %get-tuple-element.46.v_hbm.v_ref, bf16[1536,256]{1,0:T(8,128)(2,1)} %get-tuple-element.47.g_hbm.g_ref), custom_call_target="tpu_custom_call" | custom-call | flops 3623878656 | bytes 14000000 | tf_op jit(solution)/shard_map/by_clip/pallas_call | solution.py:608
  77.4 0.8 all-to-all-done.2.c_got
  78.2 4.6 %clip_send.1 = (f32[784,256]{1,0:T(8,128)S(1)}, bf16[784,256]{1,0:T(8,128)(2,1)S(1)}) custom-call(f32[32,1,128]{2,1,0:T(1,128)S(1)} %all-to-all-done.2.c_got, f32[1,128]{1,0:T(1,128)S(1)} %get-tuple-element.45.r_ref, bf16[2,1536,768]{2,1,0:T(8,128)(2,1)} %weights.1.p_ref.p_hbm, bf16[1536,256]{1,0:T(8,128)(2,1)} %get-tuple-element.47.g_hbm.g_ref, ...), custom_call_target="tpu_custom_call" | custom-call | flops 1207959552 | bytes 10000000 | tf_op jit(solution)/shard_map/clip_send/pallas_call | solution.py:629
  82.9 1.9 %collective-permute-start = (bf16[784,256]{1,0:T(8,128)(2,1)S(1)}, bf16[784,256]{1,0:T(8,128)(2,1)S(1)}, u32[]{:S(2)}, u32[]{:S(2)}) collective-permute-start(bf16[784,256]{1,0:T(8,128)(2,1)S(1)} %get-tuple-element.54), channel_id=1, source_target_pairs={{0,1},{1,0},{2,3},{3,2},{4,5},{5,4},{6,7},{7,6},{8,9},{9,8},{10,11... | collective-permute-start | bytes 1204232 | tf_op jit(solution)/shard_map/clips_by_core/ppermute | solution.py:506
  84.8 3.0 %gloss_send.1 = (bf16[32,48,256]{2,1,0:T(8,128)(2,1)}, f32[1,128]{1,0:T(1,128)S(1)}) custom-call(f32[32,1,128]{2,1,0:T(1,128)S(1)} %all-to-all-done.2.c_got, f32[16,96,512]{2,1,0:T(8,128)} %get-tuple-element.62.by_clip), custom_call_target="tpu_custom_call" | custom-call | flops 2000000 | bytes 5000000 | tf_op jit(solution)/shard_map/gloss_send/pallas_call | solution.py:645
  87.7 9.0 %all-to-all-start.3 = ((bf16[32,48,256]{2,1,0:T(8,128)(2,1)}), bf16[32,48,256]{2,1,0:T(8,128)(2,1)S(1)}, u32[]{:S(2)}, u32[]{:S(2)}) async-start(bf16[32,48,256]{2,1,0:T(8,128)(2,1)} %get-tuple-element.63), calls=%async_computation.3 | async-start | bytes 1572864 | tf_op jit(solution)/shard_map/gloss_send/all_to_all | solution.py:512
  96.7 0.2 clips_by_core.1
  97.0 2.5 %collective-permute-start.1 = (bf16[400,256]{1,0:T(8,128)(2,1)S(1)}, bf16[400,256]{1,0:T(8,128)(2,1)S(1)}, u32[]{:S(2)}, u32[]{:S(2)}) collective-permute-start(bf16[400,256]{1,0:T(8,128)(2,1)S(1)} %get-tuple-element.56), channel_id=1, source_target_pairs={{0,32},{32,0},{64,96},{96,64},{128,160},{160,128},{192,224},{224,1... | collective-permute-start | bytes 614408 | tf_op jit(solution)/shard_map/clips_by_z/ppermute | solution.py:509
  99.5 6.3 %collective-permute-done.1.got = bf16[400,256]{1,0:T(8,128)(2,1)S(1)} collective-permute-done((bf16[400,256]{1,0:T(8,128)(2,1)S(1)}, bf16[400,256]{1,0:T(8,128)(2,1)S(1)}, u32[]{:S(2)}, u32[]{:S(2)}) %collective-permute-start.1) | collective-permute-done | bytes 204832 | tf_op jit(solution)/shard_map/clips_by_z/ppermute | solution.py:509
  105.8 0.1 clips_by_z.1
  105.9 2.5 %collective-permute-start.2 = (bf16[112,256]{1,0:T(8,128)(2,1)S(1)}, bf16[112,256]{1,0:T(8,128)(2,1)S(1)}, u32[]{:S(2)}, u32[]{:S(2)}) collective-permute-start(bf16[112,256]{1,0:T(8,128)(2,1)S(1)} %get-tuple-element.69), channel_id=1, source_target_pairs={{0,64},{32,96},{64,0},{96,32},{128,192},{160,224},{192,128},{224,1... | collective-permute-start | bytes 172040 | tf_op jit(solution)/shard_map/video_grad/ppermute | solution.py:509
  108.4 5.4 %collective-permute-start.3 = (bf16[112,256]{1,0:T(8,128)(2,1)S(1)}, bf16[112,256]{1,0:T(8,128)(2,1)S(1)}, u32[]{:S(2)}, u32[]{:S(2)}) collective-permute-start(bf16[112,256]{1,0:T(8,128)(2,1)S(1)} %get-tuple-element.70), channel_id=1, source_target_pairs={{0,128},{32,160},{64,192},{96,224},{128,0},{160,32},{192,64},{224,... | collective-permute-start | bytes 172040 | tf_op jit(solution)/shard_map/video_grad/ppermute | solution.py:509
  113.8 4.3 %collective-permute-start.4 = (bf16[112,256]{1,0:T(8,128)(2,1)S(1)}, bf16[112,256]{1,0:T(8,128)(2,1)S(1)}, u32[]{:S(2)}, u32[]{:S(2)}) collective-permute-start(bf16[112,256]{1,0:T(8,128)(2,1)S(1)} %get-tuple-element.71), channel_id=1, source_target_pairs={{0,192},{32,224},{64,128},{96,160},{128,64},{160,96},{192,0},{224,... | collective-permute-start | bytes 172040 | tf_op jit(solution)/shard_map/video_grad/ppermute | solution.py:509
  118.2 0.6 diagonal.1
  118.8 0.0 all-to-all-done.3.got
  118.8 0.8 gloss_grad.1
  119.6 0.0 collective-permute-done.2.got1
  119.6 0.0 collective-permute-done.3.got2
  119.6 2.4 %collective-permute-done.4.got3 = bf16[112,256]{1,0:T(8,128)(2,1)S(1)} collective-permute-done((bf16[112,256]{1,0:T(8,128)(2,1)S(1)}, bf16[112,256]{1,0:T(8,128)(2,1)S(1)}, u32[]{:S(2)}, u32[]{:S(2)}) %collective-permute-start.4) | collective-permute-done | bytes 57376 | tf_op jit(solution)/shard_map/video_grad/ppermute | solution.py:509
  122.0 0.8 video_grad.1
  (5 shorter events, 0.0 us)
Async XLA Ops:
  2.5 38.4 %all-to-all-start = ((bf16[32,48,256]{2,1,0:T(8,128)(2,1)}), bf16[32,48,256]{2,1,0:T(8,128)(2,1)S(1)}, u32[]{:S(2)}, u32[]{:S(2)}) async-start(bf16[32,48,256]{2,1,0:T(8,128)(2,1)} %get-tuple-element.41), calls=%async_computation | async-start | bytes 1572864 | tf_op jit(solution)/shard_map/gather/all_to_all | solution.py:512
  46.0 13.0 %all-to-all-start.1 = ((f32[16,1,128]{2,1,0:T(1,128)}), f32[16,1,128]{2,1,0:T(1,128)S(1)}, u32[]{:S(2)}, u32[]{:S(2)}) async-start(f32[16,1,128]{2,1,0:T(1,128)} %get-tuple-element.42), calls=%async_computation.1 | async-start | bytes 16384 | tf_op jit(solution)/shard_map/row_sums/all_to_all | solution.py:512
  59.8 18.4 %all-to-all-start.2 = ((f32[32,1,128]{2,1,0:T(1,128)}), f32[32,1,128]{2,1,0:T(1,128)S(1)}, u32[]{:S(2)}, u32[]{:S(2)}) async-start(f32[32,1,128]{2,1,0:T(1,128)} %get-tuple-element.44), calls=%async_computation.2 | async-start | bytes 32768 | tf_op jit(solution)/shard_map/column_sums/all_to_all | solution.py:512
  82.9 13.9 %collective-permute-start = (bf16[784,256]{1,0:T(8,128)(2,1)S(1)}, bf16[784,256]{1,0:T(8,128)(2,1)S(1)}, u32[]{:S(2)}, u32[]{:S(2)}) collective-permute-start(bf16[784,256]{1,0:T(8,128)(2,1)S(1)} %get-tuple-element.54), channel_id=1, source_target_pairs={{0,1},{1,0},{2,3},{3,2},{4,5},{5,4},{6,7},{7,6},{8,9},{9,8},{10,11... | collective-permute-start | bytes 1204232 | tf_op jit(solution)/shard_map/clips_by_core/ppermute | solution.py:506
  87.7 31.0 %all-to-all-start.3 = ((bf16[32,48,256]{2,1,0:T(8,128)(2,1)}), bf16[32,48,256]{2,1,0:T(8,128)(2,1)S(1)}, u32[]{:S(2)}, u32[]{:S(2)}) async-start(bf16[32,48,256]{2,1,0:T(8,128)(2,1)} %get-tuple-element.63), calls=%async_computation.3 | async-start | bytes 1572864 | tf_op jit(solution)/shard_map/gloss_send/all_to_all | solution.py:512
  97.0 8.8 %collective-permute-start.1 = (bf16[400,256]{1,0:T(8,128)(2,1)S(1)}, bf16[400,256]{1,0:T(8,128)(2,1)S(1)}, u32[]{:S(2)}, u32[]{:S(2)}) collective-permute-start(bf16[400,256]{1,0:T(8,128)(2,1)S(1)} %get-tuple-element.56), channel_id=1, source_target_pairs={{0,32},{32,0},{64,96},{96,64},{128,160},{160,128},{192,224},{224,1... | collective-permute-start | bytes 614408 | tf_op jit(solution)/shard_map/clips_by_z/ppermute | solution.py:509
  105.8 13.0 %copy-start.1 = (bf16[3,16,256]{2,1,0:T(8,128)(2,1)S(1)}, bf16[3,16,256]{2,1,0:T(8,128)(2,1)}, u32[]{:S(2)}) copy-start(bf16[3,16,256]{2,1,0:T(8,128)(2,1)} %gloss.1) | copy-start | bytes 73732
  105.8 16.2 %copy-start = (bf16[3,32,256]{2,1,0:T(8,128)(2,1)S(1)}, bf16[3,32,256]{2,1,0:T(8,128)(2,1)}, u32[]{:S(2)}) copy-start(bf16[3,32,256]{2,1,0:T(8,128)(2,1)} %video.1) | copy-start | bytes 147460
  105.9 13.7 %collective-permute-start.2 = (bf16[112,256]{1,0:T(8,128)(2,1)S(1)}, bf16[112,256]{1,0:T(8,128)(2,1)S(1)}, u32[]{:S(2)}, u32[]{:S(2)}) collective-permute-start(bf16[112,256]{1,0:T(8,128)(2,1)S(1)} %get-tuple-element.69), channel_id=1, source_target_pairs={{0,64},{32,96},{64,0},{96,32},{128,192},{160,224},{192,128},{224,1... | collective-permute-start | bytes 172040 | tf_op jit(solution)/shard_map/video_grad/ppermute | solution.py:509
  108.4 11.2 %collective-permute-start.3 = (bf16[112,256]{1,0:T(8,128)(2,1)S(1)}, bf16[112,256]{1,0:T(8,128)(2,1)S(1)}, u32[]{:S(2)}, u32[]{:S(2)}) collective-permute-start(bf16[112,256]{1,0:T(8,128)(2,1)S(1)} %get-tuple-element.70), channel_id=1, source_target_pairs={{0,128},{32,160},{64,192},{96,224},{128,0},{160,32},{192,64},{224,... | collective-permute-start | bytes 172040 | tf_op jit(solution)/shard_map/video_grad/ppermute | solution.py:509
  113.8 8.2 %collective-permute-start.4 = (bf16[112,256]{1,0:T(8,128)(2,1)S(1)}, bf16[112,256]{1,0:T(8,128)(2,1)S(1)}, u32[]{:S(2)}, u32[]{:S(2)}) collective-permute-start(bf16[112,256]{1,0:T(8,128)(2,1)S(1)} %get-tuple-element.71), channel_id=1, source_target_pairs={{0,192},{32,224},{64,128},{96,160},{128,64},{160,96},{192,0},{224,... | collective-permute-start | bytes 172040 | tf_op jit(solution)/shard_map/video_grad/ppermute | solution.py:509

commit v12 on v11

--- a/solution.py
+++ b/solution.py
@@ -119,8 +119,8 @@
     return jnp.concatenate([ref[0, at, :], ref[1, at, :]], axis=1)
 
 
-def two_halves(rows):
-    return pltpu.VMEM((2, rows, LANES), F32)
+def two_halves(rows, stride):
+    return pltpu.VMEM((2, rows + -(-stride // 8) * 8, LANES), F32)
 
 
 def units_kernel(fc_in, gc_in, video_in, gloss_in, v_out, g_out, g_one, count_out, fc, gc, video, gloss, v_scr, g_scr, sems):
@@ -532,8 +532,8 @@
                 pltpu.SMEM((OWN,), jnp.int32),
                 pltpu.VMEM((OWN, FRAMES, WIDTH), BF16),
                 pltpu.VMEM((OWN, GLOSSES, WIDTH), BF16),
-                two_halves(VOWN),
-                two_halves(GOWN),
+                two_halves(VOWN, OWN),
+                two_halves(GOWN, OWN),
                 pltpu.SemaphoreType.DMA((4,)),
             ],
             compiler_params=params(),
@@ -565,8 +565,8 @@
             scratch_shapes=[
                 pltpu.VMEM((VROWS, WIDTH), BF16),
                 pltpu.VMEM((GROWS, WIDTH), BF16),
-                two_halves(NZC * V_PITCH),
-                two_halves(NXY * G_PITCH),
+                two_halves(NZC * V_PITCH, V_PITCH),
+                two_halves(NXY * G_PITCH, G_PITCH),
                 pltpu.VMEM((VROWS, LANES), F32),
                 pltpu.VMEM((TILES, 1, LANES), F32),
                 pltpu.VMEM((VROWS, 3 * LANES), F32),
@@ -648,7 +648,7 @@
             out_shape=(shape(NXY, GOWN, WIDTH, dtype=BF16), shape(1, LANES)),
             scratch_shapes=[
                 pltpu.VMEM((GLOSSES, TEXTS_DEV, 2 * WIDTH), F32),
-                two_halves(NXY * G_PITCH),
+                two_halves(NXY * G_PITCH, G_PITCH),
                 pltpu.SemaphoreType.DMA((QUADS,)),
             ],
             compiler_params=params(),
@@ -665,7 +665,7 @@
             clip_rows_kernel,
             in_specs=[vmem] * 2,
             out_shape=kept_and_sent(NZ // 2),
-            scratch_shapes=[two_halves(NZ * V_PITCH)],
+            scratch_shapes=[two_halves(NZ * V_PITCH, V_PITCH)],
             compiler_params=params(),
             cost_estimate=cost(1e6, 2e6),
         )(mine, to_core(twin))
@@ -693,7 +693,7 @@
             gloss_grad_kernel,
             in_specs=[vmem] * 3,
             out_shape=shape(OWN, GLOSSES, WIDTH),
-            scratch_shapes=[two_halves(GOWN)],
+            scratch_shapes=[two_halves(GOWN, OWN)],
             compiler_params=params(),
             cost_estimate=cost(1e6, 1e6),
         )(dg_got, dg_diag, gloss)
@@ -704,7 +704,7 @@
             functools.partial(video_grad_kernel, clips),
             in_specs=[vmem] * 7,
             out_shape=(shape(OWN, FRAMES, WIDTH), shape(1, 1)),
-            scratch_shapes=[two_halves(VOWN)],
+            scratch_shapes=[two_halves(VOWN, OWN)],
             compiler_params=params(),
             cost_estimate=cost(1e6, 1e6),
         )(mine, *[to_z(a, 2 * m) for m, a in enumerate(sent, start=1)], c_row, dv_diag, video)

time: 123 us -> 123 us (level)
  no operation moved by 1% of the time
where the time goes in v12:
time: 123 us
  starting transfers between devices  51.3 us (42%)
  Pallas kernels  30.7 us (25%)
  blocking collectives  28.2 us (23%)
  waiting for transfers between devices  11.9 us (10%)
    all_to_all x4, starting transfers between devices, exchanged(): lax.all_to_all(a, over_all, 0, 0, axis_index_groups=groups, tiled=True)  34.6 us
    all_gather x3, blocking collectives, gathered(): lax.all_gather(a, over_all, axis=0, axis_index_groups=groups, tiled=True)  28.2 us
    ppermute x4, starting transfers between devices, to_z(): lax.ppermute(a, 'outer', [(i, i ^ mask) for i in range(lax.axis_size('out...  14.7 us
    ppermute x4, waiting for transfers between devices, to_z(): lax.ppermute(a, 'outer', [(i, i ^ mask) for i in range(lax.axis_size('out...  8.71 us
    pallas_call x1, Pallas kernels, on_device(): pl.pallas_call(by_clip_kernel, grid=(2,), in_specs=[whole(1, LANES), pl.B...  7.71 us
    pallas_call x1, Pallas kernels, on_device(): pl.pallas_call(weights_kernel, in_specs=[hbm, hbm, vmem, vmem, vmem], out...  5.18 us
    pallas_call x1, Pallas kernels, on_device(): pl.pallas_call(forward_kernel, in_specs=[vmem] * 2, out_specs=[hbm] * 2 +...  5.09 us
    pallas_call x1, Pallas kernels, on_device(): pl.pallas_call(clip_send_kernel, in_specs=[vmem, vmem, hbm, hbm, vmem], o...  4.65 us
  transfers between devices with their start and end apart: 9, of which 4 were waited for; matrix products, arithmetic and copies ran while one was open for 0% of the time, Pallas kernels for 14%

profile of v12, /device:TPU:2, one launch (start us, length us, event | category | flops | bytes accessed | tf_op | source)
XLA Modules:
  0.0 122.8 jit_solution(9296631448043390351)
XLA Ops:
  0.6 1.9 %unit_tokens.1 = (bf16[96,256]{1,0:T(8,128)(2,1)S(1)}, bf16[32,48,256]{2,1,0:T(8,128)(2,1)}, bf16[48,256]{1,0:T(8,128)(2,1)S(1)}, s32[8,128]{1,0:T(8,128)S(1)}) custom-call(s32[3]{0:T(128)} %fc_in.1, s32[3]{0:T(128)} %gc_in.1, bf16[3,32,256]{2,1,0:T(8,128)(2,1)} %video.1, bf16[3,16,256]{2,1,0:T(8,128)(2,1)} %gloss.1), custom_call_target="tpu_custom_call" | custom-call | flops 200000 | bytes 700000 | tf_op jit(solution)/shard_map/unit_tokens/pallas_call | solution.py:521
  2.5 10.3 %all-to-all-start = ((bf16[32,48,256]{2,1,0:T(8,128)(2,1)}), bf16[32,48,256]{2,1,0:T(8,128)(2,1)S(1)}, u32[]{:S(2)}, u32[]{:S(2)}) async-start(bf16[32,48,256]{2,1,0:T(8,128)(2,1)} %get-tuple-element.41), calls=%async_computation | async-start | bytes 1572864 | tf_op jit(solution)/shard_map/gather/all_to_all | solution.py:512
  12.8 19.5 %all_gather.9 = bf16[384,256]{1,0:T(8,128)(2,1)S(1)} all-gather(bf16[96,256]{1,0:T(8,128)(2,1)S(1)} %get-tuple-element.65.v_ref), channel_id=1, replica_groups={{0,64,128,192},{32,96,160,224},{1,65,129,193},{33,97,161,225},{2,66,130..., dimensions={0}, use_global_device_ids=true | all-gather | bytes 245760 | tf_op jit(solution)/shard_map/gather/all_gather | solution.py:515
  32.3 6.3 %all_gather.10 = bf16[768,256]{1,0:T(8,128)(2,1)S(1)} all-gather(bf16[384,256]{1,0:T(8,128)(2,1)S(1)} %all_gather.9), channel_id=1, replica_groups={{0,32},{64,96},{128,160},{192,224},{1,33},{65,97},{129,161},{193,225},{..., dimensions={0}, use_global_device_ids=true | all-gather | bytes 589824 | tf_op jit(solution)/shard_map/gather/all_gather | solution.py:515
  38.6 2.4 %all_gather.11.v_got = bf16[1536,256]{1,0:T(8,128)(2,1)S(1)} all-gather(bf16[768,256]{1,0:T(8,128)(2,1)S(1)} %all_gather.10), channel_id=1, replica_groups={{0,1},{32,33},{64,65},{96,97},{128,129},{160,161},{192,193},{224,225},{..., dimensions={0}, use_global_device_ids=true | all-gather | bytes 1179648 | tf_op jit(solution)/shard_map/gather/all_gather | solution.py:515
  41.0 5.1 %forward.1 = (bf16[1536,256]{1,0:T(8,128)(2,1)}, bf16[1536,256]{1,0:T(8,128)(2,1)}, f32[1536,128]{1,0:T(8,128)S(1)}, f32[12,48,128]{2,1,0:T(8,128)S(1)}, f32[48,...) custom-call(bf16[1536,256]{1,0:T(8,128)(2,1)S(1)} %all_gather.11.v_got, ...), custom_call_target="tpu_custom_call" | custom-call | flops 1207959552 | bytes 8000000 | tf_op jit(solution)/shard_map/forward/pallas_call | solution.py:552
  46.0 5.5 %all-to-all-start.1 = ((f32[16,1,128]{2,1,0:T(1,128)}), f32[16,1,128]{2,1,0:T(1,128)S(1)}, u32[]{:S(2)}, u32[]{:S(2)}) async-start(f32[16,1,128]{2,1,0:T(1,128)} %get-tuple-element.42), calls=%async_computation.1 | async-start | bytes 16384 | tf_op jit(solution)/shard_map/row_sums/all_to_all | solution.py:512
  51.5 5.2 %weights.1.p_ref.p_hbm = bf16[2,1536,768]{2,1,0:T(8,128)(2,1)} custom-call(bf16[1536,256]{1,0:T(8,128)(2,1)} %get-tuple-element.46.v_hbm.v_ref, bf16[1536,256]{1,0:T(8,128)(2,1)} %get-tuple-element.47.g_hbm.g_ref, f32[1536,128]{1,0:T(8,128)S(1)} %get-tuple-element.48.row_ref, f32[12,48,128]{2,1,0:T(8,128)S(1)} %get-tuple-element.49.col_ref, ...), custom_call_target="tpu_custom_call" | custom-call | flops 1207959552 | bytes 12000000 | tf_op jit(solution)/shard_map/weights/pallas_call | solution.py:592
  56.7 2.3 %all-to-all-done.1.r_got = f32[16,1,128]{2,1,0:T(1,128)S(1)} async-done(((f32[16,1,128]{2,1,0:T(1,128)}), f32[16,1,128]{2,1,0:T(1,128)S(1)}, u32[]{:S(2)}, u32[]{:S(2)}) %all-to-all-start.1) | async-done | bytes 8224 | tf_op jit(solution)/shard_map/row_sums/all_to_all | solution.py:512
  59.0 0.7 row_sums.1
  59.8 9.9 %all-to-all-start.2 = ((f32[32,1,128]{2,1,0:T(1,128)}), f32[32,1,128]{2,1,0:T(1,128)S(1)}, u32[]{:S(2)}, u32[]{:S(2)}) async-start(f32[32,1,128]{2,1,0:T(1,128)} %get-tuple-element.44), calls=%async_computation.2 | async-start | bytes 32768 | tf_op jit(solution)/shard_map/column_sums/all_to_all | solution.py:512
  69.7 7.7 %by_clip.1 = (f32[16,96,512]{2,1,0:T(8,128)}, f32[1536,256]{1,0:T(8,128)S(1)}) custom-call(f32[1,128]{1,0:T(1,128)S(1)} %get-tuple-element.45.r_ref, bf16[2,1536,768]{2,1,0:T(8,128)(2,1)} %weights.1.p_ref.p_hbm, bf16[1536,256]{1,0:T(8,128)(2,1)} %get-tuple-element.46.v_hbm.v_ref, bf16[1536,256]{1,0:T(8,128)(2,1)} %get-tuple-element.47.g_hbm.g_ref), custom_call_target="tpu_custom_call" | custom-call | flops 3623878656 | bytes 14000000 | tf_op jit(solution)/shard_map/by_clip/pallas_call | solution.py:608
  77.4 0.8 all-to-all-done.2.c_got
  78.2 4.6 %clip_send.1 = (f32[784,256]{1,0:T(8,128)S(1)}, bf16[784,256]{1,0:T(8,128)(2,1)S(1)}) custom-call(f32[32,1,128]{2,1,0:T(1,128)S(1)} %all-to-all-done.2.c_got, f32[1,128]{1,0:T(1,128)S(1)} %get-tuple-element.45.r_ref, bf16[2,1536,768]{2,1,0:T(8,128)(2,1)} %weights.1.p_ref.p_hbm, bf16[1536,256]{1,0:T(8,128)(2,1)} %get-tuple-element.47.g_hbm.g_ref, ...), custom_call_target="tpu_custom_call" | custom-call | flops 1207959552 | bytes 10000000 | tf_op jit(solution)/shard_map/clip_send/pallas_call | solution.py:629
  82.9 1.9 %collective-permute-start = (bf16[784,256]{1,0:T(8,128)(2,1)S(1)}, bf16[784,256]{1,0:T(8,128)(2,1)S(1)}, u32[]{:S(2)}, u32[]{:S(2)}) collective-permute-start(bf16[784,256]{1,0:T(8,128)(2,1)S(1)} %get-tuple-element.54), channel_id=1, source_target_pairs={{0,1},{1,0},{2,3},{3,2},{4,5},{5,4},{6,7},{7,6},{8,9},{9,8},{10,11... | collective-permute-start | bytes 1204232 | tf_op jit(solution)/shard_map/clips_by_core/ppermute | solution.py:506
  84.8 3.0 %gloss_send.1 = (bf16[32,48,256]{2,1,0:T(8,128)(2,1)}, f32[1,128]{1,0:T(1,128)S(1)}) custom-call(f32[32,1,128]{2,1,0:T(1,128)S(1)} %all-to-all-done.2.c_got, f32[16,96,512]{2,1,0:T(8,128)} %get-tuple-element.62.by_clip), custom_call_target="tpu_custom_call" | custom-call | flops 2000000 | bytes 5000000 | tf_op jit(solution)/shard_map/gloss_send/pallas_call | solution.py:645
  87.7 9.0 %all-to-all-start.3 = ((bf16[32,48,256]{2,1,0:T(8,128)(2,1)}), bf16[32,48,256]{2,1,0:T(8,128)(2,1)S(1)}, u32[]{:S(2)}, u32[]{:S(2)}) async-start(bf16[32,48,256]{2,1,0:T(8,128)(2,1)} %get-tuple-element.63), calls=%async_computation.3 | async-start | bytes 1572864 | tf_op jit(solution)/shard_map/gloss_send/all_to_all | solution.py:512
  96.7 0.0 collective-permute-done.got
  96.7 0.2 clips_by_core.1
  97.0 2.5 %collective-permute-start.1 = (bf16[400,256]{1,0:T(8,128)(2,1)S(1)}, bf16[400,256]{1,0:T(8,128)(2,1)S(1)}, u32[]{:S(2)}, u32[]{:S(2)}) collective-permute-start(bf16[400,256]{1,0:T(8,128)(2,1)S(1)} %get-tuple-element.56), channel_id=1, source_target_pairs={{0,32},{32,0},{64,96},{96,64},{128,160},{160,128},{192,224},{224,1... | collective-permute-start | bytes 614408 | tf_op jit(solution)/shard_map/clips_by_z/ppermute | solution.py:509
  99.5 6.3 %collective-permute-done.1.got = bf16[400,256]{1,0:T(8,128)(2,1)S(1)} collective-permute-done((bf16[400,256]{1,0:T(8,128)(2,1)S(1)}, bf16[400,256]{1,0:T(8,128)(2,1)S(1)}, u32[]{:S(2)}, u32[]{:S(2)}) %collective-permute-start.1) | collective-permute-done | bytes 204832 | tf_op jit(solution)/shard_map/clips_by_z/ppermute | solution.py:509
  105.8 0.1 clips_by_z.1
  105.9 2.5 %collective-permute-start.2 = (bf16[112,256]{1,0:T(8,128)(2,1)S(1)}, bf16[112,256]{1,0:T(8,128)(2,1)S(1)}, u32[]{:S(2)}, u32[]{:S(2)}) collective-permute-start(bf16[112,256]{1,0:T(8,128)(2,1)S(1)} %get-tuple-element.69), channel_id=1, source_target_pairs={{0,64},{32,96},{64,0},{96,32},{128,192},{160,224},{192,128},{224,1... | collective-permute-start | bytes 172040 | tf_op jit(solution)/shard_map/video_grad/ppermute | solution.py:509
  108.4 5.4 %collective-permute-start.3 = (bf16[112,256]{1,0:T(8,128)(2,1)S(1)}, bf16[112,256]{1,0:T(8,128)(2,1)S(1)}, u32[]{:S(2)}, u32[]{:S(2)}) collective-permute-start(bf16[112,256]{1,0:T(8,128)(2,1)S(1)} %get-tuple-element.70), channel_id=1, source_target_pairs={{0,128},{32,160},{64,192},{96,224},{128,0},{160,32},{192,64},{224,... | collective-permute-start | bytes 172040 | tf_op jit(solution)/shard_map/video_grad/ppermute | solution.py:509
  113.8 4.3 %collective-permute-start.4 = (bf16[112,256]{1,0:T(8,128)(2,1)S(1)}, bf16[112,256]{1,0:T(8,128)(2,1)S(1)}, u32[]{:S(2)}, u32[]{:S(2)}) collective-permute-start(bf16[112,256]{1,0:T(8,128)(2,1)S(1)} %get-tuple-element.71), channel_id=1, source_target_pairs={{0,192},{32,224},{64,128},{96,160},{128,64},{160,96},{192,0},{224,... | collective-permute-start | bytes 172040 | tf_op jit(solution)/shard_map/video_grad/ppermute | solution.py:509
  118.2 0.6 diagonal.1
  118.8 0.0 all-to-all-done.3.got
  118.8 0.8 gloss_grad.1
  119.6 0.0 collective-permute-done.2.got1
  119.6 0.0 collective-permute-done.3.got2
  119.6 2.4 %collective-permute-done.4.got3 = bf16[112,256]{1,0:T(8,128)(2,1)S(1)} collective-permute-done((bf16[112,256]{1,0:T(8,128)(2,1)S(1)}, bf16[112,256]{1,0:T(8,128)(2,1)S(1)}, u32[]{:S(2)}, u32[]{:S(2)}) %collective-permute-start.4) | collective-permute-done | bytes 57376 | tf_op jit(solution)/shard_map/video_grad/ppermute | solution.py:509
  122.0 0.8 video_grad.1
  (5 shorter events, 0.0 us)
Async XLA Ops:
  2.5 38.4 %all-to-all-start = ((bf16[32,48,256]{2,1,0:T(8,128)(2,1)}), bf16[32,48,256]{2,1,0:T(8,128)(2,1)S(1)}, u32[]{:S(2)}, u32[]{:S(2)}) async-start(bf16[32,48,256]{2,1,0:T(8,128)(2,1)} %get-tuple-element.41), calls=%async_computation | async-start | bytes 1572864 | tf_op jit(solution)/shard_map/gather/all_to_all | solution.py:512
  46.0 13.0 %all-to-all-start.1 = ((f32[16,1,128]{2,1,0:T(1,128)}), f32[16,1,128]{2,1,0:T(1,128)S(1)}, u32[]{:S(2)}, u32[]{:S(2)}) async-start(f32[16,1,128]{2,1,0:T(1,128)} %get-tuple-element.42), calls=%async_computation.1 | async-start | bytes 16384 | tf_op jit(solution)/shard_map/row_sums/all_to_all | solution.py:512
  59.8 18.4 %all-to-all-start.2 = ((f32[32,1,128]{2,1,0:T(1,128)}), f32[32,1,128]{2,1,0:T(1,128)S(1)}, u32[]{:S(2)}, u32[]{:S(2)}) async-start(f32[32,1,128]{2,1,0:T(1,128)} %get-tuple-element.44), calls=%async_computation.2 | async-start | bytes 32768 | tf_op jit(solution)/shard_map/column_sums/all_to_all | solution.py:512
  82.9 13.9 %collective-permute-start = (bf16[784,256]{1,0:T(8,128)(2,1)S(1)}, bf16[784,256]{1,0:T(8,128)(2,1)S(1)}, u32[]{:S(2)}, u32[]{:S(2)}) collective-permute-start(bf16[784,256]{1,0:T(8,128)(2,1)S(1)} %get-tuple-element.54), channel_id=1, source_target_pairs={{0,1},{1,0},{2,3},{3,2},{4,5},{5,4},{6,7},{7,6},{8,9},{9,8},{10,11... | collective-permute-start | bytes 1204232 | tf_op jit(solution)/shard_map/clips_by_core/ppermute | solution.py:506
  87.7 31.0 %all-to-all-start.3 = ((bf16[32,48,256]{2,1,0:T(8,128)(2,1)}), bf16[32,48,256]{2,1,0:T(8,128)(2,1)S(1)}, u32[]{:S(2)}, u32[]{:S(2)}) async-start(bf16[32,48,256]{2,1,0:T(8,128)(2,1)} %get-tuple-element.63), calls=%async_computation.3 | async-start | bytes 1572864 | tf_op jit(solution)/shard_map/gloss_send/all_to_all | solution.py:512
  97.0 8.8 %collective-permute-start.1 = (bf16[400,256]{1,0:T(8,128)(2,1)S(1)}, bf16[400,256]{1,0:T(8,128)(2,1)S(1)}, u32[]{:S(2)}, u32[]{:S(2)}) collective-permute-start(bf16[400,256]{1,0:T(8,128)(2,1)S(1)} %get-tuple-element.56), channel_id=1, source_target_pairs={{0,32},{32,0},{64,96},{96,64},{128,160},{160,128},{192,224},{224,1... | collective-permute-start | bytes 614408 | tf_op jit(solution)/shard_map/clips_by_z/ppermute | solution.py:509
  105.8 13.0 %copy-start.1 = (bf16[3,16,256]{2,1,0:T(8,128)(2,1)S(1)}, bf16[3,16,256]{2,1,0:T(8,128)(2,1)}, u32[]{:S(2)}) copy-start(bf16[3,16,256]{2,1,0:T(8,128)(2,1)} %gloss.1) | copy-start | bytes 73732
  105.8 16.2 %copy-start = (bf16[3,32,256]{2,1,0:T(8,128)(2,1)S(1)}, bf16[3,32,256]{2,1,0:T(8,128)(2,1)}, u32[]{:S(2)}) copy-start(bf16[3,32,256]{2,1,0:T(8,128)(2,1)} %video.1) | copy-start | bytes 147460
  105.9 13.7 %collective-permute-start.2 = (bf16[112,256]{1,0:T(8,128)(2,1)S(1)}, bf16[112,256]{1,0:T(8,128)(2,1)S(1)}, u32[]{:S(2)}, u32[]{:S(2)}) collective-permute-start(bf16[112,256]{1,0:T(8,128)(2,1)S(1)} %get-tuple-element.69), channel_id=1, source_target_pairs={{0,64},{32,96},{64,0},{96,32},{128,192},{160,224},{192,128},{224,1... | collective-permute-start | bytes 172040 | tf_op jit(solution)/shard_map/video_grad/ppermute | solution.py:509
  108.4 11.2 %collective-permute-start.3 = (bf16[112,256]{1,0:T(8,128)(2,1)S(1)}, bf16[112,256]{1,0:T(8,128)(2,1)S(1)}, u32[]{:S(2)}, u32[]{:S(2)}) collective-permute-start(bf16[112,256]{1,0:T(8,128)(2,1)S(1)} %get-tuple-element.70), channel_id=1, source_target_pairs={{0,128},{32,160},{64,192},{96,224},{128,0},{160,32},{192,64},{224,... | collective-permute-start | bytes 172040 | tf_op jit(solution)/shard_map/video_grad/ppermute | solution.py:509
  113.8 8.2 %collective-permute-start.4 = (bf16[112,256]{1,0:T(8,128)(2,1)S(1)}, bf16[112,256]{1,0:T(8,128)(2,1)S(1)}, u32[]{:S(2)}, u32[]{:S(2)}) collective-permute-start(bf16[112,256]{1,0:T(8,128)(2,1)S(1)} %get-tuple-element.71), channel_id=1, source_target_pairs={{0,192},{32,224},{64,128},{96,160},{128,64},{160,96},{192,0},{224,... | collective-permute-start | bytes 172040 | tf_op jit(solution)/shard_map/video_grad/ppermute | solution.py:509

commit v13 on v12

--- a/solution.py
+++ b/solution.py
@@ -353,7 +353,7 @@
             both[at, :WIDTH] = v
             both[at, WIDTH:] = (v.astype(F32) * inverse).astype(BF16)
 
-    out[...] = tn(p_ref[0], both[...]).reshape(GLOSSES // 2, TEXTS_DEV, 2 * WIDTH)
+    out[...] = tn(p_ref[0], both[...]).astype(BF16).reshape(GLOSSES // 2, TEXTS_DEV, 2 * WIDTH)
     part = nn(p_ref[0], g_ref[...])
 
     @pl.when(step == 0)
@@ -379,7 +379,8 @@
         copy.wait()
         for k in range(many):
             g = q * many + k
-            block = held[g, :, :WIDTH] * col + held[g, :, WIDTH:]
+            both = held[g].astype(F32)
+            block = both[:, :WIDTH] * col + both[:, WIDTH:]
             row = g * OWN
             for x in range(NX):
                 for c in range(OWN):
@@ -618,7 +619,7 @@
                 pl.BlockSpec((GLOSSES // 2, TEXTS_DEV, 2 * WIDTH), lambda i: (i, 0, 0)),
                 whole(VROWS, WIDTH),
             ),
-            out_shape=(pltpu.HBM((GLOSSES, TEXTS_DEV, 2 * WIDTH), F32), shape(VROWS, WIDTH)),
+            out_shape=(pltpu.HBM((GLOSSES, TEXTS_DEV, 2 * WIDTH), BF16), shape(VROWS, WIDTH)),
             scratch_shapes=[pltpu.VMEM((VROWS, 2 * WIDTH), BF16)],
             compiler_params=params(),
             cost_estimate=cost(6 * VROWS * GROWS * WIDTH, 14e6),
@@ -647,7 +648,7 @@
             in_specs=[vmem, hbm],
             out_shape=(shape(NXY, GOWN, WIDTH, dtype=BF16), shape(1, LANES)),
             scratch_shapes=[
-                pltpu.VMEM((GLOSSES, TEXTS_DEV, 2 * WIDTH), F32),
+                pltpu.VMEM((GLOSSES, TEXTS_DEV, 2 * WIDTH), BF16),
                 two_halves(NXY * G_PITCH, G_PITCH),
                 pltpu.SemaphoreType.DMA((QUADS,)),
             ],

time: 123 us -> 123 us (level)
  no operation moved by 1% of the time
where the time goes in v13:
time: 123 us; the launch traced here: 122 us
  starting transfers between devices  51 us (41%)
  Pallas kernels  29.9 us (24%)
  blocking collectives  28.2 us (23%)
  waiting for transfers between devices  12.1 us (10%)
    all_to_all x4, starting transfers between devices, exchanged(): lax.all_to_all(a, over_all, 0, 0, axis_index_groups=groups, tiled=True)  34.4 us
    all_gather x3, blocking collectives, gathered(): lax.all_gather(a, over_all, axis=0, axis_index_groups=groups, tiled=True)  28.2 us
    ppermute x4, starting transfers between devices, to_z(): lax.ppermute(a, 'outer', [(i, i ^ mask) for i in range(lax.axis_size('out...  14.7 us
    ppermute x4, waiting for transfers between devices, to_z(): lax.ppermute(a, 'outer', [(i, i ^ mask) for i in range(lax.axis_size('out...  8.71 us
    pallas_call x1, Pallas kernels, on_device(): pl.pallas_call(by_clip_kernel, grid=(2,), in_specs=[whole(1, LANES), pl.B...  7.47 us
    pallas_call x1, Pallas kernels, on_device(): pl.pallas_call(weights_kernel, in_specs=[hbm, hbm, vmem, vmem, vmem], out...  5.18 us
    pallas_call x1, Pallas kernels, on_device(): pl.pallas_call(forward_kernel, in_specs=[vmem] * 2, out_specs=[hbm] * 2 +...  4.99 us
    pallas_call x1, Pallas kernels, on_device(): pl.pallas_call(clip_send_kernel, in_specs=[vmem, vmem, hbm, hbm, vmem], o...  4.65 us
  transfers between devices with their start and end apart: 9, of which 4 were waited for; matrix products, arithmetic and copies ran while one was open for 0% of the time, Pallas kernels for 14%

profile of v13, /device:TPU:2, one launch (start us, length us, event | category | flops | bytes accessed | tf_op | source)
XLA Modules:
  0.0 122.0 jit_solution(13950654622331469032)
XLA Ops:
  0.6 1.9 %unit_tokens.1 = (bf16[96,256]{1,0:T(8,128)(2,1)S(1)}, bf16[32,48,256]{2,1,0:T(8,128)(2,1)}, bf16[48,256]{1,0:T(8,128)(2,1)S(1)}, s32[8,128]{1,0:T(8,128)S(1)}) custom-call(s32[3]{0:T(128)} %fc_in.1, s32[3]{0:T(128)} %gc_in.1, bf16[3,32,256]{2,1,0:T(8,128)(2,1)} %video.1, bf16[3,16,256]{2,1,0:T(8,128)(2,1)} %gloss.1), custom_call_target="tpu_custom_call" | custom-call | flops 200000 | bytes 700000 | tf_op jit(solution)/shard_map/unit_tokens/pallas_call | solution.py:522
  2.5 10.3 %all-to-all-start = ((bf16[32,48,256]{2,1,0:T(8,128)(2,1)}), bf16[32,48,256]{2,1,0:T(8,128)(2,1)S(1)}, u32[]{:S(2)}, u32[]{:S(2)}) async-start(bf16[32,48,256]{2,1,0:T(8,128)(2,1)} %get-tuple-element.41), calls=%async_computation | async-start | bytes 1572864 | tf_op jit(solution)/shard_map/gather/all_to_all | solution.py:513
  12.8 19.5 %all_gather.9 = bf16[384,256]{1,0:T(8,128)(2,1)S(1)} all-gather(bf16[96,256]{1,0:T(8,128)(2,1)S(1)} %get-tuple-element.65.v_ref), channel_id=1, replica_groups={{0,64,128,192},{32,96,160,224},{1,65,129,193},{33,97,161,225},{2,66,130..., dimensions={0}, use_global_device_ids=true | all-gather | bytes 245760 | tf_op jit(solution)/shard_map/gather/all_gather | solution.py:516
  32.3 6.3 %all_gather.10 = bf16[768,256]{1,0:T(8,128)(2,1)S(1)} all-gather(bf16[384,256]{1,0:T(8,128)(2,1)S(1)} %all_gather.9), channel_id=1, replica_groups={{0,32},{64,96},{128,160},{192,224},{1,33},{65,97},{129,161},{193,225},{..., dimensions={0}, use_global_device_ids=true | all-gather | bytes 589824 | tf_op jit(solution)/shard_map/gather/all_gather | solution.py:516
  38.6 2.4 %all_gather.11.v_got = bf16[1536,256]{1,0:T(8,128)(2,1)S(1)} all-gather(bf16[768,256]{1,0:T(8,128)(2,1)S(1)} %all_gather.10), channel_id=1, replica_groups={{0,1},{32,33},{64,65},{96,97},{128,129},{160,161},{192,193},{224,225},{..., dimensions={0}, use_global_device_ids=true | all-gather | bytes 1179648 | tf_op jit(solution)/shard_map/gather/all_gather | solution.py:516
  40.9 0.0 all-to-all-done.g_got
  41.0 5.0 %forward.1 = (bf16[1536,256]{1,0:T(8,128)(2,1)}, bf16[1536,256]{1,0:T(8,128)(2,1)}, f32[1536,128]{1,0:T(8,128)S(1)}, f32[12,48,128]{2,1,0:T(8,128)S(1)}, f32[48,...) custom-call(bf16[1536,256]{1,0:T(8,128)(2,1)S(1)} %all_gather.11.v_got, ...), custom_call_target="tpu_custom_call" | custom-call | flops 1207959552 | bytes 8000000 | tf_op jit(solution)/shard_map/forward/pallas_call | solution.py:553
  45.9 5.5 %all-to-all-start.1 = ((f32[16,1,128]{2,1,0:T(1,128)}), f32[16,1,128]{2,1,0:T(1,128)S(1)}, u32[]{:S(2)}, u32[]{:S(2)}) async-start(f32[16,1,128]{2,1,0:T(1,128)} %get-tuple-element.42), calls=%async_computation.1 | async-start | bytes 16384 | tf_op jit(solution)/shard_map/row_sums/all_to_all | solution.py:513
  51.4 5.2 %weights.1.p_ref.p_hbm = bf16[2,1536,768]{2,1,0:T(8,128)(2,1)} custom-call(bf16[1536,256]{1,0:T(8,128)(2,1)} %get-tuple-element.46.v_hbm.v_ref, bf16[1536,256]{1,0:T(8,128)(2,1)} %get-tuple-element.47.g_hbm.g_ref, f32[1536,128]{1,0:T(8,128)S(1)} %get-tuple-element.48.row_ref, f32[12,48,128]{2,1,0:T(8,128)S(1)} %get-tuple-element.49.col_ref, ...), custom_call_target="tpu_custom_call" | custom-call | flops 1207959552 | bytes 12000000 | tf_op jit(solution)/shard_map/weights/pallas_call | solution.py:593
  56.6 2.3 %all-to-all-done.1.r_got = f32[16,1,128]{2,1,0:T(1,128)S(1)} async-done(((f32[16,1,128]{2,1,0:T(1,128)}), f32[16,1,128]{2,1,0:T(1,128)S(1)}, u32[]{:S(2)}, u32[]{:S(2)}) %all-to-all-start.1) | async-done | bytes 8224 | tf_op jit(solution)/shard_map/row_sums/all_to_all | solution.py:513
  58.9 0.7 row_sums.1
  59.7 9.9 %all-to-all-start.2 = ((f32[32,1,128]{2,1,0:T(1,128)}), f32[32,1,128]{2,1,0:T(1,128)S(1)}, u32[]{:S(2)}, u32[]{:S(2)}) async-start(f32[32,1,128]{2,1,0:T(1,128)} %get-tuple-element.44), calls=%async_computation.2 | async-start | bytes 32768 | tf_op jit(solution)/shard_map/column_sums/all_to_all | solution.py:513
  69.6 7.5 %by_clip.1 = (bf16[16,96,512]{2,1,0:T(8,128)(2,1)}, f32[1536,256]{1,0:T(8,128)S(1)}) custom-call(f32[1,128]{1,0:T(1,128)S(1)} %get-tuple-element.45.r_ref, bf16[2,1536,768]{2,1,0:T(8,128)(2,1)} %weights.1.p_ref.p_hbm, bf16[1536,256]{1,0:T(8,128)(2,1)} %get-tuple-element.46.v_hbm.v_ref, bf16[1536,256]{1,0:T(8,128)(2,1)} %get-tuple-element.47.g_hbm.g_ref), custom_call_target="tpu_custom_call" | custom-call | flops 3623878656 | bytes 14000000 | tf_op jit(solution)/shard_map/by_clip/pallas_call | solution.py:609
  77.0 1.1 all-to-all-done.2.c_got
  78.1 4.6 %clip_send.1 = (f32[784,256]{1,0:T(8,128)S(1)}, bf16[784,256]{1,0:T(8,128)(2,1)S(1)}) custom-call(f32[32,1,128]{2,1,0:T(1,128)S(1)} %all-to-all-done.2.c_got, f32[1,128]{1,0:T(1,128)S(1)} %get-tuple-element.45.r_ref, bf16[2,1536,768]{2,1,0:T(8,128)(2,1)} %weights.1.p_ref.p_hbm, bf16[1536,256]{1,0:T(8,128)(2,1)} %get-tuple-element.47.g_hbm.g_ref, ...), custom_call_target="tpu_custom_call" | custom-call | flops 1207959552 | bytes 10000000 | tf_op jit(solution)/shard_map/clip_send/pallas_call | solution.py:630
  82.8 1.9 %collective-permute-start = (bf16[784,256]{1,0:T(8,128)(2,1)S(1)}, bf16[784,256]{1,0:T(8,128)(2,1)S(1)}, u32[]{:S(2)}, u32[]{:S(2)}) collective-permute-start(bf16[784,256]{1,0:T(8,128)(2,1)S(1)} %get-tuple-element.54), channel_id=1, source_target_pairs={{0,1},{1,0},{2,3},{3,2},{4,5},{5,4},{6,7},{7,6},{8,9},{9,8},{10,11... | collective-permute-start | bytes 1204232 | tf_op jit(solution)/shard_map/clips_by_core/ppermute | solution.py:507
  84.7 2.5 %gloss_send.1 = (bf16[32,48,256]{2,1,0:T(8,128)(2,1)}, f32[1,128]{1,0:T(1,128)S(1)}) custom-call(f32[32,1,128]{2,1,0:T(1,128)S(1)} %all-to-all-done.2.c_got, bf16[16,96,512]{2,1,0:T(8,128)(2,1)} %get-tuple-element.62.by_clip), custom_call_target="tpu_custom_call" | custom-call | flops 2000000 | bytes 5000000 | tf_op jit(solution)/shard_map/gloss_send/pallas_call | solution.py:646
  87.2 8.7 %all-to-all-start.3 = ((bf16[32,48,256]{2,1,0:T(8,128)(2,1)}), bf16[32,48,256]{2,1,0:T(8,128)(2,1)S(1)}, u32[]{:S(2)}, u32[]{:S(2)}) async-start(bf16[32,48,256]{2,1,0:T(8,128)(2,1)} %get-tuple-element.63), calls=%async_computation.3 | async-start | bytes 1572864 | tf_op jit(solution)/shard_map/gloss_send/all_to_all | solution.py:513
  95.9 0.0 collective-permute-done.got
  95.9 0.2 clips_by_core.1
  96.1 2.5 %collective-permute-start.1 = (bf16[400,256]{1,0:T(8,128)(2,1)S(1)}, bf16[400,256]{1,0:T(8,128)(2,1)S(1)}, u32[]{:S(2)}, u32[]{:S(2)}) collective-permute-start(bf16[400,256]{1,0:T(8,128)(2,1)S(1)} %get-tuple-element.56), channel_id=1, source_target_pairs={{0,32},{32,0},{64,96},{96,64},{128,160},{160,128},{192,224},{224,1... | collective-permute-start | bytes 614408 | tf_op jit(solution)/shard_map/clips_by_z/ppermute | solution.py:510
  98.7 6.3 %collective-permute-done.1.got = bf16[400,256]{1,0:T(8,128)(2,1)S(1)} collective-permute-done((bf16[400,256]{1,0:T(8,128)(2,1)S(1)}, bf16[400,256]{1,0:T(8,128)(2,1)S(1)}, u32[]{:S(2)}, u32[]{:S(2)}) %collective-permute-start.1) | collective-permute-done | bytes 204832 | tf_op jit(solution)/shard_map/clips_by_z/ppermute | solution.py:510
  105.0 0.1 clips_by_z.1
  105.1 2.5 %collective-permute-start.2 = (bf16[112,256]{1,0:T(8,128)(2,1)S(1)}, bf16[112,256]{1,0:T(8,128)(2,1)S(1)}, u32[]{:S(2)}, u32[]{:S(2)}) collective-permute-start(bf16[112,256]{1,0:T(8,128)(2,1)S(1)} %get-tuple-element.69), channel_id=1, source_target_pairs={{0,64},{32,96},{64,0},{96,32},{128,192},{160,224},{192,128},{224,1... | collective-permute-start | bytes 172040 | tf_op jit(solution)/shard_map/video_grad/ppermute | solution.py:510
  107.6 5.4 %collective-permute-start.3 = (bf16[112,256]{1,0:T(8,128)(2,1)S(1)}, bf16[112,256]{1,0:T(8,128)(2,1)S(1)}, u32[]{:S(2)}, u32[]{:S(2)}) collective-permute-start(bf16[112,256]{1,0:T(8,128)(2,1)S(1)} %get-tuple-element.70), channel_id=1, source_target_pairs={{0,128},{32,160},{64,192},{96,224},{128,0},{160,32},{192,64},{224,... | collective-permute-start | bytes 172040 | tf_op jit(solution)/shard_map/video_grad/ppermute | solution.py:510
  113.0 4.3 %collective-permute-start.4 = (bf16[112,256]{1,0:T(8,128)(2,1)S(1)}, bf16[112,256]{1,0:T(8,128)(2,1)S(1)}, u32[]{:S(2)}, u32[]{:S(2)}) collective-permute-start(bf16[112,256]{1,0:T(8,128)(2,1)S(1)} %get-tuple-element.71), channel_id=1, source_target_pairs={{0,192},{32,224},{64,128},{96,160},{128,64},{160,96},{192,0},{224,... | collective-permute-start | bytes 172040 | tf_op jit(solution)/shard_map/video_grad/ppermute | solution.py:510
  117.3 0.6 diagonal.1
  117.9 0.0 all-to-all-done.3.got
  118.0 0.8 gloss_grad.1
  118.8 0.0 collective-permute-done.2.got1
  118.8 2.4 %collective-permute-done.4.got3 = bf16[112,256]{1,0:T(8,128)(2,1)S(1)} collective-permute-done((bf16[112,256]{1,0:T(8,128)(2,1)S(1)}, bf16[112,256]{1,0:T(8,128)(2,1)S(1)}, u32[]{:S(2)}, u32[]{:S(2)}) %collective-permute-start.4) | collective-permute-done | bytes 57376 | tf_op jit(solution)/shard_map/video_grad/ppermute | solution.py:510
  121.2 0.8 video_grad.1
  (5 shorter events, 0.0 us)
Async XLA Ops:
  2.5 38.4 %all-to-all-start = ((bf16[32,48,256]{2,1,0:T(8,128)(2,1)}), bf16[32,48,256]{2,1,0:T(8,128)(2,1)S(1)}, u32[]{:S(2)}, u32[]{:S(2)}) async-start(bf16[32,48,256]{2,1,0:T(8,128)(2,1)} %get-tuple-element.41), calls=%async_computation | async-start | bytes 1572864 | tf_op jit(solution)/shard_map/gather/all_to_all | solution.py:513
  45.9 13.0 %all-to-all-start.1 = ((f32[16,1,128]{2,1,0:T(1,128)}), f32[16,1,128]{2,1,0:T(1,128)S(1)}, u32[]{:S(2)}, u32[]{:S(2)}) async-start(f32[16,1,128]{2,1,0:T(1,128)} %get-tuple-element.42), calls=%async_computation.1 | async-start | bytes 16384 | tf_op jit(solution)/shard_map/row_sums/all_to_all | solution.py:513
  59.7 18.4 %all-to-all-start.2 = ((f32[32,1,128]{2,1,0:T(1,128)}), f32[32,1,128]{2,1,0:T(1,128)S(1)}, u32[]{:S(2)}, u32[]{:S(2)}) async-start(f32[32,1,128]{2,1,0:T(1,128)} %get-tuple-element.44), calls=%async_computation.2 | async-start | bytes 32768 | tf_op jit(solution)/shard_map/column_sums/all_to_all | solution.py:513
  82.8 13.2 %collective-permute-start = (bf16[784,256]{1,0:T(8,128)(2,1)S(1)}, bf16[784,256]{1,0:T(8,128)(2,1)S(1)}, u32[]{:S(2)}, u32[]{:S(2)}) collective-permute-start(bf16[784,256]{1,0:T(8,128)(2,1)S(1)} %get-tuple-element.54), channel_id=1, source_target_pairs={{0,1},{1,0},{2,3},{3,2},{4,5},{5,4},{6,7},{7,6},{8,9},{9,8},{10,11... | collective-permute-start | bytes 1204232 | tf_op jit(solution)/shard_map/clips_by_core/ppermute | solution.py:507
  87.2 30.8 %all-to-all-start.3 = ((bf16[32,48,256]{2,1,0:T(8,128)(2,1)}), bf16[32,48,256]{2,1,0:T(8,128)(2,1)S(1)}, u32[]{:S(2)}, u32[]{:S(2)}) async-start(bf16[32,48,256]{2,1,0:T(8,128)(2,1)} %get-tuple-element.63), calls=%async_computation.3 | async-start | bytes 1572864 | tf_op jit(solution)/shard_map/gloss_send/all_to_all | solution.py:513
  96.1 8.8 %collective-permute-start.1 = (bf16[400,256]{1,0:T(8,128)(2,1)S(1)}, bf16[400,256]{1,0:T(8,128)(2,1)S(1)}, u32[]{:S(2)}, u32[]{:S(2)}) collective-permute-start(bf16[400,256]{1,0:T(8,128)(2,1)S(1)} %get-tuple-element.56), channel_id=1, source_target_pairs={{0,32},{32,0},{64,96},{96,64},{128,160},{160,128},{192,224},{224,1... | collective-permute-start | bytes 614408 | tf_op jit(solution)/shard_map/clips_by_z/ppermute | solution.py:510
  105.0 13.0 %copy-start.1 = (bf16[3,16,256]{2,1,0:T(8,128)(2,1)S(1)}, bf16[3,16,256]{2,1,0:T(8,128)(2,1)}, u32[]{:S(2)}) copy-start(bf16[3,16,256]{2,1,0:T(8,128)(2,1)} %gloss.1) | copy-start | bytes 73732
  105.0 16.3 %copy-start = (bf16[3,32,256]{2,1,0:T(8,128)(2,1)S(1)}, bf16[3,32,256]{2,1,0:T(8,128)(2,1)}, u32[]{:S(2)}) copy-start(bf16[3,32,256]{2,1,0:T(8,128)(2,1)} %video.1) | copy-start | bytes 147460
  105.1 13.7 %collective-permute-start.2 = (bf16[112,256]{1,0:T(8,128)(2,1)S(1)}, bf16[112,256]{1,0:T(8,128)(2,1)S(1)}, u32[]{:S(2)}, u32[]{:S(2)}) collective-permute-start(bf16[112,256]{1,0:T(8,128)(2,1)S(1)} %get-tuple-element.69), channel_id=1, source_target_pairs={{0,64},{32,96},{64,0},{96,32},{128,192},{160,224},{192,128},{224,1... | collective-permute-start | bytes 172040 | tf_op jit(solution)/shard_map/video_grad/ppermute | solution.py:510
  107.6 11.2 %collective-permute-start.3 = (bf16[112,256]{1,0:T(8,128)(2,1)S(1)}, bf16[112,256]{1,0:T(8,128)(2,1)S(1)}, u32[]{:S(2)}, u32[]{:S(2)}) collective-permute-start(bf16[112,256]{1,0:T(8,128)(2,1)S(1)} %get-tuple-element.70), channel_id=1, source_target_pairs={{0,128},{32,160},{64,192},{96,224},{128,0},{160,32},{192,64},{224,... | collective-permute-start | bytes 172040 | tf_op jit(solution)/shard_map/video_grad/ppermute | solution.py:510
  113.0 8.2 %collective-permute-start.4 = (bf16[112,256]{1,0:T(8,128)(2,1)S(1)}, bf16[112,256]{1,0:T(8,128)(2,1)S(1)}, u32[]{:S(2)}, u32[]{:S(2)}) collective-permute-start(bf16[112,256]{1,0:T(8,128)(2,1)S(1)} %get-tuple-element.71), channel_id=1, source_target_pairs={{0,192},{32,224},{64,128},{96,160},{128,64},{160,96},{192,0},{224,... | collective-permute-start | bytes 172040 | tf_op jit(solution)/shard_map/video_grad/ppermute | solution.py:510
